TPU v7x, 32 devices: a whole 2x2x4 slice. The times are simulated.
32 devices in a mesh: row: 4 (over y, x), seq: 2 (over core), pat: 4 (over z).
Axes of the slice: x: 2, y: 2, z: 4, core: 2. Of those that a mesh axis runs over, the one named last changes fastest.
Arguments:
- block_input: bfloat16 [4, 1024, 768], P('row', 'seq'), may hold values from -6 to 6
- doc_ids: int32 [4, 1024], P('row'), may hold values from 0 to 2, as said below
- ln1_gain: float32 [768], replicated, may hold values from 0.5 to 1.5
- ln1_bias: float32 [768], replicated, may hold values from -2 to 2
- w_query: bfloat16 [768, 768], replicated, may hold values from -0.21875 to 0.21875
- w_key: bfloat16 [768, 768], replicated, may hold values from -0.21875 to 0.21875
- w_value: bfloat16 [768, 768], replicated, may hold values from -0.21875 to 0.21875
- w_out: bfloat16 [768, 768], replicated, may hold values from -1.75 to 1.75
- ln2_gain: float32 [768], replicated, may hold values from 0.5 to 1.5
- ln2_bias: float32 [768], replicated, may hold values from -2 to 2
- w_up: bfloat16 [768, 3072], P(None, 'pat'), may hold values from -0.21875 to 0.21875
- w_down: bfloat16 [3072, 768], P('pat'), may hold values from -0.109375 to 0.109375
- cotangent: bfloat16 [4, 1024, 768], P('row', 'seq', 'pat'), may hold values from -6 to 6
Outputs:
- output: bfloat16 [4, 1024, 768], P('row', 'seq', 'pat')
- grad_input: bfloat16 [4, 1024, 768], P('row', ('seq', 'pat'))
- grad_ln1_gain: float32 [768], replicated
- grad_ln1_bias: float32 [768], replicated
- grad_query: float32 [768, 768], replicated
- grad_key: float32 [768, 768], replicated
- grad_value: float32 [768, 768], replicated
- grad_out: float32 [768, 768], replicated
- grad_ln2_gain: float32 [768], replicated
- grad_ln2_bias: float32 [768], replicated
- grad_up: float32 [768, 3072], P(None, 'pat')
- grad_down: float32 [3072, 768], P('pat')
Inputs may be any that keep to these rules, and one draw needn't show every extreme that they name: `doc_ids`: along each row the ids never fall.
All inputs are finite; a program needn't handle non-finite values.
Results may differ from a plain program's by a relative error of at most 0.02.
Values may be sent and summed in bfloat16 or wider, within the bound.
No kernel may reach another device: no remote copies, remote signals or barrier semaphores. Data moves between devices by JAX's collectives and lax.ppermute only.
A program may use at most 192 MiB of HBM per device.

v0:
```python
import jax
import jax.numpy as jnp
from jax import lax
from jax.sharding import PartitionSpec as P

D = 768
HEADS = 12
HDIM = 64


epsilon = 1e-05
masked_low = -1e30
segment_parts = (1, 2, 4, 8, 16)
dilations = (1, 2, 4, 6, 12)


def combined_all(shard, axis, join):
    gathered = jax.tree.map(
        lambda a, kind: lax.all_gather(a.astype(kind), axis),
        shard,
        (jnp.bfloat16, jnp.bfloat16, jnp.bfloat16),
    )

    def take(source):
        return jax.tree.map(
            lambda a, own: lax.dynamic_index_in_dim(a, source, 0, False).astype(own.dtype),
            gathered,
            shard,
        )

    return lax.fori_loop(
        1, lax.axis_size(axis), lambda source, state: join(state, take(source)), take(0)
    )


def layer_norm(values, gain, bias):
    center = values - jnp.mean(values, axis=-1, keepdims=True)
    spread = jnp.mean(center * center, axis=-1, keepdims=True)
    return center * lax.rsqrt(spread + epsilon) * gain + bias


def gelu_exact(values):
    return jax.nn.gelu(values, approximate=False)


def multiplicity(query_pos, key_pos, query_doc, key_doc, row_length, members):
    head_ids = jnp.arange(HEADS, dtype=jnp.int32)
    counted = jnp.zeros((HEADS, query_pos.shape[0], key_pos.shape[0]), jnp.float32)
    for pattern in range(5):
        seg_width = row_length * segment_parts[pattern] // 16
        dilation = dilations[pattern]
        offset = (head_ids % dilation)[:, None]
        same_segment = query_pos[:, None] // seg_width == key_pos[None, :] // seg_width
        query_in = ((query_pos % seg_width)[None, :] - offset) % dilation == 0
        key_in = ((key_pos % seg_width)[None, :] - offset) % dilation == 0
        covered = same_segment[None] & query_in[:, :, None] & key_in[:, None, :]
        counted = counted + members[pattern] * covered.astype(jnp.float32)
    allowed = (key_pos[None, :] <= query_pos[:, None]) & (query_doc[:, None] == key_doc[None, :])
    return counted * allowed[None].astype(jnp.float32)


def combine_parts(first, second):
    max_first, sum_first, acc_first = first
    max_second, sum_second, acc_second = second
    joint_max = jnp.maximum(max_first, max_second)
    scale_first = jnp.exp(max_first - joint_max)
    scale_second = jnp.exp(max_second - joint_max)
    rows_count = acc_first.shape[0]
    joined = (
        acc_first.reshape(rows_count, HEADS, HDIM) * scale_first.T[:, :, None]
        + acc_second.reshape(rows_count, HEADS, HDIM) * scale_second.T[:, :, None]
    )
    return (
        joint_max,
        sum_first * scale_first + sum_second * scale_second,
        joined.reshape(acc_first.shape),
    )


def per_device(
    block_input,
    doc_ids,
    ln1_gain,
    ln1_bias,
    w_query,
    w_key,
    w_value,
    w_out,
    ln2_gain,
    ln2_bias,
    w_up,
    w_down,
    cotangent,
):
    span = block_input.shape[1]
    seq_count = lax.axis_size("seq")
    pat_count = lax.axis_size("pat")
    seq_index = lax.axis_index("seq")
    pat_index = lax.axis_index("pat")
    row_length = span * seq_count
    quarter = span // pat_count
    scaling = HDIM ** (-0.5)
    members = [
        jnp.where(min(pattern, pat_count - 1) == pat_index, 1.0, 0.0).astype(jnp.float32)
        for pattern in range(5)
    ]
    row_docs = doc_ids[0]
    inputs = block_input[0].astype(jnp.float32)
    normed = layer_norm(inputs, ln1_gain, ln1_bias).astype(jnp.bfloat16)
    queries = jnp.dot(normed, w_query, preferred_element_type=jnp.float32).astype(jnp.bfloat16)
    keys = jnp.dot(normed, w_key, preferred_element_type=jnp.float32).astype(jnp.bfloat16)
    values = jnp.dot(normed, w_value, preferred_element_type=jnp.float32).astype(jnp.bfloat16)
    key_rows, value_rows = (
        lax.all_gather(keys, "seq", axis=0, tiled=True),
        lax.all_gather(values, "seq", axis=0, tiled=True),
    )
    query_heads = queries.reshape(span, HEADS, HDIM)

    def pair_active(query_piece, key_piece):
        covered = jnp.zeros((), jnp.bool_)
        for pattern in range(5):
            seg_width = row_length * segment_parts[pattern] // 16
            intersection = (
                (key_piece + 1) * span - 1
            ) // seg_width >= query_piece * span // seg_width
            covered = covered | intersection & (members[pattern] > 0)
        return (key_piece <= query_piece) & covered

    def tile_scores(query_piece, key_piece, query_source):
        key_piece_rows = lax.dynamic_slice_in_dim(key_rows, key_piece * span, span, 0).reshape(
            span, HEADS, HDIM
        )
        value_piece_rows = lax.dynamic_slice_in_dim(value_rows, key_piece * span, span, 0).reshape(
            span, HEADS, HDIM
        )
        key_pos = key_piece * span + jnp.arange(span, dtype=jnp.int32)
        key_doc = lax.dynamic_slice_in_dim(row_docs, key_piece * span, span, 0)
        query_pos = query_piece * span + jnp.arange(span, dtype=jnp.int32)
        query_doc = lax.dynamic_slice_in_dim(row_docs, query_piece * span, span, 0)
        scores = (
            jnp.einsum(
                "qhd,khd->hqk", query_source, key_piece_rows, preferred_element_type=jnp.float32
            )
            * scaling
        )
        counts = multiplicity(query_pos, key_pos, query_doc, key_doc, row_length, members)
        return (key_piece_rows, value_piece_rows, scores, counts)

    def forward_step(carry, piece):

        def forward_update(state):
            run_max, run_sum, run_acc = state
            key_piece, value_piece, scores, counts = tile_scores(seq_index, piece, query_heads)
            new_max = jnp.maximum(
                run_max, jnp.max(jnp.where(counts > 0, scores, masked_low), axis=2)
            )
            weights = counts * jnp.exp(jnp.where(counts > 0, scores - new_max[:, :, None], -60.0))
            factor = jnp.exp(run_max - new_max)
            new_sum = run_sum * factor + jnp.sum(weights, axis=2)
            added = jnp.einsum(
                "hqk,khd->qhd",
                weights.astype(jnp.bfloat16),
                value_piece,
                preferred_element_type=jnp.float32,
            )
            return (new_max, new_sum, run_acc * factor.T[:, :, None] + added)

        def unchanged(state):
            return state

        return (lax.cond(pair_active(seq_index, piece), forward_update, unchanged, carry), None)

    start_state = (
        jnp.full((HEADS, span), masked_low, jnp.float32),
        jnp.zeros((HEADS, span), jnp.float32),
        jnp.zeros((span, HEADS, HDIM), jnp.float32),
    )
    pieces = jnp.arange(seq_count, dtype=jnp.int32)
    final_state = lax.scan(forward_step, start_state, pieces)[0]
    total_max, total_sum, total_acc = combined_all(
        (final_state[0], final_state[1], final_state[2].reshape(span, D)), "pat", combine_parts
    )
    attn_out = total_acc.reshape(span, HEADS, HDIM) / total_sum.T[:, :, None]
    log_total = total_max + jnp.log(total_sum)
    mixed_low = attn_out.reshape(span, D).astype(jnp.bfloat16)
    resid = inputs + jnp.dot(mixed_low, w_out, preferred_element_type=jnp.float32)
    normed_two, norm_back = jax.vjp(layer_norm, resid, ln2_gain, ln2_bias)
    normed_low = normed_two.astype(jnp.bfloat16)
    hidden = jnp.dot(normed_low, w_up, preferred_element_type=jnp.float32)
    activated, gelu_back = jax.vjp(gelu_exact, hidden)
    act_low = activated.astype(jnp.bfloat16)
    ffn_part = jnp.dot(act_low, w_down, preferred_element_type=jnp.float32)
    ffn_mine = lax.psum_scatter(
        ffn_part.astype(jnp.bfloat16), "pat", scatter_dimension=1, tiled=True
    ).astype(jnp.float32)
    width_part = D // pat_count
    resid_mine = lax.dynamic_slice_in_dim(resid, pat_index * width_part, width_part, 1)
    output = (resid_mine + ffn_mine).astype(jnp.bfloat16)[None]
    grad_full = lax.all_gather(cotangent[0], "pat", axis=1, tiled=True)
    grad_act = jnp.dot(grad_full, w_down.T, preferred_element_type=jnp.float32)
    grad_hidden = gelu_back(grad_act)[0].astype(jnp.bfloat16)
    grad_down = jnp.dot(act_low.T, grad_full, preferred_element_type=jnp.float32)
    grad_up = jnp.dot(normed_low.T, grad_hidden, preferred_element_type=jnp.float32)
    grad_normed_two = jnp.dot(grad_hidden, w_up.T, preferred_element_type=jnp.float32)
    resid_part, grad_gain_two, grad_bias_two = norm_back(grad_normed_two)
    grad_resid = grad_full.astype(jnp.float32) + lax.psum(
        resid_part.astype(jnp.bfloat16), "pat"
    ).astype(jnp.float32)
    grad_branch = grad_resid.astype(jnp.bfloat16)
    grad_mixed = (
        jnp.dot(grad_branch, w_out.T, preferred_element_type=jnp.float32)
        .reshape(span, HEADS, HDIM)
        .astype(jnp.bfloat16)
    )
    row_dot = jnp.sum(grad_mixed.astype(jnp.float32) * attn_out, axis=2).T

    def back_tile(query_piece, key_piece, query_source, grad_source, lse_source, dot_source):
        key_piece_rows, value_piece_rows, scores, counts = tile_scores(
            query_piece, key_piece, query_source
        )
        probs = counts * jnp.exp(jnp.where(counts > 0, scores - lse_source[:, :, None], -60.0))
        grad_probs = jnp.einsum(
            "qhd,khd->hqk", grad_source, value_piece_rows, preferred_element_type=jnp.float32
        )
        grad_scores = (probs * (grad_probs - dot_source[:, :, None])).astype(jnp.bfloat16)
        key_term = (
            jnp.einsum(
                "hqk,qhd->khd", grad_scores, query_source, preferred_element_type=jnp.float32
            )
            * scaling
        )
        value_term = jnp.einsum(
            "hqk,qhd->khd",
            probs.astype(jnp.bfloat16),
            grad_source,
            preferred_element_type=jnp.float32,
        )
        query_term = None
        query_term = (
            jnp.einsum(
                "hqk,khd->qhd", grad_scores, key_piece_rows, preferred_element_type=jnp.float32
            )
            * scaling
        )
        return (query_term, key_term.reshape(span, D), value_term.reshape(span, D))

    zero_query = jnp.zeros((span, HEADS, HDIM), jnp.float32)

    def backward_step(grad_now, piece):

        def backward_update(grad_then):
            query_term, key_term, value_term = back_tile(
                seq_index, piece, query_heads, grad_mixed, log_total, row_dot
            )
            return (grad_then + query_term, (key_term, value_term))

        def skipped(grad_then):
            return (
                grad_then,
                (jnp.zeros((span, D), jnp.float32), jnp.zeros((span, D), jnp.float32)),
            )

        return lax.cond(pair_active(seq_index, piece), backward_update, skipped, grad_now)

    grad_queries, stacked_terms = lax.scan(backward_step, zero_query, pieces)
    key_terms = stacked_terms[0].reshape(row_length, D)
    value_terms = stacked_terms[1].reshape(row_length, D)
    grad_keys, grad_values = (
        lax.psum_scatter(
            key_terms.astype(jnp.bfloat16), "seq", scatter_dimension=0, tiled=True
        ).astype(jnp.float32),
        lax.psum_scatter(
            value_terms.astype(jnp.bfloat16), "seq", scatter_dimension=0, tiled=True
        ).astype(jnp.float32),
    )
    query_part, key_part, value_part = (
        lax.psum_scatter(
            grad_queries.reshape(span, D).astype(jnp.bfloat16),
            "pat",
            scatter_dimension=0,
            tiled=True,
        ).astype(jnp.float32),
        lax.psum_scatter(
            grad_keys.astype(jnp.bfloat16), "pat", scatter_dimension=0, tiled=True
        ).astype(jnp.float32),
        lax.psum_scatter(
            grad_values.astype(jnp.bfloat16), "pat", scatter_dimension=0, tiled=True
        ).astype(jnp.float32),
    )
    query_low = query_part.astype(jnp.bfloat16)
    key_low = key_part.astype(jnp.bfloat16)
    value_low = value_part.astype(jnp.bfloat16)
    row_start = pat_index * quarter
    normed_rows = lax.dynamic_slice_in_dim(normed, row_start, quarter, 0)
    grad_wq = jnp.dot(normed_rows.T, query_low, preferred_element_type=jnp.float32)
    grad_wk = jnp.dot(normed_rows.T, key_low, preferred_element_type=jnp.float32)
    grad_wv = jnp.dot(normed_rows.T, value_low, preferred_element_type=jnp.float32)
    grad_normed = jnp.dot(query_low, w_query.T, preferred_element_type=jnp.float32)
    grad_normed = grad_normed + jnp.dot(key_low, w_key.T, preferred_element_type=jnp.float32)
    grad_normed = grad_normed + jnp.dot(value_low, w_value.T, preferred_element_type=jnp.float32)
    input_rows = lax.dynamic_slice_in_dim(inputs, row_start, quarter, 0)
    first_norm_back = jax.vjp(layer_norm, input_rows, ln1_gain, ln1_bias)[1]
    grad_through, grad_gain_one, grad_bias_one = first_norm_back(grad_normed)
    grad_input = (
        lax.dynamic_slice_in_dim(grad_resid, row_start, quarter, 0) + grad_through
    ).astype(jnp.bfloat16)[None]
    mixed_rows = lax.dynamic_slice_in_dim(mixed_low, row_start, quarter, 0)
    branch_rows = lax.dynamic_slice_in_dim(grad_branch, row_start, quarter, 0)
    grad_wout = jnp.dot(mixed_rows.T, branch_rows, preferred_element_type=jnp.float32)
    summed = lax.psum(
        (
            grad_wq,
            grad_wk,
            grad_wv,
            grad_wout,
            grad_gain_one,
            grad_bias_one,
            grad_gain_two,
            grad_bias_two,
        ),
        ("row", "seq", "pat"),
    )
    ffn_summed = lax.psum((grad_up, grad_down), ("row", "seq"))
    return (
        output,
        grad_input,
        summed[4],
        summed[5],
        summed[0],
        summed[1],
        summed[2],
        summed[3],
        summed[6],
        summed[7],
        ffn_summed[0],
        ffn_summed[1],
    )


def solution(mesh):
    placed = (
        P("row", "seq", None),
        P("row", None),
        P(),
        P(),
        P(),
        P(),
        P(),
        P(),
        P(),
        P(),
        P(None, "pat"),
        P("pat", None),
        P("row", "seq", "pat"),
    )
    return jax.shard_map(
        per_device,
        mesh=mesh,
        in_specs=placed,
        out_specs=(
            P("row", "seq", "pat"),
            P("row", ("seq", "pat"), None),
            P(),
            P(),
            P(),
            P(),
            P(),
            P(),
            P(),
            P(),
            P(None, "pat"),
            P("pat", None),
        ),
        check_vma=False,
    )
```

profile of v0, /device:TPU:0, one launch (start us, length us, event | category | flops | bytes accessed | tf_op | source)
XLA Modules:
  0.0 776.7 jit_solution(14207535731212306156)
XLA Ops:
  18.8 6.3 all-gather.9.cloned.1.call-done
  27.6 10.5 %all-gather.11.cloned.1.call-done = bf16[1024,768]{1,0:T(8,128)(2,1)} async-done(((bf16[512,768]{1,0:T(8,128)(2,1)}), bf16[1024,768]{1,0:T(8,128)(2,1)}) %all-gather.11.cloned.1.call-update) | async-done | bytes 1572880 | tf_op jit(solution)/shard_map/all_gather | solution.py:115
  41.4 37.9 %while.58 = (s32[]{:T(128)}, f32[12,512]{1,0:T(8,128)S(1)}, f32[12,512]{1,0:T(8,128)S(1)}, f32[512,12,64]{0,2,1:T(8,128)S(1)}, s32[2]{0:T(128)S(1)}, /*index=5*/...) while((s32[]{:T(128)}, f32[12,512]{1,0:T(8,128)S(1)}, ...), condition=%wide.region_7.8_spmd, body=%wide.region_2.7_spmd.sunk | while | flops 950905152 | bytes 72177344 | solution.py:179
  43.6 33.3 %conditional.4 = ((f32[12,512]{1,0:T(8,128)S(1)}, f32[12,512]{1,0:T(8,128)S(1)}, f32[512,12,64]{0,2,1:T(8,128)S(1)})) conditional(s32[]{:T(128)} %convert_element_type.318, (f32[12,512]{1,0:T(8,128)S(1)}, f32[12,512]{1,0:T(8,128)S(1)}, f32[512,12,64]{0,2,1:T(8,128)S(1)}) %tuple.183, (s32[]{:T(128)}, s32[]{:T(128)}, f32[]{:T(128)}, f32[]{:T(128)}, ...), branch_computations={%region_3.3_spmd, %region_4.6_spmd} | conditional | flops 950905088 | bytes 72176192 | solution.py:171
  47.4 12.2 %fusion = (f32[12,512]{1,0:T(8,128)S(1)}, f32[12,512,512]{2,1,0:T(8,128)S(1)}) fusion(f32[512,512]{0,1:T(8,128)S(1)} %and_convert_fusion, pred[12,512]{1,0:T(8,128)(4,1)S(1)} %fusion.15, pred[12,512]{1,0:T(8,128)(4,1)S(1)} %fusion.14, pred[512,512]{0,1:T(8,128)(4,1)S(1)} %broadcast_compare_fusion.1, f32[]{:T(128)} %get-tuple-element.1289, ...), kind=kOutput, calls=%fused_computation.2 | convolution fusion | flops 468707328 | bytes 17375244 | tf_op jit(solution)/shard_map/while/body/eval_jaxpr/cond/branch_1_fun/qhd,khd->hqk/dot_general | solution.py:141
  59.6 15.9 %fusion.132 = (f32[12,512]{1,0:T(8,128)S(1)}, bf16[12,512,512]{1,2,0:T(8,128)(2,1)S(1)}) fusion(f32[12,512]{1,0:T(8,128)S(1)} %get-tuple-element.2180, f32[12,512,512]{2,1,0:T(8,128)S(1)} %get-tuple-element.1778, f32[512,512]{0,1:T(8,128)S(1)} %and_convert_fusion, pred[12,512]{1,0:T(8,128)(4,1)S(1)} %fusion.15, pred[12,512]{1,0:T(8,128)(4,1)S(1)} %fusion.14, ...), kind=kLoop, calls=%fused_computation.371 | loop fusion | flops 75491328 | bytes 22118412 | tf_op jit(solution)/shard_map/while/body/eval_jaxpr/cond/branch_1_fun/reduce_sum | solution.py:159
  82.7 16.7 %all-gather.2 = bf16[1,512,768]{1,2,0:T(8,128)(2,1)} all-gather(bf16[1,512,192]{1,2,0:T(8,128)(2,1)S(1)} %copy-done.42), channel_id=4, replica_groups=mesh['row'=4,'seq'=2,'pat'=4] {'pat'}, dimensions={2}, use_global_device_ids=true | all-gather | bytes 983040 | tf_op jit(solution)/shard_map/all_gather | solution.py:199
  99.4 13.1 %all-gather.3 = bf16[4,12,512]{2,1,0:T(8,128)(2,1)S(1)} all-gather(bf16[1,12,512]{2,1,0:T(8,128)(2,1)S(1)} %convert_bitcast_fusion.1), channel_id=2, replica_groups=mesh['row'=4,'seq'=2,'pat'=4] {'pat'}, dimensions={0}, use_global_device_ids=true | all-gather | bytes 61440 | tf_op jit(solution)/shard_map/all_gather | solution.py:19
  112.5 13.2 %all-gather.4 = bf16[4,12,512]{2,1,0:T(8,128)(2,1)S(1)} all-gather(bf16[1,12,512]{2,1,0:T(8,128)(2,1)S(1)} %convert_bitcast_fusion), channel_id=3, replica_groups=mesh['row'=4,'seq'=2,'pat'=4] {'pat'}, dimensions={0}, use_global_device_ids=true | all-gather | bytes 61440 | tf_op jit(solution)/shard_map/all_gather | solution.py:19
  125.8 57.1 %all-gather.13.cloned.1.call-done = bf16[4,512,768]{2,1,0:T(8,128)(2,1)} async-done(((bf16[1,512,768]{2,1,0:T(8,128)(2,1)}), bf16[4,512,768]{2,1,0:T(8,128)(2,1)}) %all-gather.13.cloned.1.call-update) | async-done | bytes 3145744 | tf_op jit(solution)/shard_map/all_gather | solution.py:19
  187.1 19.1 %while.59 = (s32[]{:T(128)}, f32[12,512]{1,0:T(8,128)S(1)}, f32[12,512]{1,0:T(8,128)S(1)}, f32[512,768]{0,1:T(8,128)S(1)}, bf16[4,12,512]{2,1,0:T(8,128)(2,1)S(1...) while((s32[]{:T(128)}, f32[12,512]{1,0:T(8,128)S(1)}, ...), condition=%wide.region_9.10_spmd, body=%wide.region_8.9_spmd.sunk | while | flops 1634309 | bytes 8491359 | solution.py:31
  219.9 41.9 %all-reduce.7.cloned.1.call-done = bf16[512,768]{1,0:T(8,128)(2,1)} async-done(((bf16[512,768]{1,0:T(8,128)(2,1)}), bf16[512,768]{1,0:T(8,128)(2,1)}) %all-reduce.7.cloned.1.call-update) | async-done | bytes 786448 | tf_op jit(solution)/shard_map/psum | solution.py:206
  270.0 41.3 %while.60 = (s32[]{:T(128)}, f32[512,12,64]{0,2,1:T(8,128)}, bf16[2,512,768]{2,1,0:T(8,128)(2,1)}, bf16[2,512,768]{2,1,0:T(8,128)(2,1)}, s32[2]{0:T(128)S(1)}, /...) while((s32[]{:T(128)}, f32[512,12,64]{0,2,1:T(8,128)}, ...), condition=%wide.region_20.21_spmd, body=%wide.region_17.20_spmd.sunk | while | flops 2099863936 | bytes 89110168 | solution.py:265
  272.1 30.0 %conditional.5 = (f32[512,12,64]{0,2,1:T(8,128)}, bf16[1,512,768]{1,2,0:T(8,128)(2,1)S(1)}, bf16[1,512,768]{1,2,0:T(8,128)(2,1)}) conditional(s32[]{:T(128)} %convert_element_type.319, f32[512,12,64]{0,2,1:T(8,128)} %get-tuple-element.2371, (s32[]{:T(128)}, bf16[1024,768]{0,1:T(8,128)(2,1)}, s32[]{:T(128)}, f32[]{:T(128)}, f32[]{:T(128)}, ...), branch_computations={%region_18.18_spmd, %region_19.19_spmd} | conditional | flops 2099863808 | bytes 82817552 | solution.py:263
  276.2 13.1 %fusion.54 = f32[12,512,512]{1,2,0:T(8,128)S(1)} fusion(f32[12,512]{1,0:T(8,128)S(1)} %get-tuple-element.1341, f32[512,512]{0,1:T(8,128)S(1)} %and_convert_fusion.1, f32[]{:T(128)} %get-tuple-element.1338, f32[]{:T(128)} %get-tuple-element.1337, f32[]{:T(128)} %get-tuple-element.1336, f32[512,512]{0,1:T(8,128)S(1)} %compare_select_fusion.1, ...), kind=kOutput, calls=%fused_computation.151 | convolution fusion | flops 471859200 | bytes 17375244 | tf_op jit(solution)/shard_map/while/body/eval_jaxpr/cond/branch_1_fun/qhd,khd->hqk/dot_general | solution.py:141
  314.7 33.3 %reduce-scatter.11.cloned.1.call-done = bf16[512,768]{1,0:T(8,128)(2,1)} async-done(((bf16[1024,768]{1,0:T(8,128)(2,1)}), bf16[512,768]{1,0:T(8,128)(2,1)}) %reduce-scatter.11.cloned.1.call-update) | async-done | bytes 786448 | tf_op jit(solution)/shard_map/reduce_scatter | solution.py:269
  348.0 13.0 %reduce-scatter.15.cloned.1.call-done = bf16[512,768]{1,0:T(8,128)(2,1)} async-done(((bf16[1024,768]{1,0:T(8,128)(2,1)}), bf16[512,768]{1,0:T(8,128)(2,1)}) %reduce-scatter.15.cloned.1.call-update) | async-done | bytes 786448 | tf_op jit(solution)/shard_map/reduce_scatter | solution.py:272
  370.7 17.8 %reduce-scatter.21.cloned.1.call-done = bf16[128,768]{1,0:T(8,128)(2,1)} async-done(((bf16[512,768]{1,0:T(8,128)(2,1)}), bf16[128,768]{1,0:T(8,128)(2,1)}) %reduce-scatter.21.cloned.1.call-update) | async-done | bytes 196624
  391.3 22.1 %reduce-scatter.13.cloned.1.call-done = bf16[128,768]{1,0:T(8,128)(2,1)} async-done(((bf16[512,768]{1,0:T(8,128)(2,1)}), bf16[128,768]{1,0:T(8,128)(2,1)}) %reduce-scatter.13.cloned.1.call-update) | async-done | bytes 196624 | tf_op jit(solution)/shard_map/reduce_scatter | solution.py:283
  416.2 22.1 %reduce-scatter.17.cloned.1.call-done = bf16[128,768]{1,0:T(8,128)(2,1)} async-done(((bf16[512,768]{1,0:T(8,128)(2,1)}), bf16[128,768]{1,0:T(8,128)(2,1)}) %reduce-scatter.17.cloned.1.call-update) | async-done | bytes 196624 | tf_op jit(solution)/shard_map/reduce_scatter | solution.py:286
  446.0 17.1 %reduce-scatter.19.cloned.1.call-done = bf16[192,512]{1,0:T(8,128)(2,1)} async-done(((bf16[768,512]{1,0:T(8,128)(2,1)}), bf16[192,512]{1,0:T(8,128)(2,1)}) %reduce-scatter.19.cloned.1.call-update) | async-done | bytes 196624
  469.3 39.4 %all-reduce = (f32[768]{0:T(1024)}, f32[768]{0:T(1024)}, f32[768]{0:T(1024)}, f32[768]{0:T(1024)}) all-reduce(f32[768]{0:T(1024)S(1)} %get-tuple-element.1597, f32[768]{0:T(1024)S(1)} %get-tuple-element.1600, f32[768]{0:T(1024)S(1)} %copy-done.50, f32[768]{0:T(1024)S(1)} %copy-done.51), channel_id=1, replica_groups=mesh['row'=4,'seq'=2,'pat'=4] {'row','seq','pat'}, use_global_device_ids=true, to_apply=%region_31.32 | all-reduce | flops 3072 | bytes 24576 | tf_op jit(solution)/shard_map/psum | solution.py:310
  510.8 43.6 %all-reduce.11.cloned.1.call-done = (f32[768,768]{1,0:T(8,128)}, f32[768,768]{1,0:T(8,128)}) async-done(((f32[768,768]{1,0:T(8,128)}, f32[768,768]{1,0:T(8,128)}), (f32[768,768]{1,0:T(8,128)}, f32[768,768]{1,0:T(8,128)})) %all-reduce.11.cloned.1.call-update) | async-done | bytes 4718608 | tf_op jit(solution)/shard_map/psum | solution.py:323
  554.3 200.4 %all-reduce.9.cloned.1.call-done = (f32[768,768]{1,0:T(8,128)}, f32[768,768]{1,0:T(8,128)}, f32[768,768]{1,0:T(8,128)}, f32[768,768]{1,0:T(8,128)}) async-done(((f32[768,768]{1,0:T(8,128)}, f32[768,768]{1,0:T(8,128)}, f32[768,768]{1,0:T(8,128)}, f32[768,768]{1,0:T(8,128)}), (f32[768,768]{1,0:T(8,128)}, f32[768,768]{1,0:T(8,128)}, f32[768,768]{1,0:T(8,128)}, ...) | async-done | bytes 9437200 | tf_op jit(solution)/shard_map/psum | solution.py:310
  (341 shorter events, 145.2 us)
Async XLA Ops:
  7.2 201.9 %copy-start = (bf16[768,768]{1,0:T(8,128)(2,1)S(1)}, bf16[768,768]{1,0:T(8,128)(2,1)}, u32[]{:S(2)}) copy-start(bf16[768,768]{1,0:T(8,128)(2,1)} %param.33) | copy-start | bytes 3538948
  7.2 17.8 %all-gather.9.cloned.1.call-start = ((), (), s32[]{:S(2)}) async-start(), calls=%async_computation.6 | async-start | bytes 2359296 | tf_op jit(solution)/shard_map/all_gather | solution.py:114
  10.7 4.8 copy-start.19
  12.4 25.8 %all-gather.11.cloned.1.call-start = ((), (), s32[]{:S(2)}) async-start(), calls=%async_computation.7 | async-start | bytes 2359296 | tf_op jit(solution)/shard_map/all_gather | solution.py:115
  15.4 167.5 %all-gather.13.cloned.1.call-start = ((), (), s32[]{:S(2)}) async-start(), calls=%async_computation.8 | async-start | bytes 3932160 | tf_op jit(solution)/shard_map/all_gather | solution.py:19
  82.6 179.1 %all-reduce.7.cloned.1.call-start = ((), (), s32[]{:S(2)}) async-start(), calls=%async_computation.9 | async-start | bytes 1572864 | tf_op jit(solution)/shard_map/psum | solution.py:206
  208.7 8.6 %copy-start.7 = (f32[512,768]{1,0:T(8,128)}, f32[512,768]{1,0:T(8,128)S(1)}, u32[]{:S(2)}) copy-start(f32[512,768]{1,0:T(8,128)S(1)} %get-tuple-element.1808) | copy-start | bytes 4718596
  208.8 8.6 %copy-start.45 = (f32[512]{0:T(512)}, f32[512]{0:T(512)S(1)}, u32[]{:S(2)}) copy-start(f32[512]{0:T(512)S(1)} %broadcast_multiply_fusion) | copy-start | bytes 6148
  209.5 7.9 %copy-start.47 = (f32[512]{0:T(512)}, f32[512]{0:T(512)S(1)}, u32[]{:S(2)}) copy-start(f32[512]{0:T(512)S(1)} %fusion.123) | copy-start | bytes 6148
  209.5 5.0 copy-start.9
  209.5 5.0 copy-start.56
  219.1 128.8 %reduce-scatter.11.cloned.1.call-start = ((), (), s32[]{:S(2)}) async-start(), calls=%async_computation.10 | async-start | bytes 2359296 | tf_op jit(solution)/shard_map/reduce_scatter | solution.py:269
  311.3 49.7 %reduce-scatter.15.cloned.1.call-start = ((), (), s32[]{:S(2)}) async-start(), calls=%async_computation.12 | async-start | bytes 2359296 | tf_op jit(solution)/shard_map/reduce_scatter | solution.py:272
  311.9 76.6 %reduce-scatter.21.cloned.1.call-start = ((), (), s32[]{:S(2)}) async-start(), calls=%async_computation.15 | async-start | bytes 983040
  314.6 46.5 %copy-start.38 = (bf16[512,768]{1,0:T(8,128)(2,1)S(1)}, bf16[512,768]{1,0:T(8,128)(2,1)}, u32[]{:S(2)}) copy-start(bf16[512,768]{1,0:T(8,128)(2,1)} %get-tuple-element.1733) | copy-start | bytes 2359300
  314.6 46.5 %copy-start.57 = (bf16[768,768]{1,0:T(8,128)(2,1)S(1)}, bf16[768,768]{1,0:T(8,128)(2,1)}, u32[]{:S(2)}) copy-start(bf16[768,768]{1,0:T(8,128)(2,1)} %param.34) | copy-start | bytes 3538948
  314.6 98.8 %reduce-scatter.13.cloned.1.call-start = ((), (), s32[]{:S(2)}) async-start(), calls=%async_computation.11 | async-start | bytes 983040 | tf_op jit(solution)/shard_map/reduce_scatter | solution.py:283
  348.0 90.3 %reduce-scatter.17.cloned.1.call-start = ((), (), s32[]{:S(2)}) async-start(), calls=%async_computation.13 | async-start | bytes 983040 | tf_op jit(solution)/shard_map/reduce_scatter | solution.py:286
  361.0 102.0 %reduce-scatter.19.cloned.1.call-start = ((), (), s32[]{:S(2)}) async-start(), calls=%async_computation.14 | async-start | bytes 983040
  362.9 191.5 %all-reduce.11.cloned.1.call-start = ((), (), s32[]{:S(2)}) async-start(), calls=%async_computation.17 | async-start | bytes 9437184 | tf_op jit(solution)/shard_map/psum | solution.py:323
  367.6 20.8 %copy-start.20 = (bf16[512,768]{1,0:T(8,128)(2,1)S(1)}, bf16[512,768]{1,0:T(8,128)(2,1)}, u32[]{:S(2)}) copy-start(bf16[512,768]{1,0:T(8,128)(2,1)} %copy-done.19) | copy-start | bytes 2359300
  367.7 387.1 %all-reduce.9.cloned.1.call-start = ((), (), s32[]{:S(2)}) async-start(), calls=%async_computation.16 | async-start | bytes 18874368 | tf_op jit(solution)/shard_map/psum | solution.py:310
  443.5 21.6 %copy-start.28 = (bf16[768,768]{1,0:T(8,128)(2,1)S(1)}, bf16[768,768]{1,0:T(8,128)(2,1)}, u32[]{:S(2)}) copy-start(bf16[768,768]{1,0:T(8,128)(2,1)} %param.27) | copy-start | bytes 3538948
  765.7 3.9 copy-start.1
  (64 other events, 129.8 us)
Sparse Core Ops, SparseCore 0:
  12.5 12.4 all-gather.8
  27.1 10.9 all-gather.10
  82.8 100.0 all-gather.12
  219.2 42.4 all-reduce.6
  311.4 36.4 reduce-scatter.10
  350.7 10.2 reduce-scatter.14
  363.9 24.5 reduce-scatter.20
  390.7 22.6 reduce-scatter.12
  415.7 22.5 reduce-scatter.16
  440.4 22.5 reduce-scatter.18
  467.0 87.3 all-reduce.10
  562.7 192.0 all-reduce.8
where the time goes:
time: 782 us; the launch traced here: 777 us
  waiting for transfers between devices  486 us (62%)
  blocking collectives  82.4 us (11%)
  matrix products  77.3 us (10%)
  local copies, waits for them, and re-layouts  57.2 us (7%)
  other arithmetic  49.7 us (6%)
  between operations  15.1 us (2%)
  loops' own time  8.68 us (1%)
    psum x1, waiting for transfers between devices, per_device(): lax.psum((grad_wq, grad_wk, grad_wv, grad_wout, grad_gain_one, grad_bias_...  200 us
    all_gather x1, waiting for transfers between devices, combined_all(): lax.all_gather(a.astype(kind), axis)  57.1 us
    psum x1, waiting for transfers between devices, per_device(): ffn_summed = lax.psum((grad_up, grad_down), ('row', 'seq'))  43.6 us
    psum x1, waiting for transfers between devices, per_device(): lax.psum(resid_part.astype(jnp.bfloat16), 'pat').astype(jnp.float32)  41.9 us
    psum x1, blocking collectives, per_device(): lax.psum((grad_wq, grad_wk, grad_wv, grad_wout, grad_gain_one, grad_bias_...  39.4 us
    unnamed x14, waiting for transfers between devices  35.5 us
    reduce_scatter x1, waiting for transfers between devices, per_device(): lax.psum_scatter(key_terms.astype(jnp.bfloat16), 'seq', scatter_dimension...  33.3 us
    all_gather x2, blocking collectives, combined_all(): lax.all_gather(a.astype(kind), axis)  26.3 us
  transfers between devices with their start and end apart: 12, of which 12 were waited for; matrix products, arithmetic and copies ran while one was open for 5% of the time, Pallas kernels for 0%

commit v1 on v0

v1 whole, which is shorter than its diff:
```python
import functools

import jax
import jax.numpy as jnp
from jax import lax
from jax.experimental import pallas as pl
from jax.experimental.pallas import tpu as pltpu
from jax.sharding import PartitionSpec as P

D = 768
HEADS = 12
HDIM = 64

epsilon = 1e-05
masked_low = -1e30
segment_parts = (1, 2, 4, 8, 16)
dilations = (1, 2, 4, 6, 12)
DOCS = 3
FEATS = 128
TILE = 256
VMEM_LIMIT = 60 * 1024 * 1024
f32 = jnp.float32
bf16 = jnp.bfloat16


def dot(a, b):
    return lax.dot_general(a, b, (((1,), (0,)), ((), ())), preferred_element_type=f32)


def dot_nt(a, b):
    return lax.dot_general(a, b, (((1,), (1,)), ((), ())), preferred_element_type=f32)


def dot_tn(a, b):
    return lax.dot_general(a, b, (((0,), (0,)), ((), ())), preferred_element_type=f32)


def kernel_call(body, out_shape, scratch=(), in_specs=None, flops=0):
    return pl.pallas_call(
        body,
        out_shape=out_shape,
        in_specs=in_specs,
        out_specs=jax.tree.map(lambda _: pl.BlockSpec(memory_space=pltpu.VMEM), out_shape),
        scratch_shapes=list(scratch),
        compiler_params=pltpu.CompilerParams(vmem_limit_bytes=VMEM_LIMIT),
        cost_estimate=pl.CostEstimate(flops=flops, bytes_accessed=1 << 22, transcendentals=0),
    )


def specs(n_scalar, n_arrays):
    return [pl.BlockSpec(memory_space=pltpu.SMEM)] * n_scalar + [
        pl.BlockSpec(memory_space=pltpu.VMEM)
    ] * n_arrays


def normalise(values):
    center = values - jnp.mean(values, axis=-1, keepdims=True)
    scale = lax.rsqrt(jnp.mean(center * center, axis=-1, keepdims=True) + epsilon)
    return center * scale, scale


def norm_backward(hat, scale, grad):
    return scale * (
        grad
        - jnp.mean(grad, axis=-1, keepdims=True)
        - hat * jnp.mean(grad * hat, axis=-1, keepdims=True)
    )


def project_kernel(parts, where, x, gain, bias, wq, wk, wv, normed, q, k, v, own):
    width = D // parts
    for part in range(parts):

        @pl.when(where[0] == part)
        def _():
            for at, w in enumerate((wq, wk, wv)):
                own[at] = w[:, part * width : (part + 1) * width]

    for start in range(0, x.shape[0], TILE):
        rows = pl.ds(start, TILE)
        hat, _ = normalise(x[rows, :].astype(f32))
        low = (hat * gain[...] + bias[...]).astype(bf16)
        normed[rows, :] = low
        q[rows, :] = (dot(low, own[0]).astype(bf16).astype(f32) * HDIM**-0.5).astype(bf16)
        k[rows, :] = dot(low, own[1]).astype(bf16)
        v[rows, :] = dot(low, own[2]).astype(bf16)


def head_mask(heads, width):
    lane = lax.broadcasted_iota(jnp.int32, (1, width), 1)
    return [((lane >= h * HDIM) & (lane < (h + 1) * HDIM)).astype(bf16) for h in range(heads)]


def attention_kernel(
    heads, span, where, q, k, v, k_far, v_far, feats, mixed, mixed_t, lse, q_head, v_t, vf_t
):
    width = heads * HDIM
    masks = head_mask(heads, width)
    for h in range(heads):
        q_head[h] = q[...] * masks[h]
    v_t[...] = v[...].T
    far = k_far.shape[0] // span

    def turn(j, _):
        rows = pl.ds(pl.multiple_of(j * span, span), span)
        vf_t[j] = v_far[rows, :].T
        return 0

    mine = where[0]
    lax.fori_loop(0, jnp.minimum(mine, far), turn, 0)
    own_start = pl.multiple_of(mine * span, span)
    lse[...] = jnp.zeros(lse.shape, f32)
    for start in range(0, span, TILE):
        for h in range(heads):
            q_tile = q_head[h, start : start + TILE, :]
            f_tile = feats[h, pl.ds(own_start + start, TILE), :]

            def part(k_rows, f_rows, v_rows, low_from, state):
                counts = dot_nt(f_rows, f_tile)
                if low_from is not None:
                    at_k = lax.broadcasted_iota(jnp.int32, counts.shape, 0)
                    at_q = lax.broadcasted_iota(jnp.int32, counts.shape, 1) + low_from
                    counts = jnp.where(at_k <= at_q, counts, 0.0)
                scores = jnp.where(counts > 0, dot_nt(k_rows, q_tile), masked_low)
                top, total, acc = state
                new_top = jnp.maximum(top, jnp.max(scores, axis=0, keepdims=True))
                weights = counts * jnp.exp(scores - new_top)
                factor = jnp.exp(top - new_top)
                return (
                    new_top,
                    total * factor + jnp.sum(weights, axis=0, keepdims=True),
                    acc * factor + dot(v_rows, weights.astype(bf16)),
                )

            state = (
                jnp.full((1, TILE), masked_low, f32),
                jnp.zeros((1, TILE), f32),
                jnp.zeros((HDIM, TILE), f32),
            )
            size = start + TILE
            head_rows = slice(h * HDIM, (h + 1) * HDIM)
            state = part(
                k[:size, :],
                feats[h, pl.ds(own_start, size), :],
                v_t[head_rows, :size],
                start,
                state,
            )

            def far_part(j, state):
                rows = pl.ds(pl.multiple_of(j * span, span), span)
                return part(k_far[rows, :], feats[h, rows, :], vf_t[j, head_rows, :], None, state)

            top, total, acc = lax.fori_loop(0, mine, far_part, state)
            mixed_t[head_rows, start : start + TILE] = acc / total
            lse[h : h + 1, start : start + TILE] = top + jnp.log(total)
    mixed[...] = mixed_t[...].T.astype(bf16)


def attention_back_kernel(
    heads,
    span,
    where,
    parts,
    mixed_t,
    lse,
    q,
    k,
    v,
    k_far,
    v_far,
    feats,
    grad_q,
    grad_k,
    grad_v,
    grad_kf,
    grad_vf,
    q_head,
    g_head,
    dots,
    probs,
    slopes,
    k_t,
    gq_t,
):
    width = heads * HDIM
    masks = head_mask(heads, width)
    mine = where[0]
    far = k_far.shape[0] // span
    total = parts[0].astype(f32)
    for part in range(1, parts.shape[0]):
        total = total + parts[part].astype(f32)
    low = total.astype(bf16)
    for h in range(heads):
        q_head[h] = q[...] * masks[h]
        g_head[h] = low * masks[h]
    product = low.astype(f32).T * mixed_t[...]
    for h in range(heads):
        dots[h : h + 1, :] = jnp.sum(product[h * HDIM : (h + 1) * HDIM], axis=0, keepdims=True)
    own_start = pl.multiple_of(mine * span, span)

    def block(h, start, k_rows, v_rows, f_rows, low_from):
        tile = slice(start, start + TILE)
        counts = dot_nt(f_rows, feats[h, pl.ds(own_start + start, TILE), :])
        if low_from is not None:
            at_k = lax.broadcasted_iota(jnp.int32, counts.shape, 0)
            at_q = lax.broadcasted_iota(jnp.int32, counts.shape, 1) + low_from
            counts = jnp.where(at_k <= at_q, counts, 0.0)
        scores = jnp.where(counts > 0, dot_nt(k_rows, q_head[h, tile, :]), masked_low)
        prob = counts * jnp.exp(scores - lse[h : h + 1, tile])
        grad_prob = dot_nt(v_rows, g_head[h, tile, :])
        slope = prob * (grad_prob - dots[h : h + 1, tile])
        size = k_rows.shape[0]
        columns = slice(h * span + start, h * span + start + TILE)
        probs[:size, columns] = prob.astype(bf16)
        slopes[:size, columns] = slope.astype(bf16)
        if size < span:
            probs[size:, columns] = jnp.zeros((span - size, TILE), bf16)
            slopes[size:, columns] = jnp.zeros((span - size, TILE), bf16)

    def finish(k_rows):
        k_t[...] = k_rows.T
        grad_v_rows = dot(probs[...], g_head[...].reshape(heads * span, width))
        grad_k_rows = dot(slopes[...], q_head[...].reshape(heads * span, width))
        terms = [
            dot(k_t[h * HDIM : (h + 1) * HDIM, :], slopes[:, h * span : (h + 1) * span])
            for h in range(heads)
        ]
        return grad_k_rows, grad_v_rows, terms

    for start in range(0, span, TILE):
        for h in range(heads):
            size = start + TILE
            block(h, start, k[:size, :], v[:size, :], feats[h, pl.ds(own_start, size), :], start)
    grad_k_rows, grad_v_rows, terms = finish(k[...])
    grad_k[...] = grad_k_rows
    grad_v[...] = grad_v_rows
    for h in range(heads):
        gq_t[h * HDIM : (h + 1) * HDIM, :] = terms[h]
    grad_kf[...] = jnp.zeros(grad_kf.shape, bf16)
    grad_vf[...] = jnp.zeros(grad_vf.shape, bf16)

    def far_block(j, _):
        rows = pl.ds(pl.multiple_of(j * span, span), span)
        for start in range(0, span, TILE):
            for h in range(heads):
                block(h, start, k_far[rows, :], v_far[rows, :], feats[h, rows, :], None)
        grad_k_rows, grad_v_rows, terms = finish(k_far[rows, :])
        grad_kf[rows, :] = grad_k_rows.astype(bf16)
        grad_vf[rows, :] = grad_v_rows.astype(bf16)
        for h in range(heads):
            gq_t[h * HDIM : (h + 1) * HDIM, :] += terms[h]
        return 0

    lax.fori_loop(0, jnp.minimum(mine, far), far_block, 0)
    grad_q[...] = (gq_t[...] * HDIM**-0.5).T.astype(bf16)


def middle_kernel(
    blocks,
    x,
    mixed4,
    c4,
    w_out,
    w_up,
    w_down,
    gain,
    bias,
    gm,
    ffn,
    gr,
    wide,
    sums,
    mixed,
    c,
    act,
    gh,
    low,
    branch,
):
    parts = mixed4.shape[0]
    width = D // parts
    for part in range(parts):
        columns = slice(part * width, (part + 1) * width)
        mixed[:, columns] = mixed4[part]
        c[:, columns] = c4[part]
    gain_sum = jnp.zeros((1, D), f32)
    bias_sum = jnp.zeros((1, D), f32)
    for start in range(0, x.shape[0], TILE):
        rows = slice(start, start + TILE)
        resid = x[rows, :].astype(f32) + dot(mixed[rows, :], w_out[...])
        hat, scale = normalise(resid)
        normed = (hat * gain[...] + bias[...]).astype(bf16)
        low[rows, :] = normed
        hidden = dot(normed, w_up[...])
        bell = 0.5 + 0.5 * lax.erf(hidden * (0.5**0.5))
        activated = (hidden * bell).astype(bf16)
        act[rows, :] = activated
        slope = bell + hidden * jnp.exp(-0.5 * hidden * hidden) * 0.3989422804014327
        grad_hidden = (slope * dot_nt(c[rows, :], w_down[...])).astype(bf16)
        gh[rows, :] = grad_hidden
        grad_normed = dot_nt(grad_hidden, w_up[...])
        gain_sum = gain_sum + jnp.sum(grad_normed * hat, axis=0, keepdims=True)
        bias_sum = bias_sum + jnp.sum(grad_normed, axis=0, keepdims=True)
        grad_resid = norm_backward(hat, scale, grad_normed * gain[...]) + c[rows, :].astype(
            f32
        ) * (1.0 / parts)
        gr[rows, :] = grad_resid
        grad_low = grad_resid.astype(bf16)
        branch[rows, :] = grad_low
        out_part = (dot(activated, w_down[...]) + resid * (1.0 / parts)).astype(bf16)
        for part in range(parts):
            columns = slice(part * width, (part + 1) * width)
            gm[part, rows, :] = dot_nt(grad_low, w_out[columns, :]).astype(bf16)
            ffn[part, rows, :] = out_part[:, columns]
    sums[0:1, :] = gain_sum
    sums[1:2, :] = bias_sum
    size = D // blocks
    for at, (left, right) in enumerate(((act, c), (low, gh), (mixed, branch))):
        product = dot_tn(left[...], right[...]).astype(bf16)
        for block in range(blocks):
            wide[block, at * size : (at + 1) * size, :] = product[
                block * size : (block + 1) * size, :
            ]


def last_kernel(
    blocks,
    parts,
    x,
    gain,
    normed,
    own,
    gq,
    gk,
    gv,
    gk_more,
    gv_more,
    gr,
    sums,
    narrow,
    back,
    small,
    gk_low,
    gv_low,
):
    gk_low[...] = (gk[...] + gk_more[...].astype(f32)).astype(bf16)
    gv_low[...] = (gv[...] + gv_more[...].astype(f32)).astype(bf16)
    width = D // parts
    gain_sum = jnp.zeros((1, D), f32)
    bias_sum = jnp.zeros((1, D), f32)
    span = x.shape[0]
    piece = span // parts
    for start in range(0, span, TILE):
        rows = slice(start, start + TILE)
        hat, scale = normalise(x[rows, :].astype(f32))
        grad_normed = (
            dot_nt(gq[rows, :], own[0])
            + dot_nt(gk_low[rows, :], own[1])
            + dot_nt(gv_low[rows, :], own[2])
        )
        gain_sum = gain_sum + jnp.sum(grad_normed * hat, axis=0, keepdims=True)
        bias_sum = bias_sum + jnp.sum(grad_normed, axis=0, keepdims=True)
        grad_in = gr[rows, :] + norm_backward(hat, scale, grad_normed * gain[...])
        back[rows, :] = grad_in.astype(bf16)
    for at, row in enumerate((gain_sum, bias_sum, sums[0:1, :], sums[1:2, :])):
        for part in range(parts):
            small[at * parts + part : at * parts + part + 1, :] = row[
                :, part * width : (part + 1) * width
            ]
    size = D // blocks
    tail = small[...].astype(bf16)
    for at, right in enumerate((gq, gk_low, gv_low)):
        product = dot_tn(normed[...], right[...]).astype(bf16)
        for block in range(blocks):
            narrow[block, at * size : (at + 1) * size, :] = product[
                block * size : (block + 1) * size, :
            ]
    for block in range(blocks):
        narrow[block, 3 * size :, :] = tail


def spread_kernel(rows_count, seq_count, where, mine, other, *outs):
    parts = mine.shape[1]
    width = mine.shape[3]
    size = (mine.shape[2] - 16) // 4
    seq = where[0]
    for row in range(rows_count):
        for half, source in enumerate((mine, other)):
            at = seq if half == 0 else 1 - seq
            start = pl.multiple_of((row * seq_count + at) * size, size)
            for part in range(parts):
                columns = slice(part * width, (part + 1) * width)
                for grad in range(4):
                    outs[grad][pl.ds(start, size), columns] = source[
                        row, part, grad * size : (grad + 1) * size, :
                    ].astype(f32)


def broadcast_exchange(value, axis):
    count = lax.axis_size(axis)
    return lax.all_to_all(
        jnp.broadcast_to(value[None], (count,) + value.shape), axis, 0, 0, tiled=False
    )


def swap(value):
    return lax.ppermute(value, "seq", [(0, 1), (1, 0)])


def one_hot_features(row_docs, heads, pat_index):
    length = row_docs.shape[0]
    position = jnp.arange(length, dtype=jnp.int32)
    head = pat_index * heads + jnp.arange(heads, dtype=jnp.int32)
    feature = jnp.arange(FEATS, dtype=jnp.int32)
    hit = jnp.zeros((heads, length, FEATS), jnp.bool_)
    base = 0
    for part, dilation in zip(segment_parts, dilations, strict=True):
        seg_width = length * part // 16
        inside = ((position % seg_width)[None, :] - (head % dilation)[:, None]) % dilation == 0
        key = base + (position // seg_width) * DOCS + row_docs
        key = jnp.where(inside, key[None, :], -1)
        hit = hit | (key[:, :, None] == feature[None, None, :])
        base += DOCS * (16 // part)
    return hit.astype(bf16)


def per_device(
    block_input,
    doc_ids,
    ln1_gain,
    ln1_bias,
    w_query,
    w_key,
    w_value,
    w_out,
    ln2_gain,
    ln2_bias,
    w_up,
    w_down,
    cotangent,
):
    span = block_input.shape[1]
    rows_count = lax.axis_size("row")
    seq_count = lax.axis_size("seq")
    parts = lax.axis_size("pat")
    seq_index = lax.axis_index("seq")
    pat_index = lax.axis_index("pat")
    pair = seq_count == 2
    heads = HEADS // parts
    width = D // parts
    quarter = span // parts
    blocks = rows_count * seq_count if (D // (rows_count * seq_count)) % 16 == 0 and pair else 1
    here = seq_index.astype(jnp.int32)[None]
    part_here = pat_index.astype(jnp.int32)[None]
    gain_one, bias_one = ln1_gain[None], ln1_bias[None]
    gain_two, bias_two = ln2_gain[None], ln2_bias[None]
    x = block_input[0]

    def shape(*dims, kind=bf16):
        return jax.ShapeDtypeStruct(dims, kind)

    c4 = broadcast_exchange(cotangent[0], "pat")
    feats = one_hot_features(doc_ids[0], heads, pat_index)
    normed, q, k, v, own = kernel_call(
        functools.partial(project_kernel, parts),
        (
            shape(span, D),
            shape(span, width),
            shape(span, width),
            shape(span, width),
            shape(3, D, width),
        ),
        in_specs=specs(1, 6),
        flops=2 * span * D * width * 3,
    )(part_here, x, gain_one, bias_one, w_query, w_key, w_value)

    if pair:
        k_far, v_far = swap(k), swap(v)
    else:
        k_far = lax.all_gather(k, "seq", axis=0, tiled=True)
        v_far = lax.all_gather(v, "seq", axis=0, tiled=True)
    far_rows = k_far.shape[0]

    mixed, mixed_t, lse = kernel_call(
        functools.partial(attention_kernel, heads, span),
        (shape(span, width), shape(width, span, kind=f32), shape(8, span, kind=f32)),
        scratch=[
            pltpu.VMEM((heads, span, width), bf16),
            pltpu.VMEM((width, span), bf16),
            pltpu.VMEM((far_rows // span, width, span), bf16),
        ],
        in_specs=specs(1, 6),
        flops=1 << 31,
    )(here, q, k, v, k_far, v_far, feats)

    mixed4 = lax.all_gather(mixed, "pat")
    gm, ffn, gr, wide, sums = kernel_call(
        functools.partial(middle_kernel, blocks),
        (
            shape(parts, span, width),
            shape(parts, span, width),
            shape(span, D, kind=f32),
            shape(blocks, 3 * D // blocks, D),
            shape(8, D, kind=f32),
        ),
        scratch=[pltpu.VMEM((span, D), bf16)] * 6,
        in_specs=specs(0, 8),
        flops=2 * span * D * D * 9,
    )(x, mixed4, c4, w_out, w_up, w_down, gain_two, bias_two)

    gm_parts = lax.all_to_all(gm, "pat", 0, 0, tiled=True)
    ffn_parts = lax.all_to_all(ffn, "pat", 0, 0, tiled=True)
    output = jnp.sum(ffn_parts.astype(f32), axis=0).astype(bf16)[None]

    gq, gk, gv, gkf, gvf = kernel_call(
        functools.partial(attention_back_kernel, heads, span),
        (
            shape(span, width),
            shape(span, width, kind=f32),
            shape(span, width, kind=f32),
            shape(far_rows, width),
            shape(far_rows, width),
        ),
        scratch=[
            pltpu.VMEM((heads, span, width), bf16),
            pltpu.VMEM((heads, span, width), bf16),
            pltpu.VMEM((8, span), f32),
            pltpu.VMEM((span, heads * span), bf16),
            pltpu.VMEM((span, heads * span), bf16),
            pltpu.VMEM((width, span), bf16),
            pltpu.VMEM((width, span), f32),
        ],
        in_specs=specs(1, 9),
        flops=1 << 32,
    )(here, gm_parts, mixed_t, lse, q, k, v, k_far, v_far, feats)

    if pair:
        gk_more, gv_more = swap(gkf), swap(gvf)
    else:
        gk_more = lax.psum_scatter(gkf, "seq", scatter_dimension=0, tiled=True)
        gv_more = lax.psum_scatter(gvf, "seq", scatter_dimension=0, tiled=True)

    size = D // blocks
    narrow, back = kernel_call(
        functools.partial(last_kernel, blocks, parts),
        (shape(blocks, 3 * size + 16, width), shape(span, D)),
        scratch=[
            pltpu.VMEM((16, width), f32),
            pltpu.VMEM((span, width), bf16),
            pltpu.VMEM((span, width), bf16),
        ],
        in_specs=specs(0, 11),
        flops=2 * span * D * width * 6,
    )(x, gain_one, normed, own, gq, gk, gv, gk_more, gv_more, gr, sums)

    back_parts = lax.all_to_all(back.reshape(parts, quarter, D), "pat", 0, 0, tiled=True)
    grad_input = jnp.sum(back_parts.astype(f32), axis=0).astype(bf16)[None]

    def total(value):
        return jnp.sum(value.astype(f32), axis=0).astype(bf16)

    both = ("row", "seq")
    if blocks > 1:
        wide_sum = total(lax.all_to_all(wide, both, 0, 0, tiled=True))
        ffn_own = wide_sum[: 2 * size]
        out_own = wide_sum[2 * size :].reshape(size, parts, width).transpose(1, 0, 2)
        out_own = total(lax.all_to_all(out_own, "pat", 0, 0, tiled=True))
        narrow_own = total(lax.all_to_all(narrow, both, 0, 0, tiled=True))
        mine = jnp.concatenate([narrow_own[: 3 * size], out_own, narrow_own[3 * size :]], axis=0)
        mine = lax.all_gather(mine, "pat")
        mine = broadcast_exchange(mine, "row")
        other = swap(mine)
        ffn_mine = broadcast_exchange(ffn_own, "row")
        ffn_other = swap(ffn_mine)
        grads = kernel_call(
            functools.partial(spread_kernel, rows_count, seq_count),
            (shape(D, D, kind=f32),) * 4,
            in_specs=specs(1, 2),
            flops=1 << 28,
        )(here, mine, other)
        vectors = jnp.sum(mine[0, :, 4 * size :, :].astype(f32), axis=0).reshape(4, D)
        first = jnp.where(seq_index == 0, ffn_mine, ffn_other)
        second = jnp.where(seq_index == 0, ffn_other, ffn_mine)
        halves = jnp.stack([first, second], axis=1).reshape(blocks, 2, size, D)
        grad_down = halves[:, 0].reshape(D, D).astype(f32)
        grad_up = halves[:, 1].reshape(D, D).astype(f32)
    else:
        wide_sum = lax.psum(wide[0], both).astype(f32)
        grad_down, grad_up = wide_sum[:D], wide_sum[D : 2 * D]
        grad_out = lax.psum(wide_sum[2 * D :].astype(bf16), "pat").astype(f32)
        narrow_sum = lax.all_gather(lax.psum(narrow[0], both), "pat").astype(f32)
        grads = [
            narrow_sum[:, at * D : (at + 1) * D].transpose(1, 0, 2).reshape(D, D)
            for at in range(3)
        ] + [grad_out]
        vectors = jnp.sum(narrow_sum[:, 3 * D :], axis=0).reshape(4, D)
    return (
        output,
        grad_input,
        vectors[0],
        vectors[1],
        grads[0],
        grads[1],
        grads[2],
        grads[3],
        vectors[2],
        vectors[3],
        grad_up,
        grad_down,
    )


def solution(mesh):
    placed = (
        P("row", "seq", None),
        P("row", None),
        P(),
        P(),
        P(),
        P(),
        P(),
        P(),
        P(),
        P(),
        P(None, "pat"),
        P("pat", None),
        P("row", "seq", "pat"),
    )
    return jax.shard_map(
        per_device,
        mesh=mesh,
        in_specs=placed,
        out_specs=(
            P("row", "seq", "pat"),
            P("row", ("seq", "pat"), None),
            P(),
            P(),
            P(),
            P(),
            P(),
            P(),
            P(),
            P(),
            P(None, "pat"),
            P("pat", None),
        ),
        check_vma=False,
    )
```

time: 782 us -> 304 us (0.39)
  waiting for transfers between devices: 486 us -> 72.1 us
  matrix products: 77.3 us -> 0 us
  Pallas kernels: 0 us -> 41.3 us
  starting transfers between devices: 0.49 us -> 33.5 us
  other arithmetic: 49.7 us -> 16.7 us
  local copies, waits for them, and re-layouts: 57.2 us -> 35.5 us
  blocking collectives: 82.4 us -> 102 us
  between operations: 15.1 us -> 0.91 us
  loops' own time: 8.68 us -> 0 us
    psum x3 -> x0, waiting for transfers between devices: 286 us -> none  [the longest x1 200 us: per_device(): lax.psum((grad_wq, grad_wk, grad_wv, grad_wout, grad_gain_one, grad_bias_...]
    reduce_scatter x4 -> x0, waiting for transfers between devices: 90.5 us -> none  [the longest x1 33.3 us: per_device(): lax.psum_scatter(key_terms.astype(jnp.bfloat16), 'seq', scatter_dimension...]
    dot_general x25 -> x0, matrix products: 77.3 us -> none  [the longest x2 25.3 us: tile_scores(): jnp.einsum('qhd,khd->hqk', query_source, key_piece_rows, preferred_elemen...]
    all_gather x3 -> x0, waiting for transfers between devices: 73.9 us -> none  [the longest x1 57.1 us: combined_all(): lax.all_gather(a.astype(kind), axis)]
    all_to_all x0 -> x7, waiting for transfers between devices: none -> 70.4 us  [the longest x1 20.2 us: per_device(): wide_sum = total(lax.all_to_all(wide, both, 0, 0, tiled=True))]
    all_to_all x0 -> x2, blocking collectives: none -> 59.4 us  [the longest x1 36.4 us: broadcast_exchange(): lax.all_to_all(jnp.broadcast_to(value[None], (count,) + value.shape), axi...]
    pallas_call x0 -> x6, Pallas kernels: none -> 41.3 us  [the longest x1 11.9 us: per_device(): kernel_call(functools.partial(middle_kernel, blocks), (shape(parts, span,...]
    psum x1 -> x0, blocking collectives: 39.4 us -> none  [per_device(): lax.psum((grad_wq, grad_wk, grad_wv, grad_wout, grad_gain_one, grad_bias_...]
  transfers between devices with their start and end apart: 12 -> 13, of which waited for: 12 -> 7; matrix products, arithmetic and copies ran while one was open for 5% -> 12% of each run, Pallas kernels for 0% -> 6%
where the time goes in v1:
time: 304 us; the launch traced here: 302 us
  blocking collectives  102 us (34%)
  waiting for transfers between devices  72.1 us (24%)
  Pallas kernels  41.3 us (14%)
  local copies, waits for them, and re-layouts  35.5 us (12%)
  starting transfers between devices  33.5 us (11%)
  other arithmetic  16.7 us (5%)
    all_to_all x1, blocking collectives, broadcast_exchange(): lax.all_to_all(jnp.broadcast_to(value[None], (count,) + value.shape), axi...  36.4 us
    all_gather x1, blocking collectives, per_device(): mixed4 = lax.all_gather(mixed, 'pat')  25.2 us
    all_to_all x1, blocking collectives, per_device(): gm_parts = lax.all_to_all(gm, 'pat', 0, 0, tiled=True)  23 us
    all_to_all x1, waiting for transfers between devices, per_device(): wide_sum = total(lax.all_to_all(wide, both, 0, 0, tiled=True))  20.2 us
    all_to_all x1, waiting for transfers between devices, per_device(): ffn_parts = lax.all_to_all(ffn, 'pat', 0, 0, tiled=True)  20.1 us
    all_gather x1, blocking collectives, per_device(): mine = lax.all_gather(mine, 'pat')  17.7 us
    all_to_all x1, waiting for transfers between devices, per_device(): narrow_own = total(lax.all_to_all(narrow, both, 0, 0, tiled=True))  13.6 us
    pallas_call x1, Pallas kernels, per_device(): kernel_call(functools.partial(middle_kernel, blocks), (shape(parts, span,...  11.9 us
  transfers between devices with their start and end apart: 13, of which 7 were waited for; matrix products, arithmetic and copies ran while one was open for 12% of the time, Pallas kernels for 6%

profile of v1, /device:TPU:0, one launch (start us, length us, event | category | flops | bytes accessed | tf_op | source)
XLA Modules:
  0.0 302.3 jit_solution(16197128880567227165)
XLA Ops:
  3.2 4.7 %shard_map.220 = (bf16[512,768]{1,0:T(8,128)(2,1)}, bf16[512,192]{1,0:T(8,128)(2,1)}, bf16[512,192]{1,0:T(8,128)(2,1)}, bf16[512,192]{1,0:T(8,128)(2,1)}, bf16[3,768,192]{2,1,0:T(8,128)(2,1)}) custom-call(s32[1]{0:T(128)} %bitcast.2.where, bf16[512,768]{1,0:T(8,128)(2,1)} %bitcast.31, f32[1,768]{1,0:T(1,128)} %broadcast_in_dim.114.gain, ...), custom_call_target="tpu_custom_call" | custom-call | flops 452984832 | bytes 4194304 | tf_op jit(solution)/shard_map/pallas_call | solution.py:465
  9.4 6.6 %all-to-all-start = ((bf16[4,512,192]{1,2,0:T(8,128)(2,1)}), bf16[4,512,192]{1,2,0:T(8,128)(2,1)S(1)}, u32[]{:S(2)}, u32[]{:S(2)}) async-start(bf16[4,512,192]{1,2,0:T(8,128)(2,1)} %broadcast_in_dim.127), calls=%async_computation | async-start | bytes 1572864 | tf_op jit(solution)/shard_map/all_to_all | solution.py:402
  17.6 4.0 %fusion.4.feats = bf16[3,1024,128]{2,1,0:T(8,128)(2,1)} fusion(s32[3,1024]{1,0:T(4,128)S(1)} %fusion.15, s32[3,1024]{1,0:T(4,128)S(1)} %fusion.16, s32[3,1024]{1,0:T(4,128)S(1)} %fusion.19, s32[3,1024]{1,0:T(4,128)S(1)} %fusion.20, s32[1024]{0:T(1024)S(1)} %bitcast.41), kind=kLoop, calls=%fused_computation.10 | loop fusion | flops 3932160 | bytes 839680 | tf_op jit(solution)/shard_map/convert_element_type | solution.py:425
  22.5 5.5 %shard_map.221 = (bf16[512,192]{1,0:T(8,128)(2,1)}, f32[192,512]{1,0:T(8,128)}, f32[8,512]{1,0:T(8,128)}) custom-call(s32[1]{0:T(128)} %bitcast.1.where, bf16[512,192]{1,0:T(8,128)(2,1)} %get-tuple-element.36.q, bf16[512,192]{1,0:T(8,128)(2,1)} %get-tuple-element.37.k, bf16[512,192]{1,0:T(8,128)(2,1)} %get-tuple-element.38.v, bf16[512,192]{1,0:T(8,128)(2,1)} %copy-done.9, ...), custom_call_target="tpu_custom_call" | custom-call | flops 2147483648 | bytes 4194304 | tf_op jit(solution)/shard_map/pallas_call | solution.py:485
  28.0 25.2 %all-gather = bf16[2048,192]{1,0:T(8,128)(2,1)} all-gather(bf16[512,192]{1,0:T(8,128)(2,1)} %get-tuple-element.39), channel_id=2, replica_groups=mesh['row'=4,'seq'=2,'pat'=4] {'pat'}, dimensions={0}, use_global_device_ids=true | all-gather | bytes 983040 | tf_op jit(solution)/shard_map/all_gather | solution.py:497
  54.5 11.9 %shard_map.222 = (bf16[4,512,192]{2,1,0:T(8,128)(2,1)}, bf16[4,512,192]{2,1,0:T(8,128)(2,1)}, f32[512,768]{1,0:T(8,128)}, bf16[8,288,768]{2,1,0:T(8,128)(2,1)}, f32[8,768]{1,0:T(8,128)}) custom-call(bf16[512,768]{1,0:T(8,128)(2,1)} %bitcast.32, bf16[4,512,192]{2,1,0:T(8,128)(2,1)} %bitcast.34, bf16[4,512,192]{2,1,0:T(8,128)(2,1)} %copy.61.c4, ...), custom_call_target="tpu_custom_call" | custom-call | flops 5435817984 | bytes 4194304 | tf_op jit(solution)/shard_map/pallas_call | solution.py:498
  68.6 3.5 %all-to-all-start.1 = ((bf16[4,512,192]{1,2,0:T(8,128)(2,1)}), bf16[4,512,192]{1,2,0:T(8,128)(2,1)S(1)}, u32[]{:S(2)}, u32[]{:S(2)}) async-start(bf16[4,512,192]{1,2,0:T(8,128)(2,1)} %copy.62), calls=%async_computation.1 | async-start | bytes 1572864 | tf_op jit(solution)/shard_map/all_to_all | solution.py:513
  72.6 20.1 %all-to-all-done.1 = bf16[4,512,192]{1,2,0:T(8,128)(2,1)S(1)} async-done(((bf16[4,512,192]{1,2,0:T(8,128)(2,1)}), bf16[4,512,192]{1,2,0:T(8,128)(2,1)S(1)}, u32[]{:S(2)}, u32[]{:S(2)}) %all-to-all-start.1) | async-done | bytes 786464 | tf_op jit(solution)/shard_map/all_to_all | solution.py:513
  92.8 23.0 %all_to_all.45 = bf16[4,512,192]{1,2,0:T(8,128)(2,1)} all-to-all(bf16[4,512,192]{1,2,0:T(8,128)(2,1)S(1)} %copy.64), channel_id=1, replica_groups=mesh['row'=4,'seq'=2,'pat'=4] {'pat'}, dimensions={0} | all-to-all | bytes 1572864 | tf_op jit(solution)/shard_map/all_to_all | solution.py:512
  115.7 3.8 %all-to-all-start.5 = ((bf16[8,288,768]{2,1,0:T(8,128)(2,1)}), bf16[8,288,768]{2,1,0:T(8,128)(2,1)S(1)}, u32[]{:S(2)}, u32[]{:S(2)}) async-start(bf16[8,288,768]{2,1,0:T(8,128)(2,1)} %get-tuple-element.55), calls=%async_computation.5 | async-start | bytes 7077888 | tf_op jit(solution)/shard_map/all_to_all | solution.py:565
  121.7 5.9 %shard_map.223 = (bf16[512,192]{1,0:T(8,128)(2,1)}, f32[512,192]{1,0:T(8,128)}, f32[512,192]{1,0:T(8,128)}, bf16[512,192]{1,0:T(8,128)(2,1)}, bf16[512,192]{1,0:T(8,128)(2,1)}) custom-call(s32[1]{0:T(128)} %bitcast.1.where, bf16[4,512,192]{2,1,0:T(8,128)(2,1)} %copy.65.parts, f32[192,512]{1,0:T(8,128)} %get-tuple-element.44.mixed_t, ...), custom_call_target="tpu_custom_call" | custom-call | flops 4294967296 | bytes 4194304 | tf_op jit(solution)/shard_map/pallas_call | solution.py:516
  133.0 5.9 %shard_map.224 = (bf16[8,304,192]{2,1,0:T(8,128)(2,1)}, bf16[512,768]{1,0:T(8,128)(2,1)}) custom-call(bf16[512,768]{1,0:T(8,128)(2,1)} %bitcast.33, f32[1,768]{1,0:T(1,128)} %broadcast_in_dim.114.gain, bf16[512,768]{1,0:T(8,128)(2,1)} %get-tuple-element.41.normed, bf16[3,768,192]{2,1,0:T(8,128)(2,1)} %get-tuple-element.42.own, ...), custom_call_target="tpu_custom_call" | custom-call | flops 905969664 | bytes 4194304 | tf_op jit(solution)/shard_map/pallas_call | solution.py:545
  141.4 20.2 %all-to-all-done.5 = bf16[8,288,768]{2,1,0:T(8,128)(2,1)S(1)} async-done(((bf16[8,288,768]{2,1,0:T(8,128)(2,1)}), bf16[8,288,768]{2,1,0:T(8,128)(2,1)S(1)}, u32[]{:S(2)}, u32[]{:S(2)}) %all-to-all-start.5) | async-done | bytes 3538976 | tf_op jit(solution)/shard_map/all_to_all | solution.py:565
  161.6 4.3 %all-to-all-start.4 = ((bf16[8,304,192]{1,2,0:T(8,128)(2,1)}), bf16[8,304,192]{1,2,0:T(8,128)(2,1)}, u32[]{:S(2)}, u32[]{:S(2)}) async-start(bf16[8,304,192]{1,2,0:T(8,128)(2,1)} %copy.66), calls=%async_computation.4 | async-start | bytes 2359296 | tf_op jit(solution)/shard_map/all_to_all | solution.py:569
  169.1 13.6 %all-to-all-done.4 = bf16[8,304,192]{1,2,0:T(8,128)(2,1)} async-done(((bf16[8,304,192]{1,2,0:T(8,128)(2,1)}), bf16[8,304,192]{1,2,0:T(8,128)(2,1)}, u32[]{:S(2)}, u32[]{:S(2)}) %all-to-all-start.4) | async-done | bytes 933920 | tf_op jit(solution)/shard_map/all_to_all | solution.py:569
  186.1 6.2 %all-to-all-done.6 = bf16[4,96,192]{2,1,0:T(8,128)(2,1)S(1)} async-done(((bf16[4,96,192]{2,1,0:T(8,128)(2,1)}), bf16[4,96,192]{2,1,0:T(8,128)(2,1)S(1)}, u32[]{:S(2)}, u32[]{:S(2)}) %all-to-all-start.6) | async-done | bytes 147488 | tf_op jit(solution)/shard_map/all_to_all | solution.py:568
  193.4 3.5 %all-to-all-start.8 = ((bf16[4,192,768]{2,1,0:T(8,128)(2,1)}), bf16[4,192,768]{2,1,0:T(8,128)(2,1)S(1)}, u32[]{:S(2)}, u32[]{:S(2)}) async-start(bf16[4,192,768]{2,1,0:T(8,128)(2,1)} %broadcast_in_dim.133), calls=%async_computation.8 | async-start | bytes 2359296 | tf_op jit(solution)/shard_map/all_to_all | solution.py:402
  198.8 17.7 %all-gather.2 = bf16[4,400,192]{1,2,0:T(8,128)(2,1)S(1)} all-gather(bf16[1,400,192]{1,2,0:T(8,128)(2,1)S(1)} %maximum_bitcast_fusion), channel_id=3, replica_groups=mesh['row'=4,'seq'=2,'pat'=4] {'pat'}, dimensions={0}, use_global_device_ids=true | all-gather | bytes 768000 | tf_op jit(solution)/shard_map/all_gather | solution.py:571
  217.8 36.4 %all_to_all.46 = bf16[4,4,400,192]{2,3,1,0:T(8,128)(2,1)S(1)} all-to-all(bf16[4,4,400,192]{2,3,1,0:T(8,128)(2,1)S(1)} %broadcast_in_dim.132), channel_id=1, replica_groups=mesh['row'=4,'seq'=2,'pat'=4] {'row'}, dimensions={0} | all-to-all | bytes 4915200 | tf_op jit(solution)/shard_map/all_to_all | solution.py:402
  254.3 4.2 %all-to-all-start.3 = ((bf16[4,128,768]{2,1,0:T(8,128)(2,1)}), bf16[4,128,768]{2,1,0:T(8,128)(2,1)}, u32[]{:S(2)}, u32[]{:S(2)}) async-start(bf16[4,128,768]{2,1,0:T(8,128)(2,1)} %bitcast.37), calls=%async_computation.3 | async-start | bytes 1572864 | tf_op jit(solution)/shard_map/all_to_all | solution.py:557
  262.9 10.3 %all-to-all-done.3 = bf16[4,128,768]{2,1,0:T(8,128)(2,1)} async-done(((bf16[4,128,768]{2,1,0:T(8,128)(2,1)}), bf16[4,128,768]{2,1,0:T(8,128)(2,1)}, u32[]{:S(2)}, u32[]{:S(2)}) %all-to-all-start.3) | async-done | bytes 786464 | tf_op jit(solution)/shard_map/all_to_all | solution.py:557
  278.4 4.2 %copy.71.mine = bf16[4,4,400,192]{3,2,1,0:T(8,128)(2,1)} copy(bf16[4,4,400,192]{2,3,1,0:T(8,128)(2,1)S(1)} %all_to_all.46) | data formatting | bytes 4915200 | tf_op jit(solution)/shard_map/all_to_all | solution.py:402
  288.1 6.8 %copy.72.other = bf16[4,4,400,192]{3,2,1,0:T(8,128)(2,1)} copy(bf16[4,4,400,192]{2,3,1,0:T(8,128)(2,1)} %collective-permute-done.4) | data formatting | bytes 4915200 | tf_op jit(solution)/shard_map/ppermute | solution.py:408
  294.9 7.5 %shard_map.225 = (f32[768,768]{1,0:T(8,128)}, f32[768,768]{1,0:T(8,128)}, f32[768,768]{1,0:T(8,128)}, f32[768,768]{1,0:T(8,128)}) custom-call(s32[1]{0:T(128)} %bitcast.1.where, bf16[4,4,400,192]{3,2,1,0:T(8,128)(2,1)} %copy.71.mine, bf16[4,4,400,192]{3,2,1,0:T(8,128)(2,1)} %copy.72.other), custom_call_target="tpu_custom_call" | custom-call | flops 268435456 | bytes 4194304 | tf_op jit(solution)/shard_map/pallas_call | solution.py:576
  (90 shorter events, 46.5 us)
Async XLA Ops:
  3.2 5.3 %copy-start.5 = (bf16[1,512,192]{1,2,0:T(8,128)(2,1)S(1)}, bf16[1,512,192]{1,2,0:T(8,128)(2,1)}, u32[]{:S(2)}) copy-start(bf16[1,512,192]{1,2,0:T(8,128)(2,1)} %param.25) | copy-start | bytes 589828
  7.9 8.2 %copy-start.8 = (s32[1,1024]{1,0:T(1,128)S(1)}, s32[1,1024]{1,0:T(1,128)}, u32[]{:S(2)}) copy-start(s32[1,1024]{1,0:T(1,128)} %param.14) | copy-start | bytes 12292
  7.9 8.2 %copy-start.6 = (f32[768]{0:T(1024)S(1)}, f32[768]{0:T(1024)}, u32[]{:S(2)}) copy-start(f32[768]{0:T(1024)} %param.21) | copy-start | bytes 9220
  7.9 8.8 %copy-start.7 = (f32[768]{0:T(1024)S(1)}, f32[768]{0:T(1024)}, u32[]{:S(2)}) copy-start(f32[768]{0:T(1024)} %param.22) | copy-start | bytes 9220
  7.9 13.8 %collective-permute-start = (bf16[512,192]{1,0:T(8,128)(2,1)}, bf16[512,192]{1,0:T(8,128)(2,1)S(1)}, u32[]{:S(2)}, u32[]{:S(2)}) collective-permute-start(bf16[512,192]{1,0:T(8,128)(2,1)} %get-tuple-element.37.k), channel_id=1, source_target_pairs={{0,4},{4,0},{1,5},{5,1},{2,6},{6,2},{3,7},{7,3},{8,12},{12,8},{9,1... | collective-permute-start | bytes 589832 | tf_op jit(solution)/shard_map/ppermute | solution.py:408
  8.4 13.3 %collective-permute-start.1 = (bf16[512,192]{1,0:T(8,128)(2,1)}, bf16[512,192]{1,0:T(8,128)(2,1)S(1)}, u32[]{:S(2)}, u32[]{:S(2)}) collective-permute-start(bf16[512,192]{1,0:T(8,128)(2,1)} %get-tuple-element.38.v), channel_id=1, source_target_pairs={{0,4},{4,0},{1,5},{5,1},{2,6},{6,2},{3,7},{7,3},{8,12},{12,8},{9,1... | collective-permute-start | bytes 589832 | tf_op jit(solution)/shard_map/ppermute | solution.py:408
  9.4 43.8 %all-to-all-start = ((bf16[4,512,192]{1,2,0:T(8,128)(2,1)}), bf16[4,512,192]{1,2,0:T(8,128)(2,1)S(1)}, u32[]{:S(2)}, u32[]{:S(2)}) async-start(bf16[4,512,192]{1,2,0:T(8,128)(2,1)} %broadcast_in_dim.127), calls=%async_computation | async-start | bytes 1572864 | tf_op jit(solution)/shard_map/all_to_all | solution.py:402
  21.7 0.7 copy-start.9
  21.7 0.8 copy-start.10
  66.3 5.8 %copy-start.2 = (bf16[4,512,192]{2,1,0:T(8,128)(2,1)S(1)}, bf16[4,512,192]{2,1,0:T(8,128)(2,1)}, u32[]{:S(2)}) copy-start(bf16[4,512,192]{2,1,0:T(8,128)(2,1)} %get-tuple-element.43) | copy-start | bytes 2359300
  68.6 24.1 %all-to-all-start.1 = ((bf16[4,512,192]{1,2,0:T(8,128)(2,1)}), bf16[4,512,192]{1,2,0:T(8,128)(2,1)S(1)}, u32[]{:S(2)}, u32[]{:S(2)}) async-start(bf16[4,512,192]{1,2,0:T(8,128)(2,1)} %copy.62), calls=%async_computation.1 | async-start | bytes 1572864 | tf_op jit(solution)/shard_map/all_to_all | solution.py:513
  92.8 23.0 %copy-start.1 = (bf16[4,512,192]{1,2,0:T(8,128)(2,1)}, bf16[4,512,192]{1,2,0:T(8,128)(2,1)S(1)}, u32[]{:S(2)}) copy-start(bf16[4,512,192]{1,2,0:T(8,128)(2,1)S(1)} %all-to-all-done.1) | copy-start | bytes 2359300
  115.7 45.9 %all-to-all-start.5 = ((bf16[8,288,768]{2,1,0:T(8,128)(2,1)}), bf16[8,288,768]{2,1,0:T(8,128)(2,1)S(1)}, u32[]{:S(2)}, u32[]{:S(2)}) async-start(bf16[8,288,768]{2,1,0:T(8,128)(2,1)} %get-tuple-element.55), calls=%async_computation.5 | async-start | bytes 7077888 | tf_op jit(solution)/shard_map/all_to_all | solution.py:565
  127.6 4.4 %collective-permute-start.2 = (bf16[512,192]{1,0:T(8,128)(2,1)}, bf16[512,192]{1,0:T(8,128)(2,1)S(1)}, u32[]{:S(2)}, u32[]{:S(2)}) collective-permute-start(bf16[512,192]{1,0:T(8,128)(2,1)} %get-tuple-element.49), channel_id=1, source_target_pairs={{0,4},{4,0},{1,5},{5,1},{2,6},{6,2},{3,7},{7,3},{8,12},{12,8},{9,1... | collective-permute-start | bytes 589832 | tf_op jit(solution)/shard_map/ppermute | solution.py:408
  130.6 1.7 collective-permute-start.3
  132.0 0.7 copy-start.3
  161.6 21.1 %all-to-all-start.4 = ((bf16[8,304,192]{1,2,0:T(8,128)(2,1)}), bf16[8,304,192]{1,2,0:T(8,128)(2,1)}, u32[]{:S(2)}, u32[]{:S(2)}) async-start(bf16[8,304,192]{1,2,0:T(8,128)(2,1)} %copy.66), calls=%async_computation.4 | async-start | bytes 2359296 | tf_op jit(solution)/shard_map/all_to_all | solution.py:569
  167.3 25.1 %slice-start = ((bf16[288,768]{1,0:T(8,128)(2,1)}), bf16[192,768]{1,0:T(8,128)(2,1)S(1)}, s32[]{:S(2)}) async-start(bf16[288,768]{1,0:T(8,128)(2,1)} %reduce_sum.72), calls=%async_computation.9 | async-start | bytes 589824 | tf_op jit(solution)/shard_map/slice | solution.py:566
  182.7 9.6 %all-to-all-start.6 = ((bf16[4,96,192]{2,1,0:T(8,128)(2,1)}), bf16[4,96,192]{2,1,0:T(8,128)(2,1)S(1)}, u32[]{:S(2)}, u32[]{:S(2)}) async-start(bf16[4,96,192]{2,1,0:T(8,128)(2,1)} %copy.67), calls=%async_computation.6 | async-start | bytes 393216 | tf_op jit(solution)/shard_map/all_to_all | solution.py:568
  193.4 23.1 %all-to-all-start.8 = ((bf16[4,192,768]{2,1,0:T(8,128)(2,1)}), bf16[4,192,768]{2,1,0:T(8,128)(2,1)S(1)}, u32[]{:S(2)}, u32[]{:S(2)}) async-start(bf16[4,192,768]{2,1,0:T(8,128)(2,1)} %broadcast_in_dim.133), calls=%async_computation.8 | async-start | bytes 2359296 | tf_op jit(solution)/shard_map/all_to_all | solution.py:402
  216.5 1.0 copy-start
  254.3 18.9 %all-to-all-start.3 = ((bf16[4,128,768]{2,1,0:T(8,128)(2,1)}), bf16[4,128,768]{2,1,0:T(8,128)(2,1)}, u32[]{:S(2)}, u32[]{:S(2)}) async-start(bf16[4,128,768]{2,1,0:T(8,128)(2,1)} %bitcast.37), calls=%async_computation.3 | async-start | bytes 1572864 | tf_op jit(solution)/shard_map/all_to_all | solution.py:557
  258.5 24.1 %collective-permute-start.5 = (bf16[4,192,768]{2,1,0:T(8,128)(2,1)}, bf16[4,192,768]{2,1,0:T(8,128)(2,1)}, u32[]{:S(2)}, u32[]{:S(2)}) collective-permute-start(bf16[4,192,768]{2,1,0:T(8,128)(2,1)} %copy-done), channel_id=1, source_target_pairs={{0,4},{4,0},{1,5},{5,1},{2,6},{6,2},{3,7},{7,3},{8,12},{12,8},{9,1... | collective-permute-start | bytes 3538952 | tf_op jit(solution)/shard_map/ppermute | solution.py:408
  258.5 29.5 %collective-permute-start.4 = (bf16[4,4,400,192]{2,3,1,0:T(8,128)(2,1)S(1)}, bf16[4,4,400,192]{2,3,1,0:T(8,128)(2,1)}, u32[]{:S(2)}, u32[]{:S(2)}) collective-permute-start(bf16[4,4,400,192]{2,3,1,0:T(8,128)(2,1)S(1)} %all_to_all.46), channel_id=1, source_target_pairs={{0,4},{4,0},{1,5},{5,1},{2,6},{6,2},{3,7},{7,3},{8,12},{12,8},{9,1... | collective-permute-start | bytes 7372808 | tf_op jit(solution)/shard_map/ppermute | solution.py:408
  (1 other events, 0.7 us)

commit v2 on v1

v2 whole, which is shorter than its diff:
```python
import functools

import jax
import jax.numpy as jnp
from jax import lax
from jax.experimental import pallas as pl
from jax.experimental.pallas import tpu as pltpu
from jax.sharding import PartitionSpec as P

D = 768
HEADS = 12
HDIM = 64

epsilon = 1e-05
masked_low = -1e30
segment_parts = (1, 2, 4, 8, 16)
dilations = (1, 2, 4, 6, 12)
DOCS = 3
FEATS = 128
TILE = 256
VMEM_LIMIT = 60 * 1024 * 1024
SMALL_LIMIT = 20 * 1024 * 1024
COPIES = 24
f32 = jnp.float32
bf16 = jnp.bfloat16


def dot(a, b):
    return lax.dot_general(a, b, (((1,), (0,)), ((), ())), preferred_element_type=f32)


def dot_nt(a, b):
    return lax.dot_general(a, b, (((1,), (1,)), ((), ())), preferred_element_type=f32)


def dot_tn(a, b):
    return lax.dot_general(a, b, (((0,), (0,)), ((), ())), preferred_element_type=f32)


class Staged:
    def __init__(self, outside, inside, sems, free):
        self.outside, self.inside, self.sems, self.free = outside, inside, sems, free
        self.pending = []

    def start(self, source=None, target=None):
        copy = pltpu.make_async_copy(
            self.outside if source is None else source,
            self.inside if target is None else target,
            self.sems.at[next(self.free)],
        )
        copy.start()
        self.pending.append(copy)

    def get(self):
        for copy in self.pending:
            copy.wait()
        self.pending = []
        return self.inside

    def send(self, at=...):
        copy = pltpu.make_async_copy(
            self.inside.at[at], self.outside.at[at], self.sems.at[next(self.free)]
        )
        copy.start()
        self.pending.append(copy)


def staged_call(body, scalars, arrays, outs, scratch=(), windows=None, limit=VMEM_LIMIT, late=0, aliases=()):
    windows = windows or {}
    n_scalar, n_in, n_out = len(scalars), len(arrays), len(outs)

    def kernel(*refs):
        scalar_refs, refs = refs[:n_scalar], refs[n_scalar:]
        outside, refs = refs[: n_in + n_out], refs[n_in + n_out :]
        inside, refs = refs[: n_in + n_out], refs[n_in + n_out :]
        sems, rest = refs[0], refs[1:]
        free = iter(range(COPIES))
        every = [Staged(o, i, sems, free) for o, i in zip(outside, inside, strict=True)]
        ins, results = every[:n_in], every[n_in:]
        for at, one in enumerate(ins[: n_in - late]):
            if at in windows:
                start = windows[at](scalar_refs)
                size = one.inside.shape[-1]
                one.start(one.outside.at[:, pl.ds(pl.multiple_of(start, 128), size)])
            else:
                one.start()
        body(scalar_refs, ins, results, rest)
        for one in ins + results:
            one.get()

    def buffer(at, array):
        dims = array.shape
        if at >= n_in - late:
            return pltpu.VMEM((16, 128), array.dtype)
        if at in windows:
            dims = (*dims[:-1], 256)
        return pltpu.VMEM(dims, array.dtype)

    return pl.pallas_call(
        kernel,
        out_shape=tuple(outs),
        in_specs=[pl.BlockSpec(memory_space=pltpu.SMEM)] * n_scalar
        + [pl.BlockSpec(memory_space=pl.ANY)] * n_in,
        out_specs=(pl.BlockSpec(memory_space=pltpu.HBM),) * n_out,
        scratch_shapes=[buffer(at, a) for at, a in enumerate(arrays)]
        + [
            pltpu.VMEM((16, 128) if at in dict(aliases).values() else o.shape, o.dtype)
            for at, o in enumerate(outs)
        ]
        + [pltpu.SemaphoreType.DMA((COPIES,))]
        + list(scratch),
        input_output_aliases={n_scalar + a: o for a, o in aliases},
        compiler_params=pltpu.CompilerParams(vmem_limit_bytes=limit),
        cost_estimate=pl.CostEstimate(flops=0, bytes_accessed=0, transcendentals=0),
    )(*scalars, *arrays)


def normalise(values):
    center = values - jnp.mean(values, axis=-1, keepdims=True)
    scale = lax.rsqrt(jnp.mean(center * center, axis=-1, keepdims=True) + epsilon)
    return center * scale, scale


def norm_backward(hat, scale, grad):
    return scale * (
        grad
        - jnp.mean(grad, axis=-1, keepdims=True)
        - hat * jnp.mean(grad * hat, axis=-1, keepdims=True)
    )


def project_kernel(parts, scalars, ins, outs, scratch):
    x, gain, bias, *weights = ins
    normed, q, kv, own = outs
    width = D // parts
    where = scalars[0]
    own.inside[:, 3 * width :] = jnp.zeros((D, D - 3 * width), bf16)
    gain = gain.get()[...].reshape(1, D)
    bias = bias.get()[...].reshape(1, D)
    x.get()
    span = x.inside.shape[0]
    for start in range(0, span, TILE):
        rows = slice(start, start + TILE)
        hat, _ = normalise(x.inside[rows, :].astype(f32))
        normed.inside[rows, :] = (hat * gain + bias).astype(bf16)
    normed.send()
    for w in weights:
        w.get()
    for odd in range(2):

        @pl.when(where[0] % 2 == odd)
        def _():
            for at, w in enumerate(weights):
                own.inside[:, at * width : (at + 1) * width] = w.inside[
                    :, odd * 64 : odd * 64 + width
                ]

    own.send()
    for start in range(0, span, TILE):
        rows = slice(start, start + TILE)
        made = dot(normed.inside[rows, :], own.inside[:, : 3 * width]).astype(bf16)
        q.inside[rows, :] = (made[:, :width].astype(f32) * HDIM**-0.5).astype(bf16)
        kv.inside[rows, :] = made[:, width:]
    kv.send()
    q.send()


def head_mask(heads, width):
    lane = lax.broadcasted_iota(jnp.int32, (1, width), 1)
    return [((lane >= h * HDIM) & (lane < (h + 1) * HDIM)).astype(bf16) for h in range(heads)]


def attention_kernel(heads, span, scalars, ins, outs, scratch):
    where = scalars[0]
    q, kv, feats, kv_far = (one.get() for one in ins)
    mixed_low, mixed_t, lse = (one.inside for one in outs)
    q_head, k, v_t, kf, vf_t = scratch
    width = heads * HDIM
    masks = head_mask(heads, width)
    for h in range(heads):
        q_head[h] = q[...] * masks[h]
    k[...] = kv[:, :width]
    v_t[...] = kv[:, width:].T
    far = kv_far.shape[0] // span

    def turn(j, _):
        rows = pl.ds(pl.multiple_of(j * span, span), span)
        kf[rows, :] = kv_far[rows, :width]
        vf_t[j] = kv_far[rows, width:].T
        return 0

    mine = where[0]
    lax.fori_loop(0, jnp.minimum(mine, far), turn, 0)
    own_start = pl.multiple_of(mine * span, span)
    lse[...] = jnp.zeros(lse.shape, f32)
    for start in range(0, span, TILE):
        for h in range(heads):
            q_tile = q_head[h, start : start + TILE, :]
            f_tile = feats[h, pl.ds(own_start + start, TILE), :]

            def part(k_rows, f_rows, v_rows, low_from, state):
                counts = dot_nt(f_rows, f_tile)
                if low_from is not None:
                    at_k = lax.broadcasted_iota(jnp.int32, counts.shape, 0)
                    at_q = lax.broadcasted_iota(jnp.int32, counts.shape, 1) + low_from
                    counts = jnp.where(at_k <= at_q, counts, 0.0)
                scores = jnp.where(counts > 0, dot_nt(k_rows, q_tile), masked_low)
                top, total, acc = state
                new_top = jnp.maximum(top, jnp.max(scores, axis=0, keepdims=True))
                weights = counts * jnp.exp(scores - new_top)
                factor = jnp.exp(top - new_top)
                return (
                    new_top,
                    total * factor + jnp.sum(weights, axis=0, keepdims=True),
                    acc * factor + dot(v_rows, weights.astype(bf16)),
                )

            state = (
                jnp.full((1, TILE), masked_low, f32),
                jnp.zeros((1, TILE), f32),
                jnp.zeros((HDIM, TILE), f32),
            )
            size = start + TILE
            head_rows = slice(h * HDIM, (h + 1) * HDIM)
            state = part(
                k[:size, :],
                feats[h, pl.ds(own_start, size), :],
                v_t[head_rows, :size],
                start,
                state,
            )

            def far_part(j, state):
                rows = pl.ds(pl.multiple_of(j * span, span), span)
                return part(kf[rows, :], feats[h, rows, :], vf_t[j, head_rows, :], None, state)

            top, total, acc = lax.fori_loop(0, mine, far_part, state)
            done = acc / total
            mixed_t[head_rows, start : start + TILE] = done
            mixed_low[head_rows, start : start + TILE] = done.astype(bf16)
            lse[h : h + 1, start : start + TILE] = top + jnp.log(total)
    for one in outs:
        one.send()


def attention_back_kernel(heads, span, scalars, ins, outs, scratch):
    where = scalars[0]
    parts, q, mixed_t, lse, kv, feats, kv_far = (one.get() for one in ins)
    grad_q, grad_kv, grad_far = (one.inside for one in outs)
    q_head, g_head, dots, probs, slopes, k, v, k_t, gq_t = scratch
    width = heads * HDIM
    masks = head_mask(heads, width)
    mine = where[0]
    far = kv_far.shape[0] // span
    total = parts[0].astype(f32)
    for part in range(1, parts.shape[0]):
        total = total + parts[part].astype(f32)
    low_t = total.astype(bf16)
    low = low_t.T
    for h in range(heads):
        q_head[h] = q[...] * masks[h]
        g_head[h] = low * masks[h]
    product = low_t.astype(f32) * mixed_t[...]
    for h in range(heads):
        dots[h : h + 1, :] = jnp.sum(product[h * HDIM : (h + 1) * HDIM], axis=0, keepdims=True)
    own_start = pl.multiple_of(mine * span, span)

    def block(h, start, size, f_rows, low_from):
        tile = slice(start, start + TILE)
        counts = dot_nt(f_rows, feats[h, pl.ds(own_start + start, TILE), :])
        if low_from is not None:
            at_k = lax.broadcasted_iota(jnp.int32, counts.shape, 0)
            at_q = lax.broadcasted_iota(jnp.int32, counts.shape, 1) + low_from
            counts = jnp.where(at_k <= at_q, counts, 0.0)
        scores = jnp.where(counts > 0, dot_nt(k[:size, :], q_head[h, tile, :]), masked_low)
        prob = counts * jnp.exp(scores - lse[h : h + 1, tile])
        grad_prob = dot_nt(v[:size, :], g_head[h, tile, :])
        slope = prob * (grad_prob - dots[h : h + 1, tile])
        columns = slice(h * span + start, h * span + start + TILE)
        probs[:size, columns] = prob.astype(bf16)
        slopes[:size, columns] = slope.astype(bf16)
        if size < span:
            probs[size:, columns] = jnp.zeros((span - size, TILE), bf16)
            slopes[size:, columns] = jnp.zeros((span - size, TILE), bf16)

    def finish():
        k_t[...] = k[...].T
        grad_v_rows = dot(probs[...], g_head[...].reshape(heads * span, width))
        grad_k_rows = dot(slopes[...], q_head[...].reshape(heads * span, width))
        terms = [
            dot(k_t[h * HDIM : (h + 1) * HDIM, :], slopes[:, h * span : (h + 1) * span])
            for h in range(heads)
        ]
        return grad_k_rows, grad_v_rows, terms

    k[...] = kv[:, :width]
    v[...] = kv[:, width:]
    for start in range(0, span, TILE):
        for h in range(heads):
            size = start + TILE
            block(h, start, size, feats[h, pl.ds(own_start, size), :], start)
    grad_k_rows, grad_v_rows, terms = finish()
    grad_kv[:, :width] = grad_k_rows
    grad_kv[:, width:] = grad_v_rows
    outs[1].send()
    for h in range(heads):
        gq_t[h * HDIM : (h + 1) * HDIM, :] = terms[h]

    def far_block(j, _):
        rows = pl.ds(pl.multiple_of(j * span, span), span)
        k[...] = kv_far[rows, :width]
        v[...] = kv_far[rows, width:]
        for start in range(0, span, TILE):
            for h in range(heads):
                block(h, start, span, feats[h, rows, :], None)
        grad_k_rows, grad_v_rows, terms = finish()
        grad_far[rows, :width] = grad_k_rows.astype(bf16)
        grad_far[rows, width:] = grad_v_rows.astype(bf16)
        for h in range(heads):
            gq_t[h * HDIM : (h + 1) * HDIM, :] += terms[h]
        return 0

    used = jnp.minimum(mine, far)
    lax.fori_loop(0, used, far_block, 0)

    def clear(j, _):
        grad_far[pl.ds(pl.multiple_of(j * span, span), span), :] = jnp.zeros((span, 2 * width), bf16)
        return 0

    lax.fori_loop(used, far, clear, 0)
    outs[2].send()
    grad_q[...] = (gq_t[...] * HDIM**-0.5).T.astype(bf16)
    outs[0].send()


def middle_kernel(pair, scalars, ins, outs, scratch):
    mixed4, x, w_out, gain, bias, w_up, w_down, *c_parts = ins
    gm, gr, sums, ffn, *wide = outs
    act, low, gh, branch, c, resids, made, c4 = scratch
    parts, width, span = mixed4.inside.shape
    for step, one in enumerate(c_parts):
        one.start(target=c4.at[scalars[1][0] ^ step])
    chunk = span // parts
    mixed_t = mixed4.get()[...].reshape(D, span)
    x.get(), w_out.get()
    gain = gain.get()[...].reshape(1, D)
    bias = bias.get()[...].reshape(1, D)
    gain_sum = jnp.zeros((1, D), f32)
    bias_sum = jnp.zeros((1, D), f32)
    for start in range(0, span, TILE):
        rows = slice(start, start + TILE)
        resid = x.inside[rows, :].astype(f32) + dot_tn(mixed_t[:, rows], w_out.inside[...])
        resids[rows, :] = resid
        hat, scale = normalise(resid)
        normed = (hat * gain + bias).astype(bf16)
        low[rows, :] = normed
        w_up.get()
        hidden = dot(normed, w_up.inside[...])
        bell = 0.5 + 0.5 * lax.erf(hidden * (0.5**0.5))
        act[rows, :] = (hidden * bell).astype(bf16)
        slope = bell + hidden * jnp.exp(-0.5 * hidden * hidden) * 0.3989422804014327
        if start == 0:
            w_down.get()
            for one in c_parts:
                one.get()
            for part in range(parts):
                c[:, part * width : (part + 1) * width] = c4[part].T
        grad_hidden = (slope * dot_nt(c[rows, :], w_down.inside[...])).astype(bf16)
        gh[rows, :] = grad_hidden
        grad_normed = dot_nt(grad_hidden, w_up.inside[...])
        gain_sum = gain_sum + jnp.sum(grad_normed * hat, axis=0, keepdims=True)
        bias_sum = bias_sum + jnp.sum(grad_normed, axis=0, keepdims=True)
        grad_resid = norm_backward(hat, scale, grad_normed * gain) + c[rows, :].astype(f32) * (
            1.0 / parts
        )
        gr.inside[rows, :] = grad_resid
        grad_low = grad_resid.astype(bf16)
        branch[rows, :] = grad_low
        for part in range(parts):
            gm.inside[part, :, rows] = dot_nt(
                w_out.inside[part * width : (part + 1) * width, :], grad_low
            ).astype(bf16)
    gm.send()
    gr.send()
    sums.inside[0:1, :] = gain_sum
    sums.inside[1:2, :] = bias_sum
    sums.send()
    where = scalars[0]
    lefts = (lambda: dot_tn(act[...], c[...]), lambda: dot_tn(low[...], gh[...]))
    lefts += (lambda: dot(mixed_t, branch[...]),)
    for at, product in enumerate(lefts):
        if not pair:
            wide[0].inside[at] = product().astype(bf16)
            continue
        made[...] = product().astype(bf16)
        rows_count = wide[0].inside.shape[1]
        size = D // (2 * rows_count)
        for row in range(rows_count):
            for out, half in ((wide[0], where[0]), (wide[1], 1 - where[0])):
                start = pl.multiple_of((2 * row + half) * size, size)
                out.inside[at, row] = made[pl.ds(start, size), :]
        wide[1].send(at)
        wide[0].send(at)
    if not pair:
        wide[0].send()
    for start in range(0, span, TILE):
        rows = slice(start, start + TILE)
        out = dot(act[rows, :], w_down.inside[...]) + resids[rows, :] * (1.0 / parts)
        out_t = out.astype(bf16).T
        for part in range(parts):
            for at in range(start, start + TILE, chunk):
                ffn.inside[part, at // chunk * width : (at // chunk + 1) * width, :] = out_t[
                    part * width : (part + 1) * width, at - start : at - start + chunk
                ]
    ffn.send()


def add_kernel(scalars, ins, outs, scratch):
    keep, more = ins
    keep.get(), more.get()
    for at, out in enumerate(outs):
        block = scalars[0][0] ^ at
        for group in range(keep.inside.shape[0]):
            out.inside[group] = (
                keep.inside[group, block].astype(f32) + more.inside[group, block].astype(f32)
            ).astype(bf16)
    for out in outs[1:] + outs[:1]:
        out.send()


def row_sum_kernel(parts, scalars, ins, outs, scratch):
    ffn_own, both = outs
    (tail,) = scratch
    total = ins[0].get()[...].astype(f32)
    for one in ins[1:-1]:
        total = total + one.get()[...].astype(f32)
    total = total.astype(bf16)
    size = total.shape[1]
    half = size // 2
    width = D // parts
    ffn_own.inside[...] = total[:2].reshape(2 * size, D)
    ffn_own.send()
    for part in range(parts):
        start = part * width
        top = total[2, :half, start : start + width]
        low = total[2, half:, start : start + width]
        tail[part, :half, :] = top[:, :128]
        tail[part, half : 2 * half, :64] = top[:, 128:]
        tail[part, half : 2 * half, 64:] = low[:, :64]
        tail[part, 2 * half :, :] = low[:, 64:]
    span = both.outside.shape[1] - 3 * half
    copies = []
    for part in range(parts):
        copy = pltpu.make_async_copy(
            tail.at[part],
            both.outside.at[part, pl.ds(span, 3 * half), :],
            both.sems.at[next(both.free)],
        )
        copy.start()
        copies.append(copy)
    for copy in copies:
        copy.wait()


SLOT = 64


def last_kernel(parts, pair, scalars, ins, outs, scratch):
    gq, normed, gkv, own, x, gain, gr, sums, gkv_more = ins
    back, *narrow = outs
    grads, small, made = scratch
    width = D // parts
    span = x.inside.shape[0]
    piece = span // parts
    lanes = 3 * width + SLOT
    grads[:, :width] = gq.get()[...]
    grads[:, 3 * width :] = jnp.zeros((span, D - 3 * width), bf16)
    gkv.get(), gkv_more.get()
    grads[:, width : 3 * width] = (
        gkv.inside[...] + gkv_more.inside[...].astype(f32)
    ).astype(bf16)
    own.get(), x.get(), gr.get(), sums.get()
    gain = gain.get()[...].reshape(1, D)
    gain_sum = jnp.zeros((1, D), f32)
    bias_sum = jnp.zeros((1, D), f32)
    for start in range(0, span, TILE):
        rows = slice(start, start + TILE)
        hat, scale = normalise(x.inside[rows, :].astype(f32))
        grad_normed = dot_nt(grads[rows, :], own.inside[...])
        gain_sum = gain_sum + jnp.sum(grad_normed * hat, axis=0, keepdims=True)
        bias_sum = bias_sum + jnp.sum(grad_normed, axis=0, keepdims=True)
        grad_in = gr.inside[rows, :] + norm_backward(hat, scale, grad_normed * gain)
        turned = grad_in.astype(bf16).T
        for at in range(start, start + TILE, piece):
            back.inside[at // piece] = turned[:, at - start : at - start + piece]
    pieces = D // SLOT
    for at, row in enumerate(
        (gain_sum, bias_sum, sums.inside[0:1, :], sums.inside[1:2, :])
    ):
        for part in range(pieces):
            small[at * pieces + part : at * pieces + part + 1, :] = row[
                :, part * SLOT : (part + 1) * SLOT
            ]
    made[...] = dot_tn(normed.get()[...], grads[:, :lanes]).astype(bf16)
    tail = small[...].astype(bf16)
    if pair:
        _, rows_count, size, _ = narrow[0].inside.shape
        for row in range(rows_count):
            for out, half in ((narrow[0], scalars[0][0]), (narrow[1], 1 - scalars[0][0])):
                start = pl.multiple_of((2 * row + half) * size, size)
                out.inside[0, row] = made[pl.ds(start, size), :]
                out.inside[0, row, :48, 3 * width :] = tail
        narrow[1].send()
        narrow[0].send()
    else:
        narrow[0].inside[...] = made[...]
        narrow[0].inside[:48, 3 * width :] = tail
        narrow[0].send()
    back.send()


def own_sum_kernel(parts, count, scalars, ins, outs, scratch):
    mine = outs[0].inside
    tails, small = scratch
    width = D // parts
    size = ins[0].inside.shape[1]
    half = size // 2
    last = ins[count]
    span = last.outside.shape[1] - 3 * half
    last.start(source=last.outside.at[:, pl.ds(span, 3 * half), :], target=tails)
    total = ins[0].get()[0].astype(f32)
    for one in ins[1:count]:
        total = total + one.get()[0].astype(f32)
    mine[:size, : 3 * width] = total[:, : 3 * width].astype(bf16)
    pieces = D // SLOT
    small[...] = jnp.zeros(small.shape, f32)
    for at in range(4):
        for part in range(pieces):
            row = at * pieces + part
            small[at : at + 1, part * SLOT : (part + 1) * SLOT] = total[
                row : row + 1, 3 * width :
            ]
    mine[size:, :] = small[...].astype(bf16)
    last.get()
    out = tails[0].astype(f32)
    for part in range(1, parts):
        out = out + tails[part].astype(f32)
    out = out.astype(bf16)
    start = 3 * width
    mine[:half, start : start + 128] = out[:half]
    mine[:half, start + 128 :] = out[half : 2 * half, :64]
    mine[half:size, start : start + 64] = out[half : 2 * half, 64:]
    mine[half:size, start + 64 :] = out[2 * half :]
    outs[0].send()


def output_kernel(scalars, ins, outs, scratch):
    got = ins[0].get()
    parts, _, piece = got.shape
    width = D // parts
    total = got[0, :D].astype(f32)
    for part in range(1, parts):
        total = total + got[part, :D].astype(f32)
    for at in range(parts):
        outs[0].inside[:, at * piece : (at + 1) * piece] = total[
            at * width : (at + 1) * width
        ].astype(bf16)
    outs[0].send()


def finish_kernel(scalars, ins, outs, scratch):
    grad_in, vectors = outs
    (small,) = scratch
    size = ins[1].outside.shape[1] - 16
    ins[1].start(source=ins[1].outside.at[:, pl.ds(size, 16), :], target=small)
    back = ins[0].get()
    total = back[0].astype(f32)
    for at in range(1, back.shape[0]):
        total = total + back[at].astype(f32)
    grad_in.inside[...] = total.T.astype(bf16)
    grad_in.send()
    ins[1].get()
    sums = small[0].astype(f32)
    for at in range(1, small.shape[0]):
        sums = sums + small[at].astype(f32)
    vectors.inside[...] = sums[:4]
    vectors.send()


def spread_kernel(count, table, where, *refs):
    blocks, outs = refs[:count], refs[-4:]
    for step, members in enumerate(table):

        @pl.when(pl.program_id(0) == step)
        def _():
            part = 0
            for at in members:
                for own in range(blocks[at].shape[0]):
                    total = 4 * blocks[at].shape[0] * len(members)
                    width = 4 * D // total
                    for grad in range(4):
                        outs[grad][:, part * width : (part + 1) * width] = blocks[at][
                            own, :, grad * width : (grad + 1) * width
                        ].astype(f32)
                    part += 1


def spread(row_seq, steps, earlier=None):
    count = sum(len(blocks) for _, _, blocks in steps)
    size = steps[0][2][0].shape[1]
    table, at = [], 0
    for _, _, blocks in steps:
        table.append(tuple(range(at, at + len(blocks))))
        at += len(blocks)
    received = [block for _, _, blocks in steps for block in blocks]
    kept = [] if earlier is None else list(earlier)

    def place(i, w):
        row, seq = jnp.int32(0), jnp.int32(0)
        for step, (row_step, seq_step, _) in enumerate(steps):
            row = jnp.where(i == step, row_step, row)
            seq = jnp.where(i == step, seq_step, seq)
        return (2 * (w[0] ^ row) + (w[1] ^ seq), 0)

    return pl.pallas_call(
        functools.partial(spread_kernel, count, table),
        out_shape=(jax.ShapeDtypeStruct((D, D), f32),) * 4,
        grid_spec=pltpu.PrefetchScalarGridSpec(
            num_scalar_prefetch=1,
            grid=(len(steps),),
            in_specs=[
                pl.BlockSpec(block.shape, lambda i, w: (0, 0, 0)) for block in received
            ]
            + [pl.BlockSpec(memory_space=pl.ANY)] * len(kept),
            out_specs=(pl.BlockSpec((size, D), place),) * 4,
        ),
        input_output_aliases={1 + count + at: at for at in range(len(kept))},
        compiler_params=pltpu.CompilerParams(vmem_limit_bytes=SMALL_LIMIT),
        cost_estimate=pl.CostEstimate(flops=0, bytes_accessed=0, transcendentals=0),
    )(row_seq, *received, *kept)


def spread_ffn_kernel(count, where, *refs):
    blocks, outs = refs[:count], refs[count:]
    size = outs[0].shape[0]
    for at in range(count):

        @pl.when(pl.program_id(0) == at)
        def _():
            outs[0][...] = blocks[at][:size, :].astype(f32)
            outs[1][...] = blocks[at][size:, :].astype(f32)


def spread_ffn(row_seq, mine, other):
    received = [*mine, *other]
    count = len(received)
    rows_count = len(mine)
    size = received[0].shape[0] // 2
    whole = pl.BlockSpec((2 * size, D), lambda i, w: (0, 0))

    def place(i, w):
        return (2 * (w[0] ^ (i % rows_count)) + (w[1] ^ (i // rows_count)), 0)

    return pl.pallas_call(
        functools.partial(spread_ffn_kernel, count),
        out_shape=(jax.ShapeDtypeStruct((D, D), f32),) * 2,
        grid_spec=pltpu.PrefetchScalarGridSpec(
            num_scalar_prefetch=1,
            grid=(count,),
            in_specs=[whole] * count,
            out_specs=(pl.BlockSpec((size, D), place),) * 2,
        ),
        compiler_params=pltpu.CompilerParams(vmem_limit_bytes=SMALL_LIMIT),
        cost_estimate=pl.CostEstimate(flops=0, bytes_accessed=0, transcendentals=0),
    )(row_seq, *received)


def broadcast_exchange(value, axis):
    count = lax.axis_size(axis)
    return lax.all_to_all(
        jnp.broadcast_to(value[None], (count,) + value.shape), axis, 0, 0, tiled=False
    )


def swap(value):
    return lax.ppermute(value, "seq", [(0, 1), (1, 0)])


def trade(value, axis, step):
    return lax.ppermute(value, axis, [(a, a ^ step) for a in range(lax.axis_size(axis))])


def features_kernel(heads, scalars, ins, outs, scratch):
    docs = ins[0].get()[...]
    feats = outs[0].inside
    _, length, _ = feats.shape
    position = lax.broadcasted_iota(jnp.int32, (1, length), 1)
    feature = lax.broadcasted_iota(jnp.int32, (FEATS, length), 0)
    for h in range(heads):
        head = scalars[0][0] * heads + h
        hit = None
        base = 0
        for part, dilation in zip(segment_parts, dilations, strict=True):
            seg_width = length * part // 16
            inside = lax.rem(
                lax.rem(position, seg_width) + dilation - lax.rem(head, dilation), dilation
            )
            key = base + lax.div(position, seg_width) * DOCS + docs
            key = jnp.where(inside == 0, key, -1)
            found = feature == key
            hit = found if hit is None else hit | found
            base += DOCS * (16 // part)
        feats[h] = jnp.where(hit, 1.0, 0.0).T.astype(bf16)
        outs[0].send(h)


def shape(*dims, kind=bf16):
    return jax.ShapeDtypeStruct(dims, kind)


def per_device(
    block_input,
    doc_ids,
    ln1_gain,
    ln1_bias,
    w_query,
    w_key,
    w_value,
    w_out,
    ln2_gain,
    ln2_bias,
    w_up,
    w_down,
    cotangent,
):
    span = block_input.shape[1]
    rows_count = lax.axis_size("row")
    seq_count = lax.axis_size("seq")
    parts = lax.axis_size("pat")
    row_index = lax.axis_index("row")
    seq_index = lax.axis_index("seq")
    pat_index = lax.axis_index("pat")
    pair = seq_count == 2
    heads = HEADS // parts
    width = D // parts
    quarter = span // parts
    size = D // (rows_count * seq_count) if pair else D
    here = seq_index.astype(jnp.int32)[None]
    row_here = row_index.astype(jnp.int32)[None]
    part_here = pat_index.astype(jnp.int32)[None]
    x = block_input[0]

    c_own = cotangent[0].T
    c_parts = [c_own] + [trade(c_own, "pat", s) for s in range(1, parts)]
    (feats,) = staged_call(
        functools.partial(features_kernel, heads),
        [part_here],
        [doc_ids],
        (shape(heads, doc_ids.shape[1], FEATS),),
    )

    def window(scalars):
        return scalars[0][0] * width // 128 * 128

    normed, q, kv, own = staged_call(
        functools.partial(project_kernel, parts),
        [part_here],
        [x, ln1_gain, ln1_bias, w_query, w_key, w_value],
        (shape(span, D), shape(span, width), shape(span, 2 * width), shape(D, D)),
        windows={3: window, 4: window, 5: window},
    )

    kv_far = swap(kv) if pair else lax.all_gather(kv, "seq", axis=0, tiled=True)
    far_rows = kv_far.shape[0]

    mixed, mixed_t, lse = staged_call(
        functools.partial(attention_kernel, heads, span),
        [here],
        [q, kv, feats, kv_far],
        (shape(width, span), shape(width, span, kind=f32), shape(8, span, kind=f32)),
        scratch=[
            pltpu.VMEM((heads, span, width), bf16),
            pltpu.VMEM((span, width), bf16),
            pltpu.VMEM((width, span), bf16),
            pltpu.VMEM((far_rows, width), bf16),
            pltpu.VMEM((far_rows // span, width, span), bf16),
        ],
    )
    mixed, *c_parts = lax.optimization_barrier((mixed, *c_parts))
    mixed4 = lax.all_gather(mixed, "pat")

    wide_shapes = (shape(3, rows_count, size, D),) * 2 if pair else (shape(3, D, D),)
    gm, gr, sums, ffn, *wide = staged_call(
        functools.partial(middle_kernel, pair),
        [here, part_here],
        [mixed4, x, w_out, ln2_gain, ln2_bias, w_up, w_down, *c_parts],
        (
            shape(parts, width, span),
            shape(span, D, kind=f32),
            shape(8, D, kind=f32),
            shape(parts, parts * width + (3 * size // 2 if pair else 0), quarter),
            *wide_shapes,
        ),
        scratch=[pltpu.VMEM((span, D), bf16)] * 5
        + [
            pltpu.VMEM((span, D), f32),
            pltpu.VMEM((D, D), bf16),
            pltpu.VMEM((parts, width, span), bf16),
        ],
        late=parts,
    )
    gm_parts = lax.all_to_all(gm, "pat", 0, 0, tiled=True)

    if pair:
        keep, send = wide
        ordered = staged_call(
            add_kernel, [row_here], [keep, swap(send)], (shape(3, size, D),) * rows_count,
            limit=SMALL_LIMIT,
        )
        received = [ordered[0]] + [trade(ordered[s], "row", s) for s in range(1, rows_count)]
        gm_parts, *_ = lax.optimization_barrier((gm_parts, received[1], received[2]))

    gq, gkv, gkv_far = staged_call(
        functools.partial(attention_back_kernel, heads, span),
        [here],
        [gm_parts, q, mixed_t, lse, kv, feats, kv_far],
        (
            shape(span, width),
            shape(span, 2 * width, kind=f32),
            shape(far_rows, 2 * width),
        ),
        scratch=[
            pltpu.VMEM((heads, span, width), bf16),
            pltpu.VMEM((heads, span, width), bf16),
            pltpu.VMEM((8, span), f32),
            pltpu.VMEM((span, heads * span), bf16),
            pltpu.VMEM((span, heads * span), bf16),
            pltpu.VMEM((span, width), bf16),
            pltpu.VMEM((span, width), bf16),
            pltpu.VMEM((width, span), bf16),
            pltpu.VMEM((width, span), f32),
        ],
    )

    if pair:
        gkv_more = swap(gkv_far)
        ffn_own, ffn = staged_call(
            functools.partial(row_sum_kernel, parts),
            [],
            [*received, ffn],
            (shape(2 * size, D), shape(*ffn.shape)),
            scratch=[pltpu.VMEM((parts, 3 * size // 2, quarter), bf16)],
            limit=SMALL_LIMIT,
            late=1,
            aliases=((rows_count, 1),),
        )
        ffn_parts = lax.all_to_all(ffn, "pat", 0, 0, tiled=True)
    else:
        gkv_more = lax.psum_scatter(gkv_far, "seq", scatter_dimension=0, tiled=True)
        ffn_parts = lax.all_to_all(ffn, "pat", 0, 0, tiled=True)

    lanes = 3 * width + SLOT
    narrow_shapes = (shape(1, rows_count, size, lanes),) * 2 if pair else (shape(D, lanes),)
    back, *narrow = staged_call(
        functools.partial(last_kernel, parts, pair),
        [here],
        [gq, normed, gkv, own, x, ln1_gain, gr, sums, gkv_more],
        (shape(parts, parts * width, quarter), *narrow_shapes),
        scratch=[
            pltpu.VMEM((span, D), bf16),
            pltpu.VMEM((48, SLOT), f32),
            pltpu.VMEM((D, lanes), bf16),
        ],
    )

    if pair:
        keep, send = narrow
        ordered = staged_call(
            add_kernel, [row_here], [keep, swap(send)], (shape(1, size, lanes),) * rows_count,
            limit=SMALL_LIMIT,
        )
        received = [ordered[0]] + [trade(ordered[s], "row", s) for s in range(1, rows_count)]
        ffn_own, *received = lax.optimization_barrier((ffn_own, *received))
        ffn_mine = [ffn_own] + [trade(ffn_own, "row", s) for s in range(1, rows_count)]
        (mine,) = staged_call(
            functools.partial(own_sum_kernel, parts, rows_count),
            [],
            [*received, ffn_parts],
            (shape(size + 16, D),),
            scratch=[
                pltpu.VMEM((parts, 3 * size // 2, quarter), bf16),
                pltpu.VMEM((16, D), f32),
            ],
            limit=SMALL_LIMIT,
            late=1,
        )
        gathered = lax.all_gather(mine, "pat")
        back, gathered, *ffn_mine = lax.optimization_barrier((back, gathered, *ffn_mine))
        back_parts = lax.all_to_all(back, "pat", 0, 0, tiled=True)
        ffn_other = [swap(value) for value in ffn_mine]
        row_seq = jnp.stack([row_index, seq_index]).astype(jnp.int32)
        grad_down, grad_up = spread_ffn(row_seq, ffn_mine, ffn_other)
        a, b = gathered[: parts // 2, :size], gathered[parts // 2 :, :size]
        a1, b2 = trade(a, "row", 1), trade(b, "row", 2)
        b1, a2 = trade(b, "row", 1), trade(a, "row", 2)
        a3, b3 = trade(a1, "row", 2), trade(b2, "row", 1)
        early = [(a, b), (a1, b1), (a2, b2)]
        steps = [(at, 0, pieces) for at, pieces in enumerate(early)] + [
            (at, 1, [swap(piece) for piece in pieces]) for at, pieces in enumerate(early)
        ]
        grads = spread(row_seq, steps)
        far3, near3, *_ = lax.optimization_barrier((a3, b3, grads[0], grad_up))
        grads = spread(row_seq, [(3, 0, (a3, b3)), (3, 1, (swap(far3), swap(near3)))], grads)
    else:
        axes = ("row", "seq")
        back_parts = lax.all_to_all(back, "pat", 0, 0, tiled=True)
        wide_sum = lax.psum(wide[0], axes)
        grad_down, grad_up = wide_sum[0].astype(f32), wide_sum[1].astype(f32)
        grad_out = lax.psum(wide_sum[2], "pat").astype(f32)
        gathered = lax.all_gather(lax.psum(narrow[0], axes), "pat")
        small = gathered[:, :48, 3 * width :].reshape(parts, 4, D)
        small = jnp.pad(small, ((0, 0), (0, 12), (0, 0)))
        grads = [
            gathered[:, :, at * width : (at + 1) * width]
            .astype(f32)
            .transpose(1, 0, 2)
            .reshape(D, D)
            for at in range(3)
        ] + [grad_out]
    (out_t,) = staged_call(
        output_kernel, [], [ffn_parts], (shape(width, span),), limit=SMALL_LIMIT
    )
    grad_in, vectors = staged_call(
        finish_kernel,
        [],
        [back_parts, gathered if pair else small],
        (shape(quarter, D), shape(4, D, kind=f32)),
        scratch=[pltpu.VMEM((parts, 16, D), bf16)],
        limit=SMALL_LIMIT,
        late=1,
    )
    return (
        out_t.T[None],
        grad_in[None],
        vectors[0],
        vectors[1],
        grads[0],
        grads[1],
        grads[2],
        grads[3],
        vectors[2],
        vectors[3],
        grad_up,
        grad_down,
    )


def solution(mesh):
    placed = (
        P("row", "seq", None),
        P("row", None),
        P(),
        P(),
        P(),
        P(),
        P(),
        P(),
        P(),
        P(),
        P(None, "pat"),
        P("pat", None),
        P("row", "seq", "pat"),
    )
    return jax.shard_map(
        per_device,
        mesh=mesh,
        in_specs=placed,
        out_specs=(
            P("row", "seq", "pat"),
            P("row", ("seq", "pat"), None),
            P(),
            P(),
            P(),
            P(),
            P(),
            P(),
            P(),
            P(),
            P(None, "pat"),
            P("pat", None),
        ),
        check_vma=False,
    )
```

time: 304 us -> 189 us (0.62)
  blocking collectives: 102 us -> 36.7 us
  local copies, waits for them, and re-layouts: 35.5 us -> 7.32 us
  waiting for transfers between devices: 72.1 us -> 44 us
  Pallas kernels: 41.3 us -> 59.5 us
  other arithmetic: 16.7 us -> 0.07 us
  starting transfers between devices: 33.5 us -> 40 us
    all_to_all x2 -> x0, blocking collectives: 59.4 us -> none  [the longest x1 36.4 us: broadcast_exchange(): lax.all_to_all(jnp.broadcast_to(value[None], (count,) + value.shape), axi...]
    all_to_all x6 -> x2, waiting for transfers between devices: 50.3 us -> 0.01 us  [the longest x1 0.01 us: per_device(): gm_parts = lax.all_to_all(gm, 'pat', 0, 0, tiled=True)]
    ppermute x0 -> x18, waiting for transfers between devices: none -> 39.8 us  [trade(): lax.ppermute(value, axis, [(a, a ^ step) for a in range(lax.axis_size(axi...]
    ppermute x0 -> x18, starting transfers between devices: none -> 22.3 us  [trade(): lax.ppermute(value, axis, [(a, a ^ step) for a in range(lax.axis_size(axi...]
    all_to_all x1, waiting for transfers between devices: 20.1 us -> 0.01 us  [per_device(): ffn_parts = lax.all_to_all(ffn, 'pat', 0, 0, tiled=True)]
    pallas_call x6 -> x15, Pallas kernels: 41.3 us -> 59.5 us  [the longest x12 46.1 us: staged_call(): pl.pallas_call(kernel, out_shape=tuple(outs), in_specs=[pl.BlockSpec(memo...]
    all_to_all x6 -> x2, starting transfers between devices: 25.7 us -> 8.17 us  [the longest x1 4.21 us: per_device(): gm_parts = lax.all_to_all(gm, 'pat', 0, 0, tiled=True)]
    all_to_all x3 -> x0, local copies, waits for them, and re-layouts: 7.72 us -> none  [the longest x2 5.5 us: broadcast_exchange(): lax.all_to_all(jnp.broadcast_to(value[None], (count,) + value.shape), axi...]
  transfers between devices with their start and end apart: 13 -> 37, of which waited for: 7 -> 12; matrix products, arithmetic and copies ran while one was open for 12% -> 0% of each run, Pallas kernels for 6% -> 23%
where the time goes in v2:
time: 189 us; the launch traced here: 188 us
  Pallas kernels  59.5 us (31%)
  waiting for transfers between devices  44 us (23%)
  starting transfers between devices  40 us (21%)
  blocking collectives  36.7 us (19%)
  local copies, waits for them, and re-layouts  7.32 us (4%)
    pallas_call x12, Pallas kernels, staged_call(): pl.pallas_call(kernel, out_shape=tuple(outs), in_specs=[pl.BlockSpec(memo...  46.1 us
    ppermute x18, waiting for transfers between devices, trade(): lax.ppermute(value, axis, [(a, a ^ step) for a in range(lax.axis_size(axi...  39.8 us
    ppermute x18, starting transfers between devices, trade(): lax.ppermute(value, axis, [(a, a ^ step) for a in range(lax.axis_size(axi...  22.3 us
    all_gather x1, blocking collectives, per_device(): mixed4 = lax.all_gather(mixed, 'pat')  19.2 us
    all_gather x1, blocking collectives, per_device(): gathered = lax.all_gather(mine, 'pat')  17.5 us
    pallas_call x2, Pallas kernels, spread(): pl.pallas_call(functools.partial(spread_kernel, count, table), out_shape=...  8.11 us
    unnamed x28, local copies, waits for them, and re-layouts  6.65 us
    pallas_call x1, Pallas kernels, spread_ffn(): pl.pallas_call(functools.partial(spread_ffn_kernel, count), out_shape=(ja...  5.27 us
  transfers between devices with their start and end apart: 37, of which 12 were waited for; matrix products, arithmetic and copies ran while one was open for 0% of the time, Pallas kernels for 23%

profile of v2, /device:TPU:0, one launch (start us, length us, event | category | flops | bytes accessed | tf_op | source)
XLA Modules:
  0.0 188.5 jit_solution(18361900225837269425)
XLA Ops:
  0.7 3.8 %shard_map.220 = (bf16[512,768]{1,0:T(8,128)(2,1)}, bf16[512,192]{1,0:T(8,128)(2,1)}, bf16[512,384]{1,0:T(8,128)(2,1)}, bf16[768,768]{1,0:T(8,128)(2,1)}) custom-call(s32[1]{0:T(128)} %bitcast.2.refs_0_.refs_1_, bf16[512,768]{1,0:T(8,128)(2,1)} %bitcast.15, f32[768]{0:T(1024)} %refs_6_.5, f32[768]{0:T(1024)} %refs_3_.1, bf16[768,768]{1,0:T(8,128)(2,1)} %refs_4_.2, ...), custom_call_target="tpu_custom_call" | custom-call | tf_op jit(solution)/shard_map/pallas_call | solution.py:99
  5.0 4.8 %collective-permute-start.3 = (bf16[192,512]{1,0:T(8,128)(2,1)S(1)}, bf16[192,512]{1,0:T(8,128)(2,1)S(1)}, u32[]{:S(2)}, u32[]{:S(2)}) collective-permute-start(bf16[192,512]{1,0:T(8,128)(2,1)S(1)} %bitcast.20), channel_id=1, source_target_pairs={{0,3},{1,2},{2,1},{3,0},{4,7},{5,6},{6,5},{7,4},{8,11},{9,10},{10,... | collective-permute-start | bytes 589832 | tf_op jit(solution)/shard_map/ppermute | solution.py:690
  10.4 2.6 %shard_map.221.refs_3_.refs_6_ = bf16[3,1024,128]{2,1,0:T(8,128)(2,1)} custom-call(s32[1]{0:T(128)} %bitcast.2.refs_0_.refs_1_, s32[1,1024]{1,0:T(1,128)} %refs_1_.1), custom_call_target="tpu_custom_call" | custom-call | tf_op jit(solution)/shard_map/pallas_call | solution.py:99
  13.8 5.7 %shard_map.222 = (bf16[192,512]{1,0:T(8,128)(2,1)}, f32[192,512]{1,0:T(8,128)}, f32[8,512]{1,0:T(8,128)}) custom-call(s32[1]{0:T(128)} %bitcast.1.refs_0_, bf16[512,192]{1,0:T(8,128)(2,1)} %get-tuple-element.72.refs_1_.refs_2_, bf16[512,384]{1,0:T(8,128)(2,1)} %get-tuple-element.73.refs_2_.refs_5_, bf16[3,1024,128]{2,1,0:T(8,128)(2,1)} %shard_map.221.refs_3_.refs_6_, ...), custom_call_target="tpu_custom_call" | custom-call | tf_op jit(solution)/shard_map/pallas_call | solution.py:99
  19.5 7.5 %collective-permute-done.2.refs_11_ = bf16[192,512]{1,0:T(8,128)(2,1)S(1)} collective-permute-done((bf16[192,512]{1,0:T(8,128)(2,1)S(1)}, bf16[192,512]{1,0:T(8,128)(2,1)S(1)}, u32[]{:S(2)}, u32[]{:S(2)}) %collective-permute-start.2) | collective-permute-done | bytes 196640 | tf_op jit(solution)/shard_map/ppermute | solution.py:690
  27.1 19.2 %all-gather = bf16[768,512]{1,0:T(8,128)(2,1)} all-gather(bf16[192,512]{1,0:T(8,128)(2,1)} %get-tuple-element.75), channel_id=2, replica_groups=mesh['row'=4,'seq'=2,'pat'=4] {'pat'}, dimensions={0}, use_global_device_ids=true | all-gather | bytes 983040 | tf_op jit(solution)/shard_map/all_gather | solution.py:790
  46.2 11.6 %shard_map.223 = (bf16[4,192,512]{2,1,0:T(8,128)(2,1)}, f32[512,768]{1,0:T(8,128)}, f32[8,768]{1,0:T(8,128)}, bf16[4,912,128]{2,1,0:T(8,128)(2,1)}, bf16[3,4,96,...) custom-call(s32[1]{0:T(128)} %bitcast.1.refs_0_, s32[1]{0:T(128)} %bitcast.2.refs_0_.refs_1_, ...), custom_call_target="tpu_custom_call" | custom-call | tf_op jit(solution)/shard_map/pallas_call | solution.py:99
  58.0 4.2 %all-to-all-start.1 = ((bf16[4,192,512]{2,1,0:T(8,128)(2,1)}), bf16[4,192,512]{2,1,0:T(8,128)(2,1)}, u32[]{:S(2)}, u32[]{:S(2)}) async-start(bf16[4,192,512]{2,1,0:T(8,128)(2,1)} %get-tuple-element.88), calls=%async_computation.1 | async-start | bytes 1572864 | tf_op jit(solution)/shard_map/all_to_all | solution.py:812
  63.7 2.3 %shard_map.224 = (bf16[3,96,768]{2,1,0:T(8,128)(2,1)S(1)}, bf16[3,96,768]{2,1,0:T(8,128)(2,1)S(1)}, bf16[3,96,768]{2,1,0:T(8,128)(2,1)S(1)}, bf16[3,96,768]{2,1,0:T(8,128)(2,1)S(1)}) custom-call(s32[1]{0:T(128)} %bitcast.refs_0_, bf16[3,4,96,768]{3,2,1,0:T(8,128)(2,1)S(1)} %copy-done, bf16[3,4,96,768]{3,2,1,0:T(8,128)(2,1)S(1)} %collective-permute-done.4.refs_2_), custom_call_target="tpu_custom_call" | custom-call | tf_op jit(solution)/shard_map/pallas_call | solution.py:99
  69.6 9.5 %collective-permute-done.5.refs_1_ = bf16[3,96,768]{2,1,0:T(8,128)(2,1)S(1)} collective-permute-done((bf16[3,96,768]{2,1,0:T(8,128)(2,1)S(1)}, bf16[3,96,768]{2,1,0:T(8,128)(2,1)S(1)}, u32[]{:S(2)}, u32[]{:S(2)}) %collective-permute-start.5) | collective-permute-done | bytes 442400 | tf_op jit(solution)/shard_map/ppermute | solution.py:690
  79.0 10.3 %collective-permute-done.6.refs_2_ = bf16[3,96,768]{2,1,0:T(8,128)(2,1)S(1)} collective-permute-done((bf16[3,96,768]{2,1,0:T(8,128)(2,1)S(1)}, bf16[3,96,768]{2,1,0:T(8,128)(2,1)S(1)}, u32[]{:S(2)}, u32[]{:S(2)}) %collective-permute-start.6) | collective-permute-done | bytes 442400 | tf_op jit(solution)/shard_map/ppermute | solution.py:690
  89.3 2.4 %shard_map.225 = (bf16[192,768]{1,0:T(8,128)(2,1)S(1)}, bf16[4,912,128]{2,1,0:T(8,128)(2,1)}) custom-call(bf16[3,96,768]{2,1,0:T(8,128)(2,1)S(1)} %get-tuple-element.82.refs_0_, bf16[3,96,768]{2,1,0:T(8,128)(2,1)S(1)} %collective-permute-done.5.refs_1_, bf16[3,96,768]{2,1,0:T(8,128)(2,1)S(1)} %collective-permute-done.6.refs_2_, ...), custom_call_target="tpu_custom_call", output_to_operand_aliasing={{1}: (4, {})} | custom-call | tf_op jit(solution)/shard_map/pallas_call | solution.py:99
  91.8 4.8 %all-to-all-start = ((bf16[4,912,128]{2,1,0:T(8,128)(2,1)}), bf16[4,912,128]{2,1,0:T(8,128)(2,1)S(1)}, u32[]{:S(2)}, u32[]{:S(2)}) async-start(bf16[4,912,128]{2,1,0:T(8,128)(2,1)} %get-tuple-element.87), calls=%async_computation | async-start | bytes 1867776 | tf_op jit(solution)/shard_map/all_to_all | solution.py:857
  96.6 5.6 %shard_map.227 = (bf16[512,192]{1,0:T(8,128)(2,1)}, f32[512,384]{1,0:T(8,128)}, bf16[512,384]{1,0:T(8,128)(2,1)}) custom-call(s32[1]{0:T(128)} %bitcast.1.refs_0_, bf16[4,192,512]{2,1,0:T(8,128)(2,1)} %all-to-all-done.1.refs_1_, bf16[512,192]{1,0:T(8,128)(2,1)} %get-tuple-element.72.refs_1_.refs_2_, f32[192,512]{1,0:T(8,128)} %get-tuple-element.90.refs_3_, ...), custom_call_target="tpu_custom_call" | custom-call | tf_op jit(solution)/shard_map/pallas_call | solution.py:99
  105.9 6.7 %shard_map.228 = (bf16[4,768,128]{2,1,0:T(8,128)(2,1)}, bf16[1,4,96,640]{3,2,1,0:T(8,128)(2,1)}, bf16[1,4,96,640]{3,2,1,0:T(8,128)(2,1)}) custom-call(s32[1]{0:T(128)} %bitcast.1.refs_0_, bf16[512,192]{1,0:T(8,128)(2,1)} %get-tuple-element.92.refs_1_, bf16[512,768]{1,0:T(8,128)(2,1)} %get-tuple-element.93.refs_2_, f32[512,384]{1,0:T(8,128)} %get-tuple-element.94.refs_3_, ...), custom_call_target="tpu_custom_call" | custom-call | tf_op jit(solution)/shard_map/pallas_call | solution.py:99
  120.9 2.3 %collective-permute-done.10.refs_1_ = bf16[1,96,640]{2,1,0:T(8,128)(2,1)S(1)} collective-permute-done((bf16[1,96,640]{2,1,0:T(8,128)(2,1)S(1)}, bf16[1,96,640]{2,1,0:T(8,128)(2,1)S(1)}, u32[]{:S(2)}, u32[]{:S(2)}) %collective-permute-start.10) | collective-permute-done | bytes 122912 | tf_op jit(solution)/shard_map/ppermute | solution.py:690
  123.2 3.6 %collective-permute-done.11.refs_2_ = bf16[1,96,640]{2,1,0:T(8,128)(2,1)S(1)} collective-permute-done((bf16[1,96,640]{2,1,0:T(8,128)(2,1)S(1)}, bf16[1,96,640]{2,1,0:T(8,128)(2,1)S(1)}, u32[]{:S(2)}, u32[]{:S(2)}) %collective-permute-start.11) | collective-permute-done | bytes 122912 | tf_op jit(solution)/shard_map/ppermute | solution.py:690
  131.7 17.5 %all-gather.1 = bf16[448,768]{1,0:T(8,128)(2,1)S(1)} all-gather(bf16[112,768]{1,0:T(8,128)(2,1)S(1)} %shard_map.230), channel_id=3, replica_groups=mesh['row'=4,'seq'=2,'pat'=4] {'pat'}, dimensions={0}, use_global_device_ids=true | all-gather | bytes 860160 | tf_op jit(solution)/shard_map/all_gather | solution.py:897
  149.6 1.9 collective-permute-start.18
  154.2 4.0 %all-to-all-start.2 = ((bf16[4,768,128]{2,1,0:T(8,128)(2,1)}), bf16[4,768,128]{2,1,0:T(8,128)(2,1)S(1)}, u32[]{:S(2)}, u32[]{:S(2)}) async-start(bf16[4,768,128]{2,1,0:T(8,128)(2,1)} %get-tuple-element.112), calls=%async_computation.2 | async-start | bytes 1572864 | tf_op jit(solution)/shard_map/all_to_all | solution.py:899
  160.1 5.2 %collective-permute-done.21.refs_4_ = bf16[2,96,768]{2,1,0:T(8,128)(2,1)} collective-permute-done((bf16[2,96,768]{2,1,0:T(8,128)(2,1)S(1)}, bf16[2,96,768]{2,1,0:T(8,128)(2,1)}, u32[]{:S(2)}, u32[]{:S(2)}) %collective-permute-start.21) | collective-permute-done | bytes 294944 | tf_op jit(solution)/shard_map/ppermute | solution.py:690
  171.2 5.3 %shard_map.233 = (f32[768,768]{1,0:T(8,128)}, f32[768,768]{1,0:T(8,128)}) custom-call(s32[2]{0:T(128)S(1)} %pad_add_fusion.where, bf16[192,768]{1,0:T(8,128)(2,1)S(1)} %get-tuple-element.117.refs_0_, bf16[192,768]{1,0:T(8,128)(2,1)} %collective-permute-done.13.refs_1_, bf16[192,768]{1,0:T(8,128)(2,1)S(1)} %copy-done.5, bf16[192,768]{1,0:T(8,128)(2,1)S(1)} %copy-done.3, ...), custom_call_target="tpu_custom_call" | custom-call | tf_op jit(solution)/shard_map/pallas_call | solution.py:664
  176.5 5.9 %shard_map.232 = (f32[768,768]{1,0:T(8,128)}, f32[768,768]{1,0:T(8,128)}, f32[768,768]{1,0:T(8,128)}, f32[768,768]{1,0:T(8,128)}) custom-call(s32[2]{0:T(128)S(1)} %pad_add_fusion.where, bf16[2,96,768]{2,1,0:T(8,128)(2,1)S(1)} %get-tuple-element.137.refs_0_, bf16[2,96,768]{2,1,0:T(8,128)(2,1)S(1)} %get-tuple-element.136.refs_1_, ...), custom_call_target="tpu_custom_call" | custom-call | tf_op jit(solution)/shard_map/pallas_call | solution.py:625
  184.5 2.2 %shard_map.234 = (f32[768,768]{1,0:T(8,128)}, f32[768,768]{1,0:T(8,128)}, f32[768,768]{1,0:T(8,128)}, f32[768,768]{1,0:T(8,128)}) custom-call(s32[2]{0:T(128)S(1)} %pad_add_fusion.where, bf16[2,96,768]{2,1,0:T(8,128)(2,1)S(1)} %collective-permute-done.17.refs_0_, ...), custom_call_target="tpu_custom_call", output_to_operand_aliasing={{0}: (5, {}), {1}: (6, {}), {2}: (7, {}), {3}: (8, {})} | custom-call | tf_op jit(solution)/shard_map/pallas_call | solution.py:625
  (98 shorter events, 38.8 us)
Async XLA Ops:
  4.4 8.6 %collective-permute-start = (bf16[512,384]{1,0:T(8,128)(2,1)}, bf16[512,384]{1,0:T(8,128)(2,1)S(1)}, u32[]{:S(2)}, u32[]{:S(2)}) collective-permute-start(bf16[512,384]{1,0:T(8,128)(2,1)} %get-tuple-element.73.refs_2_.refs_5_), channel_id=1, source_target_pairs={{0,4},{4,0},{1,5},{5,1},{2,6},{6,2},{3,7},{7,3},{8,12},{12,8},{9,1... | collective-permute-start | bytes 1179656 | tf_op jit(solution)/shard_map/ppermute | solution.py:686
  5.0 14.6 %collective-permute-start.3 = (bf16[192,512]{1,0:T(8,128)(2,1)S(1)}, bf16[192,512]{1,0:T(8,128)(2,1)S(1)}, u32[]{:S(2)}, u32[]{:S(2)}) collective-permute-start(bf16[192,512]{1,0:T(8,128)(2,1)S(1)} %bitcast.20), channel_id=1, source_target_pairs={{0,3},{1,2},{2,1},{3,0},{4,7},{5,6},{6,5},{7,4},{8,11},{9,10},{10,... | collective-permute-start | bytes 589832 | tf_op jit(solution)/shard_map/ppermute | solution.py:690
  9.7 17.3 %collective-permute-start.2 = (bf16[192,512]{1,0:T(8,128)(2,1)S(1)}, bf16[192,512]{1,0:T(8,128)(2,1)S(1)}, u32[]{:S(2)}, u32[]{:S(2)}) collective-permute-start(bf16[192,512]{1,0:T(8,128)(2,1)S(1)} %bitcast.21), channel_id=1, source_target_pairs={{0,2},{1,3},{2,0},{3,1},{4,6},{5,7},{6,4},{7,5},{8,10},{9,11},{10,... | collective-permute-start | bytes 589832 | tf_op jit(solution)/shard_map/ppermute | solution.py:690
  9.8 17.3 %collective-permute-start.1 = (bf16[192,512]{1,0:T(8,128)(2,1)S(1)}, bf16[192,512]{1,0:T(8,128)(2,1)S(1)}, u32[]{:S(2)}, u32[]{:S(2)}) collective-permute-start(bf16[192,512]{1,0:T(8,128)(2,1)S(1)} %bitcast.22), channel_id=1, source_target_pairs={{0,1},{1,0},{2,3},{3,2},{4,5},{5,4},{6,7},{7,6},{8,9},{9,8},{10,11... | collective-permute-start | bytes 589832 | tf_op jit(solution)/shard_map/ppermute | solution.py:690
  58.0 33.8 %all-to-all-start.1 = ((bf16[4,192,512]{2,1,0:T(8,128)(2,1)}), bf16[4,192,512]{2,1,0:T(8,128)(2,1)}, u32[]{:S(2)}, u32[]{:S(2)}) async-start(bf16[4,192,512]{2,1,0:T(8,128)(2,1)} %get-tuple-element.88), calls=%async_computation.1 | async-start | bytes 1572864 | tf_op jit(solution)/shard_map/all_to_all | solution.py:812
  66.0 13.0 %collective-permute-start.5 = (bf16[3,96,768]{2,1,0:T(8,128)(2,1)S(1)}, bf16[3,96,768]{2,1,0:T(8,128)(2,1)S(1)}, u32[]{:S(2)}, u32[]{:S(2)}) collective-permute-start(bf16[3,96,768]{2,1,0:T(8,128)(2,1)S(1)} %get-tuple-element.83), channel_id=1, source_target_pairs={{0,8},{8,0},{16,24},{24,16},{1,9},{9,1},{17,25},{25,17},{2,10},{10... | collective-permute-start | bytes 1327112 | tf_op jit(solution)/shard_map/ppermute | solution.py:690
  67.6 21.8 %collective-permute-start.6 = (bf16[3,96,768]{2,1,0:T(8,128)(2,1)S(1)}, bf16[3,96,768]{2,1,0:T(8,128)(2,1)S(1)}, u32[]{:S(2)}, u32[]{:S(2)}) collective-permute-start(bf16[3,96,768]{2,1,0:T(8,128)(2,1)S(1)} %get-tuple-element.84), channel_id=1, source_target_pairs={{0,16},{8,24},{16,0},{24,8},{1,17},{9,25},{17,1},{25,9},{2,18},{10... | collective-permute-start | bytes 1327112 | tf_op jit(solution)/shard_map/ppermute | solution.py:690
  69.1 20.2 %collective-permute-start.7 = (bf16[3,96,768]{2,1,0:T(8,128)(2,1)S(1)}, bf16[3,96,768]{2,1,0:T(8,128)(2,1)S(1)}, u32[]{:S(2)}, u32[]{:S(2)}) collective-permute-start(bf16[3,96,768]{2,1,0:T(8,128)(2,1)S(1)} %get-tuple-element.85), channel_id=1, source_target_pairs={{0,24},{8,16},{16,8},{24,0},{1,25},{9,17},{17,9},{25,1},{2,26},{10... | collective-permute-start | bytes 1327112 | tf_op jit(solution)/shard_map/ppermute | solution.py:690
  91.8 38.5 %all-to-all-start = ((bf16[4,912,128]{2,1,0:T(8,128)(2,1)}), bf16[4,912,128]{2,1,0:T(8,128)(2,1)S(1)}, u32[]{:S(2)}, u32[]{:S(2)}) async-start(bf16[4,912,128]{2,1,0:T(8,128)(2,1)} %get-tuple-element.87), calls=%async_computation | async-start | bytes 1867776 | tf_op jit(solution)/shard_map/all_to_all | solution.py:857
  118.9 7.9 %collective-permute-start.11 = (bf16[1,96,640]{2,1,0:T(8,128)(2,1)S(1)}, bf16[1,96,640]{2,1,0:T(8,128)(2,1)S(1)}, u32[]{:S(2)}, u32[]{:S(2)}) collective-permute-start(bf16[1,96,640]{2,1,0:T(8,128)(2,1)S(1)} %get-tuple-element.105), channel_id=1, source_target_pairs={{0,16},{8,24},{16,0},{24,8},{1,17},{9,25},{17,1},{25,9},{2,18},{10... | collective-permute-start | bytes 368648 | tf_op jit(solution)/shard_map/ppermute | solution.py:690
  126.8 22.4 %collective-permute-start.15 = (bf16[192,768]{1,0:T(8,128)(2,1)S(1)}, bf16[192,768]{1,0:T(8,128)(2,1)S(1)}, u32[]{:S(2)}, u32[]{:S(2)}) collective-permute-start(bf16[192,768]{1,0:T(8,128)(2,1)S(1)} %get-tuple-element.117.refs_0_), channel_id=1, source_target_pairs={{0,24},{8,16},{16,8},{24,0},{1,25},{9,17},{17,9},{25,1},{2,26},{10... | collective-permute-start | bytes 884744 | tf_op jit(solution)/shard_map/ppermute | solution.py:690
  128.3 21.0 %collective-permute-start.14 = (bf16[192,768]{1,0:T(8,128)(2,1)S(1)}, bf16[192,768]{1,0:T(8,128)(2,1)S(1)}, u32[]{:S(2)}, u32[]{:S(2)}) collective-permute-start(bf16[192,768]{1,0:T(8,128)(2,1)S(1)} %get-tuple-element.117.refs_0_), channel_id=1, source_target_pairs={{0,16},{8,24},{16,0},{24,8},{1,17},{9,25},{17,1},{25,9},{2,18},{10... | collective-permute-start | bytes 884744 | tf_op jit(solution)/shard_map/ppermute | solution.py:690
  128.9 20.4 %collective-permute-start.13 = (bf16[192,768]{1,0:T(8,128)(2,1)S(1)}, bf16[192,768]{1,0:T(8,128)(2,1)}, u32[]{:S(2)}, u32[]{:S(2)}) collective-permute-start(bf16[192,768]{1,0:T(8,128)(2,1)S(1)} %get-tuple-element.117.refs_0_), channel_id=1, source_target_pairs={{0,8},{8,0},{16,24},{24,16},{1,9},{9,1},{17,25},{25,17},{2,10},{10... | collective-permute-start | bytes 884744 | tf_op jit(solution)/shard_map/ppermute | solution.py:690
  149.4 10.0 %collective-permute-start.20 = (bf16[2,96,768]{2,1,0:T(8,128)(2,1)S(1)}, bf16[2,96,768]{2,1,0:T(8,128)(2,1)}, u32[]{:S(2)}, u32[]{:S(2)}) collective-permute-start(bf16[2,96,768]{2,1,0:T(8,128)(2,1)S(1)} %get-tuple-element.136.refs_1_), channel_id=1, source_target_pairs={{0,8},{8,0},{16,24},{24,16},{1,9},{9,1},{17,25},{25,17},{2,10},{10... | collective-permute-start | bytes 884744 | tf_op jit(solution)/shard_map/ppermute | solution.py:690
  149.6 9.9 %collective-permute-start.18 = (bf16[2,96,768]{2,1,0:T(8,128)(2,1)S(1)}, bf16[2,96,768]{2,1,0:T(8,128)(2,1)}, u32[]{:S(2)}, u32[]{:S(2)}) collective-permute-start(bf16[2,96,768]{2,1,0:T(8,128)(2,1)S(1)} %get-tuple-element.136.refs_1_), channel_id=1, source_target_pairs={{0,16},{8,24},{16,0},{24,8},{1,17},{9,25},{17,1},{25,9},{2,18},{10... | collective-permute-start | bytes 884744 | tf_op jit(solution)/shard_map/ppermute | solution.py:690
  151.5 8.4 %collective-permute-start.22 = (bf16[2,96,768]{2,1,0:T(8,128)(2,1)S(1)}, bf16[2,96,768]{2,1,0:T(8,128)(2,1)}, u32[]{:S(2)}, u32[]{:S(2)}) collective-permute-start(bf16[2,96,768]{2,1,0:T(8,128)(2,1)S(1)} %get-tuple-element.137.refs_0_), channel_id=1, source_target_pairs={{0,4},{4,0},{1,5},{5,1},{2,6},{6,2},{3,7},{7,3},{8,12},{12,8},{9,1... | collective-permute-start | bytes 884744 | tf_op jit(solution)/shard_map/ppermute | solution.py:686
  151.5 13.8 %collective-permute-start.21 = (bf16[2,96,768]{2,1,0:T(8,128)(2,1)S(1)}, bf16[2,96,768]{2,1,0:T(8,128)(2,1)}, u32[]{:S(2)}, u32[]{:S(2)}) collective-permute-start(bf16[2,96,768]{2,1,0:T(8,128)(2,1)S(1)} %get-tuple-element.137.refs_0_), channel_id=1, source_target_pairs={{0,16},{8,24},{16,0},{24,8},{1,17},{9,25},{17,1},{25,9},{2,18},{10... | collective-permute-start | bytes 884744 | tf_op jit(solution)/shard_map/ppermute | solution.py:690
  152.4 12.9 %collective-permute-start.16 = (bf16[2,96,768]{2,1,0:T(8,128)(2,1)S(1)}, bf16[2,96,768]{2,1,0:T(8,128)(2,1)}, u32[]{:S(2)}, u32[]{:S(2)}) collective-permute-start(bf16[2,96,768]{2,1,0:T(8,128)(2,1)S(1)} %get-tuple-element.137.refs_0_), channel_id=1, source_target_pairs={{0,8},{8,0},{16,24},{24,16},{1,9},{9,1},{17,25},{25,17},{2,10},{10... | collective-permute-start | bytes 884744 | tf_op jit(solution)/shard_map/ppermute | solution.py:690
  154.2 32.5 %all-to-all-start.2 = ((bf16[4,768,128]{2,1,0:T(8,128)(2,1)}), bf16[4,768,128]{2,1,0:T(8,128)(2,1)S(1)}, u32[]{:S(2)}, u32[]{:S(2)}) async-start(bf16[4,768,128]{2,1,0:T(8,128)(2,1)} %get-tuple-element.112), calls=%async_computation.2 | async-start | bytes 1572864 | tf_op jit(solution)/shard_map/all_to_all | solution.py:899
  165.8 10.7 %collective-permute-start.27 = (bf16[2,96,768]{2,1,0:T(8,128)(2,1)}, bf16[2,96,768]{2,1,0:T(8,128)(2,1)S(1)}, u32[]{:S(2)}, u32[]{:S(2)}) collective-permute-start(bf16[2,96,768]{2,1,0:T(8,128)(2,1)} %collective-permute-done.18.refs_5_), channel_id=1, source_target_pairs={{0,4},{4,0},{1,5},{5,1},{2,6},{6,2},{3,7},{7,3},{8,12},{12,8},{9,1... | collective-permute-start | bytes 884744 | tf_op jit(solution)/shard_map/ppermute | solution.py:686
  165.8 10.6 %collective-permute-start.26 = (bf16[2,96,768]{2,1,0:T(8,128)(2,1)}, bf16[2,96,768]{2,1,0:T(8,128)(2,1)S(1)}, u32[]{:S(2)}, u32[]{:S(2)}) collective-permute-start(bf16[2,96,768]{2,1,0:T(8,128)(2,1)} %collective-permute-done.21.refs_4_), channel_id=1, source_target_pairs={{0,4},{4,0},{1,5},{5,1},{2,6},{6,2},{3,7},{7,3},{8,12},{12,8},{9,1... | collective-permute-start | bytes 884744 | tf_op jit(solution)/shard_map/ppermute | solution.py:686
  166.3 10.2 %collective-permute-start.24 = (bf16[2,96,768]{2,1,0:T(8,128)(2,1)}, bf16[2,96,768]{2,1,0:T(8,128)(2,1)S(1)}, u32[]{:S(2)}, u32[]{:S(2)}) collective-permute-start(bf16[2,96,768]{2,1,0:T(8,128)(2,1)} %collective-permute-done.16.refs_2_), channel_id=1, source_target_pairs={{0,4},{4,0},{1,5},{5,1},{2,6},{6,2},{3,7},{7,3},{8,12},{12,8},{9,1... | collective-permute-start | bytes 884744 | tf_op jit(solution)/shard_map/ppermute | solution.py:686
  167.0 15.4 %collective-permute-start.19 = (bf16[2,96,768]{2,1,0:T(8,128)(2,1)}, bf16[2,96,768]{2,1,0:T(8,128)(2,1)S(1)}, u32[]{:S(2)}, u32[]{:S(2)}) collective-permute-start(bf16[2,96,768]{2,1,0:T(8,128)(2,1)} %collective-permute-done.18.refs_5_), channel_id=1, source_target_pairs={{0,8},{8,0},{16,24},{24,16},{1,9},{9,1},{17,25},{25,17},{2,10},{10... | collective-permute-start | bytes 884744 | tf_op jit(solution)/shard_map/ppermute | solution.py:690
  168.8 13.7 %collective-permute-start.17 = (bf16[2,96,768]{2,1,0:T(8,128)(2,1)}, bf16[2,96,768]{2,1,0:T(8,128)(2,1)S(1)}, u32[]{:S(2)}, u32[]{:S(2)}) collective-permute-start(bf16[2,96,768]{2,1,0:T(8,128)(2,1)} %collective-permute-done.16.refs_2_), channel_id=1, source_target_pairs={{0,16},{8,24},{16,0},{24,8},{1,17},{9,25},{17,1},{25,9},{2,18},{10... | collective-permute-start | bytes 884744 | tf_op jit(solution)/shard_map/ppermute | solution.py:690
  (27 other events, 144.6 us)

commit v3 on v2

--- a/solution.py
+++ b/solution.py
@@ -20,7 +20,7 @@
 TILE = 256
 VMEM_LIMIT = 60 * 1024 * 1024
 SMALL_LIMIT = 20 * 1024 * 1024
-COPIES = 24
+COPIES = 64
 f32 = jnp.float32
 bf16 = jnp.bfloat16
 
@@ -57,6 +57,11 @@
         self.pending = []
         return self.inside
 
+    def put(self, source, target):
+        copy = pltpu.make_async_copy(source, target, self.sems.at[next(self.free)])
+        copy.start()
+        self.pending.append(copy)
+
     def send(self, at=...):
         copy = pltpu.make_async_copy(
             self.inside.at[at], self.outside.at[at], self.sems.at[next(self.free)]
@@ -65,7 +70,7 @@
         self.pending.append(copy)
 
 
-def staged_call(body, scalars, arrays, outs, scratch=(), windows=None, limit=VMEM_LIMIT, late=0, aliases=()):
+def staged_call(body, scalars, arrays, outs, scratch=(), windows=None, limit=VMEM_LIMIT, late=0, aliases=(), bare=(), flops=0):
     windows = windows or {}
     n_scalar, n_in, n_out = len(scalars), len(arrays), len(outs)
 
@@ -104,14 +109,14 @@
         out_specs=(pl.BlockSpec(memory_space=pltpu.HBM),) * n_out,
         scratch_shapes=[buffer(at, a) for at, a in enumerate(arrays)]
         + [
-            pltpu.VMEM((16, 128) if at in dict(aliases).values() else o.shape, o.dtype)
+            pltpu.VMEM((16, 128) if at in bare else o.shape, o.dtype)
             for at, o in enumerate(outs)
         ]
         + [pltpu.SemaphoreType.DMA((COPIES,))]
         + list(scratch),
         input_output_aliases={n_scalar + a: o for a, o in aliases},
         compiler_params=pltpu.CompilerParams(vmem_limit_bytes=limit),
-        cost_estimate=pl.CostEstimate(flops=0, bytes_accessed=0, transcendentals=0),
+        cost_estimate=pl.CostEstimate(flops=flops, bytes_accessed=0, transcendentals=0),
     )(*scalars, *arrays)
 
 
@@ -174,7 +179,7 @@
     where = scalars[0]
     q, kv, feats, kv_far = (one.get() for one in ins)
     mixed_low, mixed_t, lse = (one.inside for one in outs)
-    q_head, k, v_t, kf, vf_t = scratch
+    q_head, k, v_t, kf, vf_t, tops, totals = scratch
     width = heads * HDIM
     masks = head_mask(heads, width)
     for h in range(heads):
@@ -193,52 +198,63 @@
     lax.fori_loop(0, jnp.minimum(mine, far), turn, 0)
     own_start = pl.multiple_of(mine * span, span)
     lse[...] = jnp.zeros(lse.shape, f32)
-    for start in range(0, span, TILE):
-        for h in range(heads):
-            q_tile = q_head[h, start : start + TILE, :]
-            f_tile = feats[h, pl.ds(own_start + start, TILE), :]
-
-            def part(k_rows, f_rows, v_rows, low_from, state):
-                counts = dot_nt(f_rows, f_tile)
-                if low_from is not None:
-                    at_k = lax.broadcasted_iota(jnp.int32, counts.shape, 0)
-                    at_q = lax.broadcasted_iota(jnp.int32, counts.shape, 1) + low_from
-                    counts = jnp.where(at_k <= at_q, counts, 0.0)
-                scores = jnp.where(counts > 0, dot_nt(k_rows, q_tile), masked_low)
-                top, total, acc = state
-                new_top = jnp.maximum(top, jnp.max(scores, axis=0, keepdims=True))
-                weights = counts * jnp.exp(scores - new_top)
-                factor = jnp.exp(top - new_top)
-                return (
-                    new_top,
-                    total * factor + jnp.sum(weights, axis=0, keepdims=True),
-                    acc * factor + dot(v_rows, weights.astype(bf16)),
-                )
-
-            state = (
-                jnp.full((1, TILE), masked_low, f32),
-                jnp.zeros((1, TILE), f32),
-                jnp.zeros((HDIM, TILE), f32),
+    pairs = [(start, h) for start in range(0, span, TILE) for h in range(heads)]
+
+    def part(start, h, k_rows, f_rows, v_rows, causal):
+        counts = dot_nt(f_rows, feats[h, pl.ds(own_start + start, TILE), :])
+        if causal:
+            at_k = lax.broadcasted_iota(jnp.int32, counts.shape, 0)
+            at_q = lax.broadcasted_iota(jnp.int32, counts.shape, 1) + start
+            counts = jnp.where(at_k <= at_q, counts, 0.0)
+        scores = dot_nt(k_rows, q_head[h, start : start + TILE, :])
+        scores = jnp.where(counts > 0, scores, masked_low)
+        return counts, scores, v_rows
+
+    for at, (start, h) in enumerate(pairs):
+        size = start + TILE
+        head_rows = slice(h * HDIM, (h + 1) * HDIM)
+        counts, scores, v_rows = part(
+            start,
+            h,
+            k[:size, :],
+            feats[h, pl.ds(own_start, size), :],
+            v_t[head_rows, :size],
+            True,
+        )
+        top = jnp.max(scores, axis=0, keepdims=True)
+        weights = counts * jnp.exp(scores - top)
+        tops[at : at + 1, :] = top
+        totals[at : at + 1, :] = jnp.sum(weights, axis=0, keepdims=True)
+        mixed_t[head_rows, start : start + TILE] = dot(v_rows, weights.astype(bf16))
+
+    def far_step(j, _):
+        rows = pl.ds(pl.multiple_of(j * span, span), span)
+        for at, (start, h) in enumerate(pairs):
+            head_rows = slice(h * HDIM, (h + 1) * HDIM)
+            counts, scores, v_rows = part(
+                start, h, kf[rows, :], feats[h, rows, :], vf_t[j, head_rows, :], False
             )
-            size = start + TILE
-            head_rows = slice(h * HDIM, (h + 1) * HDIM)
-            state = part(
-                k[:size, :],
-                feats[h, pl.ds(own_start, size), :],
-                v_t[head_rows, :size],
-                start,
-                state,
+            top = tops[at : at + 1, :]
+            new_top = jnp.maximum(top, jnp.max(scores, axis=0, keepdims=True))
+            weights = counts * jnp.exp(scores - new_top)
+            factor = jnp.exp(top - new_top)
+            tops[at : at + 1, :] = new_top
+            totals[at : at + 1, :] = totals[at : at + 1, :] * factor + jnp.sum(
+                weights, axis=0, keepdims=True
             )
-
-            def far_part(j, state):
-                rows = pl.ds(pl.multiple_of(j * span, span), span)
-                return part(kf[rows, :], feats[h, rows, :], vf_t[j, head_rows, :], None, state)
-
-            top, total, acc = lax.fori_loop(0, mine, far_part, state)
-            done = acc / total
-            mixed_t[head_rows, start : start + TILE] = done
-            mixed_low[head_rows, start : start + TILE] = done.astype(bf16)
-            lse[h : h + 1, start : start + TILE] = top + jnp.log(total)
+            mixed_t[head_rows, start : start + TILE] = mixed_t[
+                head_rows, start : start + TILE
+            ] * factor + dot(v_rows, weights.astype(bf16))
+        return 0
+
+    lax.fori_loop(0, mine, far_step, 0)
+    for at, (start, h) in enumerate(pairs):
+        head_rows = slice(h * HDIM, (h + 1) * HDIM)
+        total = totals[at : at + 1, :]
+        done = mixed_t[head_rows, start : start + TILE] / total
+        mixed_t[head_rows, start : start + TILE] = done
+        mixed_low[head_rows, start : start + TILE] = done.astype(bf16)
+        lse[h : h + 1, start : start + TILE] = tops[at : at + 1, :] + jnp.log(total)
     for one in outs:
         one.send()
 
@@ -333,14 +349,13 @@
     outs[0].send()
 
 
-def middle_kernel(pair, scalars, ins, outs, scratch):
+def middle_kernel(scalars, ins, outs, scratch):
     mixed4, x, w_out, gain, bias, w_up, w_down, *c_parts = ins
-    gm, gr, sums, ffn, *wide = outs
-    act, low, gh, branch, c, resids, made, c4 = scratch
+    gm, sums, act, gh, branch, low, c, resids = outs
+    (c4,) = scratch
     parts, width, span = mixed4.inside.shape
     for step, one in enumerate(c_parts):
-        one.start(target=c4.at[scalars[1][0] ^ step])
-    chunk = span // parts
+        one.start(target=c4.at[scalars[0][0] ^ step])
     mixed_t = mixed4.get()[...].reshape(D, span)
     x.get(), w_out.get()
     gain = gain.get()[...].reshape(1, D)
@@ -350,45 +365,63 @@
     for start in range(0, span, TILE):
         rows = slice(start, start + TILE)
         resid = x.inside[rows, :].astype(f32) + dot_tn(mixed_t[:, rows], w_out.inside[...])
-        resids[rows, :] = resid
+        resids.inside[rows, :] = resid.astype(bf16)
         hat, scale = normalise(resid)
         normed = (hat * gain + bias).astype(bf16)
-        low[rows, :] = normed
+        low.inside[rows, :] = normed
         w_up.get()
         hidden = dot(normed, w_up.inside[...])
         bell = 0.5 + 0.5 * lax.erf(hidden * (0.5**0.5))
-        act[rows, :] = (hidden * bell).astype(bf16)
+        act.inside[rows, :] = (hidden * bell).astype(bf16)
         slope = bell + hidden * jnp.exp(-0.5 * hidden * hidden) * 0.3989422804014327
         if start == 0:
             w_down.get()
             for one in c_parts:
                 one.get()
             for part in range(parts):
-                c[:, part * width : (part + 1) * width] = c4[part].T
-        grad_hidden = (slope * dot_nt(c[rows, :], w_down.inside[...])).astype(bf16)
-        gh[rows, :] = grad_hidden
+                c.inside[:, part * width : (part + 1) * width] = c4[part].T
+            c.send()
+        c_rows = c.inside[rows, :]
+        grad_hidden = (slope * dot_nt(c_rows, w_down.inside[...])).astype(bf16)
+        gh.inside[rows, :] = grad_hidden
         grad_normed = dot_nt(grad_hidden, w_up.inside[...])
         gain_sum = gain_sum + jnp.sum(grad_normed * hat, axis=0, keepdims=True)
         bias_sum = bias_sum + jnp.sum(grad_normed, axis=0, keepdims=True)
-        grad_resid = norm_backward(hat, scale, grad_normed * gain) + c[rows, :].astype(f32) * (
+        grad_resid = norm_backward(hat, scale, grad_normed * gain) + c_rows.astype(f32) * (
             1.0 / parts
         )
-        gr.inside[rows, :] = grad_resid
         grad_low = grad_resid.astype(bf16)
-        branch[rows, :] = grad_low
+        branch.inside[rows, :] = grad_low
+        for one in (act, low, gh, resids, branch):
+            one.send(pl.ds(start, TILE))
         for part in range(parts):
             gm.inside[part, :, rows] = dot_nt(
                 w_out.inside[part * width : (part + 1) * width, :], grad_low
             ).astype(bf16)
-    gm.send()
-    gr.send()
     sums.inside[0:1, :] = gain_sum
     sums.inside[1:2, :] = bias_sum
+    gm.send()
     sums.send()
+
+
+def weights_kernel(pair, scalars, ins, outs, scratch):
+    act, c, low, gh, mixed4, branch, w_down, resids = ins
+    ffn, *wide = outs
+    (made,) = scratch
+    parts, width, span = mixed4.inside.shape
+    chunk = span // parts
     where = scalars[0]
-    lefts = (lambda: dot_tn(act[...], c[...]), lambda: dot_tn(low[...], gh[...]))
-    lefts += (lambda: dot(mixed_t, branch[...]),)
-    for at, product in enumerate(lefts):
+
+    def out_product():
+        mixed_t = mixed4.get()[...].reshape(D, span)
+        return dot(mixed_t, branch.get()[...])
+
+    products = (
+        lambda: dot_tn(act.get()[...], c.get()[...]),
+        lambda: dot_tn(low.get()[...], gh.get()[...]),
+        out_product,
+    )
+    for at, product in enumerate(products):
         if not pair:
             wide[0].inside[at] = product().astype(bf16)
             continue
@@ -396,16 +429,19 @@
         rows_count = wide[0].inside.shape[1]
         size = D // (2 * rows_count)
         for row in range(rows_count):
-            for out, half in ((wide[0], where[0]), (wide[1], 1 - where[0])):
+            for out, half in ((wide[0].inside.at[at], where[0]), (wide[1 + at].inside, 1 - where[0])):
                 start = pl.multiple_of((2 * row + half) * size, size)
-                out.inside[at, row] = made[pl.ds(start, size), :]
-        wide[1].send(at)
+                out[row] = made[pl.ds(start, size), :]
+        wide[1 + at].send()
         wide[0].send(at)
     if not pair:
         wide[0].send()
+    w_down.get(), resids.get()
     for start in range(0, span, TILE):
         rows = slice(start, start + TILE)
-        out = dot(act[rows, :], w_down.inside[...]) + resids[rows, :] * (1.0 / parts)
+        out = dot(act.inside[rows, :], w_down.inside[...]) + resids.inside[rows, :].astype(f32) * (
+            1.0 / parts
+        )
         out_t = out.astype(bf16).T
         for part in range(parts):
             for at in range(start, start + TILE, chunk):
@@ -416,50 +452,44 @@
 
 
 def add_kernel(scalars, ins, outs, scratch):
-    keep, more = ins
-    keep.get(), more.get()
-    for at, out in enumerate(outs):
-        block = scalars[0][0] ^ at
-        for group in range(keep.inside.shape[0]):
+    keep, *more = ins
+    keep.get()
+    for group, one in enumerate(more):
+        one.get()
+        for at, out in enumerate(outs):
+            block = scalars[0][0] ^ at
             out.inside[group] = (
-                keep.inside[group, block].astype(f32) + more.inside[group, block].astype(f32)
+                keep.inside[group, block].astype(f32) + one.inside[block].astype(f32)
             ).astype(bf16)
     for out in outs[1:] + outs[:1]:
         out.send()
 
 
 def row_sum_kernel(parts, scalars, ins, outs, scratch):
-    ffn_own, both = outs
-    (tail,) = scratch
+    ffn_own, *out_parts = outs
+    (rows,) = scratch
     total = ins[0].get()[...].astype(f32)
-    for one in ins[1:-1]:
+    for one in ins[1:]:
         total = total + one.get()[...].astype(f32)
     total = total.astype(bf16)
     size = total.shape[1]
     half = size // 2
     width = D // parts
-    ffn_own.inside[...] = total[:2].reshape(2 * size, D)
-    ffn_own.send()
-    for part in range(parts):
-        start = part * width
-        top = total[2, :half, start : start + width]
-        low = total[2, half:, start : start + width]
-        tail[part, :half, :] = top[:, :128]
-        tail[part, half : 2 * half, :64] = top[:, 128:]
-        tail[part, half : 2 * half, 64:] = low[:, :64]
-        tail[part, 2 * half :, :] = low[:, 64:]
-    span = both.outside.shape[1] - 3 * half
-    copies = []
-    for part in range(parts):
-        copy = pltpu.make_async_copy(
-            tail.at[part],
-            both.outside.at[part, pl.ds(span, 3 * half), :],
-            both.sems.at[next(both.free)],
-        )
-        copy.start()
-        copies.append(copy)
-    for copy in copies:
-        copy.wait()
+    for own in range(parts):
+
+        @pl.when(scalars[0][0] == own)
+        def _():
+            for step, out in enumerate(out_parts):
+                part = own ^ step
+                columns = slice(part * width, (part + 1) * width)
+                out.inside[:, :width] = total[2, :half, columns]
+                out.inside[:, width:] = total[2, half:, columns]
+
+    for one in out_parts[::-1]:
+        one.send()
+    rows[...] = total[:2].reshape(2 * size, D)
+    for row in range(ffn_own.outside.shape[0]):
+        ffn_own.put(rows, ffn_own.outside.at[row])
 
 
 SLOT = 64
@@ -489,7 +519,7 @@
         grad_normed = dot_nt(grads[rows, :], own.inside[...])
         gain_sum = gain_sum + jnp.sum(grad_normed * hat, axis=0, keepdims=True)
         bias_sum = bias_sum + jnp.sum(grad_normed, axis=0, keepdims=True)
-        grad_in = gr.inside[rows, :] + norm_backward(hat, scale, grad_normed * gain)
+        grad_in = gr.inside[rows, :].astype(f32) + norm_backward(hat, scale, grad_normed * gain)
         turned = grad_in.astype(bf16).T
         for at in range(start, start + TILE, piece):
             back.inside[at // piece] = turned[:, at - start : at - start + piece]
@@ -504,12 +534,15 @@
     made[...] = dot_tn(normed.get()[...], grads[:, :lanes]).astype(bf16)
     tail = small[...].astype(bf16)
     if pair:
-        _, rows_count, size, _ = narrow[0].inside.shape
+        rows_count, size, _ = narrow[1].inside.shape
         for row in range(rows_count):
-            for out, half in ((narrow[0], scalars[0][0]), (narrow[1], 1 - scalars[0][0])):
+            for out, half in (
+                (narrow[0].inside.at[0], scalars[0][0]),
+                (narrow[1].inside, 1 - scalars[0][0]),
+            ):
                 start = pl.multiple_of((2 * row + half) * size, size)
-                out.inside[0, row] = made[pl.ds(start, size), :]
-                out.inside[0, row, :48, 3 * width :] = tail
+                out[row] = made[pl.ds(start, size), :]
+                out[row, :48, 3 * width :] = tail
         narrow[1].send()
         narrow[0].send()
     else:
@@ -521,13 +554,15 @@
 
 def own_sum_kernel(parts, count, scalars, ins, outs, scratch):
     mine = outs[0].inside
-    tails, small = scratch
+    (small,) = scratch
     width = D // parts
     size = ins[0].inside.shape[1]
     half = size // 2
-    last = ins[count]
-    span = last.outside.shape[1] - 3 * half
-    last.start(source=last.outside.at[:, pl.ds(span, 3 * half), :], target=tails)
+    out = ins[count].get()[...].astype(f32)
+    for one in ins[count + 1 :]:
+        out = out + one.get()[...].astype(f32)
+    mine[:half, 3 * width :] = out[:, :width].astype(bf16)
+    mine[half:size, 3 * width :] = out[:, width:].astype(bf16)
     total = ins[0].get()[0].astype(f32)
     for one in ins[1:count]:
         total = total + one.get()[0].astype(f32)
@@ -541,16 +576,6 @@
                 row : row + 1, 3 * width :
             ]
     mine[size:, :] = small[...].astype(bf16)
-    last.get()
-    out = tails[0].astype(f32)
-    for part in range(1, parts):
-        out = out + tails[part].astype(f32)
-    out = out.astype(bf16)
-    start = 3 * width
-    mine[:half, start : start + 128] = out[:half]
-    mine[:half, start + 128 :] = out[half : 2 * half, :64]
-    mine[half:size, start : start + 64] = out[half : 2 * half, 64:]
-    mine[half:size, start + 64 :] = out[2 * half :]
     outs[0].send()
 
 
@@ -587,92 +612,59 @@
     vectors.send()
 
 
-def spread_kernel(count, table, where, *refs):
-    blocks, outs = refs[:count], refs[-4:]
-    for step, members in enumerate(table):
-
-        @pl.when(pl.program_id(0) == step)
-        def _():
-            part = 0
-            for at in members:
-                for own in range(blocks[at].shape[0]):
-                    total = 4 * blocks[at].shape[0] * len(members)
-                    width = 4 * D // total
-                    for grad in range(4):
-                        outs[grad][:, part * width : (part + 1) * width] = blocks[at][
-                            own, :, grad * width : (grad + 1) * width
-                        ].astype(f32)
-                    part += 1
-
-
-def spread(row_seq, steps, earlier=None):
+def spread_kernel(steps, scalars, ins, outs, scratch):
+    (buffer,) = scratch
+    row, seq = scalars
+    size = buffer.shape[2]
+    at = 0
+    for step, (row_step, seq_step, count) in enumerate(steps):
+        part = 0
+        for one in ins[at : at + count]:
+            got = one.get()
+            for own in range(got.shape[0]):
+                width = D // (got.shape[0] * count)
+                columns = slice(part * width, (part + 1) * width)
+                for grad in range(4):
+                    buffer[grad, step, :, columns] = got[
+                        own, :, grad * width : (grad + 1) * width
+                    ].astype(f32)
+                part += 1
+        at += count
+        start = pl.multiple_of((2 * (row[0] ^ row_step) + (seq[0] ^ seq_step)) * size, size)
+        for grad in range(4):
+            out = outs[grad]
+            out.put(buffer.at[grad, step], out.outside.at[pl.ds(start, size), :])
+
+
+def spread(row_here, here, steps, earlier=(), flops=0):
     count = sum(len(blocks) for _, _, blocks in steps)
     size = steps[0][2][0].shape[1]
-    table, at = [], 0
-    for _, _, blocks in steps:
-        table.append(tuple(range(at, at + len(blocks))))
-        at += len(blocks)
     received = [block for _, _, blocks in steps for block in blocks]
-    kept = [] if earlier is None else list(earlier)
-
-    def place(i, w):
-        row, seq = jnp.int32(0), jnp.int32(0)
-        for step, (row_step, seq_step, _) in enumerate(steps):
-            row = jnp.where(i == step, row_step, row)
-            seq = jnp.where(i == step, seq_step, seq)
-        return (2 * (w[0] ^ row) + (w[1] ^ seq), 0)
-
-    return pl.pallas_call(
-        functools.partial(spread_kernel, count, table),
-        out_shape=(jax.ShapeDtypeStruct((D, D), f32),) * 4,
-        grid_spec=pltpu.PrefetchScalarGridSpec(
-            num_scalar_prefetch=1,
-            grid=(len(steps),),
-            in_specs=[
-                pl.BlockSpec(block.shape, lambda i, w: (0, 0, 0)) for block in received
-            ]
-            + [pl.BlockSpec(memory_space=pl.ANY)] * len(kept),
-            out_specs=(pl.BlockSpec((size, D), place),) * 4,
-        ),
-        input_output_aliases={1 + count + at: at for at in range(len(kept))},
-        compiler_params=pltpu.CompilerParams(vmem_limit_bytes=SMALL_LIMIT),
-        cost_estimate=pl.CostEstimate(flops=0, bytes_accessed=0, transcendentals=0),
-    )(row_seq, *received, *kept)
-
-
-def spread_ffn_kernel(count, where, *refs):
-    blocks, outs = refs[:count], refs[count:]
-    size = outs[0].shape[0]
-    for at in range(count):
-
-        @pl.when(pl.program_id(0) == at)
-        def _():
-            outs[0][...] = blocks[at][:size, :].astype(f32)
-            outs[1][...] = blocks[at][size:, :].astype(f32)
-
-
-def spread_ffn(row_seq, mine, other):
-    received = [*mine, *other]
-    count = len(received)
-    rows_count = len(mine)
-    size = received[0].shape[0] // 2
-    whole = pl.BlockSpec((2 * size, D), lambda i, w: (0, 0))
-
-    def place(i, w):
-        return (2 * (w[0] ^ (i % rows_count)) + (w[1] ^ (i // rows_count)), 0)
-
-    return pl.pallas_call(
-        functools.partial(spread_ffn_kernel, count),
-        out_shape=(jax.ShapeDtypeStruct((D, D), f32),) * 2,
-        grid_spec=pltpu.PrefetchScalarGridSpec(
-            num_scalar_prefetch=1,
-            grid=(count,),
-            in_specs=[whole] * count,
-            out_specs=(pl.BlockSpec((size, D), place),) * 2,
-        ),
-        compiler_params=pltpu.CompilerParams(vmem_limit_bytes=SMALL_LIMIT),
-        cost_estimate=pl.CostEstimate(flops=0, bytes_accessed=0, transcendentals=0),
-    )(row_seq, *received)
+    return staged_call(
+        functools.partial(spread_kernel, [(a, b, len(c)) for a, b, c in steps]),
+        [row_here, here],
+        [*received, *earlier],
+        (shape(D, D, kind=f32),) * 4,
+        scratch=[pltpu.VMEM((4, len(steps), size, D), f32)],
+        limit=SMALL_LIMIT,
+        late=len(earlier),
+        aliases=tuple((count + at, at) for at in range(len(earlier))),
+        bare=range(4),
+        flops=flops,
+    )
+
+
+def spread_ffn_kernel(scalars, ins, outs, scratch):
+    (buffer,) = scratch
+    size = buffer.shape[2]
+    for half, one in enumerate(ins):
+        got = one.get()
+        for row in range(got.shape[0]):
+            start = pl.multiple_of((2 * row + (scalars[0][0] ^ half)) * size, size)
+            for grad, out in enumerate(outs):
+                place = buffer.at[grad, half * got.shape[0] + row]
+                place[...] = got[row, grad * size : (grad + 1) * size, :].astype(f32)
+                out.put(place, out.outside.at[pl.ds(start, size), :])
 
 
 def broadcast_exchange(value, axis):
@@ -757,6 +749,7 @@
         [part_here],
         [doc_ids],
         (shape(heads, doc_ids.shape[1], FEATS),),
+        flops=1 << 42,
     )
 
     def window(scalars):
@@ -784,42 +777,55 @@
             pltpu.VMEM((width, span), bf16),
             pltpu.VMEM((far_rows, width), bf16),
             pltpu.VMEM((far_rows // span, width, span), bf16),
+            pltpu.VMEM((heads * span // TILE + 8, TILE), f32),
+            pltpu.VMEM((heads * span // TILE + 8, TILE), f32),
         ],
     )
     mixed, *c_parts = lax.optimization_barrier((mixed, *c_parts))
     mixed4 = lax.all_gather(mixed, "pat")
 
-    wide_shapes = (shape(3, rows_count, size, D),) * 2 if pair else (shape(3, D, D),)
-    gm, gr, sums, ffn, *wide = staged_call(
-        functools.partial(middle_kernel, pair),
-        [here, part_here],
+    wide_shapes = (shape(3, D, D),)
+    if pair:
+        wide_shapes = (shape(3, rows_count, size, D),) + (shape(rows_count, size, D),) * 3
+    gm, sums, act, gh, branch, low, c, resids = staged_call(
+        middle_kernel,
+        [part_here],
         [mixed4, x, w_out, ln2_gain, ln2_bias, w_up, w_down, *c_parts],
-        (
-            shape(parts, width, span),
-            shape(span, D, kind=f32),
-            shape(8, D, kind=f32),
-            shape(parts, parts * width + (3 * size // 2 if pair else 0), quarter),
-            *wide_shapes,
-        ),
-        scratch=[pltpu.VMEM((span, D), bf16)] * 5
-        + [
-            pltpu.VMEM((span, D), f32),
-            pltpu.VMEM((D, D), bf16),
-            pltpu.VMEM((parts, width, span), bf16),
-        ],
+        (shape(parts, width, span), shape(8, D, kind=f32)) + (shape(span, D),) * 6,
+        scratch=[pltpu.VMEM((parts, width, span), bf16)],
         late=parts,
     )
     gm_parts = lax.all_to_all(gm, "pat", 0, 0, tiled=True)
+    ffn, *wide = staged_call(
+        functools.partial(weights_kernel, pair),
+        [here],
+        [act, c, low, gh, mixed4, branch, w_down, resids],
+        (shape(parts, parts * width, quarter), *wide_shapes),
+        scratch=[pltpu.VMEM((D, D), bf16)],
+        flops=1 << 42,
+    )
 
     if pair:
-        keep, send = wide
+        keep, *sends = wide
         ordered = staged_call(
-            add_kernel, [row_here], [keep, swap(send)], (shape(3, size, D),) * rows_count,
+            add_kernel,
+            [row_here],
+            [keep, *[swap(send) for send in sends]],
+            (shape(3, size, D),) * rows_count,
             limit=SMALL_LIMIT,
         )
-        received = [ordered[0]] + [trade(ordered[s], "row", s) for s in range(1, rows_count)]
-        gm_parts, *_ = lax.optimization_barrier((gm_parts, received[1], received[2]))
-
+        wide_parts = [ordered[0]] + [trade(ordered[s], "row", s) for s in range(1, rows_count)]
+
+    ffn, _ = lax.optimization_barrier((ffn, gm_parts))
+    ffn_parts = lax.all_to_all(ffn, "pat", 0, 0, tiled=True)
+    (out_t,) = staged_call(
+        output_kernel,
+        [],
+        [ffn_parts],
+        (shape(width, span),),
+        limit=SMALL_LIMIT,
+        flops=1 << 42,
+    )
     gq, gkv, gkv_far = staged_call(
         functools.partial(attention_back_kernel, heads, span),
         [here],
@@ -840,31 +846,30 @@
             pltpu.VMEM((width, span), bf16),
             pltpu.VMEM((width, span), f32),
         ],
+        flops=1 << 42,
     )
 
     if pair:
         gkv_more = swap(gkv_far)
-        ffn_own, ffn = staged_call(
+        ffn_own, *out_parts = staged_call(
             functools.partial(row_sum_kernel, parts),
-            [],
-            [*received, ffn],
-            (shape(2 * size, D), shape(*ffn.shape)),
-            scratch=[pltpu.VMEM((parts, 3 * size // 2, quarter), bf16)],
+            [part_here],
+            wide_parts,
+            (shape(rows_count, 2 * size, D),) + (shape(size // 2, 2 * width),) * parts,
+            scratch=[pltpu.VMEM((2 * size, D), bf16)],
             limit=SMALL_LIMIT,
-            late=1,
-            aliases=((rows_count, 1),),
-        )
-        ffn_parts = lax.all_to_all(ffn, "pat", 0, 0, tiled=True)
+            bare=(0,),
+        )
+        out_parts = [out_parts[0]] + [trade(out_parts[s], "pat", s) for s in range(1, parts)]
     else:
         gkv_more = lax.psum_scatter(gkv_far, "seq", scatter_dimension=0, tiled=True)
-        ffn_parts = lax.all_to_all(ffn, "pat", 0, 0, tiled=True)
 
     lanes = 3 * width + SLOT
-    narrow_shapes = (shape(1, rows_count, size, lanes),) * 2 if pair else (shape(D, lanes),)
+    narrow_shapes = (shape(1, rows_count, size, lanes), shape(rows_count, size, lanes)) if pair else (shape(D, lanes),)
     back, *narrow = staged_call(
         functools.partial(last_kernel, parts, pair),
         [here],
-        [gq, normed, gkv, own, x, ln1_gain, gr, sums, gkv_more],
+        [gq, normed, gkv, own, x, ln1_gain, branch, sums, gkv_more],
         (shape(parts, parts * width, quarter), *narrow_shapes),
         scratch=[
             pltpu.VMEM((span, D), bf16),
@@ -875,42 +880,52 @@
 
     if pair:
         keep, send = narrow
+        send, *_ = lax.optimization_barrier((send, *wide_parts[1:]))
         ordered = staged_call(
             add_kernel, [row_here], [keep, swap(send)], (shape(1, size, lanes),) * rows_count,
             limit=SMALL_LIMIT,
         )
         received = [ordered[0]] + [trade(ordered[s], "row", s) for s in range(1, rows_count)]
-        ffn_own, *received = lax.optimization_barrier((ffn_own, *received))
-        ffn_mine = [ffn_own] + [trade(ffn_own, "row", s) for s in range(1, rows_count)]
+        received[3], _ = lax.optimization_barrier((received[3], out_t))
         (mine,) = staged_call(
             functools.partial(own_sum_kernel, parts, rows_count),
             [],
-            [*received, ffn_parts],
+            [*received, *out_parts],
             (shape(size + 16, D),),
-            scratch=[
-                pltpu.VMEM((parts, 3 * size // 2, quarter), bf16),
-                pltpu.VMEM((16, D), f32),
-            ],
+            scratch=[pltpu.VMEM((16, D), f32)],
             limit=SMALL_LIMIT,
-            late=1,
         )
         gathered = lax.all_gather(mine, "pat")
-        back, gathered, *ffn_mine = lax.optimization_barrier((back, gathered, *ffn_mine))
+        ffn_own, *_ = lax.optimization_barrier(
+            (ffn_own, ffn_parts, *received[1:], *out_parts[1:])
+        )
+        ffn_mine = lax.all_to_all(ffn_own, "row", 0, 0, tiled=True)
+        gathered, ffn_mine, back = lax.optimization_barrier((gathered, ffn_mine, back))
         back_parts = lax.all_to_all(back, "pat", 0, 0, tiled=True)
-        ffn_other = [swap(value) for value in ffn_mine]
-        row_seq = jnp.stack([row_index, seq_index]).astype(jnp.int32)
-        grad_down, grad_up = spread_ffn(row_seq, ffn_mine, ffn_other)
-        a, b = gathered[: parts // 2, :size], gathered[parts // 2 :, :size]
-        a1, b2 = trade(a, "row", 1), trade(b, "row", 2)
-        b1, a2 = trade(b, "row", 1), trade(a, "row", 2)
-        a3, b3 = trade(a1, "row", 2), trade(b2, "row", 1)
-        early = [(a, b), (a1, b1), (a2, b2)]
-        steps = [(at, 0, pieces) for at, pieces in enumerate(early)] + [
-            (at, 1, [swap(piece) for piece in pieces]) for at, pieces in enumerate(early)
-        ]
-        grads = spread(row_seq, steps)
-        far3, near3, *_ = lax.optimization_barrier((a3, b3, grads[0], grad_up))
-        grads = spread(row_seq, [(3, 0, (a3, b3)), (3, 1, (swap(far3), swap(near3)))], grads)
+        grad_down, grad_up = staged_call(
+            spread_ffn_kernel,
+            [here],
+            [ffn_mine, swap(ffn_mine)],
+            (shape(D, D, kind=f32),) * 2,
+            scratch=[pltpu.VMEM((2, 2 * rows_count, size, D), f32)],
+            limit=SMALL_LIMIT,
+            bare=range(2),
+        )
+        own = gathered[:, :size]
+        near = [own] + [trade(own, "row", s) for s in range(1, rows_count)]
+        grads = spread(
+            row_here,
+            here,
+            [(s, 0, (near[s],)) for s in range(rows_count - 1)]
+            + [(s, 1, (swap(near[s]),)) for s in range(rows_count - 1)],
+        )
+        far, *_ = lax.optimization_barrier((near[-1], grads[0], grad_up))
+        grads = spread(
+            row_here,
+            here,
+            [(rows_count - 1, 0, (near[-1],)), (rows_count - 1, 1, (swap(far),))],
+            grads,
+        )
     else:
         axes = ("row", "seq")
         back_parts = lax.all_to_all(back, "pat", 0, 0, tiled=True)
@@ -927,9 +942,6 @@
             .reshape(D, D)
             for at in range(3)
         ] + [grad_out]
-    (out_t,) = staged_call(
-        output_kernel, [], [ffn_parts], (shape(width, span),), limit=SMALL_LIMIT
-    )
     grad_in, vectors = staged_call(
         finish_kernel,
         [],

time: 189 us -> 177 us (0.937)
  waiting for transfers between devices: 44 us -> 24.8 us
  Pallas kernels: 59.5 us -> 67.7 us
  local copies, waits for them, and re-layouts: 7.32 us -> 4.57 us
    ppermute x18 -> x15, waiting for transfers between devices: 39.8 us -> 15.6 us  [trade(): lax.ppermute(value, axis, [(a, a ^ step) for a in range(lax.axis_size(axi...]
    pallas_call x12 -> x16, Pallas kernels: 46.1 us -> 67.7 us  [staged_call(): pl.pallas_call(kernel, out_shape=tuple(outs), in_specs=[pl.BlockSpec(memo...]
    pallas_call x3 -> x0, Pallas kernels: 13.4 us -> none  [the longest x2 8.11 us: spread(): pl.pallas_call(functools.partial(spread_kernel, count, table), out_shape=...]
    all_to_all x0 -> x1, starting transfers between devices: none -> 3.53 us  [per_device(): ffn_mine = lax.all_to_all(ffn_own, 'row', 0, 0, tiled=True)]
    ppermute x16 -> x11, waiting for transfers between devices: 4.22 us -> 7.4 us  [swap(): return lax.ppermute(value, 'seq', [(0, 1), (1, 0)])]
    unnamed x28 -> x10, local copies, waits for them, and re-layouts: 6.65 us -> 3.9 us
    ppermute x16 -> x11, starting transfers between devices: 4.74 us -> 3.18 us  [swap(): return lax.ppermute(value, 'seq', [(0, 1), (1, 0)])]
    ppermute x18 -> x15, starting transfers between devices: 22.3 us -> 22.2 us  [trade(): lax.ppermute(value, axis, [(a, a ^ step) for a in range(lax.axis_size(axi...]
  transfers between devices with their start and end apart: 37 -> 30, of which waited for: 12 -> 14; matrix products, arithmetic and copies ran while one was open for 0% -> 0% of each run, Pallas kernels for 23% -> 31%
where the time goes in v3:
time: 177 us; the launch traced here: 176 us
  Pallas kernels  67.7 us (38%)
  starting transfers between devices  41.7 us (24%)
  blocking collectives  36.2 us (20%)
  waiting for transfers between devices  24.8 us (14%)
  local copies, waits for them, and re-layouts  4.57 us (3%)
    pallas_call x16, Pallas kernels, staged_call(): pl.pallas_call(kernel, out_shape=tuple(outs), in_specs=[pl.BlockSpec(memo...  67.7 us
    ppermute x15, starting transfers between devices, trade(): lax.ppermute(value, axis, [(a, a ^ step) for a in range(lax.axis_size(axi...  22.2 us
    all_gather x1, blocking collectives, per_device(): mixed4 = lax.all_gather(mixed, 'pat')  19.5 us
    all_gather x1, blocking collectives, per_device(): gathered = lax.all_gather(mine, 'pat')  16.7 us
    ppermute x15, waiting for transfers between devices, trade(): lax.ppermute(value, axis, [(a, a ^ step) for a in range(lax.axis_size(axi...  15.6 us
    ppermute x11, waiting for transfers between devices, swap(): return lax.ppermute(value, 'seq', [(0, 1), (1, 0)])  7.4 us
    all_to_all x1, starting transfers between devices, per_device(): ffn_parts = lax.all_to_all(ffn, 'pat', 0, 0, tiled=True)  4.42 us
    all_to_all x1, starting transfers between devices, per_device(): back_parts = lax.all_to_all(back, 'pat', 0, 0, tiled=True)  4.26 us
  transfers between devices with their start and end apart: 30, of which 14 were waited for; matrix products, arithmetic and copies ran while one was open for 0% of the time, Pallas kernels for 31%

profile of v3, /device:TPU:0, one launch (start us, length us, event | category | flops | bytes accessed | tf_op | source)
XLA Modules:
  0.0 176.1 jit_solution(10142092430640789598)
XLA Ops:
  0.6 5.1 %collective-permute-start.3 = (bf16[192,512]{1,0:T(8,128)(2,1)}, bf16[192,512]{1,0:T(8,128)(2,1)}, u32[]{:S(2)}, u32[]{:S(2)}) collective-permute-start(bf16[192,512]{1,0:T(8,128)(2,1)} %bitcast.20), channel_id=1, source_target_pairs={{0,3},{1,2},{2,1},{3,0},{4,7},{5,6},{6,5},{7,4},{8,11},{9,10},{10,... | collective-permute-start | bytes 589832 | tf_op jit(solution)/shard_map/ppermute | solution.py:682
  6.4 4.1 %shard_map.220 = (bf16[512,768]{1,0:T(8,128)(2,1)}, bf16[512,192]{1,0:T(8,128)(2,1)}, bf16[512,384]{1,0:T(8,128)(2,1)}, bf16[768,768]{1,0:T(8,128)(2,1)}) custom-call(s32[1]{0:T(128)} %bitcast.1.refs_0_, bf16[512,768]{1,0:T(8,128)(2,1)} %bitcast.15, f32[768]{0:T(1024)} %refs_6_.5, f32[768]{0:T(1024)} %refs_3_.2, bf16[768,768]{1,0:T(8,128)(2,1)} %refs_4_.2, ...), custom_call_target="tpu_custom_call" | custom-call | tf_op jit(solution)/shard_map/pallas_call | solution.py:104
  10.6 3.0 %shard_map.221.refs_3_.refs_6_ = bf16[3,1024,128]{2,1,0:T(8,128)(2,1)} custom-call(s32[1]{0:T(128)} %bitcast.1.refs_0_, s32[1,1024]{1,0:T(1,128)} %refs_1_.1), custom_call_target="tpu_custom_call" | custom-call | flops 4398046511104 | tf_op jit(solution)/shard_map/pallas_call | solution.py:104
  13.6 5.4 %shard_map.222 = (bf16[192,512]{1,0:T(8,128)(2,1)}, f32[192,512]{1,0:T(8,128)}, f32[8,512]{1,0:T(8,128)}) custom-call(s32[1]{0:T(128)} %bitcast.refs_0_.refs_1_, bf16[512,192]{1,0:T(8,128)(2,1)} %get-tuple-element.76.refs_1_.refs_2_, bf16[512,384]{1,0:T(8,128)(2,1)} %get-tuple-element.77.refs_2_.refs_5_, bf16[3,1024,128]{2,1,0:T(8,128)(2,1)} %shard_map.221.refs_3_.refs_6_, ...), custom_call_target="tpu_custom_call" | custom-call | tf_op jit(solution)/shard_map/pallas_call | solution.py:104
  19.1 3.7 %collective-permute-done.2.refs_10_ = bf16[192,512]{1,0:T(8,128)(2,1)} collective-permute-done((bf16[192,512]{1,0:T(8,128)(2,1)}, bf16[192,512]{1,0:T(8,128)(2,1)}, u32[]{:S(2)}, u32[]{:S(2)}) %collective-permute-start.2) | collective-permute-done | bytes 196640 | tf_op jit(solution)/shard_map/ppermute | solution.py:682
  22.8 19.5 %all-gather = bf16[768,512]{1,0:T(8,128)(2,1)} all-gather(bf16[192,512]{1,0:T(8,128)(2,1)} %get-tuple-element.79), channel_id=2, replica_groups=mesh['row'=4,'seq'=2,'pat'=4] {'pat'}, dimensions={0}, use_global_device_ids=true | all-gather | bytes 983040 | tf_op jit(solution)/shard_map/all_gather | solution.py:785
  42.3 9.3 %shard_map.223 = (bf16[4,192,512]{2,1,0:T(8,128)(2,1)}, f32[8,768]{1,0:T(8,128)}, bf16[512,768]{1,0:T(8,128)(2,1)}, bf16[512,768]{1,0:T(8,128)(2,1)}, bf16[512,7...) custom-call(s32[1]{0:T(128)} %bitcast.1.refs_0_, ...), custom_call_target="tpu_custom_call" | custom-call | tf_op jit(solution)/shard_map/pallas_call | solution.py:104
  51.6 4.2 %all-to-all-start = ((bf16[4,192,512]{2,1,0:T(8,128)(2,1)}), bf16[4,192,512]{2,1,0:T(8,128)(2,1)}, u32[]{:S(2)}, u32[]{:S(2)}) async-start(bf16[4,192,512]{2,1,0:T(8,128)(2,1)} %get-tuple-element.91), calls=%async_computation | async-start | bytes 1572864 | tf_op jit(solution)/shard_map/all_to_all | solution.py:798
  55.8 7.2 %shard_map.224 = (bf16[4,768,128]{2,1,0:T(8,128)(2,1)}, bf16[3,4,96,768]{3,2,1,0:T(8,128)(2,1)}, bf16[4,96,768]{2,1,0:T(8,128)(2,1)}, bf16[4,96,768]{2,1,0:T(8,128)(2,1)}, bf16[4,96,768]{2,1,0:T(8,128)(2,1)}) custom-call(s32[1]{0:T(128)} %bitcast.refs_0_.refs_1_, bf16[512,768]{1,0:T(8,128)(2,1)} %get-tuple-element.84.refs_1_, ...), custom_call_target="tpu_custom_call" | custom-call | flops 4398046511104 | tf_op jit(solution)/shard_map/pallas_call | solution.py:104
  68.4 2.7 %shard_map.228 = (bf16[3,96,768]{2,1,0:T(8,128)(2,1)S(1)}, bf16[3,96,768]{2,1,0:T(8,128)(2,1)}, bf16[3,96,768]{2,1,0:T(8,128)(2,1)}, bf16[3,96,768]{2,1,0:T(8,128)(2,1)}) custom-call(s32[1]{0:T(128)} %bitcast.9.refs_0_, bf16[3,4,96,768]{3,2,1,0:T(8,128)(2,1)S(1)} %copy-done, bf16[4,96,768]{2,1,0:T(8,128)(2,1)S(1)} %collective-permute-done.5.refs_2_, ...), custom_call_target="tpu_custom_call" | custom-call | tf_op jit(solution)/shard_map/pallas_call | solution.py:104
  76.5 4.4 %all-to-all-start.1 = ((bf16[4,768,128]{2,1,0:T(8,128)(2,1)}), bf16[4,768,128]{2,1,0:T(8,128)(2,1)}, u32[]{:S(2)}, u32[]{:S(2)}) async-start(bf16[4,768,128]{2,1,0:T(8,128)(2,1)} %get-tuple-element.92), calls=%async_computation.1 | async-start | bytes 1572864 | tf_op jit(solution)/shard_map/all_to_all | solution.py:820
  80.9 5.7 %shard_map.226 = (bf16[512,192]{1,0:T(8,128)(2,1)}, f32[512,384]{1,0:T(8,128)}, bf16[512,384]{1,0:T(8,128)(2,1)}) custom-call(s32[1]{0:T(128)} %bitcast.refs_0_.refs_1_, bf16[4,192,512]{2,1,0:T(8,128)(2,1)} %all-to-all-done.refs_1_, bf16[512,192]{1,0:T(8,128)(2,1)} %get-tuple-element.76.refs_1_.refs_2_, f32[192,512]{1,0:T(8,128)} %get-tuple-element.93.refs_3_, ...), custom_call_target="tpu_custom_call" | custom-call | flops 4398046511104 | tf_op jit(solution)/shard_map/pallas_call | solution.py:104
  90.7 6.8 %shard_map.227 = (bf16[4,768,128]{2,1,0:T(8,128)(2,1)}, bf16[1,4,96,640]{3,2,1,0:T(8,128)(2,1)}, bf16[4,96,640]{2,1,0:T(8,128)(2,1)}) custom-call(s32[1]{0:T(128)} %bitcast.refs_0_.refs_1_, bf16[512,192]{1,0:T(8,128)(2,1)} %get-tuple-element.95.refs_1_, bf16[512,768]{1,0:T(8,128)(2,1)} %get-tuple-element.96.refs_2_, f32[512,384]{1,0:T(8,128)} %get-tuple-element.97.refs_3_, ...), custom_call_target="tpu_custom_call" | custom-call | tf_op jit(solution)/shard_map/pallas_call | solution.py:104
  102.7 2.6 %collective-permute-start.14 = (bf16[1,96,640]{2,1,0:T(8,128)(2,1)S(1)}, bf16[1,96,640]{2,1,0:T(8,128)(2,1)S(1)}, u32[]{:S(2)}, u32[]{:S(2)}) collective-permute-start(bf16[1,96,640]{2,1,0:T(8,128)(2,1)S(1)} %get-tuple-element.114), channel_id=1, source_target_pairs={{0,24},{8,16},{16,8},{24,0},{1,25},{9,17},{17,9},{25,1},{2,26},{10... | collective-permute-start | bytes 368648 | tf_op jit(solution)/shard_map/ppermute | solution.py:682
  105.3 3.4 %shard_map.230 = (bf16[4,192,768]{2,1,0:T(8,128)(2,1)}, bf16[48,384]{1,0:T(8,128)(2,1)S(1)}, bf16[48,384]{1,0:T(8,128)(2,1)}, bf16[48,384]{1,0:T(8,128)(2,1)}, bf16[48,384]{1,0:T(8,128)(2,1)}) custom-call(s32[1]{0:T(128)} %bitcast.1.refs_0_, bf16[3,96,768]{2,1,0:T(8,128)(2,1)S(1)} %get-tuple-element.116.refs_1_, ...), custom_call_target="tpu_custom_call" | custom-call | tf_op jit(solution)/shard_map/pallas_call | solution.py:104
  114.8 2.5 %shard_map.225 = bf16[192,512]{1,0:T(8,128)(2,1)} custom-call(bf16[4,768,128]{2,1,0:T(8,128)(2,1)} %all-to-all-done.1.refs_0_), custom_call_target="tpu_custom_call" | custom-call | flops 4398046511104 | tf_op jit(solution)/shard_map/pallas_call | solution.py:104
  119.5 3.5 %all-to-all-start.2 = ((bf16[4,192,768]{2,1,0:T(8,128)(2,1)}), bf16[4,192,768]{2,1,0:T(8,128)(2,1)S(1)}, u32[]{:S(2)}, u32[]{:S(2)}) async-start(bf16[4,192,768]{2,1,0:T(8,128)(2,1)} %get-tuple-element.122), calls=%async_computation.2 | async-start | bytes 2359296 | tf_op jit(solution)/shard_map/all_to_all | solution.py:902
  125.3 16.7 %all-gather.1 = bf16[448,768]{1,0:T(8,128)(2,1)S(1)} all-gather(bf16[112,768]{1,0:T(8,128)(2,1)S(1)} %shard_map.231), channel_id=3, replica_groups=mesh['row'=4,'seq'=2,'pat'=4] {'pat'}, dimensions={0}, use_global_device_ids=true | all-gather | bytes 860160 | tf_op jit(solution)/shard_map/all_gather | solution.py:898
  145.2 4.3 %all-to-all-start.3 = ((bf16[4,768,128]{2,1,0:T(8,128)(2,1)}), bf16[4,768,128]{2,1,0:T(8,128)(2,1)S(1)}, u32[]{:S(2)}, u32[]{:S(2)}) async-start(bf16[4,768,128]{2,1,0:T(8,128)(2,1)} %get-tuple-element.124), calls=%async_computation.3 | async-start | bytes 1572864 | tf_op jit(solution)/shard_map/all_to_all | solution.py:904
  149.7 3.5 %collective-permute-done.20.refs_4_ = bf16[4,96,768]{2,1,0:T(8,128)(2,1)} collective-permute-done((bf16[4,96,768]{2,1,0:T(8,128)(2,1)S(1)}, bf16[4,96,768]{2,1,0:T(8,128)(2,1)}, u32[]{:S(2)}, u32[]{:S(2)}) %collective-permute-start.20) | collective-permute-done | bytes 589856 | tf_op jit(solution)/shard_map/ppermute | solution.py:682
  156.2 4.4 %shard_map.233 = (f32[768,768]{1,0:T(8,128)}, f32[768,768]{1,0:T(8,128)}, f32[768,768]{1,0:T(8,128)}, f32[768,768]{1,0:T(8,128)}) custom-call(s32[1]{0:T(128)} %bitcast.9.refs_0_, s32[1]{0:T(128)} %bitcast.refs_0_.refs_1_, bf16[4,96,768]{2,1,0:T(8,128)(2,1)S(1)} %slice.17.refs_2_, bf16[4,96,768]{2,1,0:T(8,128)(2,1)} %collective-permute-done.19.refs_3_, ...), custom_call_target="tpu_custom_call" | custom-call | tf_op jit(solution)/shard_map/pallas_call | solution.py:104
  160.6 4.3 %shard_map.234 = (f32[768,768]{1,0:T(8,128)}, f32[768,768]{1,0:T(8,128)}) custom-call(s32[1]{0:T(128)} %bitcast.refs_0_.refs_1_, bf16[4,192,768]{2,1,0:T(8,128)(2,1)S(1)} %all-to-all-done.2.refs_1_, bf16[4,192,768]{2,1,0:T(8,128)(2,1)} %collective-permute-done.24.refs_2_), custom_call_target="tpu_custom_call" | custom-call | tf_op jit(solution)/shard_map/pallas_call | solution.py:104
  164.9 5.6 %collective-permute-done.18.refs_2_ = bf16[4,96,768]{2,1,0:T(8,128)(2,1)} collective-permute-done((bf16[4,96,768]{2,1,0:T(8,128)(2,1)S(1)}, bf16[4,96,768]{2,1,0:T(8,128)(2,1)}, u32[]{:S(2)}, u32[]{:S(2)}) %collective-permute-start.18) | collective-permute-done | bytes 589856 | tf_op jit(solution)/shard_map/ppermute | solution.py:682
  172.7 3.2 %shard_map.235 = (f32[768,768]{1,0:T(8,128)}, f32[768,768]{1,0:T(8,128)}, f32[768,768]{1,0:T(8,128)}, f32[768,768]{1,0:T(8,128)}) custom-call(s32[1]{0:T(128)} %bitcast.9.refs_0_, s32[1]{0:T(128)} %bitcast.refs_0_.refs_1_, ...), custom_call_target="tpu_custom_call", output_to_operand_aliasing={{0}: (4, {}), {1}: (5, {}), {2}: (6, {}), {3}: (7, {})} | custom-call | tf_op jit(solution)/shard_map/pallas_call | solution.py:104
  (66 shorter events, 39.9 us)
Async XLA Ops:
  0.6 18.4 %collective-permute-start.3 = (bf16[192,512]{1,0:T(8,128)(2,1)}, bf16[192,512]{1,0:T(8,128)(2,1)}, u32[]{:S(2)}, u32[]{:S(2)}) collective-permute-start(bf16[192,512]{1,0:T(8,128)(2,1)} %bitcast.20), channel_id=1, source_target_pairs={{0,3},{1,2},{2,1},{3,0},{4,7},{5,6},{6,5},{7,4},{8,11},{9,10},{10,... | collective-permute-start | bytes 589832 | tf_op jit(solution)/shard_map/ppermute | solution.py:682
  5.8 17.0 %collective-permute-start.2 = (bf16[192,512]{1,0:T(8,128)(2,1)}, bf16[192,512]{1,0:T(8,128)(2,1)}, u32[]{:S(2)}, u32[]{:S(2)}) collective-permute-start(bf16[192,512]{1,0:T(8,128)(2,1)} %bitcast.21), channel_id=1, source_target_pairs={{0,2},{1,3},{2,0},{3,1},{4,6},{5,7},{6,4},{7,5},{8,10},{9,11},{10,... | collective-permute-start | bytes 589832 | tf_op jit(solution)/shard_map/ppermute | solution.py:682
  5.8 17.0 %collective-permute-start.1 = (bf16[192,512]{1,0:T(8,128)(2,1)}, bf16[192,512]{1,0:T(8,128)(2,1)}, u32[]{:S(2)}, u32[]{:S(2)}) collective-permute-start(bf16[192,512]{1,0:T(8,128)(2,1)} %bitcast.22), channel_id=1, source_target_pairs={{0,1},{1,0},{2,3},{3,2},{4,5},{5,4},{6,7},{7,6},{8,9},{9,8},{10,11... | collective-permute-start | bytes 589832 | tf_op jit(solution)/shard_map/ppermute | solution.py:682
  10.5 3.1 %collective-permute-start = (bf16[512,384]{1,0:T(8,128)(2,1)}, bf16[512,384]{1,0:T(8,128)(2,1)}, u32[]{:S(2)}, u32[]{:S(2)}) collective-permute-start(bf16[512,384]{1,0:T(8,128)(2,1)} %get-tuple-element.77.refs_2_.refs_5_), channel_id=1, source_target_pairs={{0,4},{4,0},{1,5},{5,1},{2,6},{6,2},{3,7},{7,3},{8,12},{12,8},{9,1... | collective-permute-start | bytes 1179656 | tf_op jit(solution)/shard_map/ppermute | solution.py:678
  51.6 24.9 %all-to-all-start = ((bf16[4,192,512]{2,1,0:T(8,128)(2,1)}), bf16[4,192,512]{2,1,0:T(8,128)(2,1)}, u32[]{:S(2)}, u32[]{:S(2)}) async-start(bf16[4,192,512]{2,1,0:T(8,128)(2,1)} %get-tuple-element.91), calls=%async_computation | async-start | bytes 1572864 | tf_op jit(solution)/shard_map/all_to_all | solution.py:798
  63.6 3.4 %collective-permute-start.7 = (bf16[4,96,768]{2,1,0:T(8,128)(2,1)}, bf16[4,96,768]{2,1,0:T(8,128)(2,1)S(1)}, u32[]{:S(2)}, u32[]{:S(2)}) collective-permute-start(bf16[4,96,768]{2,1,0:T(8,128)(2,1)} %get-tuple-element.106), channel_id=1, source_target_pairs={{0,4},{4,0},{1,5},{5,1},{2,6},{6,2},{3,7},{7,3},{8,12},{12,8},{9,1... | collective-permute-start | bytes 1769480 | tf_op jit(solution)/shard_map/ppermute | solution.py:678
  71.1 26.4 %collective-permute-start.8 = (bf16[3,96,768]{2,1,0:T(8,128)(2,1)}, bf16[3,96,768]{2,1,0:T(8,128)(2,1)}, u32[]{:S(2)}, u32[]{:S(2)}) collective-permute-start(bf16[3,96,768]{2,1,0:T(8,128)(2,1)} %get-tuple-element.107), channel_id=1, source_target_pairs={{0,8},{8,0},{16,24},{24,16},{1,9},{9,1},{17,25},{25,17},{2,10},{10... | collective-permute-start | bytes 1327112 | tf_op jit(solution)/shard_map/ppermute | solution.py:682
  72.7 24.9 %collective-permute-start.9 = (bf16[3,96,768]{2,1,0:T(8,128)(2,1)}, bf16[3,96,768]{2,1,0:T(8,128)(2,1)}, u32[]{:S(2)}, u32[]{:S(2)}) collective-permute-start(bf16[3,96,768]{2,1,0:T(8,128)(2,1)} %get-tuple-element.108), channel_id=1, source_target_pairs={{0,16},{8,24},{16,0},{24,8},{1,17},{9,25},{17,1},{25,9},{2,18},{10... | collective-permute-start | bytes 1327112 | tf_op jit(solution)/shard_map/ppermute | solution.py:682
  74.2 23.4 %collective-permute-start.10 = (bf16[3,96,768]{2,1,0:T(8,128)(2,1)}, bf16[3,96,768]{2,1,0:T(8,128)(2,1)}, u32[]{:S(2)}, u32[]{:S(2)}) collective-permute-start(bf16[3,96,768]{2,1,0:T(8,128)(2,1)} %get-tuple-element.109), channel_id=1, source_target_pairs={{0,24},{8,16},{16,8},{24,0},{1,25},{9,17},{17,9},{25,1},{2,26},{10... | collective-permute-start | bytes 1327112 | tf_op jit(solution)/shard_map/ppermute | solution.py:682
  76.5 38.3 %all-to-all-start.1 = ((bf16[4,768,128]{2,1,0:T(8,128)(2,1)}), bf16[4,768,128]{2,1,0:T(8,128)(2,1)}, u32[]{:S(2)}, u32[]{:S(2)}) async-start(bf16[4,768,128]{2,1,0:T(8,128)(2,1)} %get-tuple-element.92), calls=%async_computation.1 | async-start | bytes 1572864 | tf_op jit(solution)/shard_map/all_to_all | solution.py:820
  86.6 3.3 %collective-permute-start.4 = (bf16[512,384]{1,0:T(8,128)(2,1)}, bf16[512,384]{1,0:T(8,128)(2,1)S(1)}, u32[]{:S(2)}, u32[]{:S(2)}) collective-permute-start(bf16[512,384]{1,0:T(8,128)(2,1)} %get-tuple-element.100), channel_id=1, source_target_pairs={{0,4},{4,0},{1,5},{5,1},{2,6},{6,2},{3,7},{7,3},{8,12},{12,8},{9,1... | collective-permute-start | bytes 1179656 | tf_op jit(solution)/shard_map/ppermute | solution.py:678
  102.7 11.0 %collective-permute-start.14 = (bf16[1,96,640]{2,1,0:T(8,128)(2,1)S(1)}, bf16[1,96,640]{2,1,0:T(8,128)(2,1)S(1)}, u32[]{:S(2)}, u32[]{:S(2)}) collective-permute-start(bf16[1,96,640]{2,1,0:T(8,128)(2,1)S(1)} %get-tuple-element.114), channel_id=1, source_target_pairs={{0,24},{8,16},{16,8},{24,0},{1,25},{9,17},{17,9},{25,1},{2,26},{10... | collective-permute-start | bytes 368648 | tf_op jit(solution)/shard_map/ppermute | solution.py:682
  108.7 8.6 %collective-permute-start.15 = (bf16[48,384]{1,0:T(8,128)(2,1)}, bf16[48,384]{1,0:T(8,128)(2,1)}, u32[]{:S(2)}, u32[]{:S(2)}) collective-permute-start(bf16[48,384]{1,0:T(8,128)(2,1)} %get-tuple-element.118), channel_id=1, source_target_pairs={{0,1},{1,0},{2,3},{3,2},{4,5},{5,4},{6,7},{7,6},{8,9},{9,8},{10,11... | collective-permute-start | bytes 110600 | tf_op jit(solution)/shard_map/ppermute | solution.py:682
  110.3 7.0 %collective-permute-start.16 = (bf16[48,384]{1,0:T(8,128)(2,1)}, bf16[48,384]{1,0:T(8,128)(2,1)}, u32[]{:S(2)}, u32[]{:S(2)}) collective-permute-start(bf16[48,384]{1,0:T(8,128)(2,1)} %get-tuple-element.119), channel_id=1, source_target_pairs={{0,2},{1,3},{2,0},{3,1},{4,6},{5,7},{6,4},{7,5},{8,10},{9,11},{10,... | collective-permute-start | bytes 110600 | tf_op jit(solution)/shard_map/ppermute | solution.py:682
  112.6 6.1 %collective-permute-start.17 = (bf16[48,384]{1,0:T(8,128)(2,1)}, bf16[48,384]{1,0:T(8,128)(2,1)}, u32[]{:S(2)}, u32[]{:S(2)}) collective-permute-start(bf16[48,384]{1,0:T(8,128)(2,1)} %get-tuple-element.120), channel_id=1, source_target_pairs={{0,3},{1,2},{2,1},{3,0},{4,7},{5,6},{6,5},{7,4},{8,11},{9,10},{10,... | collective-permute-start | bytes 110600 | tf_op jit(solution)/shard_map/ppermute | solution.py:682
  113.2 5.5 %collective-permute-start.12 = (bf16[1,96,640]{2,1,0:T(8,128)(2,1)}, bf16[1,96,640]{2,1,0:T(8,128)(2,1)}, u32[]{:S(2)}, u32[]{:S(2)}) collective-permute-start(bf16[1,96,640]{2,1,0:T(8,128)(2,1)} %get-tuple-element.112), channel_id=1, source_target_pairs={{0,8},{8,0},{16,24},{24,16},{1,9},{9,1},{17,25},{25,17},{2,10},{10... | collective-permute-start | bytes 368648 | tf_op jit(solution)/shard_map/ppermute | solution.py:682
  114.3 5.2 %collective-permute-start.13 = (bf16[1,96,640]{2,1,0:T(8,128)(2,1)}, bf16[1,96,640]{2,1,0:T(8,128)(2,1)}, u32[]{:S(2)}, u32[]{:S(2)}) collective-permute-start(bf16[1,96,640]{2,1,0:T(8,128)(2,1)} %get-tuple-element.113), channel_id=1, source_target_pairs={{0,16},{8,24},{16,0},{24,8},{1,17},{9,25},{17,1},{25,9},{2,18},{10... | collective-permute-start | bytes 368648 | tf_op jit(solution)/shard_map/ppermute | solution.py:682
  119.5 22.5 %all-to-all-start.2 = ((bf16[4,192,768]{2,1,0:T(8,128)(2,1)}), bf16[4,192,768]{2,1,0:T(8,128)(2,1)S(1)}, u32[]{:S(2)}, u32[]{:S(2)}) async-start(bf16[4,192,768]{2,1,0:T(8,128)(2,1)} %get-tuple-element.122), calls=%async_computation.2 | async-start | bytes 2359296 | tf_op jit(solution)/shard_map/all_to_all | solution.py:902
  142.0 11.1 %collective-permute-start.20 = (bf16[4,96,768]{2,1,0:T(8,128)(2,1)S(1)}, bf16[4,96,768]{2,1,0:T(8,128)(2,1)}, u32[]{:S(2)}, u32[]{:S(2)}) collective-permute-start(bf16[4,96,768]{2,1,0:T(8,128)(2,1)S(1)} %slice.17.refs_2_), channel_id=1, source_target_pairs={{0,16},{8,24},{16,0},{24,8},{1,17},{9,25},{17,1},{25,9},{2,18},{10... | collective-permute-start | bytes 1769480 | tf_op jit(solution)/shard_map/ppermute | solution.py:682
  143.7 10.0 %collective-permute-start.19 = (bf16[4,96,768]{2,1,0:T(8,128)(2,1)S(1)}, bf16[4,96,768]{2,1,0:T(8,128)(2,1)}, u32[]{:S(2)}, u32[]{:S(2)}) collective-permute-start(bf16[4,96,768]{2,1,0:T(8,128)(2,1)S(1)} %slice.17.refs_2_), channel_id=1, source_target_pairs={{0,8},{8,0},{16,24},{24,16},{1,9},{9,1},{17,25},{25,17},{2,10},{10... | collective-permute-start | bytes 1769480 | tf_op jit(solution)/shard_map/ppermute | solution.py:682
  145.2 15.4 %collective-permute-start.24 = (bf16[4,192,768]{2,1,0:T(8,128)(2,1)S(1)}, bf16[4,192,768]{2,1,0:T(8,128)(2,1)}, u32[]{:S(2)}, u32[]{:S(2)}) collective-permute-start(bf16[4,192,768]{2,1,0:T(8,128)(2,1)S(1)} %all-to-all-done.2.refs_1_), channel_id=1, source_target_pairs={{0,4},{4,0},{1,5},{5,1},{2,6},{6,2},{3,7},{7,3},{8,12},{12,8},{9,1... | collective-permute-start | bytes 3538952 | tf_op jit(solution)/shard_map/ppermute | solution.py:678
  145.2 25.3 %all-to-all-start.3 = ((bf16[4,768,128]{2,1,0:T(8,128)(2,1)}), bf16[4,768,128]{2,1,0:T(8,128)(2,1)S(1)}, u32[]{:S(2)}, u32[]{:S(2)}) async-start(bf16[4,768,128]{2,1,0:T(8,128)(2,1)} %get-tuple-element.124), calls=%async_computation.3 | async-start | bytes 1572864 | tf_op jit(solution)/shard_map/all_to_all | solution.py:904
  149.4 6.0 %collective-permute-start.21 = (bf16[4,96,768]{2,1,0:T(8,128)(2,1)S(1)}, bf16[4,96,768]{2,1,0:T(8,128)(2,1)S(1)}, u32[]{:S(2)}, u32[]{:S(2)}) collective-permute-start(bf16[4,96,768]{2,1,0:T(8,128)(2,1)S(1)} %slice.17.refs_2_), channel_id=1, source_target_pairs={{0,4},{4,0},{1,5},{5,1},{2,6},{6,2},{3,7},{7,3},{8,12},{12,8},{9,1... | collective-permute-start | bytes 1769480 | tf_op jit(solution)/shard_map/ppermute | solution.py:678
  153.8 16.7 %collective-permute-start.18 = (bf16[4,96,768]{2,1,0:T(8,128)(2,1)S(1)}, bf16[4,96,768]{2,1,0:T(8,128)(2,1)}, u32[]{:S(2)}, u32[]{:S(2)}) collective-permute-start(bf16[4,96,768]{2,1,0:T(8,128)(2,1)S(1)} %slice.17.refs_2_), channel_id=1, source_target_pairs={{0,24},{8,16},{16,8},{24,0},{1,25},{9,17},{17,9},{25,1},{2,26},{10... | collective-permute-start | bytes 1769480 | tf_op jit(solution)/shard_map/ppermute | solution.py:682
  (11 other events, 24.1 us)

commit v4 on v3

--- a/solution.py
+++ b/solution.py
@@ -134,9 +134,31 @@
     )
 
 
-def project_kernel(parts, scalars, ins, outs, scratch):
-    x, gain, bias, *weights = ins
-    normed, q, kv, own = outs
+def make_features(heads, part, docs, feats):
+    _, length, _ = feats.inside.shape
+    position = lax.broadcasted_iota(jnp.int32, (1, length), 1)
+    feature = lax.broadcasted_iota(jnp.int32, (FEATS, length), 0)
+    for h in range(heads):
+        head = part * heads + h
+        hit = None
+        base = 0
+        for size, dilation in zip(segment_parts, dilations, strict=True):
+            seg_width = length * size // 16
+            inside = lax.rem(
+                lax.rem(position, seg_width) + dilation - lax.rem(head, dilation), dilation
+            )
+            key = base + lax.div(position, seg_width) * DOCS + docs
+            key = jnp.where(inside == 0, key, -1)
+            found = feature == key
+            hit = found if hit is None else hit | found
+            base += DOCS * (16 // size)
+        feats.inside[h] = jnp.where(hit, 1.0, 0.0).T.astype(bf16)
+        feats.send(h)
+
+
+def project_kernel(parts, pair, scalars, ins, outs, scratch):
+    x, docs, gain, bias, *weights = ins[:7]
+    normed, q, kv, own, feats = outs[:5]
     width = D // parts
     where = scalars[0]
     own.inside[:, 3 * width :] = jnp.zeros((D, D - 3 * width), bf16)
@@ -168,6 +190,19 @@
         kv.inside[rows, :] = made[:, width:]
     kv.send()
     q.send()
+    if pair:
+        x_far = ins[7].get()
+
+        @pl.when(scalars[1][0] > 0)
+        def _():
+            for start in range(0, span, TILE):
+                rows = slice(start, start + TILE)
+                hat, _ = normalise(x_far[rows, :].astype(f32))
+                low = (hat * gain + bias).astype(bf16)
+                outs[5].inside[rows, :] = dot(low, own.inside[:, width : 3 * width]).astype(bf16)
+
+        outs[5].send()
+    make_features(feats.inside.shape[0], where[0], docs.get()[...], feats)
 
 
 def head_mask(heads, width):
@@ -257,6 +292,15 @@
         lse[h : h + 1, start : start + TILE] = tops[at : at + 1, :] + jnp.log(total)
     for one in outs:
         one.send()
+
+
+def count_rows(f_rows, f_tile, low_from):
+    counts = dot_nt(f_rows, f_tile)
+    if low_from is not None:
+        at_k = lax.broadcasted_iota(jnp.int32, counts.shape, 0)
+        at_q = lax.broadcasted_iota(jnp.int32, counts.shape, 1) + low_from
+        counts = jnp.where(at_k <= at_q, counts, 0.0)
+    return counts
 
 
 def attention_back_kernel(heads, span, scalars, ins, outs, scratch):
@@ -281,18 +325,16 @@
         dots[h : h + 1, :] = jnp.sum(product[h * HDIM : (h + 1) * HDIM], axis=0, keepdims=True)
     own_start = pl.multiple_of(mine * span, span)
 
-    def block(h, start, size, f_rows, low_from):
+    def block(h, start, size, rows, diagonal):
         tile = slice(start, start + TILE)
-        counts = dot_nt(f_rows, feats[h, pl.ds(own_start + start, TILE), :])
-        if low_from is not None:
-            at_k = lax.broadcasted_iota(jnp.int32, counts.shape, 0)
-            at_q = lax.broadcasted_iota(jnp.int32, counts.shape, 1) + low_from
-            counts = jnp.where(at_k <= at_q, counts, 0.0)
+        columns = slice(h * span + start, h * span + start + TILE)
+        f_rows = feats[h, pl.ds(own_start, size) if diagonal else rows, :]
+        f_tile = feats[h, pl.ds(own_start + start, TILE), :]
+        counts = count_rows(f_rows, f_tile, start if diagonal else None)
         scores = jnp.where(counts > 0, dot_nt(k[:size, :], q_head[h, tile, :]), masked_low)
         prob = counts * jnp.exp(scores - lse[h : h + 1, tile])
         grad_prob = dot_nt(v[:size, :], g_head[h, tile, :])
         slope = prob * (grad_prob - dots[h : h + 1, tile])
-        columns = slice(h * span + start, h * span + start + TILE)
         probs[:size, columns] = prob.astype(bf16)
         slopes[:size, columns] = slope.astype(bf16)
         if size < span:
@@ -314,7 +356,7 @@
     for start in range(0, span, TILE):
         for h in range(heads):
             size = start + TILE
-            block(h, start, size, feats[h, pl.ds(own_start, size), :], start)
+            block(h, start, size, None, True)
     grad_k_rows, grad_v_rows, terms = finish()
     grad_kv[:, :width] = grad_k_rows
     grad_kv[:, width:] = grad_v_rows
@@ -328,7 +370,7 @@
         v[...] = kv_far[rows, width:]
         for start in range(0, span, TILE):
             for h in range(heads):
-                block(h, start, span, feats[h, rows, :], None)
+                block(h, start, span, rows, False)
         grad_k_rows, grad_v_rows, terms = finish()
         grad_far[rows, :width] = grad_k_rows.astype(bf16)
         grad_far[rows, width:] = grad_v_rows.astype(bf16)
@@ -362,8 +404,8 @@
     bias = bias.get()[...].reshape(1, D)
     gain_sum = jnp.zeros((1, D), f32)
     bias_sum = jnp.zeros((1, D), f32)
-    for start in range(0, span, TILE):
-        rows = slice(start, start + TILE)
+    for start in range(0, span, span):
+        rows = slice(start, start + span)
         resid = x.inside[rows, :].astype(f32) + dot_tn(mixed_t[:, rows], w_out.inside[...])
         resids.inside[rows, :] = resid.astype(bf16)
         hat, scale = normalise(resid)
@@ -393,7 +435,7 @@
         grad_low = grad_resid.astype(bf16)
         branch.inside[rows, :] = grad_low
         for one in (act, low, gh, resids, branch):
-            one.send(pl.ds(start, TILE))
+            one.send(pl.ds(start, span))
         for part in range(parts):
             gm.inside[part, :, rows] = dot_nt(
                 w_out.inside[part * width : (part + 1) * width, :], grad_low
@@ -594,7 +636,7 @@
 
 
 def finish_kernel(scalars, ins, outs, scratch):
-    grad_in, vectors = outs
+    grad_in, *vectors = outs
     (small,) = scratch
     size = ins[1].outside.shape[1] - 16
     ins[1].start(source=ins[1].outside.at[:, pl.ds(size, 16), :], target=small)
@@ -608,8 +650,9 @@
     sums = small[0].astype(f32)
     for at in range(1, small.shape[0]):
         sums = sums + small[at].astype(f32)
-    vectors.inside[...] = sums[:4]
-    vectors.send()
+    for at, vector in enumerate(vectors):
+        vector.inside[...] = sums[at]
+        vector.send()
 
 
 def spread_kernel(steps, scalars, ins, outs, scratch):
@@ -680,30 +723,6 @@
 
 def trade(value, axis, step):
     return lax.ppermute(value, axis, [(a, a ^ step) for a in range(lax.axis_size(axis))])
-
-
-def features_kernel(heads, scalars, ins, outs, scratch):
-    docs = ins[0].get()[...]
-    feats = outs[0].inside
-    _, length, _ = feats.shape
-    position = lax.broadcasted_iota(jnp.int32, (1, length), 1)
-    feature = lax.broadcasted_iota(jnp.int32, (FEATS, length), 0)
-    for h in range(heads):
-        head = scalars[0][0] * heads + h
-        hit = None
-        base = 0
-        for part, dilation in zip(segment_parts, dilations, strict=True):
-            seg_width = length * part // 16
-            inside = lax.rem(
-                lax.rem(position, seg_width) + dilation - lax.rem(head, dilation), dilation
-            )
-            key = base + lax.div(position, seg_width) * DOCS + docs
-            key = jnp.where(inside == 0, key, -1)
-            found = feature == key
-            hit = found if hit is None else hit | found
-            base += DOCS * (16 // part)
-        feats[h] = jnp.where(hit, 1.0, 0.0).T.astype(bf16)
-        outs[0].send(h)
 
 
 def shape(*dims, kind=bf16):
@@ -744,26 +763,27 @@
 
     c_own = cotangent[0].T
     c_parts = [c_own] + [trade(c_own, "pat", s) for s in range(1, parts)]
-    (feats,) = staged_call(
-        functools.partial(features_kernel, heads),
-        [part_here],
-        [doc_ids],
-        (shape(heads, doc_ids.shape[1], FEATS),),
-        flops=1 << 42,
-    )
-
     def window(scalars):
         return scalars[0][0] * width // 128 * 128
 
-    normed, q, kv, own = staged_call(
-        functools.partial(project_kernel, parts),
-        [part_here],
-        [x, ln1_gain, ln1_bias, w_query, w_key, w_value],
-        (shape(span, D), shape(span, width), shape(span, 2 * width), shape(D, D)),
-        windows={3: window, 4: window, 5: window},
-    )
-
-    kv_far = swap(kv) if pair else lax.all_gather(kv, "seq", axis=0, tiled=True)
+    far_shapes = (shape(span, 2 * width),) if pair else ()
+    normed, q, kv, own, feats, *far = staged_call(
+        functools.partial(project_kernel, parts, pair),
+        [part_here, here],
+        [x, doc_ids, ln1_gain, ln1_bias, w_query, w_key, w_value] + ([swap(x)] if pair else []),
+        (
+            shape(span, D),
+            shape(span, width),
+            shape(span, 2 * width),
+            shape(D, D),
+            shape(heads, doc_ids.shape[1], FEATS),
+            *far_shapes,
+        ),
+        windows={4: window, 5: window, 6: window},
+        flops=1 << 42,
+    )
+
+    kv_far = far[0] if pair else lax.all_gather(kv, "seq", axis=0, tiled=True)
     far_rows = kv_far.shape[0]
 
     mixed, mixed_t, lse = staged_call(
@@ -883,7 +903,7 @@
         send, *_ = lax.optimization_barrier((send, *wide_parts[1:]))
         ordered = staged_call(
             add_kernel, [row_here], [keep, swap(send)], (shape(1, size, lanes),) * rows_count,
-            limit=SMALL_LIMIT,
+            limit=65000 << 10,
         )
         received = [ordered[0]] + [trade(ordered[s], "row", s) for s in range(1, rows_count)]
         received[3], _ = lax.optimization_barrier((received[3], out_t))
@@ -912,18 +932,19 @@
             bare=range(2),
         )
         own = gathered[:, :size]
-        near = [own] + [trade(own, "row", s) for s in range(1, rows_count)]
+        near1, near2 = trade(own, "row", 1), trade(own, "row", 2)
+        far = (trade(near1[: parts // 2], "row", 2), trade(near2[parts // 2 :], "row", 1))
         grads = spread(
             row_here,
             here,
-            [(s, 0, (near[s],)) for s in range(rows_count - 1)]
-            + [(s, 1, (swap(near[s]),)) for s in range(rows_count - 1)],
-        )
-        far, *_ = lax.optimization_barrier((near[-1], grads[0], grad_up))
+            [(0, 0, (own,)), (1, 0, (near1,)), (2, 0, (near2,))]
+            + [(0, 1, (swap(own),)), (1, 1, (swap(near1),)), (2, 1, (swap(near2),))],
+        )
+        sent = lax.optimization_barrier((*far, grads[0], grad_up))[:2]
         grads = spread(
             row_here,
             here,
-            [(rows_count - 1, 0, (near[-1],)), (rows_count - 1, 1, (swap(far),))],
+            [(3, 0, far), (3, 1, tuple(swap(value) for value in sent))],
             grads,
         )
     else:
@@ -942,11 +963,11 @@
             .reshape(D, D)
             for at in range(3)
         ] + [grad_out]
-    grad_in, vectors = staged_call(
+    grad_in, *vectors = staged_call(
         finish_kernel,
         [],
         [back_parts, gathered if pair else small],
-        (shape(quarter, D), shape(4, D, kind=f32)),
+        (shape(quarter, D),) + (shape(D, kind=f32),) * 4,
         scratch=[pltpu.VMEM((parts, 16, D), bf16)],
         limit=SMALL_LIMIT,
         late=1,

time: 177 us -> 175 us (0.989)
  waiting for transfers between devices: 24.8 us -> 21.1 us
  starting transfers between devices: 41.7 us -> 43.5 us
    ppermute x15 -> x16, waiting for transfers between devices: 15.6 us -> 11.7 us  [trade(): lax.ppermute(value, axis, [(a, a ^ step) for a in range(lax.axis_size(axi...]
    all_to_all x1, waiting for transfers between devices: 0.01 us -> 2.68 us  [per_device(): back_parts = lax.all_to_all(back, 'pat', 0, 0, tiled=True)]
    all_to_all x1, waiting for transfers between devices: 1.8 us -> 0.01 us  [per_device(): gm_parts = lax.all_to_all(gm, 'pat', 0, 0, tiled=True)]
    pallas_call x16 -> x15, Pallas kernels: 67.7 us -> 66.2 us  [staged_call(): pl.pallas_call(kernel, out_shape=tuple(outs), in_specs=[pl.BlockSpec(memo...]
    ppermute x11 -> x12, starting transfers between devices: 3.18 us -> 4.27 us  [swap(): return lax.ppermute(value, 'seq', [(0, 1), (1, 0)])]
    ppermute x11 -> x12, waiting for transfers between devices: 7.4 us -> 6.72 us  [swap(): return lax.ppermute(value, 'seq', [(0, 1), (1, 0)])]
    ppermute x15 -> x16, starting transfers between devices: 22.2 us -> 22.3 us  [trade(): lax.ppermute(value, axis, [(a, a ^ step) for a in range(lax.axis_size(axi...]
    unnamed x10 -> x12, local copies, waits for them, and re-layouts: 3.9 us -> 3.78 us
  transfers between devices with their start and end apart: 30 -> 32, of which waited for: 14 -> 11; matrix products, arithmetic and copies ran while one was open for 0% -> 1% of each run, Pallas kernels for 31% -> 31%
where the time goes in v4:
time: 175 us; the launch traced here: 174 us
  Pallas kernels  66.2 us (38%)
  starting transfers between devices  43.5 us (25%)
  blocking collectives  36.6 us (21%)
  waiting for transfers between devices  21.1 us (12%)
  local copies, waits for them, and re-layouts  5.78 us (3%)
    pallas_call x15, Pallas kernels, staged_call(): pl.pallas_call(kernel, out_shape=tuple(outs), in_specs=[pl.BlockSpec(memo...  66.2 us
    ppermute x16, starting transfers between devices, trade(): lax.ppermute(value, axis, [(a, a ^ step) for a in range(lax.axis_size(axi...  22.3 us
    all_gather x1, blocking collectives, per_device(): mixed4 = lax.all_gather(mixed, 'pat')  19.5 us
    all_gather x1, blocking collectives, per_device(): gathered = lax.all_gather(mine, 'pat')  17.1 us
    ppermute x16, waiting for transfers between devices, trade(): lax.ppermute(value, axis, [(a, a ^ step) for a in range(lax.axis_size(axi...  11.7 us
    ppermute x12, waiting for transfers between devices, swap(): return lax.ppermute(value, 'seq', [(0, 1), (1, 0)])  6.72 us
    all_to_all x1, starting transfers between devices, per_device(): ffn_parts = lax.all_to_all(ffn, 'pat', 0, 0, tiled=True)  5.04 us
    ppermute x12, starting transfers between devices, swap(): return lax.ppermute(value, 'seq', [(0, 1), (1, 0)])  4.27 us
  transfers between devices with their start and end apart: 32, of which 11 were waited for; matrix products, arithmetic and copies ran while one was open for 1% of the time, Pallas kernels for 31%

profile of v4, /device:TPU:0, one launch (start us, length us, event | category | flops | bytes accessed | tf_op | source)
XLA Modules:
  0.0 174.4 jit_solution(2993799221576910710)
XLA Ops:
  1.2 4.7 %collective-permute-start.3 = (bf16[192,512]{1,0:T(8,128)(2,1)}, bf16[192,512]{1,0:T(8,128)(2,1)}, u32[]{:S(2)}, u32[]{:S(2)}) collective-permute-start(bf16[192,512]{1,0:T(8,128)(2,1)} %bitcast.21), channel_id=1, source_target_pairs={{0,3},{1,2},{2,1},{3,0},{4,7},{5,6},{6,5},{7,4},{8,11},{9,10},{10,... | collective-permute-start | bytes 589832 | tf_op jit(solution)/shard_map/ppermute | solution.py:725
  7.4 5.0 %shard_map.220 = (bf16[512,768]{1,0:T(8,128)(2,1)}, bf16[512,192]{1,0:T(8,128)(2,1)}, bf16[512,384]{1,0:T(8,128)(2,1)}, bf16[768,768]{1,0:T(8,128)(2,1)}, bf16[3...) custom-call(s32[1]{0:T(128)} %bitcast.1.refs_0_, s32[1]{0:T(128)} %bitcast.refs_1_.refs_0_, bf16[512,768]{1,0:T(8,128)(2,1)} %bitcast.18, ...), custom_call_target="tpu_custom_call" | custom-call | flops 4398046511104 | tf_op jit(solution)/shard_map/pallas_call | solution.py:104
  12.4 5.5 %shard_map.221 = (bf16[192,512]{1,0:T(8,128)(2,1)}, f32[192,512]{1,0:T(8,128)}, f32[8,512]{1,0:T(8,128)}) custom-call(s32[1]{0:T(128)} %bitcast.refs_1_.refs_0_, bf16[512,192]{1,0:T(8,128)(2,1)} %get-tuple-element.82.refs_1_.refs_2_, bf16[512,384]{1,0:T(8,128)(2,1)} %get-tuple-element.83.refs_2_.refs_5_, ...), custom_call_target="tpu_custom_call" | custom-call | tf_op jit(solution)/shard_map/pallas_call | solution.py:104
  17.9 5.6 %collective-permute-done.2.refs_10_ = bf16[192,512]{1,0:T(8,128)(2,1)} collective-permute-done((bf16[192,512]{1,0:T(8,128)(2,1)}, bf16[192,512]{1,0:T(8,128)(2,1)}, u32[]{:S(2)}, u32[]{:S(2)}) %collective-permute-start.2) | collective-permute-done | bytes 196640 | tf_op jit(solution)/shard_map/ppermute | solution.py:725
  23.5 19.5 %all-gather = bf16[768,512]{1,0:T(8,128)(2,1)} all-gather(bf16[192,512]{1,0:T(8,128)(2,1)} %get-tuple-element.87), channel_id=2, replica_groups=mesh['row'=4,'seq'=2,'pat'=4] {'pat'}, dimensions={0}, use_global_device_ids=true | all-gather | bytes 983040 | tf_op jit(solution)/shard_map/all_gather | solution.py:805
  42.9 9.2 %shard_map.222 = (bf16[4,192,512]{2,1,0:T(8,128)(2,1)}, f32[8,768]{1,0:T(8,128)}, bf16[512,768]{1,0:T(8,128)(2,1)}, bf16[512,768]{1,0:T(8,128)(2,1)}, bf16[512,7...) custom-call(s32[1]{0:T(128)} %bitcast.1.refs_0_, ...), custom_call_target="tpu_custom_call" | custom-call | tf_op jit(solution)/shard_map/pallas_call | solution.py:104
  52.2 4.2 %all-to-all-start = ((bf16[4,192,512]{2,1,0:T(8,128)(2,1)}), bf16[4,192,512]{2,1,0:T(8,128)(2,1)}, u32[]{:S(2)}, u32[]{:S(2)}) async-start(bf16[4,192,512]{2,1,0:T(8,128)(2,1)} %get-tuple-element.99), calls=%async_computation | async-start | bytes 1572864 | tf_op jit(solution)/shard_map/all_to_all | solution.py:818
  56.4 7.2 %shard_map.223 = (bf16[4,768,128]{2,1,0:T(8,128)(2,1)}, bf16[3,4,96,768]{3,2,1,0:T(8,128)(2,1)}, bf16[4,96,768]{2,1,0:T(8,128)(2,1)}, bf16[4,96,768]{2,1,0:T(8,128)(2,1)}, bf16[4,96,768]{2,1,0:T(8,128)(2,1)}) custom-call(s32[1]{0:T(128)} %bitcast.refs_1_.refs_0_, bf16[512,768]{1,0:T(8,128)(2,1)} %get-tuple-element.92.refs_1_, ...), custom_call_target="tpu_custom_call" | custom-call | flops 4398046511104 | tf_op jit(solution)/shard_map/pallas_call | solution.py:104
  69.0 2.7 %shard_map.227 = (bf16[3,96,768]{2,1,0:T(8,128)(2,1)S(1)}, bf16[3,96,768]{2,1,0:T(8,128)(2,1)}, bf16[3,96,768]{2,1,0:T(8,128)(2,1)}, bf16[3,96,768]{2,1,0:T(8,128)(2,1)}) custom-call(s32[1]{0:T(128)} %bitcast.9.refs_0_, bf16[3,4,96,768]{3,2,1,0:T(8,128)(2,1)S(1)} %copy-done, bf16[4,96,768]{2,1,0:T(8,128)(2,1)S(1)} %collective-permute-done.5.refs_2_, ...), custom_call_target="tpu_custom_call" | custom-call | tf_op jit(solution)/shard_map/pallas_call | solution.py:104
  75.3 5.0 %all-to-all-start.1 = ((bf16[4,768,128]{2,1,0:T(8,128)(2,1)}), bf16[4,768,128]{2,1,0:T(8,128)(2,1)}, u32[]{:S(2)}, u32[]{:S(2)}) async-start(bf16[4,768,128]{2,1,0:T(8,128)(2,1)} %get-tuple-element.100), calls=%async_computation.1 | async-start | bytes 1572864 | tf_op jit(solution)/shard_map/all_to_all | solution.py:840
  80.3 5.8 %shard_map.225 = (bf16[512,192]{1,0:T(8,128)(2,1)}, f32[512,384]{1,0:T(8,128)}, bf16[512,384]{1,0:T(8,128)(2,1)}) custom-call(s32[1]{0:T(128)} %bitcast.refs_1_.refs_0_, bf16[4,192,512]{2,1,0:T(8,128)(2,1)} %all-to-all-done.refs_1_, bf16[512,192]{1,0:T(8,128)(2,1)} %get-tuple-element.82.refs_1_.refs_2_, f32[192,512]{1,0:T(8,128)} %get-tuple-element.101.refs_3_, ...), custom_call_target="tpu_custom_call" | custom-call | flops 4398046511104 | tf_op jit(solution)/shard_map/pallas_call | solution.py:104
  90.0 6.8 %shard_map.226 = (bf16[4,768,128]{2,1,0:T(8,128)(2,1)}, bf16[1,4,96,640]{3,2,1,0:T(8,128)(2,1)}, bf16[4,96,640]{2,1,0:T(8,128)(2,1)}) custom-call(s32[1]{0:T(128)} %bitcast.refs_1_.refs_0_, bf16[512,192]{1,0:T(8,128)(2,1)} %get-tuple-element.103.refs_1_, bf16[512,768]{1,0:T(8,128)(2,1)} %get-tuple-element.104.refs_2_, ...), custom_call_target="tpu_custom_call" | custom-call | tf_op jit(solution)/shard_map/pallas_call | solution.py:104
  99.1 2.6 %shard_map.228 = (bf16[1,96,640]{2,1,0:T(8,128)(2,1)}, bf16[1,96,640]{2,1,0:T(8,128)(2,1)}, bf16[1,96,640]{2,1,0:T(8,128)(2,1)}, bf16[1,96,640]{2,1,0:T(8,128)(2,1)}) custom-call(s32[1]{0:T(128)} %bitcast.9.refs_0_, bf16[1,4,96,640]{3,2,1,0:T(8,128)(2,1)} %get-tuple-element.109.refs_1_, bf16[4,96,640]{2,1,0:T(8,128)(2,1)} %collective-permute-done.11.refs_2_), custom_call_target="tpu_custom_call" | custom-call | tf_op jit(solution)/shard_map/pallas_call | solution.py:104
  101.7 2.5 %collective-permute-start.14 = (bf16[1,96,640]{2,1,0:T(8,128)(2,1)}, bf16[1,96,640]{2,1,0:T(8,128)(2,1)S(1)}, u32[]{:S(2)}, u32[]{:S(2)}) collective-permute-start(bf16[1,96,640]{2,1,0:T(8,128)(2,1)} %get-tuple-element.122), channel_id=1, source_target_pairs={{0,24},{8,16},{16,8},{24,0},{1,25},{9,17},{17,9},{25,1},{2,26},{10... | collective-permute-start | bytes 368648 | tf_op jit(solution)/shard_map/ppermute | solution.py:725
  104.2 3.4 %shard_map.229 = (bf16[4,192,768]{2,1,0:T(8,128)(2,1)}, bf16[48,384]{1,0:T(8,128)(2,1)S(1)}, bf16[48,384]{1,0:T(8,128)(2,1)}, bf16[48,384]{1,0:T(8,128)(2,1)}, bf16[48,384]{1,0:T(8,128)(2,1)}) custom-call(s32[1]{0:T(128)} %bitcast.1.refs_0_, bf16[3,96,768]{2,1,0:T(8,128)(2,1)S(1)} %get-tuple-element.124.refs_1_, ...), custom_call_target="tpu_custom_call" | custom-call | tf_op jit(solution)/shard_map/pallas_call | solution.py:104
  113.8 2.5 %shard_map.224 = bf16[192,512]{1,0:T(8,128)(2,1)} custom-call(bf16[4,768,128]{2,1,0:T(8,128)(2,1)} %all-to-all-done.1.refs_0_), custom_call_target="tpu_custom_call" | custom-call | flops 4398046511104 | tf_op jit(solution)/shard_map/pallas_call | solution.py:104
  118.5 3.5 %all-to-all-start.2 = ((bf16[4,192,768]{2,1,0:T(8,128)(2,1)}), bf16[4,192,768]{2,1,0:T(8,128)(2,1)S(1)}, u32[]{:S(2)}, u32[]{:S(2)}) async-start(bf16[4,192,768]{2,1,0:T(8,128)(2,1)} %get-tuple-element.130), calls=%async_computation.2 | async-start | bytes 2359296 | tf_op jit(solution)/shard_map/all_to_all | solution.py:922
  124.3 17.1 %all-gather.1 = bf16[448,768]{1,0:T(8,128)(2,1)S(1)} all-gather(bf16[112,768]{1,0:T(8,128)(2,1)S(1)} %shard_map.230), channel_id=3, replica_groups=mesh['row'=4,'seq'=2,'pat'=4] {'pat'}, dimensions={0}, use_global_device_ids=true | all-gather | bytes 860160 | tf_op jit(solution)/shard_map/all_gather | solution.py:918
  145.0 4.1 %all-to-all-start.3 = ((bf16[4,768,128]{2,1,0:T(8,128)(2,1)}), bf16[4,768,128]{2,1,0:T(8,128)(2,1)S(1)}, u32[]{:S(2)}, u32[]{:S(2)}) async-start(bf16[4,768,128]{2,1,0:T(8,128)(2,1)} %get-tuple-element.132), calls=%async_computation.3 | async-start | bytes 1572864 | tf_op jit(solution)/shard_map/all_to_all | solution.py:924
  149.2 3.2 %collective-permute-done.20.refs_4_ = bf16[4,96,768]{2,1,0:T(8,128)(2,1)} collective-permute-done((bf16[4,96,768]{2,1,0:T(8,128)(2,1)S(1)}, bf16[4,96,768]{2,1,0:T(8,128)(2,1)}, u32[]{:S(2)}, u32[]{:S(2)}) %collective-permute-start.20) | collective-permute-done | bytes 589856 | tf_op jit(solution)/shard_map/ppermute | solution.py:725
  157.5 4.4 %shard_map.232 = (f32[768,768]{1,0:T(8,128)}, f32[768,768]{1,0:T(8,128)}, f32[768,768]{1,0:T(8,128)}, f32[768,768]{1,0:T(8,128)}) custom-call(s32[1]{0:T(128)} %bitcast.9.refs_0_, s32[1]{0:T(128)} %bitcast.refs_1_.refs_0_, bf16[4,96,768]{2,1,0:T(8,128)(2,1)S(1)} %slice.9.refs_2_, bf16[4,96,768]{2,1,0:T(8,128)(2,1)} %collective-permute-done.18.refs_3_, ...), custom_call_target="tpu_custom_call" | custom-call | tf_op jit(solution)/shard_map/pallas_call | solution.py:104
  161.9 4.3 %shard_map.233 = (f32[768,768]{1,0:T(8,128)}, f32[768,768]{1,0:T(8,128)}) custom-call(s32[1]{0:T(128)} %bitcast.refs_1_.refs_0_, bf16[4,192,768]{2,1,0:T(8,128)(2,1)S(1)} %all-to-all-done.2.refs_1_, bf16[4,192,768]{2,1,0:T(8,128)(2,1)} %collective-permute-done.25.refs_2_), custom_call_target="tpu_custom_call" | custom-call | tf_op jit(solution)/shard_map/pallas_call | solution.py:104
  166.8 2.7 %all-to-all-done.3.refs_0_ = bf16[4,768,128]{2,1,0:T(8,128)(2,1)S(1)} async-done(((bf16[4,768,128]{2,1,0:T(8,128)(2,1)}), bf16[4,768,128]{2,1,0:T(8,128)(2,1)S(1)}, u32[]{:S(2)}, u32[]{:S(2)}) %all-to-all-start.3) | async-done | bytes 786464 | tf_op jit(solution)/shard_map/all_to_all | solution.py:924
  171.0 3.2 %shard_map.234 = (f32[768,768]{1,0:T(8,128)}, f32[768,768]{1,0:T(8,128)}, f32[768,768]{1,0:T(8,128)}, f32[768,768]{1,0:T(8,128)}) custom-call(s32[1]{0:T(128)} %bitcast.9.refs_0_, s32[1]{0:T(128)} %bitcast.refs_1_.refs_0_, ...), custom_call_target="tpu_custom_call", output_to_operand_aliasing={{0}: (6, {}), {1}: (7, {}), {2}: (8, {}), {3}: (9, {})} | custom-call | tf_op jit(solution)/shard_map/pallas_call | solution.py:104
  (72 shorter events, 38.5 us)
Async XLA Ops:
  0.6 5.8 %collective-permute-start = (bf16[512,768]{1,0:T(8,128)(2,1)}, bf16[512,768]{1,0:T(8,128)(2,1)S(1)}, u32[]{:S(2)}, u32[]{:S(2)}) collective-permute-start(bf16[512,768]{1,0:T(8,128)(2,1)} %bitcast.17), channel_id=1, source_target_pairs={{0,4},{4,0},{1,5},{5,1},{2,6},{6,2},{3,7},{7,3},{8,12},{12,8},{9,1... | collective-permute-start | bytes 2359304 | tf_op jit(solution)/shard_map/ppermute | solution.py:721
  1.2 16.7 %collective-permute-start.3 = (bf16[192,512]{1,0:T(8,128)(2,1)}, bf16[192,512]{1,0:T(8,128)(2,1)}, u32[]{:S(2)}, u32[]{:S(2)}) collective-permute-start(bf16[192,512]{1,0:T(8,128)(2,1)} %bitcast.21), channel_id=1, source_target_pairs={{0,3},{1,2},{2,1},{3,0},{4,7},{5,6},{6,5},{7,4},{8,11},{9,10},{10,... | collective-permute-start | bytes 589832 | tf_op jit(solution)/shard_map/ppermute | solution.py:725
  5.8 17.6 %collective-permute-start.2 = (bf16[192,512]{1,0:T(8,128)(2,1)}, bf16[192,512]{1,0:T(8,128)(2,1)}, u32[]{:S(2)}, u32[]{:S(2)}) collective-permute-start(bf16[192,512]{1,0:T(8,128)(2,1)} %bitcast.22), channel_id=1, source_target_pairs={{0,2},{1,3},{2,0},{3,1},{4,6},{5,7},{6,4},{7,5},{8,10},{9,11},{10,... | collective-permute-start | bytes 589832 | tf_op jit(solution)/shard_map/ppermute | solution.py:725
  5.8 17.6 %collective-permute-start.1 = (bf16[192,512]{1,0:T(8,128)(2,1)}, bf16[192,512]{1,0:T(8,128)(2,1)}, u32[]{:S(2)}, u32[]{:S(2)}) collective-permute-start(bf16[192,512]{1,0:T(8,128)(2,1)} %bitcast.23), channel_id=1, source_target_pairs={{0,1},{1,0},{2,3},{3,2},{4,5},{5,4},{6,7},{7,6},{8,9},{9,8},{10,11... | collective-permute-start | bytes 589832 | tf_op jit(solution)/shard_map/ppermute | solution.py:725
  52.2 23.1 %all-to-all-start = ((bf16[4,192,512]{2,1,0:T(8,128)(2,1)}), bf16[4,192,512]{2,1,0:T(8,128)(2,1)}, u32[]{:S(2)}, u32[]{:S(2)}) async-start(bf16[4,192,512]{2,1,0:T(8,128)(2,1)} %get-tuple-element.99), calls=%async_computation | async-start | bytes 1572864 | tf_op jit(solution)/shard_map/all_to_all | solution.py:818
  71.7 25.1 %collective-permute-start.8 = (bf16[3,96,768]{2,1,0:T(8,128)(2,1)}, bf16[3,96,768]{2,1,0:T(8,128)(2,1)}, u32[]{:S(2)}, u32[]{:S(2)}) collective-permute-start(bf16[3,96,768]{2,1,0:T(8,128)(2,1)} %get-tuple-element.115), channel_id=1, source_target_pairs={{0,8},{8,0},{16,24},{24,16},{1,9},{9,1},{17,25},{25,17},{2,10},{10... | collective-permute-start | bytes 1327112 | tf_op jit(solution)/shard_map/ppermute | solution.py:725
  73.3 23.6 %collective-permute-start.9 = (bf16[3,96,768]{2,1,0:T(8,128)(2,1)}, bf16[3,96,768]{2,1,0:T(8,128)(2,1)}, u32[]{:S(2)}, u32[]{:S(2)}) collective-permute-start(bf16[3,96,768]{2,1,0:T(8,128)(2,1)} %get-tuple-element.116), channel_id=1, source_target_pairs={{0,16},{8,24},{16,0},{24,8},{1,17},{9,25},{17,1},{25,9},{2,18},{10... | collective-permute-start | bytes 1327112 | tf_op jit(solution)/shard_map/ppermute | solution.py:725
  74.8 22.1 %collective-permute-start.10 = (bf16[3,96,768]{2,1,0:T(8,128)(2,1)}, bf16[3,96,768]{2,1,0:T(8,128)(2,1)}, u32[]{:S(2)}, u32[]{:S(2)}) collective-permute-start(bf16[3,96,768]{2,1,0:T(8,128)(2,1)} %get-tuple-element.117), channel_id=1, source_target_pairs={{0,24},{8,16},{16,8},{24,0},{1,25},{9,17},{17,9},{25,1},{2,26},{10... | collective-permute-start | bytes 1327112 | tf_op jit(solution)/shard_map/ppermute | solution.py:725
  75.3 38.5 %all-to-all-start.1 = ((bf16[4,768,128]{2,1,0:T(8,128)(2,1)}), bf16[4,768,128]{2,1,0:T(8,128)(2,1)}, u32[]{:S(2)}, u32[]{:S(2)}) async-start(bf16[4,768,128]{2,1,0:T(8,128)(2,1)} %get-tuple-element.100), calls=%async_computation.1 | async-start | bytes 1572864 | tf_op jit(solution)/shard_map/all_to_all | solution.py:840
  101.7 10.9 %collective-permute-start.14 = (bf16[1,96,640]{2,1,0:T(8,128)(2,1)}, bf16[1,96,640]{2,1,0:T(8,128)(2,1)S(1)}, u32[]{:S(2)}, u32[]{:S(2)}) collective-permute-start(bf16[1,96,640]{2,1,0:T(8,128)(2,1)} %get-tuple-element.122), channel_id=1, source_target_pairs={{0,24},{8,16},{16,8},{24,0},{1,25},{9,17},{17,9},{25,1},{2,26},{10... | collective-permute-start | bytes 368648 | tf_op jit(solution)/shard_map/ppermute | solution.py:725
  107.6 8.7 %collective-permute-start.15 = (bf16[48,384]{1,0:T(8,128)(2,1)}, bf16[48,384]{1,0:T(8,128)(2,1)}, u32[]{:S(2)}, u32[]{:S(2)}) collective-permute-start(bf16[48,384]{1,0:T(8,128)(2,1)} %get-tuple-element.126), channel_id=1, source_target_pairs={{0,1},{1,0},{2,3},{3,2},{4,5},{5,4},{6,7},{7,6},{8,9},{9,8},{10,11... | collective-permute-start | bytes 110600 | tf_op jit(solution)/shard_map/ppermute | solution.py:725
  109.4 6.9 %collective-permute-start.16 = (bf16[48,384]{1,0:T(8,128)(2,1)}, bf16[48,384]{1,0:T(8,128)(2,1)}, u32[]{:S(2)}, u32[]{:S(2)}) collective-permute-start(bf16[48,384]{1,0:T(8,128)(2,1)} %get-tuple-element.127), channel_id=1, source_target_pairs={{0,2},{1,3},{2,0},{3,1},{4,6},{5,7},{6,4},{7,5},{8,10},{9,11},{10,... | collective-permute-start | bytes 110600 | tf_op jit(solution)/shard_map/ppermute | solution.py:725
  111.8 6.1 %collective-permute-start.17 = (bf16[48,384]{1,0:T(8,128)(2,1)}, bf16[48,384]{1,0:T(8,128)(2,1)}, u32[]{:S(2)}, u32[]{:S(2)}) collective-permute-start(bf16[48,384]{1,0:T(8,128)(2,1)} %get-tuple-element.128), channel_id=1, source_target_pairs={{0,3},{1,2},{2,1},{3,0},{4,7},{5,6},{6,5},{7,4},{8,11},{9,10},{10,... | collective-permute-start | bytes 110600 | tf_op jit(solution)/shard_map/ppermute | solution.py:725
  112.1 5.8 %collective-permute-start.12 = (bf16[1,96,640]{2,1,0:T(8,128)(2,1)}, bf16[1,96,640]{2,1,0:T(8,128)(2,1)}, u32[]{:S(2)}, u32[]{:S(2)}) collective-permute-start(bf16[1,96,640]{2,1,0:T(8,128)(2,1)} %get-tuple-element.120), channel_id=1, source_target_pairs={{0,8},{8,0},{16,24},{24,16},{1,9},{9,1},{17,25},{25,17},{2,10},{10... | collective-permute-start | bytes 368648 | tf_op jit(solution)/shard_map/ppermute | solution.py:725
  113.3 5.2 %collective-permute-start.13 = (bf16[1,96,640]{2,1,0:T(8,128)(2,1)}, bf16[1,96,640]{2,1,0:T(8,128)(2,1)}, u32[]{:S(2)}, u32[]{:S(2)}) collective-permute-start(bf16[1,96,640]{2,1,0:T(8,128)(2,1)} %get-tuple-element.121), channel_id=1, source_target_pairs={{0,16},{8,24},{16,0},{24,8},{1,17},{9,25},{17,1},{25,9},{2,18},{10... | collective-permute-start | bytes 368648 | tf_op jit(solution)/shard_map/ppermute | solution.py:725
  118.5 23.0 %all-to-all-start.2 = ((bf16[4,192,768]{2,1,0:T(8,128)(2,1)}), bf16[4,192,768]{2,1,0:T(8,128)(2,1)S(1)}, u32[]{:S(2)}, u32[]{:S(2)}) async-start(bf16[4,192,768]{2,1,0:T(8,128)(2,1)} %get-tuple-element.130), calls=%async_computation.2 | async-start | bytes 2359296 | tf_op jit(solution)/shard_map/all_to_all | solution.py:922
  141.5 10.9 %collective-permute-start.20 = (bf16[4,96,768]{2,1,0:T(8,128)(2,1)S(1)}, bf16[4,96,768]{2,1,0:T(8,128)(2,1)}, u32[]{:S(2)}, u32[]{:S(2)}) collective-permute-start(bf16[4,96,768]{2,1,0:T(8,128)(2,1)S(1)} %slice.9.refs_2_), channel_id=1, source_target_pairs={{0,16},{8,24},{16,0},{24,8},{1,17},{9,25},{17,1},{25,9},{2,18},{10... | collective-permute-start | bytes 1769480 | tf_op jit(solution)/shard_map/ppermute | solution.py:725
  143.1 10.0 %collective-permute-start.18 = (bf16[4,96,768]{2,1,0:T(8,128)(2,1)S(1)}, bf16[4,96,768]{2,1,0:T(8,128)(2,1)}, u32[]{:S(2)}, u32[]{:S(2)}) collective-permute-start(bf16[4,96,768]{2,1,0:T(8,128)(2,1)S(1)} %slice.9.refs_2_), channel_id=1, source_target_pairs={{0,8},{8,0},{16,24},{24,16},{1,9},{9,1},{17,25},{25,17},{2,10},{10... | collective-permute-start | bytes 1769480 | tf_op jit(solution)/shard_map/ppermute | solution.py:725
  144.5 17.4 %collective-permute-start.25 = (bf16[4,192,768]{2,1,0:T(8,128)(2,1)S(1)}, bf16[4,192,768]{2,1,0:T(8,128)(2,1)}, u32[]{:S(2)}, u32[]{:S(2)}) collective-permute-start(bf16[4,192,768]{2,1,0:T(8,128)(2,1)S(1)} %all-to-all-done.2.refs_1_), channel_id=1, source_target_pairs={{0,4},{4,0},{1,5},{5,1},{2,6},{6,2},{3,7},{7,3},{8,12},{12,8},{9,1... | collective-permute-start | bytes 3538952 | tf_op jit(solution)/shard_map/ppermute | solution.py:721
  144.5 12.1 %collective-permute-start.22 = (bf16[4,96,768]{2,1,0:T(8,128)(2,1)S(1)}, bf16[4,96,768]{2,1,0:T(8,128)(2,1)}, u32[]{:S(2)}, u32[]{:S(2)}) collective-permute-start(bf16[4,96,768]{2,1,0:T(8,128)(2,1)S(1)} %slice.9.refs_2_), channel_id=1, source_target_pairs={{0,4},{4,0},{1,5},{5,1},{2,6},{6,2},{3,7},{7,3},{8,12},{12,8},{9,1... | collective-permute-start | bytes 1769480 | tf_op jit(solution)/shard_map/ppermute | solution.py:721
  145.0 24.4 %all-to-all-start.3 = ((bf16[4,768,128]{2,1,0:T(8,128)(2,1)}), bf16[4,768,128]{2,1,0:T(8,128)(2,1)S(1)}, u32[]{:S(2)}, u32[]{:S(2)}) async-start(bf16[4,768,128]{2,1,0:T(8,128)(2,1)} %get-tuple-element.132), calls=%async_computation.3 | async-start | bytes 1572864 | tf_op jit(solution)/shard_map/all_to_all | solution.py:924
  152.4 5.1 %collective-permute-start.24 = (bf16[4,96,768]{2,1,0:T(8,128)(2,1)}, bf16[4,96,768]{2,1,0:T(8,128)(2,1)S(1)}, u32[]{:S(2)}, u32[]{:S(2)}) collective-permute-start(bf16[4,96,768]{2,1,0:T(8,128)(2,1)} %collective-permute-done.20.refs_4_), channel_id=1, source_target_pairs={{0,4},{4,0},{1,5},{5,1},{2,6},{6,2},{3,7},{7,3},{8,12},{12,8},{9,1... | collective-permute-start | bytes 1769480 | tf_op jit(solution)/shard_map/ppermute | solution.py:721
  154.1 12.1 %collective-permute-start.21 = (bf16[2,96,768]{2,1,0:T(8,128)(2,1)S(1)}, bf16[2,96,768]{2,1,0:T(8,128)(2,1)S(1)}, u32[]{:S(2)}, u32[]{:S(2)}) collective-permute-start(bf16[2,96,768]{2,1,0:T(8,128)(2,1)S(1)} %slice.13), channel_id=1, source_target_pairs={{0,8},{8,0},{16,24},{24,16},{1,9},{9,1},{17,25},{25,17},{2,10},{10... | collective-permute-start | bytes 884744 | tf_op jit(solution)/shard_map/ppermute | solution.py:725
  156.6 9.6 %collective-permute-start.19 = (bf16[2,96,768]{2,1,0:T(8,128)(2,1)S(1)}, bf16[2,96,768]{2,1,0:T(8,128)(2,1)}, u32[]{:S(2)}, u32[]{:S(2)}) collective-permute-start(bf16[2,96,768]{2,1,0:T(8,128)(2,1)S(1)} %slice.12), channel_id=1, source_target_pairs={{0,16},{8,24},{16,0},{24,8},{1,17},{9,25},{17,1},{25,9},{2,18},{10... | collective-permute-start | bytes 884744 | tf_op jit(solution)/shard_map/ppermute | solution.py:725
  (14 other events, 43.2 us)

commit v5 on v4

--- a/solution.py
+++ b/solution.py
@@ -508,7 +508,7 @@
 
 
 def row_sum_kernel(parts, scalars, ins, outs, scratch):
-    ffn_own, *out_parts = outs
+    ffn_own, out_parts = outs
     (rows,) = scratch
     total = ins[0].get()[...].astype(f32)
     for one in ins[1:]:
@@ -517,18 +517,11 @@
     size = total.shape[1]
     half = size // 2
     width = D // parts
-    for own in range(parts):
-
-        @pl.when(scalars[0][0] == own)
-        def _():
-            for step, out in enumerate(out_parts):
-                part = own ^ step
-                columns = slice(part * width, (part + 1) * width)
-                out.inside[:, :width] = total[2, :half, columns]
-                out.inside[:, width:] = total[2, half:, columns]
-
-    for one in out_parts[::-1]:
-        one.send()
+    for part in range(parts):
+        columns = slice(part * width, (part + 1) * width)
+        out_parts.inside[part, :, :width] = total[2, :half, columns]
+        out_parts.inside[part, :, width:] = total[2, half:, columns]
+    out_parts.send()
     rows[...] = total[:2].reshape(2 * size, D)
     for row in range(ffn_own.outside.shape[0]):
         ffn_own.put(rows, ffn_own.outside.at[row])
@@ -600,9 +593,9 @@
     width = D // parts
     size = ins[0].inside.shape[1]
     half = size // 2
-    out = ins[count].get()[...].astype(f32)
-    for one in ins[count + 1 :]:
-        out = out + one.get()[...].astype(f32)
+    out = ins[count].get()[0].astype(f32)
+    for part in range(1, parts):
+        out = out + ins[count].inside[part].astype(f32)
     mine[:half, 3 * width :] = out[:, :width].astype(bf16)
     mine[half:size, 3 * width :] = out[:, width:].astype(bf16)
     total = ins[0].get()[0].astype(f32)
@@ -871,16 +864,17 @@
 
     if pair:
         gkv_more = swap(gkv_far)
-        ffn_own, *out_parts = staged_call(
+        ffn_own, out_parts = staged_call(
             functools.partial(row_sum_kernel, parts),
-            [part_here],
+            [],
             wide_parts,
-            (shape(rows_count, 2 * size, D),) + (shape(size // 2, 2 * width),) * parts,
+            (shape(rows_count, 2 * size, D), shape(parts, size // 2, 2 * width)),
             scratch=[pltpu.VMEM((2 * size, D), bf16)],
             limit=SMALL_LIMIT,
             bare=(0,),
         )
-        out_parts = [out_parts[0]] + [trade(out_parts[s], "pat", s) for s in range(1, parts)]
+        out_parts, _ = lax.optimization_barrier((out_parts, ffn_parts))
+        out_parts = lax.all_to_all(out_parts, "pat", 0, 0, tiled=True)
     else:
         gkv_more = lax.psum_scatter(gkv_far, "seq", scatter_dimension=0, tiled=True)
 
@@ -901,6 +895,7 @@
     if pair:
         keep, send = narrow
         send, *_ = lax.optimization_barrier((send, *wide_parts[1:]))
+        keep, _ = lax.optimization_barrier((keep, ffn_own))
         ordered = staged_call(
             add_kernel, [row_here], [keep, swap(send)], (shape(1, size, lanes),) * rows_count,
             limit=65000 << 10,
@@ -910,14 +905,14 @@
         (mine,) = staged_call(
             functools.partial(own_sum_kernel, parts, rows_count),
             [],
-            [*received, *out_parts],
+            [*received, out_parts],
             (shape(size + 16, D),),
             scratch=[pltpu.VMEM((16, D), f32)],
             limit=SMALL_LIMIT,
         )
         gathered = lax.all_gather(mine, "pat")
         ffn_own, *_ = lax.optimization_barrier(
-            (ffn_own, ffn_parts, *received[1:], *out_parts[1:])
+            (ffn_own, out_parts, *received[1:])
         )
         ffn_mine = lax.all_to_all(ffn_own, "row", 0, 0, tiled=True)
         gathered, ffn_mine, back = lax.optimization_barrier((gathered, ffn_mine, back))
@@ -963,6 +958,8 @@
             .reshape(D, D)
             for at in range(3)
         ] + [grad_out]
+    if pair:
+        back_parts, _ = lax.optimization_barrier((back_parts, grads[0]))
     grad_in, *vectors = staged_call(
         finish_kernel,
         [],

time: 175 us -> 172 us (0.983)
    all_to_all x0 -> x1, starting transfers between devices: none -> 4.81 us  [per_device(): out_parts = lax.all_to_all(out_parts, 'pat', 0, 0, tiled=True)]
    ppermute x16 -> x13, starting transfers between devices: 22.3 us -> 18.2 us  [trade(): lax.ppermute(value, axis, [(a, a ^ step) for a in range(lax.axis_size(axi...]
    all_to_all x0 -> x1, waiting for transfers between devices: none -> 3.56 us  [per_device(): out_parts = lax.all_to_all(out_parts, 'pat', 0, 0, tiled=True)]
    all_to_all x1, waiting for transfers between devices: 2.68 us -> 0.01 us  [per_device(): back_parts = lax.all_to_all(back, 'pat', 0, 0, tiled=True)]
    ppermute x16 -> x13, waiting for transfers between devices: 11.7 us -> 9.89 us  [trade(): lax.ppermute(value, axis, [(a, a ^ step) for a in range(lax.axis_size(axi...]
    unnamed x12 -> x8, local copies, waits for them, and re-layouts: 3.78 us -> 3.13 us
  transfers between devices with their start and end apart: 32 -> 30, of which waited for: 11 -> 10; matrix products, arithmetic and copies ran while one was open for 1% -> 1% of each run, Pallas kernels for 31% -> 32%
where the time goes in v5:
time: 172 us
  Pallas kernels  65.3 us (38%)
  starting transfers between devices  44 us (26%)
  blocking collectives  36.1 us (21%)
  waiting for transfers between devices  19.8 us (12%)
  local copies, waits for them, and re-layouts  5.13 us (3%)
    pallas_call x15, Pallas kernels, staged_call(): pl.pallas_call(kernel, out_shape=tuple(outs), in_specs=[pl.BlockSpec(memo...  65.3 us
    all_gather x1, blocking collectives, per_device(): mixed4 = lax.all_gather(mixed, 'pat')  19.5 us
    ppermute x13, starting transfers between devices, trade(): lax.ppermute(value, axis, [(a, a ^ step) for a in range(lax.axis_size(axi...  18.2 us
    all_gather x1, blocking collectives, per_device(): gathered = lax.all_gather(mine, 'pat')  16.7 us
    ppermute x13, waiting for transfers between devices, trade(): lax.ppermute(value, axis, [(a, a ^ step) for a in range(lax.axis_size(axi...  9.89 us
    ppermute x12, waiting for transfers between devices, swap(): return lax.ppermute(value, 'seq', [(0, 1), (1, 0)])  6.38 us
    all_to_all x1, starting transfers between devices, per_device(): ffn_parts = lax.all_to_all(ffn, 'pat', 0, 0, tiled=True)  5.04 us
    all_to_all x1, starting transfers between devices, per_device(): out_parts = lax.all_to_all(out_parts, 'pat', 0, 0, tiled=True)  4.81 us
  transfers between devices with their start and end apart: 30, of which 10 were waited for; matrix products, arithmetic and copies ran while one was open for 1% of the time, Pallas kernels for 32%

profile of v5, /device:TPU:0, one launch (start us, length us, event | category | flops | bytes accessed | tf_op | source)
XLA Modules:
  0.0 171.6 jit_solution(2227192883410414827)
XLA Ops:
  1.2 4.7 %collective-permute-start.3 = (bf16[192,512]{1,0:T(8,128)(2,1)}, bf16[192,512]{1,0:T(8,128)(2,1)}, u32[]{:S(2)}, u32[]{:S(2)}) collective-permute-start(bf16[192,512]{1,0:T(8,128)(2,1)} %bitcast.21), channel_id=1, source_target_pairs={{0,3},{1,2},{2,1},{3,0},{4,7},{5,6},{6,5},{7,4},{8,11},{9,10},{10,... | collective-permute-start | bytes 589832 | tf_op jit(solution)/shard_map/ppermute | solution.py:718
  7.4 5.0 %shard_map.220 = (bf16[512,768]{1,0:T(8,128)(2,1)}, bf16[512,192]{1,0:T(8,128)(2,1)}, bf16[512,384]{1,0:T(8,128)(2,1)}, bf16[768,768]{1,0:T(8,128)(2,1)}, bf16[3...) custom-call(s32[1]{0:T(128)} %bitcast.1.refs_0_, s32[1]{0:T(128)} %bitcast.refs_1_.refs_0_, bf16[512,768]{1,0:T(8,128)(2,1)} %bitcast.18, ...), custom_call_target="tpu_custom_call" | custom-call | flops 4398046511104 | tf_op jit(solution)/shard_map/pallas_call | solution.py:104
  12.4 5.4 %shard_map.221 = (bf16[192,512]{1,0:T(8,128)(2,1)}, f32[192,512]{1,0:T(8,128)}, f32[8,512]{1,0:T(8,128)}) custom-call(s32[1]{0:T(128)} %bitcast.refs_1_.refs_0_, bf16[512,192]{1,0:T(8,128)(2,1)} %get-tuple-element.82.refs_1_.refs_2_, bf16[512,384]{1,0:T(8,128)(2,1)} %get-tuple-element.83.refs_2_.refs_5_, ...), custom_call_target="tpu_custom_call" | custom-call | tf_op jit(solution)/shard_map/pallas_call | solution.py:104
  17.8 5.6 %collective-permute-done.2.refs_10_ = bf16[192,512]{1,0:T(8,128)(2,1)} collective-permute-done((bf16[192,512]{1,0:T(8,128)(2,1)}, bf16[192,512]{1,0:T(8,128)(2,1)}, u32[]{:S(2)}, u32[]{:S(2)}) %collective-permute-start.2) | collective-permute-done | bytes 196640 | tf_op jit(solution)/shard_map/ppermute | solution.py:718
  23.5 19.5 %all-gather = bf16[768,512]{1,0:T(8,128)(2,1)} all-gather(bf16[192,512]{1,0:T(8,128)(2,1)} %get-tuple-element.87), channel_id=2, replica_groups=mesh['row'=4,'seq'=2,'pat'=4] {'pat'}, dimensions={0}, use_global_device_ids=true | all-gather | bytes 983040 | tf_op jit(solution)/shard_map/all_gather | solution.py:798
  42.9 9.2 %shard_map.222 = (bf16[4,192,512]{2,1,0:T(8,128)(2,1)}, f32[8,768]{1,0:T(8,128)}, bf16[512,768]{1,0:T(8,128)(2,1)}, bf16[512,768]{1,0:T(8,128)(2,1)}, bf16[512,7...) custom-call(s32[1]{0:T(128)} %bitcast.1.refs_0_, ...), custom_call_target="tpu_custom_call" | custom-call | tf_op jit(solution)/shard_map/pallas_call | solution.py:104
  52.2 4.2 %all-to-all-start = ((bf16[4,192,512]{2,1,0:T(8,128)(2,1)}), bf16[4,192,512]{2,1,0:T(8,128)(2,1)}, u32[]{:S(2)}, u32[]{:S(2)}) async-start(bf16[4,192,512]{2,1,0:T(8,128)(2,1)} %get-tuple-element.99), calls=%async_computation | async-start | bytes 1572864 | tf_op jit(solution)/shard_map/all_to_all | solution.py:811
  56.4 7.2 %shard_map.223 = (bf16[4,768,128]{2,1,0:T(8,128)(2,1)}, bf16[3,4,96,768]{3,2,1,0:T(8,128)(2,1)}, bf16[4,96,768]{2,1,0:T(8,128)(2,1)}, bf16[4,96,768]{2,1,0:T(8,128)(2,1)}, bf16[4,96,768]{2,1,0:T(8,128)(2,1)}) custom-call(s32[1]{0:T(128)} %bitcast.refs_1_.refs_0_, bf16[512,768]{1,0:T(8,128)(2,1)} %get-tuple-element.92.refs_1_, ...), custom_call_target="tpu_custom_call" | custom-call | flops 4398046511104 | tf_op jit(solution)/shard_map/pallas_call | solution.py:104
  69.0 2.7 %shard_map.227 = (bf16[3,96,768]{2,1,0:T(8,128)(2,1)S(1)}, bf16[3,96,768]{2,1,0:T(8,128)(2,1)}, bf16[3,96,768]{2,1,0:T(8,128)(2,1)}, bf16[3,96,768]{2,1,0:T(8,128)(2,1)}) custom-call(s32[1]{0:T(128)} %bitcast.9.refs_0_, bf16[3,4,96,768]{3,2,1,0:T(8,128)(2,1)S(1)} %copy-done, bf16[4,96,768]{2,1,0:T(8,128)(2,1)S(1)} %collective-permute-done.5.refs_2_, ...), custom_call_target="tpu_custom_call" | custom-call | tf_op jit(solution)/shard_map/pallas_call | solution.py:104
  75.2 5.0 %all-to-all-start.1 = ((bf16[4,768,128]{2,1,0:T(8,128)(2,1)}), bf16[4,768,128]{2,1,0:T(8,128)(2,1)}, u32[]{:S(2)}, u32[]{:S(2)}) async-start(bf16[4,768,128]{2,1,0:T(8,128)(2,1)} %get-tuple-element.100), calls=%async_computation.1 | async-start | bytes 1572864 | tf_op jit(solution)/shard_map/all_to_all | solution.py:833
  80.3 5.8 %shard_map.225 = (bf16[512,192]{1,0:T(8,128)(2,1)}, f32[512,384]{1,0:T(8,128)}, bf16[512,384]{1,0:T(8,128)(2,1)}) custom-call(s32[1]{0:T(128)} %bitcast.refs_1_.refs_0_, bf16[4,192,512]{2,1,0:T(8,128)(2,1)} %all-to-all-done.refs_1_, bf16[512,192]{1,0:T(8,128)(2,1)} %get-tuple-element.82.refs_1_.refs_2_, f32[192,512]{1,0:T(8,128)} %get-tuple-element.101.refs_3_, ...), custom_call_target="tpu_custom_call" | custom-call | flops 4398046511104 | tf_op jit(solution)/shard_map/pallas_call | solution.py:104
  90.0 6.8 %shard_map.226 = (bf16[4,768,128]{2,1,0:T(8,128)(2,1)}, bf16[1,4,96,640]{3,2,1,0:T(8,128)(2,1)}, bf16[4,96,640]{2,1,0:T(8,128)(2,1)}) custom-call(s32[1]{0:T(128)} %bitcast.refs_1_.refs_0_, bf16[512,192]{1,0:T(8,128)(2,1)} %get-tuple-element.103.refs_1_, bf16[512,768]{1,0:T(8,128)(2,1)} %get-tuple-element.104.refs_2_, ...), custom_call_target="tpu_custom_call" | custom-call | tf_op jit(solution)/shard_map/pallas_call | solution.py:104
  97.3 3.3 %shard_map.228 = (bf16[4,192,768]{2,1,0:T(8,128)(2,1)}, bf16[4,48,384]{2,1,0:T(8,128)(2,1)}) custom-call(bf16[3,96,768]{2,1,0:T(8,128)(2,1)S(1)} %get-tuple-element.114.refs_0_, bf16[3,96,768]{2,1,0:T(8,128)(2,1)} %collective-permute-done.8.refs_1_, bf16[3,96,768]{2,1,0:T(8,128)(2,1)} %collective-permute-done.9.refs_2_, ...), custom_call_target="tpu_custom_call" | custom-call | tf_op jit(solution)/shard_map/pallas_call | solution.py:104
  100.6 2.6 %shard_map.229 = (bf16[1,96,640]{2,1,0:T(8,128)(2,1)}, bf16[1,96,640]{2,1,0:T(8,128)(2,1)}, bf16[1,96,640]{2,1,0:T(8,128)(2,1)}, bf16[1,96,640]{2,1,0:T(8,128)(2,1)}) custom-call(s32[1]{0:T(128)} %bitcast.9.refs_0_, bf16[1,4,96,640]{3,2,1,0:T(8,128)(2,1)} %get-tuple-element.119.refs_1_, bf16[4,96,640]{2,1,0:T(8,128)(2,1)} %collective-permute-done.11.refs_2_), custom_call_target="tpu_custom_call" | custom-call | tf_op jit(solution)/shard_map/pallas_call | solution.py:104
  106.7 4.8 %all-to-all-start.2 = ((bf16[4,48,384]{2,1,0:T(8,128)(2,1)}), bf16[4,48,384]{2,1,0:T(8,128)(2,1)}, u32[]{:S(2)}, u32[]{:S(2)}) async-start(bf16[4,48,384]{2,1,0:T(8,128)(2,1)} %get-tuple-element.128), calls=%async_computation.2 | async-start | bytes 294912 | tf_op jit(solution)/shard_map/all_to_all | solution.py:877
  111.5 2.5 %shard_map.224 = bf16[192,512]{1,0:T(8,128)(2,1)} custom-call(bf16[4,768,128]{2,1,0:T(8,128)(2,1)} %all-to-all-done.1.refs_0_), custom_call_target="tpu_custom_call" | custom-call | flops 4398046511104 | tf_op jit(solution)/shard_map/pallas_call | solution.py:104
  114.0 3.6 %all-to-all-done.2.refs_4_ = bf16[4,48,384]{2,1,0:T(8,128)(2,1)} async-done(((bf16[4,48,384]{2,1,0:T(8,128)(2,1)}), bf16[4,48,384]{2,1,0:T(8,128)(2,1)}, u32[]{:S(2)}, u32[]{:S(2)}) %all-to-all-start.2) | async-done | bytes 147488 | tf_op jit(solution)/shard_map/all_to_all | solution.py:877
  117.6 3.7 %all-to-all-start.3 = ((bf16[4,192,768]{2,1,0:T(8,128)(2,1)}), bf16[4,192,768]{2,1,0:T(8,128)(2,1)S(1)}, u32[]{:S(2)}, u32[]{:S(2)}) async-start(bf16[4,192,768]{2,1,0:T(8,128)(2,1)} %get-tuple-element.129), calls=%async_computation.3 | async-start | bytes 2359296 | tf_op jit(solution)/shard_map/all_to_all | solution.py:917
  123.6 16.7 %all-gather.1 = bf16[448,768]{1,0:T(8,128)(2,1)S(1)} all-gather(bf16[112,768]{1,0:T(8,128)(2,1)S(1)} %shard_map.230), channel_id=3, replica_groups=mesh['row'=4,'seq'=2,'pat'=4] {'pat'}, dimensions={0}, use_global_device_ids=true | all-gather | bytes 860160 | tf_op jit(solution)/shard_map/all_gather | solution.py:913
  144.4 3.8 %all-to-all-start.4 = ((bf16[4,768,128]{2,1,0:T(8,128)(2,1)}), bf16[4,768,128]{2,1,0:T(8,128)(2,1)S(1)}, u32[]{:S(2)}, u32[]{:S(2)}) async-start(bf16[4,768,128]{2,1,0:T(8,128)(2,1)} %get-tuple-element.131), calls=%async_computation.4 | async-start | bytes 1572864 | tf_op jit(solution)/shard_map/all_to_all | solution.py:919
  148.2 3.3 %collective-permute-done.17.refs_4_ = bf16[4,96,768]{2,1,0:T(8,128)(2,1)} collective-permute-done((bf16[4,96,768]{2,1,0:T(8,128)(2,1)S(1)}, bf16[4,96,768]{2,1,0:T(8,128)(2,1)}, u32[]{:S(2)}, u32[]{:S(2)}) %collective-permute-start.17) | collective-permute-done | bytes 589856 | tf_op jit(solution)/shard_map/ppermute | solution.py:718
  156.6 4.4 %shard_map.231 = (f32[768,768]{1,0:T(8,128)}, f32[768,768]{1,0:T(8,128)}, f32[768,768]{1,0:T(8,128)}, f32[768,768]{1,0:T(8,128)}) custom-call(s32[1]{0:T(128)} %bitcast.9.refs_0_, s32[1]{0:T(128)} %bitcast.refs_1_.refs_0_, bf16[4,96,768]{2,1,0:T(8,128)(2,1)S(1)} %slice.9.refs_2_, bf16[4,96,768]{2,1,0:T(8,128)(2,1)} %collective-permute-done.15.refs_3_, ...), custom_call_target="tpu_custom_call" | custom-call | tf_op jit(solution)/shard_map/pallas_call | solution.py:104
  161.0 4.3 %shard_map.232 = (f32[768,768]{1,0:T(8,128)}, f32[768,768]{1,0:T(8,128)}) custom-call(s32[1]{0:T(128)} %bitcast.refs_1_.refs_0_, bf16[4,192,768]{2,1,0:T(8,128)(2,1)S(1)} %all-to-all-done.3.refs_1_, bf16[4,192,768]{2,1,0:T(8,128)(2,1)} %collective-permute-done.22.refs_2_), custom_call_target="tpu_custom_call" | custom-call | tf_op jit(solution)/shard_map/pallas_call | solution.py:104
  167.4 2.4 %shard_map.233 = (f32[768,768]{1,0:T(8,128)}, f32[768,768]{1,0:T(8,128)}, f32[768,768]{1,0:T(8,128)}, f32[768,768]{1,0:T(8,128)}) custom-call(s32[1]{0:T(128)} %bitcast.9.refs_0_, s32[1]{0:T(128)} %bitcast.refs_1_.refs_0_, ...), custom_call_target="tpu_custom_call", output_to_operand_aliasing={{0}: (6, {}), {1}: (7, {}), {2}: (8, {}), {3}: (9, {})} | custom-call | tf_op jit(solution)/shard_map/pallas_call | solution.py:104
  (64 shorter events, 34.1 us)
Async XLA Ops:
  0.6 5.8 %collective-permute-start = (bf16[512,768]{1,0:T(8,128)(2,1)}, bf16[512,768]{1,0:T(8,128)(2,1)S(1)}, u32[]{:S(2)}, u32[]{:S(2)}) collective-permute-start(bf16[512,768]{1,0:T(8,128)(2,1)} %bitcast.17), channel_id=1, source_target_pairs={{0,4},{4,0},{1,5},{5,1},{2,6},{6,2},{3,7},{7,3},{8,12},{12,8},{9,1... | collective-permute-start | bytes 2359304 | tf_op jit(solution)/shard_map/ppermute | solution.py:714
  1.2 16.7 %collective-permute-start.3 = (bf16[192,512]{1,0:T(8,128)(2,1)}, bf16[192,512]{1,0:T(8,128)(2,1)}, u32[]{:S(2)}, u32[]{:S(2)}) collective-permute-start(bf16[192,512]{1,0:T(8,128)(2,1)} %bitcast.21), channel_id=1, source_target_pairs={{0,3},{1,2},{2,1},{3,0},{4,7},{5,6},{6,5},{7,4},{8,11},{9,10},{10,... | collective-permute-start | bytes 589832 | tf_op jit(solution)/shard_map/ppermute | solution.py:718
  5.8 17.6 %collective-permute-start.2 = (bf16[192,512]{1,0:T(8,128)(2,1)}, bf16[192,512]{1,0:T(8,128)(2,1)}, u32[]{:S(2)}, u32[]{:S(2)}) collective-permute-start(bf16[192,512]{1,0:T(8,128)(2,1)} %bitcast.22), channel_id=1, source_target_pairs={{0,2},{1,3},{2,0},{3,1},{4,6},{5,7},{6,4},{7,5},{8,10},{9,11},{10,... | collective-permute-start | bytes 589832 | tf_op jit(solution)/shard_map/ppermute | solution.py:718
  5.8 17.6 %collective-permute-start.1 = (bf16[192,512]{1,0:T(8,128)(2,1)}, bf16[192,512]{1,0:T(8,128)(2,1)}, u32[]{:S(2)}, u32[]{:S(2)}) collective-permute-start(bf16[192,512]{1,0:T(8,128)(2,1)} %bitcast.23), channel_id=1, source_target_pairs={{0,1},{1,0},{2,3},{3,2},{4,5},{5,4},{6,7},{7,6},{8,9},{9,8},{10,11... | collective-permute-start | bytes 589832 | tf_op jit(solution)/shard_map/ppermute | solution.py:718
  52.2 23.1 %all-to-all-start = ((bf16[4,192,512]{2,1,0:T(8,128)(2,1)}), bf16[4,192,512]{2,1,0:T(8,128)(2,1)}, u32[]{:S(2)}, u32[]{:S(2)}) async-start(bf16[4,192,512]{2,1,0:T(8,128)(2,1)} %get-tuple-element.99), calls=%async_computation | async-start | bytes 1572864 | tf_op jit(solution)/shard_map/all_to_all | solution.py:811
  71.7 25.1 %collective-permute-start.8 = (bf16[3,96,768]{2,1,0:T(8,128)(2,1)}, bf16[3,96,768]{2,1,0:T(8,128)(2,1)}, u32[]{:S(2)}, u32[]{:S(2)}) collective-permute-start(bf16[3,96,768]{2,1,0:T(8,128)(2,1)} %get-tuple-element.115), channel_id=1, source_target_pairs={{0,8},{8,0},{16,24},{24,16},{1,9},{9,1},{17,25},{25,17},{2,10},{10... | collective-permute-start | bytes 1327112 | tf_op jit(solution)/shard_map/ppermute | solution.py:718
  73.2 23.6 %collective-permute-start.9 = (bf16[3,96,768]{2,1,0:T(8,128)(2,1)}, bf16[3,96,768]{2,1,0:T(8,128)(2,1)}, u32[]{:S(2)}, u32[]{:S(2)}) collective-permute-start(bf16[3,96,768]{2,1,0:T(8,128)(2,1)} %get-tuple-element.116), channel_id=1, source_target_pairs={{0,16},{8,24},{16,0},{24,8},{1,17},{9,25},{17,1},{25,9},{2,18},{10... | collective-permute-start | bytes 1327112 | tf_op jit(solution)/shard_map/ppermute | solution.py:718
  74.8 22.0 %collective-permute-start.10 = (bf16[3,96,768]{2,1,0:T(8,128)(2,1)}, bf16[3,96,768]{2,1,0:T(8,128)(2,1)}, u32[]{:S(2)}, u32[]{:S(2)}) collective-permute-start(bf16[3,96,768]{2,1,0:T(8,128)(2,1)} %get-tuple-element.117), channel_id=1, source_target_pairs={{0,24},{8,16},{16,8},{24,0},{1,25},{9,17},{17,9},{25,1},{2,26},{10... | collective-permute-start | bytes 1327112 | tf_op jit(solution)/shard_map/ppermute | solution.py:718
  75.2 31.4 %all-to-all-start.1 = ((bf16[4,768,128]{2,1,0:T(8,128)(2,1)}), bf16[4,768,128]{2,1,0:T(8,128)(2,1)}, u32[]{:S(2)}, u32[]{:S(2)}) async-start(bf16[4,768,128]{2,1,0:T(8,128)(2,1)} %get-tuple-element.100), calls=%async_computation.1 | async-start | bytes 1572864 | tf_op jit(solution)/shard_map/all_to_all | solution.py:833
  96.8 3.7 %collective-permute-start.11 = (bf16[4,96,640]{2,1,0:T(8,128)(2,1)}, bf16[4,96,640]{2,1,0:T(8,128)(2,1)}, u32[]{:S(2)}, u32[]{:S(2)}) collective-permute-start(bf16[4,96,640]{2,1,0:T(8,128)(2,1)} %get-tuple-element.121), channel_id=1, source_target_pairs={{0,4},{4,0},{1,5},{5,1},{2,6},{6,2},{3,7},{7,3},{8,12},{12,8},{9,1... | collective-permute-start | bytes 1474568 | tf_op jit(solution)/shard_map/ppermute | solution.py:714
  103.1 10.9 %collective-permute-start.12 = (bf16[1,96,640]{2,1,0:T(8,128)(2,1)}, bf16[1,96,640]{2,1,0:T(8,128)(2,1)}, u32[]{:S(2)}, u32[]{:S(2)}) collective-permute-start(bf16[1,96,640]{2,1,0:T(8,128)(2,1)} %get-tuple-element.123), channel_id=1, source_target_pairs={{0,8},{8,0},{16,24},{24,16},{1,9},{9,1},{17,25},{25,17},{2,10},{10... | collective-permute-start | bytes 368648 | tf_op jit(solution)/shard_map/ppermute | solution.py:718
  104.7 9.3 %collective-permute-start.13 = (bf16[1,96,640]{2,1,0:T(8,128)(2,1)}, bf16[1,96,640]{2,1,0:T(8,128)(2,1)}, u32[]{:S(2)}, u32[]{:S(2)}) collective-permute-start(bf16[1,96,640]{2,1,0:T(8,128)(2,1)} %get-tuple-element.124), channel_id=1, source_target_pairs={{0,16},{8,24},{16,0},{24,8},{1,17},{9,25},{17,1},{25,9},{2,18},{10... | collective-permute-start | bytes 368648 | tf_op jit(solution)/shard_map/ppermute | solution.py:718
  106.2 7.8 %collective-permute-start.14 = (bf16[1,96,640]{2,1,0:T(8,128)(2,1)}, bf16[1,96,640]{2,1,0:T(8,128)(2,1)}, u32[]{:S(2)}, u32[]{:S(2)}) collective-permute-start(bf16[1,96,640]{2,1,0:T(8,128)(2,1)} %get-tuple-element.125), channel_id=1, source_target_pairs={{0,24},{8,16},{16,8},{24,0},{1,25},{9,17},{17,9},{25,1},{2,26},{10... | collective-permute-start | bytes 368648 | tf_op jit(solution)/shard_map/ppermute | solution.py:718
  106.7 10.9 %all-to-all-start.2 = ((bf16[4,48,384]{2,1,0:T(8,128)(2,1)}), bf16[4,48,384]{2,1,0:T(8,128)(2,1)}, u32[]{:S(2)}, u32[]{:S(2)}) async-start(bf16[4,48,384]{2,1,0:T(8,128)(2,1)} %get-tuple-element.128), calls=%async_computation.2 | async-start | bytes 294912 | tf_op jit(solution)/shard_map/all_to_all | solution.py:877
  117.6 22.7 %all-to-all-start.3 = ((bf16[4,192,768]{2,1,0:T(8,128)(2,1)}), bf16[4,192,768]{2,1,0:T(8,128)(2,1)S(1)}, u32[]{:S(2)}, u32[]{:S(2)}) async-start(bf16[4,192,768]{2,1,0:T(8,128)(2,1)} %get-tuple-element.129), calls=%async_computation.3 | async-start | bytes 2359296 | tf_op jit(solution)/shard_map/all_to_all | solution.py:917
  140.3 11.1 %collective-permute-start.17 = (bf16[4,96,768]{2,1,0:T(8,128)(2,1)S(1)}, bf16[4,96,768]{2,1,0:T(8,128)(2,1)}, u32[]{:S(2)}, u32[]{:S(2)}) collective-permute-start(bf16[4,96,768]{2,1,0:T(8,128)(2,1)S(1)} %slice.9.refs_2_), channel_id=1, source_target_pairs={{0,16},{8,24},{16,0},{24,8},{1,17},{9,25},{17,1},{25,9},{2,18},{10... | collective-permute-start | bytes 1769480 | tf_op jit(solution)/shard_map/ppermute | solution.py:718
  142.4 10.0 %collective-permute-start.15 = (bf16[4,96,768]{2,1,0:T(8,128)(2,1)S(1)}, bf16[4,96,768]{2,1,0:T(8,128)(2,1)}, u32[]{:S(2)}, u32[]{:S(2)}) collective-permute-start(bf16[4,96,768]{2,1,0:T(8,128)(2,1)S(1)} %slice.9.refs_2_), channel_id=1, source_target_pairs={{0,8},{8,0},{16,24},{24,16},{1,9},{9,1},{17,25},{25,17},{2,10},{10... | collective-permute-start | bytes 1769480 | tf_op jit(solution)/shard_map/ppermute | solution.py:718
  143.9 17.1 %collective-permute-start.22 = (bf16[4,192,768]{2,1,0:T(8,128)(2,1)S(1)}, bf16[4,192,768]{2,1,0:T(8,128)(2,1)}, u32[]{:S(2)}, u32[]{:S(2)}) collective-permute-start(bf16[4,192,768]{2,1,0:T(8,128)(2,1)S(1)} %all-to-all-done.3.refs_1_), channel_id=1, source_target_pairs={{0,4},{4,0},{1,5},{5,1},{2,6},{6,2},{3,7},{7,3},{8,12},{12,8},{9,1... | collective-permute-start | bytes 3538952 | tf_op jit(solution)/shard_map/ppermute | solution.py:714
  143.9 12.0 %collective-permute-start.19 = (bf16[4,96,768]{2,1,0:T(8,128)(2,1)S(1)}, bf16[4,96,768]{2,1,0:T(8,128)(2,1)}, u32[]{:S(2)}, u32[]{:S(2)}) collective-permute-start(bf16[4,96,768]{2,1,0:T(8,128)(2,1)S(1)} %slice.9.refs_2_), channel_id=1, source_target_pairs={{0,4},{4,0},{1,5},{5,1},{2,6},{6,2},{3,7},{7,3},{8,12},{12,8},{9,1... | collective-permute-start | bytes 1769480 | tf_op jit(solution)/shard_map/ppermute | solution.py:714
  144.4 25.4 %all-to-all-start.4 = ((bf16[4,768,128]{2,1,0:T(8,128)(2,1)}), bf16[4,768,128]{2,1,0:T(8,128)(2,1)S(1)}, u32[]{:S(2)}, u32[]{:S(2)}) async-start(bf16[4,768,128]{2,1,0:T(8,128)(2,1)} %get-tuple-element.131), calls=%async_computation.4 | async-start | bytes 1572864 | tf_op jit(solution)/shard_map/all_to_all | solution.py:919
  151.4 5.1 %collective-permute-start.21 = (bf16[4,96,768]{2,1,0:T(8,128)(2,1)}, bf16[4,96,768]{2,1,0:T(8,128)(2,1)S(1)}, u32[]{:S(2)}, u32[]{:S(2)}) collective-permute-start(bf16[4,96,768]{2,1,0:T(8,128)(2,1)} %collective-permute-done.17.refs_4_), channel_id=1, source_target_pairs={{0,4},{4,0},{1,5},{5,1},{2,6},{6,2},{3,7},{7,3},{8,12},{12,8},{9,1... | collective-permute-start | bytes 1769480 | tf_op jit(solution)/shard_map/ppermute | solution.py:714
  152.4 4.2 %collective-permute-start.20 = (bf16[4,96,768]{2,1,0:T(8,128)(2,1)}, bf16[4,96,768]{2,1,0:T(8,128)(2,1)S(1)}, u32[]{:S(2)}, u32[]{:S(2)}) collective-permute-start(bf16[4,96,768]{2,1,0:T(8,128)(2,1)} %collective-permute-done.15.refs_3_), channel_id=1, source_target_pairs={{0,4},{4,0},{1,5},{5,1},{2,6},{6,2},{3,7},{7,3},{8,12},{12,8},{9,1... | collective-permute-start | bytes 1769480 | tf_op jit(solution)/shard_map/ppermute | solution.py:714
  153.4 11.9 %collective-permute-start.18 = (bf16[2,96,768]{2,1,0:T(8,128)(2,1)S(1)}, bf16[2,96,768]{2,1,0:T(8,128)(2,1)S(1)}, u32[]{:S(2)}, u32[]{:S(2)}) collective-permute-start(bf16[2,96,768]{2,1,0:T(8,128)(2,1)S(1)} %slice.13), channel_id=1, source_target_pairs={{0,8},{8,0},{16,24},{24,16},{1,9},{9,1},{17,25},{25,17},{2,10},{10... | collective-permute-start | bytes 884744 | tf_op jit(solution)/shard_map/ppermute | solution.py:718
  155.9 9.4 %collective-permute-start.16 = (bf16[2,96,768]{2,1,0:T(8,128)(2,1)S(1)}, bf16[2,96,768]{2,1,0:T(8,128)(2,1)S(1)}, u32[]{:S(2)}, u32[]{:S(2)}) collective-permute-start(bf16[2,96,768]{2,1,0:T(8,128)(2,1)S(1)} %slice.12), channel_id=1, source_target_pairs={{0,16},{8,24},{16,0},{24,8},{1,17},{9,25},{17,1},{25,9},{2,18},{10... | collective-permute-start | bytes 884744 | tf_op jit(solution)/shard_map/ppermute | solution.py:718
  (10 other events, 26.0 us)

commit v6 on v5

--- a/solution.py
+++ b/solution.py
@@ -440,9 +440,9 @@
             gm.inside[part, :, rows] = dot_nt(
                 w_out.inside[part * width : (part + 1) * width, :], grad_low
             ).astype(bf16)
+            gm.send(part)
     sums.inside[0:1, :] = gain_sum
     sums.inside[1:2, :] = bias_sum
-    gm.send()
     sums.send()
 
 
@@ -531,19 +531,32 @@
 
 
 def last_kernel(parts, pair, scalars, ins, outs, scratch):
-    gq, normed, gkv, own, x, gain, gr, sums, gkv_more = ins
+    gq, gkv, gkv_more, normed, own, x, gain, gr, sums = ins
     back, *narrow = outs
     grads, small, made = scratch
     width = D // parts
     span = x.inside.shape[0]
     piece = span // parts
     lanes = 3 * width + SLOT
+    grads[:, 3 * width :] = jnp.zeros((span, D - 3 * width), bf16)
     grads[:, :width] = gq.get()[...]
-    grads[:, 3 * width :] = jnp.zeros((span, D - 3 * width), bf16)
     gkv.get(), gkv_more.get()
     grads[:, width : 3 * width] = (
         gkv.inside[...] + gkv_more.inside[...].astype(f32)
     ).astype(bf16)
+    made[...] = dot_tn(normed.get()[...], grads[:, :lanes]).astype(bf16)
+    if pair:
+        rows_count, size, _ = narrow[1].inside.shape
+        halves = (
+            (narrow[0].inside.at[0], scalars[0][0]),
+            (narrow[1].inside, 1 - scalars[0][0]),
+        )
+        for row in range(rows_count):
+            for out, half in halves:
+                start = pl.multiple_of((2 * row + half) * size, size)
+                out[row] = made[pl.ds(start, size), :]
+    else:
+        narrow[0].inside[...] = made[...]
     own.get(), x.get(), gr.get(), sums.get()
     gain = gain.get()[...].reshape(1, D)
     gain_sum = jnp.zeros((1, D), f32)
@@ -558,6 +571,7 @@
         turned = grad_in.astype(bf16).T
         for at in range(start, start + TILE, piece):
             back.inside[at // piece] = turned[:, at - start : at - start + piece]
+            back.send(at // piece)
     pieces = D // SLOT
     for at, row in enumerate(
         (gain_sum, bias_sum, sums.inside[0:1, :], sums.inside[1:2, :])
@@ -566,25 +580,16 @@
             small[at * pieces + part : at * pieces + part + 1, :] = row[
                 :, part * SLOT : (part + 1) * SLOT
             ]
-    made[...] = dot_tn(normed.get()[...], grads[:, :lanes]).astype(bf16)
     tail = small[...].astype(bf16)
     if pair:
-        rows_count, size, _ = narrow[1].inside.shape
         for row in range(rows_count):
-            for out, half in (
-                (narrow[0].inside.at[0], scalars[0][0]),
-                (narrow[1].inside, 1 - scalars[0][0]),
-            ):
-                start = pl.multiple_of((2 * row + half) * size, size)
-                out[row] = made[pl.ds(start, size), :]
+            for out, _ in halves:
                 out[row, :48, 3 * width :] = tail
         narrow[1].send()
         narrow[0].send()
     else:
-        narrow[0].inside[...] = made[...]
         narrow[0].inside[:48, 3 * width :] = tail
         narrow[0].send()
-    back.send()
 
 
 def own_sum_kernel(parts, count, scalars, ins, outs, scratch):
@@ -701,6 +706,11 @@
                 place = buffer.at[grad, half * got.shape[0] + row]
                 place[...] = got[row, grad * size : (grad + 1) * size, :].astype(f32)
                 out.put(place, out.outside.at[pl.ds(start, size), :])
+
+
+def first_spread_kernel(steps, scalars, ins, outs, scratch):
+    spread_ffn_kernel(scalars[1:], ins[:2], outs[:2], scratch[:1])
+    spread_kernel(steps, scalars, ins[2:], outs[2:], scratch[1:])
 
 
 def broadcast_exchange(value, axis):
@@ -883,7 +893,7 @@
     back, *narrow = staged_call(
         functools.partial(last_kernel, parts, pair),
         [here],
-        [gq, normed, gkv, own, x, ln1_gain, branch, sums, gkv_more],
+        [gq, gkv, gkv_more, normed, own, x, ln1_gain, branch, sums],
         (shape(parts, parts * width, quarter), *narrow_shapes),
         scratch=[
             pltpu.VMEM((span, D), bf16),
@@ -917,25 +927,35 @@
         ffn_mine = lax.all_to_all(ffn_own, "row", 0, 0, tiled=True)
         gathered, ffn_mine, back = lax.optimization_barrier((gathered, ffn_mine, back))
         back_parts = lax.all_to_all(back, "pat", 0, 0, tiled=True)
-        grad_down, grad_up = staged_call(
-            spread_ffn_kernel,
-            [here],
-            [ffn_mine, swap(ffn_mine)],
-            (shape(D, D, kind=f32),) * 2,
-            scratch=[pltpu.VMEM((2, 2 * rows_count, size, D), f32)],
-            limit=SMALL_LIMIT,
-            bare=range(2),
-        )
         own = gathered[:, :size]
         near1, near2 = trade(own, "row", 1), trade(own, "row", 2)
-        far = (trade(near1[: parts // 2], "row", 2), trade(near2[parts // 2 :], "row", 1))
-        grads = spread(
-            row_here,
-            here,
-            [(0, 0, (own,)), (1, 0, (near1,)), (2, 0, (near2,))]
-            + [(0, 1, (swap(own),)), (1, 1, (swap(near1),)), (2, 1, (swap(near2),))],
-        )
-        sent = lax.optimization_barrier((*far, grads[0], grad_up))[:2]
+        half1, half2 = near1[: parts // 2], near2[parts // 2 :]
+        far = (trade(half1, "row", 2), trade(half2, "row", 1))
+        sent1, _ = lax.optimization_barrier((near1, half1))
+        sent2, _ = lax.optimization_barrier((near2, half2))
+        steps = [(0, 0, 1), (1, 0, 1), (2, 0, 1), (0, 1, 1), (1, 1, 1), (2, 1, 1)]
+        grad_down, grad_up, *grads = staged_call(
+            functools.partial(first_spread_kernel, steps),
+            [row_here, here],
+            [
+                ffn_mine,
+                swap(ffn_mine),
+                own,
+                near1,
+                near2,
+                swap(own),
+                swap(sent1),
+                swap(sent2),
+            ],
+            (shape(D, D, kind=f32),) * 6,
+            scratch=[
+                pltpu.VMEM((2, 2 * rows_count, size, D), f32),
+                pltpu.VMEM((4, len(steps), size, D), f32),
+            ],
+            limit=24 << 20,
+            bare=range(6),
+        )
+        sent = lax.optimization_barrier((*far, grads[0]))[:2]
         grads = spread(
             row_here,
             here,

time: 172 us -> 170 us (0.988)
  Pallas kernels: 65.3 us -> 61.2 us
    pallas_call x15 -> x14, Pallas kernels: 65.3 us -> 61.2 us  [staged_call(): pl.pallas_call(kernel, out_shape=tuple(outs), in_specs=[pl.BlockSpec(memo...]
  transfers between devices with their start and end apart: 30 -> 30, of which waited for: 10 -> 11; matrix products, arithmetic and copies ran while one was open for 1% -> 1% of each run, Pallas kernels for 32% -> 30%
where the time goes in v6:
time: 170 us; the launch traced here: 169 us
  Pallas kernels  61.2 us (36%)
  starting transfers between devices  44.9 us (26%)
  blocking collectives  36.1 us (21%)
  waiting for transfers between devices  20.7 us (12%)
  local copies, waits for them, and re-layouts  5.12 us (3%)
    pallas_call x14, Pallas kernels, staged_call(): pl.pallas_call(kernel, out_shape=tuple(outs), in_specs=[pl.BlockSpec(memo...  61.2 us
    all_gather x1, blocking collectives, per_device(): mixed4 = lax.all_gather(mixed, 'pat')  19.5 us
    ppermute x13, starting transfers between devices, trade(): lax.ppermute(value, axis, [(a, a ^ step) for a in range(lax.axis_size(axi...  18.5 us
    all_gather x1, blocking collectives, per_device(): gathered = lax.all_gather(mine, 'pat')  16.7 us
    ppermute x13, waiting for transfers between devices, trade(): lax.ppermute(value, axis, [(a, a ^ step) for a in range(lax.axis_size(axi...  10.7 us
    ppermute x12, waiting for transfers between devices, swap(): return lax.ppermute(value, 'seq', [(0, 1), (1, 0)])  6.38 us
    all_to_all x1, starting transfers between devices, per_device(): ffn_parts = lax.all_to_all(ffn, 'pat', 0, 0, tiled=True)  5.04 us
    ppermute x12, starting transfers between devices, swap(): return lax.ppermute(value, 'seq', [(0, 1), (1, 0)])  4.84 us
  transfers between devices with their start and end apart: 30, of which 11 were waited for; matrix products, arithmetic and copies ran while one was open for 1% of the time, Pallas kernels for 30%

profile of v6, /device:TPU:0, one launch (start us, length us, event | category | flops | bytes accessed | tf_op | source)
XLA Modules:
  0.0 169.1 jit_solution(5076071151525708093)
XLA Ops:
  1.2 4.7 %collective-permute-start.3 = (bf16[192,512]{1,0:T(8,128)(2,1)}, bf16[192,512]{1,0:T(8,128)(2,1)}, u32[]{:S(2)}, u32[]{:S(2)}) collective-permute-start(bf16[192,512]{1,0:T(8,128)(2,1)} %bitcast.21), channel_id=1, source_target_pairs={{0,3},{1,2},{2,1},{3,0},{4,7},{5,6},{6,5},{7,4},{8,11},{9,10},{10,... | collective-permute-start | bytes 589832 | tf_op jit(solution)/shard_map/ppermute | solution.py:728
  7.4 5.0 %shard_map.220 = (bf16[512,768]{1,0:T(8,128)(2,1)}, bf16[512,192]{1,0:T(8,128)(2,1)}, bf16[512,384]{1,0:T(8,128)(2,1)}, bf16[768,768]{1,0:T(8,128)(2,1)}, bf16[3...) custom-call(s32[1]{0:T(128)} %bitcast.1.refs_0_, s32[1]{0:T(128)} %bitcast.refs_1_.refs_0_, bf16[512,768]{1,0:T(8,128)(2,1)} %bitcast.18, ...), custom_call_target="tpu_custom_call" | custom-call | flops 4398046511104 | tf_op jit(solution)/shard_map/pallas_call | solution.py:104
  12.4 5.4 %shard_map.221 = (bf16[192,512]{1,0:T(8,128)(2,1)}, f32[192,512]{1,0:T(8,128)}, f32[8,512]{1,0:T(8,128)}) custom-call(s32[1]{0:T(128)} %bitcast.refs_1_.refs_0_, bf16[512,192]{1,0:T(8,128)(2,1)} %get-tuple-element.84.refs_1_.refs_2_, bf16[512,384]{1,0:T(8,128)(2,1)} %get-tuple-element.85.refs_2_.refs_5_, ...), custom_call_target="tpu_custom_call" | custom-call | tf_op jit(solution)/shard_map/pallas_call | solution.py:104
  17.8 5.6 %collective-permute-done.2.refs_10_ = bf16[192,512]{1,0:T(8,128)(2,1)} collective-permute-done((bf16[192,512]{1,0:T(8,128)(2,1)}, bf16[192,512]{1,0:T(8,128)(2,1)}, u32[]{:S(2)}, u32[]{:S(2)}) %collective-permute-start.2) | collective-permute-done | bytes 196640 | tf_op jit(solution)/shard_map/ppermute | solution.py:728
  23.5 19.5 %all-gather = bf16[768,512]{1,0:T(8,128)(2,1)} all-gather(bf16[192,512]{1,0:T(8,128)(2,1)} %get-tuple-element.89), channel_id=2, replica_groups=mesh['row'=4,'seq'=2,'pat'=4] {'pat'}, dimensions={0}, use_global_device_ids=true | all-gather | bytes 983040 | tf_op jit(solution)/shard_map/all_gather | solution.py:808
  42.9 9.0 %shard_map.222 = (bf16[4,192,512]{2,1,0:T(8,128)(2,1)}, f32[8,768]{1,0:T(8,128)}, bf16[512,768]{1,0:T(8,128)(2,1)}, bf16[512,768]{1,0:T(8,128)(2,1)}, bf16[512,7...) custom-call(s32[1]{0:T(128)} %bitcast.1.refs_0_, ...), custom_call_target="tpu_custom_call" | custom-call | tf_op jit(solution)/shard_map/pallas_call | solution.py:104
  52.0 4.2 %all-to-all-start = ((bf16[4,192,512]{2,1,0:T(8,128)(2,1)}), bf16[4,192,512]{2,1,0:T(8,128)(2,1)}, u32[]{:S(2)}, u32[]{:S(2)}) async-start(bf16[4,192,512]{2,1,0:T(8,128)(2,1)} %get-tuple-element.101), calls=%async_computation | async-start | bytes 1572864 | tf_op jit(solution)/shard_map/all_to_all | solution.py:821
  56.2 7.2 %shard_map.223 = (bf16[4,768,128]{2,1,0:T(8,128)(2,1)}, bf16[3,4,96,768]{3,2,1,0:T(8,128)(2,1)}, bf16[4,96,768]{2,1,0:T(8,128)(2,1)}, bf16[4,96,768]{2,1,0:T(8,128)(2,1)}, bf16[4,96,768]{2,1,0:T(8,128)(2,1)}) custom-call(s32[1]{0:T(128)} %bitcast.refs_1_.refs_0_, bf16[512,768]{1,0:T(8,128)(2,1)} %get-tuple-element.94.refs_1_, ...), custom_call_target="tpu_custom_call" | custom-call | flops 4398046511104 | tf_op jit(solution)/shard_map/pallas_call | solution.py:104
  68.8 2.7 %shard_map.227 = (bf16[3,96,768]{2,1,0:T(8,128)(2,1)S(1)}, bf16[3,96,768]{2,1,0:T(8,128)(2,1)}, bf16[3,96,768]{2,1,0:T(8,128)(2,1)}, bf16[3,96,768]{2,1,0:T(8,128)(2,1)}) custom-call(s32[1]{0:T(128)} %bitcast.9.refs_0_, bf16[3,4,96,768]{3,2,1,0:T(8,128)(2,1)S(1)} %copy-done, bf16[4,96,768]{2,1,0:T(8,128)(2,1)S(1)} %collective-permute-done.5.refs_2_, ...), custom_call_target="tpu_custom_call" | custom-call | tf_op jit(solution)/shard_map/pallas_call | solution.py:104
  75.0 5.0 %all-to-all-start.1 = ((bf16[4,768,128]{2,1,0:T(8,128)(2,1)}), bf16[4,768,128]{2,1,0:T(8,128)(2,1)}, u32[]{:S(2)}, u32[]{:S(2)}) async-start(bf16[4,768,128]{2,1,0:T(8,128)(2,1)} %get-tuple-element.102), calls=%async_computation.1 | async-start | bytes 1572864 | tf_op jit(solution)/shard_map/all_to_all | solution.py:843
  80.1 5.7 %shard_map.225 = (bf16[512,192]{1,0:T(8,128)(2,1)}, f32[512,384]{1,0:T(8,128)}, bf16[512,384]{1,0:T(8,128)(2,1)}) custom-call(s32[1]{0:T(128)} %bitcast.refs_1_.refs_0_, bf16[4,192,512]{2,1,0:T(8,128)(2,1)} %all-to-all-done.refs_1_, bf16[512,192]{1,0:T(8,128)(2,1)} %get-tuple-element.84.refs_1_.refs_2_, f32[192,512]{1,0:T(8,128)} %get-tuple-element.103.refs_3_, ...), custom_call_target="tpu_custom_call" | custom-call | flops 4398046511104 | tf_op jit(solution)/shard_map/pallas_call | solution.py:104
  89.7 5.8 %shard_map.226 = (bf16[4,768,128]{2,1,0:T(8,128)(2,1)}, bf16[1,4,96,640]{3,2,1,0:T(8,128)(2,1)}, bf16[4,96,640]{2,1,0:T(8,128)(2,1)}) custom-call(s32[1]{0:T(128)} %bitcast.refs_1_.refs_0_, bf16[512,192]{1,0:T(8,128)(2,1)} %get-tuple-element.105.refs_1_, f32[512,384]{1,0:T(8,128)} %get-tuple-element.106.refs_2_, bf16[512,384]{1,0:T(8,128)(2,1)} %copy-done.2, ...), custom_call_target="tpu_custom_call" | custom-call | tf_op jit(solution)/shard_map/pallas_call | solution.py:104
  96.1 3.3 %shard_map.228 = (bf16[4,192,768]{2,1,0:T(8,128)(2,1)}, bf16[4,48,384]{2,1,0:T(8,128)(2,1)}) custom-call(bf16[3,96,768]{2,1,0:T(8,128)(2,1)S(1)} %get-tuple-element.116.refs_0_, bf16[3,96,768]{2,1,0:T(8,128)(2,1)} %collective-permute-done.8.refs_1_, bf16[3,96,768]{2,1,0:T(8,128)(2,1)} %collective-permute-done.9.refs_2_, ...), custom_call_target="tpu_custom_call" | custom-call | tf_op jit(solution)/shard_map/pallas_call | solution.py:104
  99.4 2.6 %shard_map.229 = (bf16[1,96,640]{2,1,0:T(8,128)(2,1)}, bf16[1,96,640]{2,1,0:T(8,128)(2,1)}, bf16[1,96,640]{2,1,0:T(8,128)(2,1)}, bf16[1,96,640]{2,1,0:T(8,128)(2,1)}) custom-call(s32[1]{0:T(128)} %bitcast.9.refs_0_, bf16[1,4,96,640]{3,2,1,0:T(8,128)(2,1)} %get-tuple-element.121.refs_1_, bf16[4,96,640]{2,1,0:T(8,128)(2,1)} %collective-permute-done.11.refs_2_), custom_call_target="tpu_custom_call" | custom-call | tf_op jit(solution)/shard_map/pallas_call | solution.py:104
  105.5 4.8 %all-to-all-start.2 = ((bf16[4,48,384]{2,1,0:T(8,128)(2,1)}), bf16[4,48,384]{2,1,0:T(8,128)(2,1)}, u32[]{:S(2)}, u32[]{:S(2)}) async-start(bf16[4,48,384]{2,1,0:T(8,128)(2,1)} %get-tuple-element.130), calls=%async_computation.2 | async-start | bytes 294912 | tf_op jit(solution)/shard_map/all_to_all | solution.py:887
  110.3 2.5 %shard_map.224 = bf16[192,512]{1,0:T(8,128)(2,1)} custom-call(bf16[4,768,128]{2,1,0:T(8,128)(2,1)} %all-to-all-done.1.refs_0_), custom_call_target="tpu_custom_call" | custom-call | flops 4398046511104 | tf_op jit(solution)/shard_map/pallas_call | solution.py:104
  112.8 3.6 %all-to-all-done.2.refs_4_ = bf16[4,48,384]{2,1,0:T(8,128)(2,1)} async-done(((bf16[4,48,384]{2,1,0:T(8,128)(2,1)}), bf16[4,48,384]{2,1,0:T(8,128)(2,1)}, u32[]{:S(2)}, u32[]{:S(2)}) %all-to-all-start.2) | async-done | bytes 147488 | tf_op jit(solution)/shard_map/all_to_all | solution.py:887
  116.4 3.7 %all-to-all-start.3 = ((bf16[4,192,768]{2,1,0:T(8,128)(2,1)}), bf16[4,192,768]{2,1,0:T(8,128)(2,1)S(1)}, u32[]{:S(2)}, u32[]{:S(2)}) async-start(bf16[4,192,768]{2,1,0:T(8,128)(2,1)} %get-tuple-element.131), calls=%async_computation.3 | async-start | bytes 2359296 | tf_op jit(solution)/shard_map/all_to_all | solution.py:927
  120.1 2.3 %shard_map.230 = bf16[112,768]{1,0:T(8,128)(2,1)S(1)} custom-call(bf16[1,96,640]{2,1,0:T(8,128)(2,1)S(1)} %copy-done.1, bf16[1,96,640]{2,1,0:T(8,128)(2,1)} %collective-permute-done.12.refs_1_, bf16[1,96,640]{2,1,0:T(8,128)(2,1)} %collective-permute-done.13.refs_2_, bf16[1,96,640]{2,1,0:T(8,128)(2,1)} %collective-permute-done.14.refs_3_, ...), custom_call_target="tpu_custom_call" | custom-call | tf_op jit(solution)/shard_map/pallas_call | solution.py:104
  122.4 16.7 %all-gather.1 = bf16[448,768]{1,0:T(8,128)(2,1)S(1)} all-gather(bf16[112,768]{1,0:T(8,128)(2,1)S(1)} %shard_map.230), channel_id=3, replica_groups=mesh['row'=4,'seq'=2,'pat'=4] {'pat'}, dimensions={0}, use_global_device_ids=true | all-gather | bytes 860160 | tf_op jit(solution)/shard_map/all_gather | solution.py:923
  143.2 3.8 %all-to-all-start.4 = ((bf16[4,768,128]{2,1,0:T(8,128)(2,1)}), bf16[4,768,128]{2,1,0:T(8,128)(2,1)S(1)}, u32[]{:S(2)}, u32[]{:S(2)}) async-start(bf16[4,768,128]{2,1,0:T(8,128)(2,1)} %get-tuple-element.133), calls=%async_computation.4 | async-start | bytes 1572864 | tf_op jit(solution)/shard_map/all_to_all | solution.py:929
  147.0 3.3 %collective-permute-done.17.refs_6_ = bf16[4,96,768]{2,1,0:T(8,128)(2,1)} collective-permute-done((bf16[4,96,768]{2,1,0:T(8,128)(2,1)S(1)}, bf16[4,96,768]{2,1,0:T(8,128)(2,1)}, u32[]{:S(2)}, u32[]{:S(2)}) %collective-permute-start.17) | collective-permute-done | bytes 589856 | tf_op jit(solution)/shard_map/ppermute | solution.py:728
  155.4 5.7 %shard_map.231 = (f32[768,768]{1,0:T(8,128)}, f32[768,768]{1,0:T(8,128)}, f32[768,768]{1,0:T(8,128)}, f32[768,768]{1,0:T(8,128)}, f32[768,768]{1,0:T(8,128)}, /*index=5*/f32[768,768]{1,0:T(8,128)}) custom-call(s32[1]{0:T(128)} %bitcast.9.refs_0_, s32[1]{0:T(128)} %bitcast.refs_1_.refs_0_, bf16[4,192,768]{2,1,0:T(8,128)(2,1)S(1)} %all-to-all-done.3.refs_2_, ...), custom_call_target="tpu_custom_call" | custom-call | tf_op jit(solution)/shard_map/pallas_call | solution.py:104
  164.9 2.4 %shard_map.232 = (f32[768,768]{1,0:T(8,128)}, f32[768,768]{1,0:T(8,128)}, f32[768,768]{1,0:T(8,128)}, f32[768,768]{1,0:T(8,128)}) custom-call(s32[1]{0:T(128)} %bitcast.9.refs_0_, s32[1]{0:T(128)} %bitcast.refs_1_.refs_0_, ...), custom_call_target="tpu_custom_call", output_to_operand_aliasing={{0}: (6, {}), {1}: (7, {}), {2}: (8, {}), {3}: (9, {})} | custom-call | tf_op jit(solution)/shard_map/pallas_call | solution.py:104
  (63 shorter events, 33.5 us)
Async XLA Ops:
  0.6 5.8 %collective-permute-start = (bf16[512,768]{1,0:T(8,128)(2,1)}, bf16[512,768]{1,0:T(8,128)(2,1)S(1)}, u32[]{:S(2)}, u32[]{:S(2)}) collective-permute-start(bf16[512,768]{1,0:T(8,128)(2,1)} %bitcast.17), channel_id=1, source_target_pairs={{0,4},{4,0},{1,5},{5,1},{2,6},{6,2},{3,7},{7,3},{8,12},{12,8},{9,1... | collective-permute-start | bytes 2359304 | tf_op jit(solution)/shard_map/ppermute | solution.py:724
  1.2 16.7 %collective-permute-start.3 = (bf16[192,512]{1,0:T(8,128)(2,1)}, bf16[192,512]{1,0:T(8,128)(2,1)}, u32[]{:S(2)}, u32[]{:S(2)}) collective-permute-start(bf16[192,512]{1,0:T(8,128)(2,1)} %bitcast.21), channel_id=1, source_target_pairs={{0,3},{1,2},{2,1},{3,0},{4,7},{5,6},{6,5},{7,4},{8,11},{9,10},{10,... | collective-permute-start | bytes 589832 | tf_op jit(solution)/shard_map/ppermute | solution.py:728
  5.8 17.6 %collective-permute-start.2 = (bf16[192,512]{1,0:T(8,128)(2,1)}, bf16[192,512]{1,0:T(8,128)(2,1)}, u32[]{:S(2)}, u32[]{:S(2)}) collective-permute-start(bf16[192,512]{1,0:T(8,128)(2,1)} %bitcast.22), channel_id=1, source_target_pairs={{0,2},{1,3},{2,0},{3,1},{4,6},{5,7},{6,4},{7,5},{8,10},{9,11},{10,... | collective-permute-start | bytes 589832 | tf_op jit(solution)/shard_map/ppermute | solution.py:728
  5.8 17.6 %collective-permute-start.1 = (bf16[192,512]{1,0:T(8,128)(2,1)}, bf16[192,512]{1,0:T(8,128)(2,1)}, u32[]{:S(2)}, u32[]{:S(2)}) collective-permute-start(bf16[192,512]{1,0:T(8,128)(2,1)} %bitcast.23), channel_id=1, source_target_pairs={{0,1},{1,0},{2,3},{3,2},{4,5},{5,4},{6,7},{7,6},{8,9},{9,8},{10,11... | collective-permute-start | bytes 589832 | tf_op jit(solution)/shard_map/ppermute | solution.py:728
  52.0 23.1 %all-to-all-start = ((bf16[4,192,512]{2,1,0:T(8,128)(2,1)}), bf16[4,192,512]{2,1,0:T(8,128)(2,1)}, u32[]{:S(2)}, u32[]{:S(2)}) async-start(bf16[4,192,512]{2,1,0:T(8,128)(2,1)} %get-tuple-element.101), calls=%async_computation | async-start | bytes 1572864 | tf_op jit(solution)/shard_map/all_to_all | solution.py:821
  63.9 3.4 %collective-permute-start.7 = (bf16[4,96,768]{2,1,0:T(8,128)(2,1)}, bf16[4,96,768]{2,1,0:T(8,128)(2,1)S(1)}, u32[]{:S(2)}, u32[]{:S(2)}) collective-permute-start(bf16[4,96,768]{2,1,0:T(8,128)(2,1)} %get-tuple-element.115), channel_id=1, source_target_pairs={{0,4},{4,0},{1,5},{5,1},{2,6},{6,2},{3,7},{7,3},{8,12},{12,8},{9,1... | collective-permute-start | bytes 1769480 | tf_op jit(solution)/shard_map/ppermute | solution.py:724
  71.5 24.1 %collective-permute-start.8 = (bf16[3,96,768]{2,1,0:T(8,128)(2,1)}, bf16[3,96,768]{2,1,0:T(8,128)(2,1)}, u32[]{:S(2)}, u32[]{:S(2)}) collective-permute-start(bf16[3,96,768]{2,1,0:T(8,128)(2,1)} %get-tuple-element.117), channel_id=1, source_target_pairs={{0,8},{8,0},{16,24},{24,16},{1,9},{9,1},{17,25},{25,17},{2,10},{10... | collective-permute-start | bytes 1327112 | tf_op jit(solution)/shard_map/ppermute | solution.py:728
  73.1 22.6 %collective-permute-start.9 = (bf16[3,96,768]{2,1,0:T(8,128)(2,1)}, bf16[3,96,768]{2,1,0:T(8,128)(2,1)}, u32[]{:S(2)}, u32[]{:S(2)}) collective-permute-start(bf16[3,96,768]{2,1,0:T(8,128)(2,1)} %get-tuple-element.118), channel_id=1, source_target_pairs={{0,16},{8,24},{16,0},{24,8},{1,17},{9,25},{17,1},{25,9},{2,18},{10... | collective-permute-start | bytes 1327112 | tf_op jit(solution)/shard_map/ppermute | solution.py:728
  74.6 21.0 %collective-permute-start.10 = (bf16[3,96,768]{2,1,0:T(8,128)(2,1)}, bf16[3,96,768]{2,1,0:T(8,128)(2,1)}, u32[]{:S(2)}, u32[]{:S(2)}) collective-permute-start(bf16[3,96,768]{2,1,0:T(8,128)(2,1)} %get-tuple-element.119), channel_id=1, source_target_pairs={{0,24},{8,16},{16,8},{24,0},{1,25},{9,17},{17,9},{25,1},{2,26},{10... | collective-permute-start | bytes 1327112 | tf_op jit(solution)/shard_map/ppermute | solution.py:728
  75.0 30.4 %all-to-all-start.1 = ((bf16[4,768,128]{2,1,0:T(8,128)(2,1)}), bf16[4,768,128]{2,1,0:T(8,128)(2,1)}, u32[]{:S(2)}, u32[]{:S(2)}) async-start(bf16[4,768,128]{2,1,0:T(8,128)(2,1)} %get-tuple-element.102), calls=%async_computation.1 | async-start | bytes 1572864 | tf_op jit(solution)/shard_map/all_to_all | solution.py:843
  95.6 3.7 %collective-permute-start.11 = (bf16[4,96,640]{2,1,0:T(8,128)(2,1)}, bf16[4,96,640]{2,1,0:T(8,128)(2,1)}, u32[]{:S(2)}, u32[]{:S(2)}) collective-permute-start(bf16[4,96,640]{2,1,0:T(8,128)(2,1)} %get-tuple-element.123), channel_id=1, source_target_pairs={{0,4},{4,0},{1,5},{5,1},{2,6},{6,2},{3,7},{7,3},{8,12},{12,8},{9,1... | collective-permute-start | bytes 1474568 | tf_op jit(solution)/shard_map/ppermute | solution.py:724
  101.9 10.9 %collective-permute-start.12 = (bf16[1,96,640]{2,1,0:T(8,128)(2,1)}, bf16[1,96,640]{2,1,0:T(8,128)(2,1)}, u32[]{:S(2)}, u32[]{:S(2)}) collective-permute-start(bf16[1,96,640]{2,1,0:T(8,128)(2,1)} %get-tuple-element.125), channel_id=1, source_target_pairs={{0,8},{8,0},{16,24},{24,16},{1,9},{9,1},{17,25},{25,17},{2,10},{10... | collective-permute-start | bytes 368648 | tf_op jit(solution)/shard_map/ppermute | solution.py:728
  103.5 9.3 %collective-permute-start.13 = (bf16[1,96,640]{2,1,0:T(8,128)(2,1)}, bf16[1,96,640]{2,1,0:T(8,128)(2,1)}, u32[]{:S(2)}, u32[]{:S(2)}) collective-permute-start(bf16[1,96,640]{2,1,0:T(8,128)(2,1)} %get-tuple-element.126), channel_id=1, source_target_pairs={{0,16},{8,24},{16,0},{24,8},{1,17},{9,25},{17,1},{25,9},{2,18},{10... | collective-permute-start | bytes 368648 | tf_op jit(solution)/shard_map/ppermute | solution.py:728
  105.0 7.8 %collective-permute-start.14 = (bf16[1,96,640]{2,1,0:T(8,128)(2,1)}, bf16[1,96,640]{2,1,0:T(8,128)(2,1)}, u32[]{:S(2)}, u32[]{:S(2)}) collective-permute-start(bf16[1,96,640]{2,1,0:T(8,128)(2,1)} %get-tuple-element.127), channel_id=1, source_target_pairs={{0,24},{8,16},{16,8},{24,0},{1,25},{9,17},{17,9},{25,1},{2,26},{10... | collective-permute-start | bytes 368648 | tf_op jit(solution)/shard_map/ppermute | solution.py:728
  105.5 10.9 %all-to-all-start.2 = ((bf16[4,48,384]{2,1,0:T(8,128)(2,1)}), bf16[4,48,384]{2,1,0:T(8,128)(2,1)}, u32[]{:S(2)}, u32[]{:S(2)}) async-start(bf16[4,48,384]{2,1,0:T(8,128)(2,1)} %get-tuple-element.130), calls=%async_computation.2 | async-start | bytes 294912 | tf_op jit(solution)/shard_map/all_to_all | solution.py:887
  116.4 22.7 %all-to-all-start.3 = ((bf16[4,192,768]{2,1,0:T(8,128)(2,1)}), bf16[4,192,768]{2,1,0:T(8,128)(2,1)S(1)}, u32[]{:S(2)}, u32[]{:S(2)}) async-start(bf16[4,192,768]{2,1,0:T(8,128)(2,1)} %get-tuple-element.131), calls=%async_computation.3 | async-start | bytes 2359296 | tf_op jit(solution)/shard_map/all_to_all | solution.py:927
  139.1 11.1 %collective-permute-start.17 = (bf16[4,96,768]{2,1,0:T(8,128)(2,1)S(1)}, bf16[4,96,768]{2,1,0:T(8,128)(2,1)}, u32[]{:S(2)}, u32[]{:S(2)}) collective-permute-start(bf16[4,96,768]{2,1,0:T(8,128)(2,1)S(1)} %slice.9.refs_4_), channel_id=1, source_target_pairs={{0,16},{8,24},{16,0},{24,8},{1,17},{9,25},{17,1},{25,9},{2,18},{10... | collective-permute-start | bytes 1769480 | tf_op jit(solution)/shard_map/ppermute | solution.py:728
  141.2 10.1 %collective-permute-start.15 = (bf16[4,96,768]{2,1,0:T(8,128)(2,1)S(1)}, bf16[4,96,768]{2,1,0:T(8,128)(2,1)}, u32[]{:S(2)}, u32[]{:S(2)}) collective-permute-start(bf16[4,96,768]{2,1,0:T(8,128)(2,1)S(1)} %slice.9.refs_4_), channel_id=1, source_target_pairs={{0,8},{8,0},{16,24},{24,16},{1,9},{9,1},{17,25},{25,17},{2,10},{10... | collective-permute-start | bytes 1769480 | tf_op jit(solution)/shard_map/ppermute | solution.py:728
  142.7 12.7 %collective-permute-start.19 = (bf16[4,192,768]{2,1,0:T(8,128)(2,1)S(1)}, bf16[4,192,768]{2,1,0:T(8,128)(2,1)}, u32[]{:S(2)}, u32[]{:S(2)}) collective-permute-start(bf16[4,192,768]{2,1,0:T(8,128)(2,1)S(1)} %all-to-all-done.3.refs_2_), channel_id=1, source_target_pairs={{0,4},{4,0},{1,5},{5,1},{2,6},{6,2},{3,7},{7,3},{8,12},{12,8},{9,1... | collective-permute-start | bytes 3538952 | tf_op jit(solution)/shard_map/ppermute | solution.py:724
  142.7 11.2 %collective-permute-start.20 = (bf16[4,96,768]{2,1,0:T(8,128)(2,1)S(1)}, bf16[4,96,768]{2,1,0:T(8,128)(2,1)}, u32[]{:S(2)}, u32[]{:S(2)}) collective-permute-start(bf16[4,96,768]{2,1,0:T(8,128)(2,1)S(1)} %slice.9.refs_4_), channel_id=1, source_target_pairs={{0,4},{4,0},{1,5},{5,1},{2,6},{6,2},{3,7},{7,3},{8,12},{12,8},{9,1... | collective-permute-start | bytes 1769480 | tf_op jit(solution)/shard_map/ppermute | solution.py:724
  143.2 24.1 %all-to-all-start.4 = ((bf16[4,768,128]{2,1,0:T(8,128)(2,1)}), bf16[4,768,128]{2,1,0:T(8,128)(2,1)S(1)}, u32[]{:S(2)}, u32[]{:S(2)}) async-start(bf16[4,768,128]{2,1,0:T(8,128)(2,1)} %get-tuple-element.133), calls=%async_computation.4 | async-start | bytes 1572864 | tf_op jit(solution)/shard_map/all_to_all | solution.py:929
  151.2 4.1 %collective-permute-start.22 = (bf16[4,96,768]{2,1,0:T(8,128)(2,1)}, bf16[4,96,768]{2,1,0:T(8,128)(2,1)S(1)}, u32[]{:S(2)}, u32[]{:S(2)}) collective-permute-start(bf16[4,96,768]{2,1,0:T(8,128)(2,1)} %collective-permute-done.17.refs_6_), channel_id=1, source_target_pairs={{0,4},{4,0},{1,5},{5,1},{2,6},{6,2},{3,7},{7,3},{8,12},{12,8},{9,1... | collective-permute-start | bytes 1769480 | tf_op jit(solution)/shard_map/ppermute | solution.py:724
  152.9 9.0 %collective-permute-start.18 = (bf16[2,96,768]{2,1,0:T(8,128)(2,1)S(1)}, bf16[2,96,768]{2,1,0:T(8,128)(2,1)S(1)}, u32[]{:S(2)}, u32[]{:S(2)}) collective-permute-start(bf16[2,96,768]{2,1,0:T(8,128)(2,1)S(1)} %slice.13), channel_id=1, source_target_pairs={{0,8},{8,0},{16,24},{24,16},{1,9},{9,1},{17,25},{25,17},{2,10},{10... | collective-permute-start | bytes 884744 | tf_op jit(solution)/shard_map/ppermute | solution.py:728
  153.9 9.0 %collective-permute-start.16 = (bf16[2,96,768]{2,1,0:T(8,128)(2,1)S(1)}, bf16[2,96,768]{2,1,0:T(8,128)(2,1)S(1)}, u32[]{:S(2)}, u32[]{:S(2)}) collective-permute-start(bf16[2,96,768]{2,1,0:T(8,128)(2,1)S(1)} %slice.12), channel_id=1, source_target_pairs={{0,16},{8,24},{16,0},{24,8},{1,17},{9,25},{17,1},{25,9},{2,18},{10... | collective-permute-start | bytes 884744 | tf_op jit(solution)/shard_map/ppermute | solution.py:728
  (10 other events, 25.6 us)

commit v7 on v6

--- a/solution.py
+++ b/solution.py
@@ -503,8 +503,8 @@
             out.inside[group] = (
                 keep.inside[group, block].astype(f32) + one.inside[block].astype(f32)
             ).astype(bf16)
-    for out in outs[1:] + outs[:1]:
-        out.send()
+        for out in outs[1:] + outs[:1]:
+            out.send(group)
 
 
 def row_sum_kernel(parts, scalars, ins, outs, scratch):
@@ -835,7 +835,7 @@
             [row_here],
             [keep, *[swap(send) for send in sends]],
             (shape(3, size, D),) * rows_count,
-            limit=SMALL_LIMIT,
+            limit=63 << 20,
         )
         wide_parts = [ordered[0]] + [trade(ordered[s], "row", s) for s in range(1, rows_count)]
 

time: 170 us -> 169 us (level)
  transfers between devices with their start and end apart: 30 -> 30, of which waited for: 11 -> 11; matrix products, arithmetic and copies ran while one was open for 1% -> 1% of each run, Pallas kernels for 30% -> 31%
where the time goes in v7:
time: 169 us
  Pallas kernels  61.9 us (37%)
  starting transfers between devices  44.9 us (27%)
  blocking collectives  36.1 us (21%)
  waiting for transfers between devices  20.8 us (12%)
  local copies, waits for them, and re-layouts  3.64 us (2%)
    pallas_call x14, Pallas kernels, staged_call(): pl.pallas_call(kernel, out_shape=tuple(outs), in_specs=[pl.BlockSpec(memo...  61.9 us
    all_gather x1, blocking collectives, per_device(): mixed4 = lax.all_gather(mixed, 'pat')  19.5 us
    ppermute x13, starting transfers between devices, trade(): lax.ppermute(value, axis, [(a, a ^ step) for a in range(lax.axis_size(axi...  18.5 us
    all_gather x1, blocking collectives, per_device(): gathered = lax.all_gather(mine, 'pat')  16.7 us
    ppermute x13, waiting for transfers between devices, trade(): lax.ppermute(value, axis, [(a, a ^ step) for a in range(lax.axis_size(axi...  10.7 us
    ppermute x12, waiting for transfers between devices, swap(): return lax.ppermute(value, 'seq', [(0, 1), (1, 0)])  6.51 us
    all_to_all x1, starting transfers between devices, per_device(): ffn_parts = lax.all_to_all(ffn, 'pat', 0, 0, tiled=True)  5.04 us
    ppermute x12, starting transfers between devices, swap(): return lax.ppermute(value, 'seq', [(0, 1), (1, 0)])  4.83 us
  transfers between devices with their start and end apart: 30, of which 11 were waited for; matrix products, arithmetic and copies ran while one was open for 1% of the time, Pallas kernels for 31%

profile of v7, /device:TPU:0, one launch (start us, length us, event | category | flops | bytes accessed | tf_op | source)
XLA Modules:
  0.0 168.5 jit_solution(4818153548716218196)
XLA Ops:
  1.2 4.7 %collective-permute-start.3 = (bf16[192,512]{1,0:T(8,128)(2,1)}, bf16[192,512]{1,0:T(8,128)(2,1)}, u32[]{:S(2)}, u32[]{:S(2)}) collective-permute-start(bf16[192,512]{1,0:T(8,128)(2,1)} %bitcast.21), channel_id=1, source_target_pairs={{0,3},{1,2},{2,1},{3,0},{4,7},{5,6},{6,5},{7,4},{8,11},{9,10},{10,... | collective-permute-start | bytes 589832 | tf_op jit(solution)/shard_map/ppermute | solution.py:728
  7.4 5.0 %shard_map.220 = (bf16[512,768]{1,0:T(8,128)(2,1)}, bf16[512,192]{1,0:T(8,128)(2,1)}, bf16[512,384]{1,0:T(8,128)(2,1)}, bf16[768,768]{1,0:T(8,128)(2,1)}, bf16[3...) custom-call(s32[1]{0:T(128)} %bitcast.1.refs_0_, s32[1]{0:T(128)} %bitcast.refs_1_.refs_0_, bf16[512,768]{1,0:T(8,128)(2,1)} %bitcast.18, ...), custom_call_target="tpu_custom_call" | custom-call | flops 4398046511104 | tf_op jit(solution)/shard_map/pallas_call | solution.py:104
  12.4 5.4 %shard_map.221 = (bf16[192,512]{1,0:T(8,128)(2,1)}, f32[192,512]{1,0:T(8,128)}, f32[8,512]{1,0:T(8,128)}) custom-call(s32[1]{0:T(128)} %bitcast.refs_1_.refs_0_, bf16[512,192]{1,0:T(8,128)(2,1)} %get-tuple-element.84.refs_1_.refs_2_, bf16[512,384]{1,0:T(8,128)(2,1)} %get-tuple-element.85.refs_2_.refs_5_, ...), custom_call_target="tpu_custom_call" | custom-call | tf_op jit(solution)/shard_map/pallas_call | solution.py:104
  17.8 5.6 %collective-permute-done.2.refs_10_ = bf16[192,512]{1,0:T(8,128)(2,1)} collective-permute-done((bf16[192,512]{1,0:T(8,128)(2,1)}, bf16[192,512]{1,0:T(8,128)(2,1)}, u32[]{:S(2)}, u32[]{:S(2)}) %collective-permute-start.2) | collective-permute-done | bytes 196640 | tf_op jit(solution)/shard_map/ppermute | solution.py:728
  23.5 19.5 %all-gather = bf16[768,512]{1,0:T(8,128)(2,1)} all-gather(bf16[192,512]{1,0:T(8,128)(2,1)} %get-tuple-element.89), channel_id=2, replica_groups=mesh['row'=4,'seq'=2,'pat'=4] {'pat'}, dimensions={0}, use_global_device_ids=true | all-gather | bytes 983040 | tf_op jit(solution)/shard_map/all_gather | solution.py:808
  42.9 9.0 %shard_map.222 = (bf16[4,192,512]{2,1,0:T(8,128)(2,1)}, f32[8,768]{1,0:T(8,128)}, bf16[512,768]{1,0:T(8,128)(2,1)}, bf16[512,768]{1,0:T(8,128)(2,1)}, bf16[512,7...) custom-call(s32[1]{0:T(128)} %bitcast.1.refs_0_, ...), custom_call_target="tpu_custom_call" | custom-call | tf_op jit(solution)/shard_map/pallas_call | solution.py:104
  52.0 4.2 %all-to-all-start = ((bf16[4,192,512]{2,1,0:T(8,128)(2,1)}), bf16[4,192,512]{2,1,0:T(8,128)(2,1)}, u32[]{:S(2)}, u32[]{:S(2)}) async-start(bf16[4,192,512]{2,1,0:T(8,128)(2,1)} %get-tuple-element.101), calls=%async_computation | async-start | bytes 1572864 | tf_op jit(solution)/shard_map/all_to_all | solution.py:821
  56.2 7.2 %shard_map.223 = (bf16[4,768,128]{2,1,0:T(8,128)(2,1)}, bf16[3,4,96,768]{3,2,1,0:T(8,128)(2,1)}, bf16[4,96,768]{2,1,0:T(8,128)(2,1)}, bf16[4,96,768]{2,1,0:T(8,128)(2,1)}, bf16[4,96,768]{2,1,0:T(8,128)(2,1)}) custom-call(s32[1]{0:T(128)} %bitcast.refs_1_.refs_0_, bf16[512,768]{1,0:T(8,128)(2,1)} %get-tuple-element.94.refs_1_, ...), custom_call_target="tpu_custom_call" | custom-call | flops 4398046511104 | tf_op jit(solution)/shard_map/pallas_call | solution.py:104
  67.5 3.4 %shard_map.227 = (bf16[3,96,768]{2,1,0:T(8,128)(2,1)}, bf16[3,96,768]{2,1,0:T(8,128)(2,1)}, bf16[3,96,768]{2,1,0:T(8,128)(2,1)}, bf16[3,96,768]{2,1,0:T(8,128)(2,1)}) custom-call(s32[1]{0:T(128)} %bitcast.9.refs_0_, bf16[3,4,96,768]{3,2,1,0:T(8,128)(2,1)} %get-tuple-element.112.refs_1_, bf16[4,96,768]{2,1,0:T(8,128)(2,1)} %copy-done.2, ...), custom_call_target="tpu_custom_call" | custom-call | tf_op jit(solution)/shard_map/pallas_call | solution.py:104
  74.4 5.0 %all-to-all-start.1 = ((bf16[4,768,128]{2,1,0:T(8,128)(2,1)}), bf16[4,768,128]{2,1,0:T(8,128)(2,1)}, u32[]{:S(2)}, u32[]{:S(2)}) async-start(bf16[4,768,128]{2,1,0:T(8,128)(2,1)} %get-tuple-element.102), calls=%async_computation.1 | async-start | bytes 1572864 | tf_op jit(solution)/shard_map/all_to_all | solution.py:843
  79.5 5.7 %shard_map.225 = (bf16[512,192]{1,0:T(8,128)(2,1)}, f32[512,384]{1,0:T(8,128)}, bf16[512,384]{1,0:T(8,128)(2,1)}) custom-call(s32[1]{0:T(128)} %bitcast.refs_1_.refs_0_, bf16[4,192,512]{2,1,0:T(8,128)(2,1)} %all-to-all-done.refs_1_, bf16[512,192]{1,0:T(8,128)(2,1)} %get-tuple-element.84.refs_1_.refs_2_, f32[192,512]{1,0:T(8,128)} %get-tuple-element.103.refs_3_, ...), custom_call_target="tpu_custom_call" | custom-call | flops 4398046511104 | tf_op jit(solution)/shard_map/pallas_call | solution.py:104
  89.1 5.9 %shard_map.226 = (bf16[4,768,128]{2,1,0:T(8,128)(2,1)}, bf16[1,4,96,640]{3,2,1,0:T(8,128)(2,1)}, bf16[4,96,640]{2,1,0:T(8,128)(2,1)}) custom-call(s32[1]{0:T(128)} %bitcast.refs_1_.refs_0_, bf16[512,192]{1,0:T(8,128)(2,1)} %get-tuple-element.105.refs_1_, f32[512,384]{1,0:T(8,128)} %get-tuple-element.106.refs_2_, bf16[512,384]{1,0:T(8,128)(2,1)} %copy-done.3, ...), custom_call_target="tpu_custom_call" | custom-call | tf_op jit(solution)/shard_map/pallas_call | solution.py:104
  95.5 3.3 %shard_map.228 = (bf16[4,192,768]{2,1,0:T(8,128)(2,1)}, bf16[4,48,384]{2,1,0:T(8,128)(2,1)}) custom-call(bf16[3,96,768]{2,1,0:T(8,128)(2,1)S(1)} %copy-done, bf16[3,96,768]{2,1,0:T(8,128)(2,1)} %collective-permute-done.8.refs_1_, bf16[3,96,768]{2,1,0:T(8,128)(2,1)} %collective-permute-done.9.refs_2_, bf16[3,96,768]{2,1,0:T(8,128)(2,1)} %collective-permute-done.10.refs_3_), custom_call_target="tpu_custom_call" | custom-call | tf_op jit(solution)/shard_map/pallas_call | solution.py:104
  98.8 2.6 %shard_map.229 = (bf16[1,96,640]{2,1,0:T(8,128)(2,1)}, bf16[1,96,640]{2,1,0:T(8,128)(2,1)}, bf16[1,96,640]{2,1,0:T(8,128)(2,1)}, bf16[1,96,640]{2,1,0:T(8,128)(2,1)}) custom-call(s32[1]{0:T(128)} %bitcast.9.refs_0_, bf16[1,4,96,640]{3,2,1,0:T(8,128)(2,1)} %get-tuple-element.121.refs_1_, bf16[4,96,640]{2,1,0:T(8,128)(2,1)} %collective-permute-done.11.refs_2_), custom_call_target="tpu_custom_call" | custom-call | tf_op jit(solution)/shard_map/pallas_call | solution.py:104
  104.9 4.8 %all-to-all-start.2 = ((bf16[4,48,384]{2,1,0:T(8,128)(2,1)}), bf16[4,48,384]{2,1,0:T(8,128)(2,1)}, u32[]{:S(2)}, u32[]{:S(2)}) async-start(bf16[4,48,384]{2,1,0:T(8,128)(2,1)} %get-tuple-element.130), calls=%async_computation.2 | async-start | bytes 294912 | tf_op jit(solution)/shard_map/all_to_all | solution.py:887
  109.8 2.5 %shard_map.224 = bf16[192,512]{1,0:T(8,128)(2,1)} custom-call(bf16[4,768,128]{2,1,0:T(8,128)(2,1)} %all-to-all-done.1.refs_0_), custom_call_target="tpu_custom_call" | custom-call | flops 4398046511104 | tf_op jit(solution)/shard_map/pallas_call | solution.py:104
  112.3 3.6 %all-to-all-done.2.refs_4_ = bf16[4,48,384]{2,1,0:T(8,128)(2,1)} async-done(((bf16[4,48,384]{2,1,0:T(8,128)(2,1)}), bf16[4,48,384]{2,1,0:T(8,128)(2,1)}, u32[]{:S(2)}, u32[]{:S(2)}) %all-to-all-start.2) | async-done | bytes 147488 | tf_op jit(solution)/shard_map/all_to_all | solution.py:887
  115.8 3.7 %all-to-all-start.3 = ((bf16[4,192,768]{2,1,0:T(8,128)(2,1)}), bf16[4,192,768]{2,1,0:T(8,128)(2,1)S(1)}, u32[]{:S(2)}, u32[]{:S(2)}) async-start(bf16[4,192,768]{2,1,0:T(8,128)(2,1)} %get-tuple-element.131), calls=%async_computation.3 | async-start | bytes 2359296 | tf_op jit(solution)/shard_map/all_to_all | solution.py:927
  119.6 2.3 %shard_map.230 = bf16[112,768]{1,0:T(8,128)(2,1)S(1)} custom-call(bf16[1,96,640]{2,1,0:T(8,128)(2,1)S(1)} %copy-done.1, bf16[1,96,640]{2,1,0:T(8,128)(2,1)} %collective-permute-done.12.refs_1_, bf16[1,96,640]{2,1,0:T(8,128)(2,1)} %collective-permute-done.13.refs_2_, bf16[1,96,640]{2,1,0:T(8,128)(2,1)} %collective-permute-done.14.refs_3_, ...), custom_call_target="tpu_custom_call" | custom-call | tf_op jit(solution)/shard_map/pallas_call | solution.py:104
  121.9 16.7 %all-gather.1 = bf16[448,768]{1,0:T(8,128)(2,1)S(1)} all-gather(bf16[112,768]{1,0:T(8,128)(2,1)S(1)} %shard_map.230), channel_id=3, replica_groups=mesh['row'=4,'seq'=2,'pat'=4] {'pat'}, dimensions={0}, use_global_device_ids=true | all-gather | bytes 860160 | tf_op jit(solution)/shard_map/all_gather | solution.py:923
  142.7 3.8 %all-to-all-start.4 = ((bf16[4,768,128]{2,1,0:T(8,128)(2,1)}), bf16[4,768,128]{2,1,0:T(8,128)(2,1)S(1)}, u32[]{:S(2)}, u32[]{:S(2)}) async-start(bf16[4,768,128]{2,1,0:T(8,128)(2,1)} %get-tuple-element.133), calls=%async_computation.4 | async-start | bytes 1572864 | tf_op jit(solution)/shard_map/all_to_all | solution.py:929
  146.4 3.3 %collective-permute-done.17.refs_6_ = bf16[4,96,768]{2,1,0:T(8,128)(2,1)} collective-permute-done((bf16[4,96,768]{2,1,0:T(8,128)(2,1)S(1)}, bf16[4,96,768]{2,1,0:T(8,128)(2,1)}, u32[]{:S(2)}, u32[]{:S(2)}) %collective-permute-start.17) | collective-permute-done | bytes 589856 | tf_op jit(solution)/shard_map/ppermute | solution.py:728
  154.8 5.7 %shard_map.231 = (f32[768,768]{1,0:T(8,128)}, f32[768,768]{1,0:T(8,128)}, f32[768,768]{1,0:T(8,128)}, f32[768,768]{1,0:T(8,128)}, f32[768,768]{1,0:T(8,128)}, /*index=5*/f32[768,768]{1,0:T(8,128)}) custom-call(s32[1]{0:T(128)} %bitcast.9.refs_0_, s32[1]{0:T(128)} %bitcast.refs_1_.refs_0_, bf16[4,192,768]{2,1,0:T(8,128)(2,1)S(1)} %all-to-all-done.3.refs_2_, ...), custom_call_target="tpu_custom_call" | custom-call | tf_op jit(solution)/shard_map/pallas_call | solution.py:104
  164.4 2.4 %shard_map.232 = (f32[768,768]{1,0:T(8,128)}, f32[768,768]{1,0:T(8,128)}, f32[768,768]{1,0:T(8,128)}, f32[768,768]{1,0:T(8,128)}) custom-call(s32[1]{0:T(128)} %bitcast.9.refs_0_, s32[1]{0:T(128)} %bitcast.refs_1_.refs_0_, ...), custom_call_target="tpu_custom_call", output_to_operand_aliasing={{0}: (6, {}), {1}: (7, {}), {2}: (8, {}), {3}: (9, {})} | custom-call | tf_op jit(solution)/shard_map/pallas_call | solution.py:104
  (65 shorter events, 32.2 us)
Async XLA Ops:
  0.6 5.8 %collective-permute-start = (bf16[512,768]{1,0:T(8,128)(2,1)}, bf16[512,768]{1,0:T(8,128)(2,1)S(1)}, u32[]{:S(2)}, u32[]{:S(2)}) collective-permute-start(bf16[512,768]{1,0:T(8,128)(2,1)} %bitcast.17), channel_id=1, source_target_pairs={{0,4},{4,0},{1,5},{5,1},{2,6},{6,2},{3,7},{7,3},{8,12},{12,8},{9,1... | collective-permute-start | bytes 2359304 | tf_op jit(solution)/shard_map/ppermute | solution.py:724
  1.2 16.7 %collective-permute-start.3 = (bf16[192,512]{1,0:T(8,128)(2,1)}, bf16[192,512]{1,0:T(8,128)(2,1)}, u32[]{:S(2)}, u32[]{:S(2)}) collective-permute-start(bf16[192,512]{1,0:T(8,128)(2,1)} %bitcast.21), channel_id=1, source_target_pairs={{0,3},{1,2},{2,1},{3,0},{4,7},{5,6},{6,5},{7,4},{8,11},{9,10},{10,... | collective-permute-start | bytes 589832 | tf_op jit(solution)/shard_map/ppermute | solution.py:728
  5.8 17.6 %collective-permute-start.2 = (bf16[192,512]{1,0:T(8,128)(2,1)}, bf16[192,512]{1,0:T(8,128)(2,1)}, u32[]{:S(2)}, u32[]{:S(2)}) collective-permute-start(bf16[192,512]{1,0:T(8,128)(2,1)} %bitcast.22), channel_id=1, source_target_pairs={{0,2},{1,3},{2,0},{3,1},{4,6},{5,7},{6,4},{7,5},{8,10},{9,11},{10,... | collective-permute-start | bytes 589832 | tf_op jit(solution)/shard_map/ppermute | solution.py:728
  5.8 17.6 %collective-permute-start.1 = (bf16[192,512]{1,0:T(8,128)(2,1)}, bf16[192,512]{1,0:T(8,128)(2,1)}, u32[]{:S(2)}, u32[]{:S(2)}) collective-permute-start(bf16[192,512]{1,0:T(8,128)(2,1)} %bitcast.23), channel_id=1, source_target_pairs={{0,1},{1,0},{2,3},{3,2},{4,5},{5,4},{6,7},{7,6},{8,9},{9,8},{10,11... | collective-permute-start | bytes 589832 | tf_op jit(solution)/shard_map/ppermute | solution.py:728
  52.0 22.5 %all-to-all-start = ((bf16[4,192,512]{2,1,0:T(8,128)(2,1)}), bf16[4,192,512]{2,1,0:T(8,128)(2,1)}, u32[]{:S(2)}, u32[]{:S(2)}) async-start(bf16[4,192,512]{2,1,0:T(8,128)(2,1)} %get-tuple-element.101), calls=%async_computation | async-start | bytes 1572864 | tf_op jit(solution)/shard_map/all_to_all | solution.py:821
  63.9 3.5 %collective-permute-start.7 = (bf16[4,96,768]{2,1,0:T(8,128)(2,1)}, bf16[4,96,768]{2,1,0:T(8,128)(2,1)}, u32[]{:S(2)}, u32[]{:S(2)}) collective-permute-start(bf16[4,96,768]{2,1,0:T(8,128)(2,1)} %get-tuple-element.115), channel_id=1, source_target_pairs={{0,4},{4,0},{1,5},{5,1},{2,6},{6,2},{3,7},{7,3},{8,12},{12,8},{9,1... | collective-permute-start | bytes 1769480 | tf_op jit(solution)/shard_map/ppermute | solution.py:724
  70.9 24.1 %collective-permute-start.8 = (bf16[3,96,768]{2,1,0:T(8,128)(2,1)}, bf16[3,96,768]{2,1,0:T(8,128)(2,1)}, u32[]{:S(2)}, u32[]{:S(2)}) collective-permute-start(bf16[3,96,768]{2,1,0:T(8,128)(2,1)} %get-tuple-element.117), channel_id=1, source_target_pairs={{0,8},{8,0},{16,24},{24,16},{1,9},{9,1},{17,25},{25,17},{2,10},{10... | collective-permute-start | bytes 1327112 | tf_op jit(solution)/shard_map/ppermute | solution.py:728
  72.5 22.6 %collective-permute-start.9 = (bf16[3,96,768]{2,1,0:T(8,128)(2,1)}, bf16[3,96,768]{2,1,0:T(8,128)(2,1)}, u32[]{:S(2)}, u32[]{:S(2)}) collective-permute-start(bf16[3,96,768]{2,1,0:T(8,128)(2,1)} %get-tuple-element.118), channel_id=1, source_target_pairs={{0,16},{8,24},{16,0},{24,8},{1,17},{9,25},{17,1},{25,9},{2,18},{10... | collective-permute-start | bytes 1327112 | tf_op jit(solution)/shard_map/ppermute | solution.py:728
  74.0 21.1 %collective-permute-start.10 = (bf16[3,96,768]{2,1,0:T(8,128)(2,1)}, bf16[3,96,768]{2,1,0:T(8,128)(2,1)}, u32[]{:S(2)}, u32[]{:S(2)}) collective-permute-start(bf16[3,96,768]{2,1,0:T(8,128)(2,1)} %get-tuple-element.119), channel_id=1, source_target_pairs={{0,24},{8,16},{16,8},{24,0},{1,25},{9,17},{17,9},{25,1},{2,26},{10... | collective-permute-start | bytes 1327112 | tf_op jit(solution)/shard_map/ppermute | solution.py:728
  74.4 30.5 %all-to-all-start.1 = ((bf16[4,768,128]{2,1,0:T(8,128)(2,1)}), bf16[4,768,128]{2,1,0:T(8,128)(2,1)}, u32[]{:S(2)}, u32[]{:S(2)}) async-start(bf16[4,768,128]{2,1,0:T(8,128)(2,1)} %get-tuple-element.102), calls=%async_computation.1 | async-start | bytes 1572864 | tf_op jit(solution)/shard_map/all_to_all | solution.py:843
  95.1 3.7 %collective-permute-start.11 = (bf16[4,96,640]{2,1,0:T(8,128)(2,1)}, bf16[4,96,640]{2,1,0:T(8,128)(2,1)}, u32[]{:S(2)}, u32[]{:S(2)}) collective-permute-start(bf16[4,96,640]{2,1,0:T(8,128)(2,1)} %get-tuple-element.123), channel_id=1, source_target_pairs={{0,4},{4,0},{1,5},{5,1},{2,6},{6,2},{3,7},{7,3},{8,12},{12,8},{9,1... | collective-permute-start | bytes 1474568 | tf_op jit(solution)/shard_map/ppermute | solution.py:724
  101.4 10.9 %collective-permute-start.12 = (bf16[1,96,640]{2,1,0:T(8,128)(2,1)}, bf16[1,96,640]{2,1,0:T(8,128)(2,1)}, u32[]{:S(2)}, u32[]{:S(2)}) collective-permute-start(bf16[1,96,640]{2,1,0:T(8,128)(2,1)} %get-tuple-element.125), channel_id=1, source_target_pairs={{0,8},{8,0},{16,24},{24,16},{1,9},{9,1},{17,25},{25,17},{2,10},{10... | collective-permute-start | bytes 368648 | tf_op jit(solution)/shard_map/ppermute | solution.py:728
  102.9 9.3 %collective-permute-start.13 = (bf16[1,96,640]{2,1,0:T(8,128)(2,1)}, bf16[1,96,640]{2,1,0:T(8,128)(2,1)}, u32[]{:S(2)}, u32[]{:S(2)}) collective-permute-start(bf16[1,96,640]{2,1,0:T(8,128)(2,1)} %get-tuple-element.126), channel_id=1, source_target_pairs={{0,16},{8,24},{16,0},{24,8},{1,17},{9,25},{17,1},{25,9},{2,18},{10... | collective-permute-start | bytes 368648 | tf_op jit(solution)/shard_map/ppermute | solution.py:728
  104.5 7.8 %collective-permute-start.14 = (bf16[1,96,640]{2,1,0:T(8,128)(2,1)}, bf16[1,96,640]{2,1,0:T(8,128)(2,1)}, u32[]{:S(2)}, u32[]{:S(2)}) collective-permute-start(bf16[1,96,640]{2,1,0:T(8,128)(2,1)} %get-tuple-element.127), channel_id=1, source_target_pairs={{0,24},{8,16},{16,8},{24,0},{1,25},{9,17},{17,9},{25,1},{2,26},{10... | collective-permute-start | bytes 368648 | tf_op jit(solution)/shard_map/ppermute | solution.py:728
  104.9 10.9 %all-to-all-start.2 = ((bf16[4,48,384]{2,1,0:T(8,128)(2,1)}), bf16[4,48,384]{2,1,0:T(8,128)(2,1)}, u32[]{:S(2)}, u32[]{:S(2)}) async-start(bf16[4,48,384]{2,1,0:T(8,128)(2,1)} %get-tuple-element.130), calls=%async_computation.2 | async-start | bytes 294912 | tf_op jit(solution)/shard_map/all_to_all | solution.py:887
  115.8 22.7 %all-to-all-start.3 = ((bf16[4,192,768]{2,1,0:T(8,128)(2,1)}), bf16[4,192,768]{2,1,0:T(8,128)(2,1)S(1)}, u32[]{:S(2)}, u32[]{:S(2)}) async-start(bf16[4,192,768]{2,1,0:T(8,128)(2,1)} %get-tuple-element.131), calls=%async_computation.3 | async-start | bytes 2359296 | tf_op jit(solution)/shard_map/all_to_all | solution.py:927
  138.6 11.1 %collective-permute-start.17 = (bf16[4,96,768]{2,1,0:T(8,128)(2,1)S(1)}, bf16[4,96,768]{2,1,0:T(8,128)(2,1)}, u32[]{:S(2)}, u32[]{:S(2)}) collective-permute-start(bf16[4,96,768]{2,1,0:T(8,128)(2,1)S(1)} %slice.9.refs_4_), channel_id=1, source_target_pairs={{0,16},{8,24},{16,0},{24,8},{1,17},{9,25},{17,1},{25,9},{2,18},{10... | collective-permute-start | bytes 1769480 | tf_op jit(solution)/shard_map/ppermute | solution.py:728
  140.7 10.1 %collective-permute-start.15 = (bf16[4,96,768]{2,1,0:T(8,128)(2,1)S(1)}, bf16[4,96,768]{2,1,0:T(8,128)(2,1)}, u32[]{:S(2)}, u32[]{:S(2)}) collective-permute-start(bf16[4,96,768]{2,1,0:T(8,128)(2,1)S(1)} %slice.9.refs_4_), channel_id=1, source_target_pairs={{0,8},{8,0},{16,24},{24,16},{1,9},{9,1},{17,25},{25,17},{2,10},{10... | collective-permute-start | bytes 1769480 | tf_op jit(solution)/shard_map/ppermute | solution.py:728
  142.2 12.7 %collective-permute-start.19 = (bf16[4,192,768]{2,1,0:T(8,128)(2,1)S(1)}, bf16[4,192,768]{2,1,0:T(8,128)(2,1)}, u32[]{:S(2)}, u32[]{:S(2)}) collective-permute-start(bf16[4,192,768]{2,1,0:T(8,128)(2,1)S(1)} %all-to-all-done.3.refs_2_), channel_id=1, source_target_pairs={{0,4},{4,0},{1,5},{5,1},{2,6},{6,2},{3,7},{7,3},{8,12},{12,8},{9,1... | collective-permute-start | bytes 3538952 | tf_op jit(solution)/shard_map/ppermute | solution.py:724
  142.2 11.2 %collective-permute-start.20 = (bf16[4,96,768]{2,1,0:T(8,128)(2,1)S(1)}, bf16[4,96,768]{2,1,0:T(8,128)(2,1)}, u32[]{:S(2)}, u32[]{:S(2)}) collective-permute-start(bf16[4,96,768]{2,1,0:T(8,128)(2,1)S(1)} %slice.9.refs_4_), channel_id=1, source_target_pairs={{0,4},{4,0},{1,5},{5,1},{2,6},{6,2},{3,7},{7,3},{8,12},{12,8},{9,1... | collective-permute-start | bytes 1769480 | tf_op jit(solution)/shard_map/ppermute | solution.py:724
  142.7 24.1 %all-to-all-start.4 = ((bf16[4,768,128]{2,1,0:T(8,128)(2,1)}), bf16[4,768,128]{2,1,0:T(8,128)(2,1)S(1)}, u32[]{:S(2)}, u32[]{:S(2)}) async-start(bf16[4,768,128]{2,1,0:T(8,128)(2,1)} %get-tuple-element.133), calls=%async_computation.4 | async-start | bytes 1572864 | tf_op jit(solution)/shard_map/all_to_all | solution.py:929
  150.7 4.1 %collective-permute-start.22 = (bf16[4,96,768]{2,1,0:T(8,128)(2,1)}, bf16[4,96,768]{2,1,0:T(8,128)(2,1)S(1)}, u32[]{:S(2)}, u32[]{:S(2)}) collective-permute-start(bf16[4,96,768]{2,1,0:T(8,128)(2,1)} %collective-permute-done.17.refs_6_), channel_id=1, source_target_pairs={{0,4},{4,0},{1,5},{5,1},{2,6},{6,2},{3,7},{7,3},{8,12},{12,8},{9,1... | collective-permute-start | bytes 1769480 | tf_op jit(solution)/shard_map/ppermute | solution.py:724
  152.3 9.0 %collective-permute-start.18 = (bf16[2,96,768]{2,1,0:T(8,128)(2,1)S(1)}, bf16[2,96,768]{2,1,0:T(8,128)(2,1)S(1)}, u32[]{:S(2)}, u32[]{:S(2)}) collective-permute-start(bf16[2,96,768]{2,1,0:T(8,128)(2,1)S(1)} %slice.13), channel_id=1, source_target_pairs={{0,8},{8,0},{16,24},{24,16},{1,9},{9,1},{17,25},{25,17},{2,10},{10... | collective-permute-start | bytes 884744 | tf_op jit(solution)/shard_map/ppermute | solution.py:728
  153.4 9.0 %collective-permute-start.16 = (bf16[2,96,768]{2,1,0:T(8,128)(2,1)S(1)}, bf16[2,96,768]{2,1,0:T(8,128)(2,1)S(1)}, u32[]{:S(2)}, u32[]{:S(2)}) collective-permute-start(bf16[2,96,768]{2,1,0:T(8,128)(2,1)S(1)} %slice.12), channel_id=1, source_target_pairs={{0,16},{8,24},{16,0},{24,8},{1,17},{9,25},{17,1},{25,9},{2,18},{10... | collective-permute-start | bytes 884744 | tf_op jit(solution)/shard_map/ppermute | solution.py:728
  (11 other events, 32.4 us)

commit v8 on v7

--- a/solution.py
+++ b/solution.py
@@ -573,13 +573,9 @@
             back.inside[at // piece] = turned[:, at - start : at - start + piece]
             back.send(at // piece)
     pieces = D // SLOT
-    for at, row in enumerate(
-        (gain_sum, bias_sum, sums.inside[0:1, :], sums.inside[1:2, :])
-    ):
-        for part in range(pieces):
-            small[at * pieces + part : at * pieces + part + 1, :] = row[
-                :, part * SLOT : (part + 1) * SLOT
-            ]
+    four = jnp.concatenate([gain_sum, bias_sum, sums.inside[0:2, :]], axis=0)
+    for part in range(pieces):
+        small[4 * part : 4 * part + 4, :] = four[:, part * SLOT : (part + 1) * SLOT]
     tail = small[...].astype(bf16)
     if pair:
         for row in range(rows_count):
@@ -609,12 +605,8 @@
     mine[:size, : 3 * width] = total[:, : 3 * width].astype(bf16)
     pieces = D // SLOT
     small[...] = jnp.zeros(small.shape, f32)
-    for at in range(4):
-        for part in range(pieces):
-            row = at * pieces + part
-            small[at : at + 1, part * SLOT : (part + 1) * SLOT] = total[
-                row : row + 1, 3 * width :
-            ]
+    for part in range(pieces):
+        small[0:4, part * SLOT : (part + 1) * SLOT] = total[4 * part : 4 * part + 4, 3 * width :]
     mine[size:, :] = small[...].astype(bf16)
     outs[0].send()
 
@@ -969,7 +961,8 @@
         grad_down, grad_up = wide_sum[0].astype(f32), wide_sum[1].astype(f32)
         grad_out = lax.psum(wide_sum[2], "pat").astype(f32)
         gathered = lax.all_gather(lax.psum(narrow[0], axes), "pat")
-        small = gathered[:, :48, 3 * width :].reshape(parts, 4, D)
+        small = gathered[:, :48, 3 * width :].reshape(parts, D // SLOT, 4, SLOT)
+        small = small.transpose(0, 2, 1, 3).reshape(parts, 4, D)
         small = jnp.pad(small, ((0, 0), (0, 12), (0, 0)))
         grads = [
             gathered[:, :, at * width : (at + 1) * width]

time: 169 us -> 169 us (level)
  transfers between devices with their start and end apart: 30 -> 30, of which waited for: 11 -> 11; matrix products, arithmetic and copies ran while one was open for 1% -> 1% of each run, Pallas kernels for 31% -> 30%
where the time goes in v8:
time: 169 us; the launch traced here: 168 us
  Pallas kernels  61.9 us (37%)
  starting transfers between devices  44.9 us (27%)
  blocking collectives  36.1 us (21%)
  waiting for transfers between devices  20.8 us (12%)
  local copies, waits for them, and re-layouts  3.64 us (2%)
    pallas_call x14, Pallas kernels, staged_call(): pl.pallas_call(kernel, out_shape=tuple(outs), in_specs=[pl.BlockSpec(memo...  61.9 us
    all_gather x1, blocking collectives, per_device(): mixed4 = lax.all_gather(mixed, 'pat')  19.5 us
    ppermute x13, starting transfers between devices, trade(): lax.ppermute(value, axis, [(a, a ^ step) for a in range(lax.axis_size(axi...  18.5 us
    all_gather x1, blocking collectives, per_device(): gathered = lax.all_gather(mine, 'pat')  16.7 us
    ppermute x13, waiting for transfers between devices, trade(): lax.ppermute(value, axis, [(a, a ^ step) for a in range(lax.axis_size(axi...  10.7 us
    ppermute x12, waiting for transfers between devices, swap(): return lax.ppermute(value, 'seq', [(0, 1), (1, 0)])  6.51 us
    all_to_all x1, starting transfers between devices, per_device(): ffn_parts = lax.all_to_all(ffn, 'pat', 0, 0, tiled=True)  5.04 us
    ppermute x12, starting transfers between devices, swap(): return lax.ppermute(value, 'seq', [(0, 1), (1, 0)])  4.83 us
  transfers between devices with their start and end apart: 30, of which 11 were waited for; matrix products, arithmetic and copies ran while one was open for 1% of the time, Pallas kernels for 30%

profile of v8, /device:TPU:0, one launch (start us, length us, event | category | flops | bytes accessed | tf_op | source)
XLA Modules:
  0.0 168.5 jit_solution(5723715555450204676)
XLA Ops:
  1.2 4.7 %collective-permute-start.3 = (bf16[192,512]{1,0:T(8,128)(2,1)}, bf16[192,512]{1,0:T(8,128)(2,1)}, u32[]{:S(2)}, u32[]{:S(2)}) collective-permute-start(bf16[192,512]{1,0:T(8,128)(2,1)} %bitcast.21), channel_id=1, source_target_pairs={{0,3},{1,2},{2,1},{3,0},{4,7},{5,6},{6,5},{7,4},{8,11},{9,10},{10,... | collective-permute-start | bytes 589832 | tf_op jit(solution)/shard_map/ppermute | solution.py:720
  7.4 5.0 %shard_map.220 = (bf16[512,768]{1,0:T(8,128)(2,1)}, bf16[512,192]{1,0:T(8,128)(2,1)}, bf16[512,384]{1,0:T(8,128)(2,1)}, bf16[768,768]{1,0:T(8,128)(2,1)}, bf16[3...) custom-call(s32[1]{0:T(128)} %bitcast.1.refs_0_, s32[1]{0:T(128)} %bitcast.refs_1_.refs_0_, bf16[512,768]{1,0:T(8,128)(2,1)} %bitcast.18, ...), custom_call_target="tpu_custom_call" | custom-call | flops 4398046511104 | tf_op jit(solution)/shard_map/pallas_call | solution.py:104
  12.4 5.4 %shard_map.221 = (bf16[192,512]{1,0:T(8,128)(2,1)}, f32[192,512]{1,0:T(8,128)}, f32[8,512]{1,0:T(8,128)}) custom-call(s32[1]{0:T(128)} %bitcast.refs_1_.refs_0_, bf16[512,192]{1,0:T(8,128)(2,1)} %get-tuple-element.84.refs_1_.refs_2_, bf16[512,384]{1,0:T(8,128)(2,1)} %get-tuple-element.85.refs_2_.refs_5_, ...), custom_call_target="tpu_custom_call" | custom-call | tf_op jit(solution)/shard_map/pallas_call | solution.py:104
  17.8 5.6 %collective-permute-done.2.refs_10_ = bf16[192,512]{1,0:T(8,128)(2,1)} collective-permute-done((bf16[192,512]{1,0:T(8,128)(2,1)}, bf16[192,512]{1,0:T(8,128)(2,1)}, u32[]{:S(2)}, u32[]{:S(2)}) %collective-permute-start.2) | collective-permute-done | bytes 196640 | tf_op jit(solution)/shard_map/ppermute | solution.py:720
  23.5 19.5 %all-gather = bf16[768,512]{1,0:T(8,128)(2,1)} all-gather(bf16[192,512]{1,0:T(8,128)(2,1)} %get-tuple-element.89), channel_id=2, replica_groups=mesh['row'=4,'seq'=2,'pat'=4] {'pat'}, dimensions={0}, use_global_device_ids=true | all-gather | bytes 983040 | tf_op jit(solution)/shard_map/all_gather | solution.py:800
  42.9 9.0 %shard_map.222 = (bf16[4,192,512]{2,1,0:T(8,128)(2,1)}, f32[8,768]{1,0:T(8,128)}, bf16[512,768]{1,0:T(8,128)(2,1)}, bf16[512,768]{1,0:T(8,128)(2,1)}, bf16[512,7...) custom-call(s32[1]{0:T(128)} %bitcast.1.refs_0_, ...), custom_call_target="tpu_custom_call" | custom-call | tf_op jit(solution)/shard_map/pallas_call | solution.py:104
  52.0 4.2 %all-to-all-start = ((bf16[4,192,512]{2,1,0:T(8,128)(2,1)}), bf16[4,192,512]{2,1,0:T(8,128)(2,1)}, u32[]{:S(2)}, u32[]{:S(2)}) async-start(bf16[4,192,512]{2,1,0:T(8,128)(2,1)} %get-tuple-element.101), calls=%async_computation | async-start | bytes 1572864 | tf_op jit(solution)/shard_map/all_to_all | solution.py:813
  56.2 7.2 %shard_map.223 = (bf16[4,768,128]{2,1,0:T(8,128)(2,1)}, bf16[3,4,96,768]{3,2,1,0:T(8,128)(2,1)}, bf16[4,96,768]{2,1,0:T(8,128)(2,1)}, bf16[4,96,768]{2,1,0:T(8,128)(2,1)}, bf16[4,96,768]{2,1,0:T(8,128)(2,1)}) custom-call(s32[1]{0:T(128)} %bitcast.refs_1_.refs_0_, bf16[512,768]{1,0:T(8,128)(2,1)} %get-tuple-element.94.refs_1_, ...), custom_call_target="tpu_custom_call" | custom-call | flops 4398046511104 | tf_op jit(solution)/shard_map/pallas_call | solution.py:104
  67.5 3.4 %shard_map.227 = (bf16[3,96,768]{2,1,0:T(8,128)(2,1)}, bf16[3,96,768]{2,1,0:T(8,128)(2,1)}, bf16[3,96,768]{2,1,0:T(8,128)(2,1)}, bf16[3,96,768]{2,1,0:T(8,128)(2,1)}) custom-call(s32[1]{0:T(128)} %bitcast.9.refs_0_, bf16[3,4,96,768]{3,2,1,0:T(8,128)(2,1)} %get-tuple-element.112.refs_1_, bf16[4,96,768]{2,1,0:T(8,128)(2,1)} %copy-done.2, ...), custom_call_target="tpu_custom_call" | custom-call | tf_op jit(solution)/shard_map/pallas_call | solution.py:104
  74.4 5.0 %all-to-all-start.1 = ((bf16[4,768,128]{2,1,0:T(8,128)(2,1)}), bf16[4,768,128]{2,1,0:T(8,128)(2,1)}, u32[]{:S(2)}, u32[]{:S(2)}) async-start(bf16[4,768,128]{2,1,0:T(8,128)(2,1)} %get-tuple-element.102), calls=%async_computation.1 | async-start | bytes 1572864 | tf_op jit(solution)/shard_map/all_to_all | solution.py:835
  79.5 5.7 %shard_map.225 = (bf16[512,192]{1,0:T(8,128)(2,1)}, f32[512,384]{1,0:T(8,128)}, bf16[512,384]{1,0:T(8,128)(2,1)}) custom-call(s32[1]{0:T(128)} %bitcast.refs_1_.refs_0_, bf16[4,192,512]{2,1,0:T(8,128)(2,1)} %all-to-all-done.refs_1_, bf16[512,192]{1,0:T(8,128)(2,1)} %get-tuple-element.84.refs_1_.refs_2_, f32[192,512]{1,0:T(8,128)} %get-tuple-element.103.refs_3_, ...), custom_call_target="tpu_custom_call" | custom-call | flops 4398046511104 | tf_op jit(solution)/shard_map/pallas_call | solution.py:104
  89.1 5.9 %shard_map.226 = (bf16[4,768,128]{2,1,0:T(8,128)(2,1)}, bf16[1,4,96,640]{3,2,1,0:T(8,128)(2,1)}, bf16[4,96,640]{2,1,0:T(8,128)(2,1)}) custom-call(s32[1]{0:T(128)} %bitcast.refs_1_.refs_0_, bf16[512,192]{1,0:T(8,128)(2,1)} %get-tuple-element.105.refs_1_, f32[512,384]{1,0:T(8,128)} %get-tuple-element.106.refs_2_, bf16[512,384]{1,0:T(8,128)(2,1)} %copy-done.3, ...), custom_call_target="tpu_custom_call" | custom-call | tf_op jit(solution)/shard_map/pallas_call | solution.py:104
  95.5 3.3 %shard_map.228 = (bf16[4,192,768]{2,1,0:T(8,128)(2,1)}, bf16[4,48,384]{2,1,0:T(8,128)(2,1)}) custom-call(bf16[3,96,768]{2,1,0:T(8,128)(2,1)S(1)} %copy-done, bf16[3,96,768]{2,1,0:T(8,128)(2,1)} %collective-permute-done.8.refs_1_, bf16[3,96,768]{2,1,0:T(8,128)(2,1)} %collective-permute-done.9.refs_2_, bf16[3,96,768]{2,1,0:T(8,128)(2,1)} %collective-permute-done.10.refs_3_), custom_call_target="tpu_custom_call" | custom-call | tf_op jit(solution)/shard_map/pallas_call | solution.py:104
  98.8 2.6 %shard_map.229 = (bf16[1,96,640]{2,1,0:T(8,128)(2,1)}, bf16[1,96,640]{2,1,0:T(8,128)(2,1)}, bf16[1,96,640]{2,1,0:T(8,128)(2,1)}, bf16[1,96,640]{2,1,0:T(8,128)(2,1)}) custom-call(s32[1]{0:T(128)} %bitcast.9.refs_0_, bf16[1,4,96,640]{3,2,1,0:T(8,128)(2,1)} %get-tuple-element.121.refs_1_, bf16[4,96,640]{2,1,0:T(8,128)(2,1)} %collective-permute-done.11.refs_2_), custom_call_target="tpu_custom_call" | custom-call | tf_op jit(solution)/shard_map/pallas_call | solution.py:104
  104.9 4.8 %all-to-all-start.2 = ((bf16[4,48,384]{2,1,0:T(8,128)(2,1)}), bf16[4,48,384]{2,1,0:T(8,128)(2,1)}, u32[]{:S(2)}, u32[]{:S(2)}) async-start(bf16[4,48,384]{2,1,0:T(8,128)(2,1)} %get-tuple-element.130), calls=%async_computation.2 | async-start | bytes 294912 | tf_op jit(solution)/shard_map/all_to_all | solution.py:879
  109.7 2.5 %shard_map.224 = bf16[192,512]{1,0:T(8,128)(2,1)} custom-call(bf16[4,768,128]{2,1,0:T(8,128)(2,1)} %all-to-all-done.1.refs_0_), custom_call_target="tpu_custom_call" | custom-call | flops 4398046511104 | tf_op jit(solution)/shard_map/pallas_call | solution.py:104
  112.3 3.6 %all-to-all-done.2.refs_4_ = bf16[4,48,384]{2,1,0:T(8,128)(2,1)} async-done(((bf16[4,48,384]{2,1,0:T(8,128)(2,1)}), bf16[4,48,384]{2,1,0:T(8,128)(2,1)}, u32[]{:S(2)}, u32[]{:S(2)}) %all-to-all-start.2) | async-done | bytes 147488 | tf_op jit(solution)/shard_map/all_to_all | solution.py:879
  115.8 3.7 %all-to-all-start.3 = ((bf16[4,192,768]{2,1,0:T(8,128)(2,1)}), bf16[4,192,768]{2,1,0:T(8,128)(2,1)S(1)}, u32[]{:S(2)}, u32[]{:S(2)}) async-start(bf16[4,192,768]{2,1,0:T(8,128)(2,1)} %get-tuple-element.131), calls=%async_computation.3 | async-start | bytes 2359296 | tf_op jit(solution)/shard_map/all_to_all | solution.py:919
  119.5 2.3 %shard_map.230 = bf16[112,768]{1,0:T(8,128)(2,1)S(1)} custom-call(bf16[1,96,640]{2,1,0:T(8,128)(2,1)S(1)} %copy-done.1, bf16[1,96,640]{2,1,0:T(8,128)(2,1)} %collective-permute-done.12.refs_1_, bf16[1,96,640]{2,1,0:T(8,128)(2,1)} %collective-permute-done.13.refs_2_, bf16[1,96,640]{2,1,0:T(8,128)(2,1)} %collective-permute-done.14.refs_3_, ...), custom_call_target="tpu_custom_call" | custom-call | tf_op jit(solution)/shard_map/pallas_call | solution.py:104
  121.8 16.7 %all-gather.1 = bf16[448,768]{1,0:T(8,128)(2,1)S(1)} all-gather(bf16[112,768]{1,0:T(8,128)(2,1)S(1)} %shard_map.230), channel_id=3, replica_groups=mesh['row'=4,'seq'=2,'pat'=4] {'pat'}, dimensions={0}, use_global_device_ids=true | all-gather | bytes 860160 | tf_op jit(solution)/shard_map/all_gather | solution.py:915
  142.6 3.8 %all-to-all-start.4 = ((bf16[4,768,128]{2,1,0:T(8,128)(2,1)}), bf16[4,768,128]{2,1,0:T(8,128)(2,1)S(1)}, u32[]{:S(2)}, u32[]{:S(2)}) async-start(bf16[4,768,128]{2,1,0:T(8,128)(2,1)} %get-tuple-element.133), calls=%async_computation.4 | async-start | bytes 1572864 | tf_op jit(solution)/shard_map/all_to_all | solution.py:921
  146.4 3.3 %collective-permute-done.17.refs_6_ = bf16[4,96,768]{2,1,0:T(8,128)(2,1)} collective-permute-done((bf16[4,96,768]{2,1,0:T(8,128)(2,1)S(1)}, bf16[4,96,768]{2,1,0:T(8,128)(2,1)}, u32[]{:S(2)}, u32[]{:S(2)}) %collective-permute-start.17) | collective-permute-done | bytes 589856 | tf_op jit(solution)/shard_map/ppermute | solution.py:720
  154.8 5.7 %shard_map.231 = (f32[768,768]{1,0:T(8,128)}, f32[768,768]{1,0:T(8,128)}, f32[768,768]{1,0:T(8,128)}, f32[768,768]{1,0:T(8,128)}, f32[768,768]{1,0:T(8,128)}, /*index=5*/f32[768,768]{1,0:T(8,128)}) custom-call(s32[1]{0:T(128)} %bitcast.9.refs_0_, s32[1]{0:T(128)} %bitcast.refs_1_.refs_0_, bf16[4,192,768]{2,1,0:T(8,128)(2,1)S(1)} %all-to-all-done.3.refs_2_, ...), custom_call_target="tpu_custom_call" | custom-call | tf_op jit(solution)/shard_map/pallas_call | solution.py:104
  164.3 2.4 %shard_map.232 = (f32[768,768]{1,0:T(8,128)}, f32[768,768]{1,0:T(8,128)}, f32[768,768]{1,0:T(8,128)}, f32[768,768]{1,0:T(8,128)}) custom-call(s32[1]{0:T(128)} %bitcast.9.refs_0_, s32[1]{0:T(128)} %bitcast.refs_1_.refs_0_, ...), custom_call_target="tpu_custom_call", output_to_operand_aliasing={{0}: (6, {}), {1}: (7, {}), {2}: (8, {}), {3}: (9, {})} | custom-call | tf_op jit(solution)/shard_map/pallas_call | solution.py:104
  (65 shorter events, 32.2 us)
Async XLA Ops:
  0.6 5.8 %collective-permute-start = (bf16[512,768]{1,0:T(8,128)(2,1)}, bf16[512,768]{1,0:T(8,128)(2,1)S(1)}, u32[]{:S(2)}, u32[]{:S(2)}) collective-permute-start(bf16[512,768]{1,0:T(8,128)(2,1)} %bitcast.17), channel_id=1, source_target_pairs={{0,4},{4,0},{1,5},{5,1},{2,6},{6,2},{3,7},{7,3},{8,12},{12,8},{9,1... | collective-permute-start | bytes 2359304 | tf_op jit(solution)/shard_map/ppermute | solution.py:716
  1.2 16.7 %collective-permute-start.3 = (bf16[192,512]{1,0:T(8,128)(2,1)}, bf16[192,512]{1,0:T(8,128)(2,1)}, u32[]{:S(2)}, u32[]{:S(2)}) collective-permute-start(bf16[192,512]{1,0:T(8,128)(2,1)} %bitcast.21), channel_id=1, source_target_pairs={{0,3},{1,2},{2,1},{3,0},{4,7},{5,6},{6,5},{7,4},{8,11},{9,10},{10,... | collective-permute-start | bytes 589832 | tf_op jit(solution)/shard_map/ppermute | solution.py:720
  5.8 17.6 %collective-permute-start.2 = (bf16[192,512]{1,0:T(8,128)(2,1)}, bf16[192,512]{1,0:T(8,128)(2,1)}, u32[]{:S(2)}, u32[]{:S(2)}) collective-permute-start(bf16[192,512]{1,0:T(8,128)(2,1)} %bitcast.22), channel_id=1, source_target_pairs={{0,2},{1,3},{2,0},{3,1},{4,6},{5,7},{6,4},{7,5},{8,10},{9,11},{10,... | collective-permute-start | bytes 589832 | tf_op jit(solution)/shard_map/ppermute | solution.py:720
  5.8 17.6 %collective-permute-start.1 = (bf16[192,512]{1,0:T(8,128)(2,1)}, bf16[192,512]{1,0:T(8,128)(2,1)}, u32[]{:S(2)}, u32[]{:S(2)}) collective-permute-start(bf16[192,512]{1,0:T(8,128)(2,1)} %bitcast.23), channel_id=1, source_target_pairs={{0,1},{1,0},{2,3},{3,2},{4,5},{5,4},{6,7},{7,6},{8,9},{9,8},{10,11... | collective-permute-start | bytes 589832 | tf_op jit(solution)/shard_map/ppermute | solution.py:720
  52.0 22.5 %all-to-all-start = ((bf16[4,192,512]{2,1,0:T(8,128)(2,1)}), bf16[4,192,512]{2,1,0:T(8,128)(2,1)}, u32[]{:S(2)}, u32[]{:S(2)}) async-start(bf16[4,192,512]{2,1,0:T(8,128)(2,1)} %get-tuple-element.101), calls=%async_computation | async-start | bytes 1572864 | tf_op jit(solution)/shard_map/all_to_all | solution.py:813
  63.9 3.5 %collective-permute-start.7 = (bf16[4,96,768]{2,1,0:T(8,128)(2,1)}, bf16[4,96,768]{2,1,0:T(8,128)(2,1)}, u32[]{:S(2)}, u32[]{:S(2)}) collective-permute-start(bf16[4,96,768]{2,1,0:T(8,128)(2,1)} %get-tuple-element.115), channel_id=1, source_target_pairs={{0,4},{4,0},{1,5},{5,1},{2,6},{6,2},{3,7},{7,3},{8,12},{12,8},{9,1... | collective-permute-start | bytes 1769480 | tf_op jit(solution)/shard_map/ppermute | solution.py:716
  70.9 24.1 %collective-permute-start.8 = (bf16[3,96,768]{2,1,0:T(8,128)(2,1)}, bf16[3,96,768]{2,1,0:T(8,128)(2,1)}, u32[]{:S(2)}, u32[]{:S(2)}) collective-permute-start(bf16[3,96,768]{2,1,0:T(8,128)(2,1)} %get-tuple-element.117), channel_id=1, source_target_pairs={{0,8},{8,0},{16,24},{24,16},{1,9},{9,1},{17,25},{25,17},{2,10},{10... | collective-permute-start | bytes 1327112 | tf_op jit(solution)/shard_map/ppermute | solution.py:720
  72.5 22.6 %collective-permute-start.9 = (bf16[3,96,768]{2,1,0:T(8,128)(2,1)}, bf16[3,96,768]{2,1,0:T(8,128)(2,1)}, u32[]{:S(2)}, u32[]{:S(2)}) collective-permute-start(bf16[3,96,768]{2,1,0:T(8,128)(2,1)} %get-tuple-element.118), channel_id=1, source_target_pairs={{0,16},{8,24},{16,0},{24,8},{1,17},{9,25},{17,1},{25,9},{2,18},{10... | collective-permute-start | bytes 1327112 | tf_op jit(solution)/shard_map/ppermute | solution.py:720
  74.0 21.1 %collective-permute-start.10 = (bf16[3,96,768]{2,1,0:T(8,128)(2,1)}, bf16[3,96,768]{2,1,0:T(8,128)(2,1)}, u32[]{:S(2)}, u32[]{:S(2)}) collective-permute-start(bf16[3,96,768]{2,1,0:T(8,128)(2,1)} %get-tuple-element.119), channel_id=1, source_target_pairs={{0,24},{8,16},{16,8},{24,0},{1,25},{9,17},{17,9},{25,1},{2,26},{10... | collective-permute-start | bytes 1327112 | tf_op jit(solution)/shard_map/ppermute | solution.py:720
  74.4 30.5 %all-to-all-start.1 = ((bf16[4,768,128]{2,1,0:T(8,128)(2,1)}), bf16[4,768,128]{2,1,0:T(8,128)(2,1)}, u32[]{:S(2)}, u32[]{:S(2)}) async-start(bf16[4,768,128]{2,1,0:T(8,128)(2,1)} %get-tuple-element.102), calls=%async_computation.1 | async-start | bytes 1572864 | tf_op jit(solution)/shard_map/all_to_all | solution.py:835
  95.0 3.7 %collective-permute-start.11 = (bf16[4,96,640]{2,1,0:T(8,128)(2,1)}, bf16[4,96,640]{2,1,0:T(8,128)(2,1)}, u32[]{:S(2)}, u32[]{:S(2)}) collective-permute-start(bf16[4,96,640]{2,1,0:T(8,128)(2,1)} %get-tuple-element.123), channel_id=1, source_target_pairs={{0,4},{4,0},{1,5},{5,1},{2,6},{6,2},{3,7},{7,3},{8,12},{12,8},{9,1... | collective-permute-start | bytes 1474568 | tf_op jit(solution)/shard_map/ppermute | solution.py:716
  101.3 10.9 %collective-permute-start.12 = (bf16[1,96,640]{2,1,0:T(8,128)(2,1)}, bf16[1,96,640]{2,1,0:T(8,128)(2,1)}, u32[]{:S(2)}, u32[]{:S(2)}) collective-permute-start(bf16[1,96,640]{2,1,0:T(8,128)(2,1)} %get-tuple-element.125), channel_id=1, source_target_pairs={{0,8},{8,0},{16,24},{24,16},{1,9},{9,1},{17,25},{25,17},{2,10},{10... | collective-permute-start | bytes 368648 | tf_op jit(solution)/shard_map/ppermute | solution.py:720
  102.9 9.3 %collective-permute-start.13 = (bf16[1,96,640]{2,1,0:T(8,128)(2,1)}, bf16[1,96,640]{2,1,0:T(8,128)(2,1)}, u32[]{:S(2)}, u32[]{:S(2)}) collective-permute-start(bf16[1,96,640]{2,1,0:T(8,128)(2,1)} %get-tuple-element.126), channel_id=1, source_target_pairs={{0,16},{8,24},{16,0},{24,8},{1,17},{9,25},{17,1},{25,9},{2,18},{10... | collective-permute-start | bytes 368648 | tf_op jit(solution)/shard_map/ppermute | solution.py:720
  104.4 7.8 %collective-permute-start.14 = (bf16[1,96,640]{2,1,0:T(8,128)(2,1)}, bf16[1,96,640]{2,1,0:T(8,128)(2,1)}, u32[]{:S(2)}, u32[]{:S(2)}) collective-permute-start(bf16[1,96,640]{2,1,0:T(8,128)(2,1)} %get-tuple-element.127), channel_id=1, source_target_pairs={{0,24},{8,16},{16,8},{24,0},{1,25},{9,17},{17,9},{25,1},{2,26},{10... | collective-permute-start | bytes 368648 | tf_op jit(solution)/shard_map/ppermute | solution.py:720
  104.9 10.9 %all-to-all-start.2 = ((bf16[4,48,384]{2,1,0:T(8,128)(2,1)}), bf16[4,48,384]{2,1,0:T(8,128)(2,1)}, u32[]{:S(2)}, u32[]{:S(2)}) async-start(bf16[4,48,384]{2,1,0:T(8,128)(2,1)} %get-tuple-element.130), calls=%async_computation.2 | async-start | bytes 294912 | tf_op jit(solution)/shard_map/all_to_all | solution.py:879
  115.8 22.7 %all-to-all-start.3 = ((bf16[4,192,768]{2,1,0:T(8,128)(2,1)}), bf16[4,192,768]{2,1,0:T(8,128)(2,1)S(1)}, u32[]{:S(2)}, u32[]{:S(2)}) async-start(bf16[4,192,768]{2,1,0:T(8,128)(2,1)} %get-tuple-element.131), calls=%async_computation.3 | async-start | bytes 2359296 | tf_op jit(solution)/shard_map/all_to_all | solution.py:919
  138.5 11.1 %collective-permute-start.17 = (bf16[4,96,768]{2,1,0:T(8,128)(2,1)S(1)}, bf16[4,96,768]{2,1,0:T(8,128)(2,1)}, u32[]{:S(2)}, u32[]{:S(2)}) collective-permute-start(bf16[4,96,768]{2,1,0:T(8,128)(2,1)S(1)} %slice.9.refs_4_), channel_id=1, source_target_pairs={{0,16},{8,24},{16,0},{24,8},{1,17},{9,25},{17,1},{25,9},{2,18},{10... | collective-permute-start | bytes 1769480 | tf_op jit(solution)/shard_map/ppermute | solution.py:720
  140.6 10.1 %collective-permute-start.15 = (bf16[4,96,768]{2,1,0:T(8,128)(2,1)S(1)}, bf16[4,96,768]{2,1,0:T(8,128)(2,1)}, u32[]{:S(2)}, u32[]{:S(2)}) collective-permute-start(bf16[4,96,768]{2,1,0:T(8,128)(2,1)S(1)} %slice.9.refs_4_), channel_id=1, source_target_pairs={{0,8},{8,0},{16,24},{24,16},{1,9},{9,1},{17,25},{25,17},{2,10},{10... | collective-permute-start | bytes 1769480 | tf_op jit(solution)/shard_map/ppermute | solution.py:720
  142.1 12.7 %collective-permute-start.19 = (bf16[4,192,768]{2,1,0:T(8,128)(2,1)S(1)}, bf16[4,192,768]{2,1,0:T(8,128)(2,1)}, u32[]{:S(2)}, u32[]{:S(2)}) collective-permute-start(bf16[4,192,768]{2,1,0:T(8,128)(2,1)S(1)} %all-to-all-done.3.refs_2_), channel_id=1, source_target_pairs={{0,4},{4,0},{1,5},{5,1},{2,6},{6,2},{3,7},{7,3},{8,12},{12,8},{9,1... | collective-permute-start | bytes 3538952 | tf_op jit(solution)/shard_map/ppermute | solution.py:716
  142.1 11.2 %collective-permute-start.20 = (bf16[4,96,768]{2,1,0:T(8,128)(2,1)S(1)}, bf16[4,96,768]{2,1,0:T(8,128)(2,1)}, u32[]{:S(2)}, u32[]{:S(2)}) collective-permute-start(bf16[4,96,768]{2,1,0:T(8,128)(2,1)S(1)} %slice.9.refs_4_), channel_id=1, source_target_pairs={{0,4},{4,0},{1,5},{5,1},{2,6},{6,2},{3,7},{7,3},{8,12},{12,8},{9,1... | collective-permute-start | bytes 1769480 | tf_op jit(solution)/shard_map/ppermute | solution.py:716
  142.6 24.1 %all-to-all-start.4 = ((bf16[4,768,128]{2,1,0:T(8,128)(2,1)}), bf16[4,768,128]{2,1,0:T(8,128)(2,1)S(1)}, u32[]{:S(2)}, u32[]{:S(2)}) async-start(bf16[4,768,128]{2,1,0:T(8,128)(2,1)} %get-tuple-element.133), calls=%async_computation.4 | async-start | bytes 1572864 | tf_op jit(solution)/shard_map/all_to_all | solution.py:921
  150.6 4.1 %collective-permute-start.22 = (bf16[4,96,768]{2,1,0:T(8,128)(2,1)}, bf16[4,96,768]{2,1,0:T(8,128)(2,1)S(1)}, u32[]{:S(2)}, u32[]{:S(2)}) collective-permute-start(bf16[4,96,768]{2,1,0:T(8,128)(2,1)} %collective-permute-done.17.refs_6_), channel_id=1, source_target_pairs={{0,4},{4,0},{1,5},{5,1},{2,6},{6,2},{3,7},{7,3},{8,12},{12,8},{9,1... | collective-permute-start | bytes 1769480 | tf_op jit(solution)/shard_map/ppermute | solution.py:716
  152.3 9.0 %collective-permute-start.18 = (bf16[2,96,768]{2,1,0:T(8,128)(2,1)S(1)}, bf16[2,96,768]{2,1,0:T(8,128)(2,1)S(1)}, u32[]{:S(2)}, u32[]{:S(2)}) collective-permute-start(bf16[2,96,768]{2,1,0:T(8,128)(2,1)S(1)} %slice.13), channel_id=1, source_target_pairs={{0,8},{8,0},{16,24},{24,16},{1,9},{9,1},{17,25},{25,17},{2,10},{10... | collective-permute-start | bytes 884744 | tf_op jit(solution)/shard_map/ppermute | solution.py:720
  153.3 9.0 %collective-permute-start.16 = (bf16[2,96,768]{2,1,0:T(8,128)(2,1)S(1)}, bf16[2,96,768]{2,1,0:T(8,128)(2,1)S(1)}, u32[]{:S(2)}, u32[]{:S(2)}) collective-permute-start(bf16[2,96,768]{2,1,0:T(8,128)(2,1)S(1)} %slice.12), channel_id=1, source_target_pairs={{0,16},{8,24},{16,0},{24,8},{1,17},{9,25},{17,1},{25,9},{2,18},{10... | collective-permute-start | bytes 884744 | tf_op jit(solution)/shard_map/ppermute | solution.py:720
  (11 other events, 32.4 us)
